TPU v7x, 256 devices: a whole 4x4x8 slice. The times are simulated.
256 devices in a mesh: grp: 8 (over x, core), row: 4 (over y), col: 8 (over z).
Axes of the slice: x: 4, y: 4, z: 8, core: 2. Of those that a mesh axis runs over, the one named last changes fastest.
Arguments:
- amplitudes: bfloat16 [8, 2048, 4608], P('grp', ('row', 'col')), may hold values from -6 to 6
- integrals: bfloat16 [8, 4608, 12288], P('grp', None, ('row', 'col')), may hold values from -0.0546875 to 0.0546875
- block_tiles: int32 [8], replicated, may hold values from 1 to 36, 96 in all
- assign: int32 [8], replicated, may hold values from 0 to 7, each once
Outputs:
- residual: float32 [2048, 12288], P('grp', ('row', 'col'))
Inputs may be any that keep to these rules, and one draw needn't show every extreme that they name: `block_tiles`: the entries sum to 96; the largest is exactly 36. Each block b is held in slot assign[b]; the slots form a permutation, and consecutive slots belong to one group in the order of grp.
All inputs are finite; a program needn't handle non-finite values.
Results may differ from a plain program's by a relative error of at most 0.0003.
Values may be sent and summed in bfloat16 or wider, within the bound.
No kernel may reach another device: no remote copies, remote signals or barrier semaphores. Data moves between devices by JAX's collectives and lax.ppermute only.
A program may use at most 128 MiB of HBM per device.

v0:
```python
import functools

import jax
import jax.numpy as jnp
from jax import lax
from jax.experimental import pallas as pl
from jax.experimental.pallas import tpu as pltpu
from jax.sharding import PartitionSpec as P

TP = 128
ANY = pl.BlockSpec(memory_space=pl.ANY)
SMEM = pl.BlockSpec(memory_space=pltpu.SMEM)
VMEM = pl.BlockSpec(memory_space=pltpu.VMEM)


def balance(tiles_ref, assign_ref, held_ref, block_ref, groups):
    for b in range(groups):
        held_ref[assign_ref[b]] = tiles_ref[b]
        block_ref[assign_ref[b]] = b
    chips = groups // 2
    held = [held_ref[s] for s in range(groups)]
    total = [held[2 * x] + held[2 * x + 1] for x in range(chips)]
    share = 0
    for x in range(chips):
        share = share + total[x]
    share = share // chips
    running, prefix = 0, []
    for x in range(chips):
        running = running + total[x] - share
        prefix.append(running)
    high = functools.reduce(jnp.maximum, prefix)
    low = functools.reduce(jnp.minimum, prefix)
    middle = lax.shift_right_arithmetic(high + low, jnp.int32(1))
    flow = [p - middle for p in prefix]
    right = [jnp.maximum(flow[x], 0) for x in range(chips)]
    left = [jnp.maximum(-flow[(x - 1) % chips], 0) for x in range(chips)]
    return held, total, right, left


def half(n, core):
    first = lax.shift_right_arithmetic(n + 1, jnp.int32(1))
    if isinstance(core, int):
        return (0, first) if core == 0 else (first, n - first)
    return jnp.where(core == 0, 0, first), jnp.where(core == 0, first, n - first)


def pick(values, index):
    out = values[0]
    for i in range(1, len(values)):
        out = jnp.where(index == i, values[i], out)
    return out


def plan(x, core, total, right, left, own):
    chips = len(total)
    if isinstance(x, int):
        xl, xr = (x - 1) % chips, (x + 1) % chips
        from_left, from_right = right[xl], left[xr]
        left_first, kept_first = total[xl] - right[xl], left[x]
    else:
        xl, xr = lax.rem(x + chips - 1, chips), lax.rem(x + 1, chips)
        from_left, from_right = pick(right, xl), pick(left, xr)
        left_first, kept_first = pick(total, xl) - from_left, pick(left, x)
    l0, nl = half(from_left, core)
    r0, nr = half(from_right, core)
    first = own - half(from_left, 0)[1] - half(from_right, 0)[1]
    k0 = core * first if isinstance(core, int) else jnp.where(core == 0, 0, first)
    return (xl, left_first + l0, nl), (xr, r0, nr), (x, kept_first + k0, own - nl - nr)


def pack_amplitudes(groups, own, tiles_ref, assign_ref, src_ref, out_ref, held_ref, block_ref):
    held, total, right, left = balance(tiles_ref, assign_ref, held_ref, block_ref, groups)
    blocks = [block_ref[s] for s in range(groups)]
    for g in range(groups):
        x, c = g // 2, g % 2
        place = 0
        for chip, start, count in plan(x, c, total, right, left, own):
            n0 = jnp.clip(held[2 * chip] - start, 0, count)
            second = jnp.maximum(start - held[2 * chip], 0)
            for block, tile, many in ((blocks[2 * chip], start, n0), (blocks[2 * chip + 1], second, count - n0)):

                def move(i, carry, block=block, tile=tile, place=place):
                    data = src_ref[block, :, pl.ds(pl.multiple_of((tile + i) * TP, TP), TP)]
                    for to in range(2):
                        into = pl.ds(pl.multiple_of((place + i + (own if to != c else 0)) * TP, TP), TP)
                        for j in range(2):
                            out_ref[4 * x + 2 * to + j, :, into] = data
                    return carry

                lax.fori_loop(0, many, move, 0)
                place = place + many


def tile_rows(index):
    return pl.ds(pl.multiple_of(index * TP, TP), TP)


def send_tiles(groups, own, tiles_ref, assign_ref, mine_ref, other_ref, right_ref, left_ref, held_ref, block_ref, sems):
    held, total, right, left = balance(tiles_ref, assign_ref, held_ref, block_ref, groups)
    group = lax.axis_index("grp")
    x, core = lax.div(group, 2), lax.rem(group, 2)
    border = pick(held[0::2], x)
    go_right, go_left = pick(right, x), pick(left, x)
    r0, nr = half(go_right, core)
    l0, nl = half(go_left, core)
    jobs = []
    for way, (ref, start, count) in enumerate(((right_ref, pick(total, x) - go_right + r0, nr), (left_ref, l0, nl))):
        for i in range(own):
            tile = start + i
            upper = (tile >= border).astype(jnp.int32)
            row = tile - upper * border
            for source, here in ((mine_ref, upper == core), (other_ref, upper != core)):
                jobs.append((jnp.logical_and(i < count, here), source, row, ref, i, way * own + i))
    run_copies(jobs, sems)


def run_copies(jobs, sems):
    for go, source, row, ref, i, sem in jobs:

        @pl.when(go)
        def _():
            pltpu.make_async_copy(source.at[tile_rows(row)], ref.at[pl.ds(i * TP, TP)], sems.at[sem]).start()

    for go, source, row, ref, i, sem in jobs:

        @pl.when(go)
        def _():
            pltpu.make_async_copy(source.at[tile_rows(row)], ref.at[pl.ds(i * TP, TP)], sems.at[sem]).wait()


def join_tiles(groups, own, tiles_ref, assign_ref, mine_ref, other_ref, fl_ref, fr_ref, out_ref, held_ref, block_ref, sems):
    held, total, right, left = balance(tiles_ref, assign_ref, held_ref, block_ref, groups)
    group = lax.axis_index("grp")
    x, core = lax.div(group, 2), lax.rem(group, 2)
    border = pick(held[0::2], x)
    (_, _, nl), (_, _, nr), (_, start, _) = plan(x, core, total, right, left, own)
    jobs = []
    for i in range(own):
        jobs.append((i < nl, fl_ref, i, out_ref, i, i))
        jobs.append((jnp.logical_and(i >= nl, i < nl + nr), fr_ref, jnp.maximum(i - nl, 0), out_ref, i, i))
        tile = jnp.maximum(start + i - nl - nr, 0)
        upper = (tile >= border).astype(jnp.int32)
        row = tile - upper * border
        kept = i >= nl + nr
        jobs.append((jnp.logical_and(kept, upper == core), mine_ref, row, out_ref, i, i))
        jobs.append((jnp.logical_and(kept, upper != core), other_ref, row, out_ref, i, i))
    run_copies(jobs, sems)


def multiply(ny, nz, first, *refs):
    count = (len(refs) - 4) // 2
    refs, (b0_ref, b1_ref, out_ref, a_ref) = refs[:-4], refs[-4:]
    x, y = lax.div(lax.axis_index("grp"), 2), lax.axis_index("row")
    parity = lax.rem(y, 2)
    at = 0
    for ref in refs:
        n, octet, wide = ref.shape
        a_ref[at : at + n * octet, :] = ref[...].reshape(n * octet, wide)
        at += n * octet
    mid = b0_ref.shape[0]
    out = jnp.dot(a_ref[:, :mid], b0_ref[...], preferred_element_type=jnp.float32)
    out += jnp.dot(a_ref[:, mid:], b1_ref[...], preferred_element_type=jnp.float32)
    at = 0
    for side in range(2):
        row = 0
        for ref in refs[side * count : (side + 1) * count]:
            n, octet, _ = ref.shape
            for j in range(2):
                d = lax.rem(lax.rem(parity + side, 2) + 2 * j - x + ny, ny)
                for g in range(n // 2):
                    start = at + (2 * g + j) * octet
                    out_ref[d, row + g * octet : row + (g + 1) * octet, :] = out[start : start + octet]
            at += n * octet
            row += n // 2 * octet


def finish(nz, rows, mine_ref, other_ref, out_ref):
    core, z = lax.rem(lax.axis_index("grp"), 2), lax.axis_index("col")
    h = rows // 2
    last = nz // 2 * rows - h
    for q in range(nz // 2):
        r = lax.rem(core * (nz // 2) + q - z + nz, nz)
        ends = jnp.logical_or(r == 0, r == nz // 2)
        above = r < nz // 2
        step = jnp.where(above, r, nz - r)
        for part in range(2):
            start = jnp.where(r == 0, 0, jnp.where(r == nz // 2, last, h + rows * (step - 1) + part * h))
            holder = jnp.where(ends, part, jnp.where(above, 1, 0))
            rows_in = pl.ds(pl.multiple_of(start, h), h)
            for ref, here in ((mine_ref, holder == core), (other_ref, holder != core)):

                @pl.when(here)
                def _(ref=ref, q=q, part=part, rows_in=rows_in):
                    out_ref[q * rows + part * h : q * rows + (part + 1) * h, :] = ref[rows_in, :]


def reduce_x(p, up, down):
    h = p.shape[1] // 2
    a = lax.ppermute(jnp.concatenate([p[2, :h], p[1, h:]]), "grp", up)
    b = lax.ppermute(jnp.concatenate([p[2, h:], p[3, :h]]), "grp", down)
    a2 = lax.ppermute(p[1, :h] + a[:h], "grp", up)
    b2 = lax.ppermute(p[3, h:] + b[:h], "grp", down)
    return p[0] + jnp.concatenate([a2, a[h:]]) + jnp.concatenate([b[h:], b2])


def body(amplitudes, integrals, block_tiles, assign):
    groups = assign.shape[0]
    _, rows, cap = amplitudes.shape
    cols = integrals.shape[2]
    ny, nz = lax.axis_size("row"), lax.axis_size("col")
    own = 12
    wide = own * TP
    octet = rows // groups
    small = [pltpu.SMEM((groups,), jnp.int32)] * 2
    swap = [(g, g ^ 1) for g in range(groups)]
    up = [(g, (g + 2) % groups) for g in range(groups)]
    down = [(g, (g - 2) % groups) for g in range(groups)]
    along = [(g * nz + z, g * nz + (z + 1 - 2 * (g % 2)) % nz) for g in range(groups) for z in range(nz)]
    beside = [(g * ny + y, g * ny + (y - 1 + 2 * (g % 2)) % ny) for g in range(groups) for y in range(ny)]
    pairs = [[g * ny + y for g in range(groups) for y in (p, p + 2)] for p in range(2)]
    barrier = lax.optimization_barrier
    limit = pltpu.CompilerParams(vmem_limit_bytes=32 * 2**20)
    core = lax.rem(lax.axis_index("grp"), 2)

    mine = integrals[0]
    other = lax.ppermute(mine, "grp", swap)
    moved = lax.all_to_all(amplitudes[0].reshape(groups, octet, cap), "grp", 0, 0, tiled=True)
    packed = pl.pallas_call(
        functools.partial(pack_amplitudes, groups, own),
        out_shape=jax.ShapeDtypeStruct((2 * groups, octet, 2 * wide), jnp.bfloat16),
        in_specs=[SMEM, SMEM, VMEM],
        out_specs=VMEM,
        scratch_shapes=small,
    )(block_tiles, assign, moved)
    pair = lax.all_to_all(packed, ("grp", "row"), 0, 0, axis_index_groups=pairs, tiled=True)

    sends = jax.ShapeDtypeStruct((wide, cols), jnp.bfloat16)
    to_right, to_left = pl.pallas_call(
        functools.partial(send_tiles, groups, own),
        out_shape=(sends, sends),
        in_specs=[SMEM, SMEM, ANY, ANY],
        out_specs=(VMEM, VMEM),
        scratch_shapes=small + [pltpu.SemaphoreType.DMA((2 * own,))],
        compiler_params=limit,
    )(block_tiles, assign, mine, other)
    pair, to_right, to_left = barrier((pair, to_right, to_left))
    from_left = lax.ppermute(to_right, "grp", up)
    from_right = lax.ppermute(to_left, "grp", down)

    def half_of(block):
        return jnp.where(core == 0, block[:groups], block[groups:])

    def z_step(block):
        return lax.ppermute(block, ("grp", "col"), along)

    def y_step(block):
        return lax.ppermute(block, ("grp", "row"), beside)

    w0 = half_of(pair)
    w1, v0 = barrier((z_step(pair), y_step(w0)))
    w2, v1 = barrier((z_step(w1), y_step(w1)))
    w3, v2 = barrier((z_step(w2), y_step(w2)))
    w4, v3 = z_step(half_of(w3)), y_step(w3)
    v4 = y_step(w4)

    held = pl.pallas_call(
        functools.partial(join_tiles, groups, own),
        out_shape=sends,
        in_specs=[SMEM, SMEM, ANY, ANY, ANY, ANY],
        out_specs=VMEM,
        scratch_shapes=small + [pltpu.SemaphoreType.DMA((own,))],
        compiler_params=limit,
    )(block_tiles, assign, mine, other, from_left, from_right)
    theirs = lax.ppermute(held, "grp", swap)

    def sums(*parts):
        n = sum(part.shape[0] for part in parts) * octet
        return pl.pallas_call(
            functools.partial(multiply, ny, nz, 0),
            out_shape=jax.ShapeDtypeStruct((ny, n // 4, cols), jnp.float32),
            in_specs=[VMEM] * (len(parts) + 2),
            out_specs=VMEM,
            scratch_shapes=[pltpu.VMEM((n, 2 * wide), jnp.bfloat16)],
            compiler_params=limit,
        )(*parts, held, theirs)

    early = reduce_x(sums(w0, w1, w2, v0, v1, v2), up, down)
    late = reduce_x(sums(w3, w4, v3, v4), up, down)
    done = jnp.concatenate([early, late])
    return pl.pallas_call(
        functools.partial(finish, nz, rows),
        out_shape=jax.ShapeDtypeStruct((nz // 2 * rows, cols), jnp.float32),
        in_specs=[VMEM, VMEM],
        out_specs=VMEM,
    )(done, lax.ppermute(done, "grp", swap))


def solution(mesh):
    in_specs = (P("grp", ("row", "col"), None), P("grp", None, ("row", "col")), P(), P())
    out_specs = P("grp", ("row", "col"))
    return jax.shard_map(body, mesh=mesh, in_specs=in_specs, out_specs=out_specs, check_vma=False)
```

profile of v0, /device:TPU:1, one launch (start us, length us, event | category | flops | bytes accessed | tf_op | source)
XLA Modules:
  0.0 128.0 jit_solution(4748650934126725785)
XLA Ops:
  0.0 3.2 %collective-permute-start = (bf16[4608,384]{1,0:T(8,128)(2,1)}, bf16[4608,384]{1,0:T(8,128)(2,1)}, u32[]{:S(2)}, u32[]{:S(2)}) collective-permute-start(bf16[4608,384]{1,0:T(8,128)(2,1)} %bitcast.46), channel_id=1, source_target_pairs={{0,32},{32,0},{64,96},{96,64},{128,160},{160,128},{192,224},{224,1... | collective-permute-start | bytes 10616840 | tf_op jit(solution)/shard_map/ppermute | solution.py:226
  3.2 14.8 %all_to_all.10.src_ref = bf16[8,8,4608]{2,1,0:T(8,128)(2,1)} all-to-all(bf16[8,8,4608]{2,1,0:T(8,128)(2,1)} %bitcast.49), channel_id=1, replica_groups=mesh['grp'=8,'row'=4,'col'=8] {'grp'}, dimensions={0} | all-to-all | bytes 1179648 | tf_op jit(solution)/shard_map/all_to_all | solution.py:227
  18.0 3.3 %shard_map.46 = bf16[16,8,3072]{2,1,0:T(8,128)(2,1)} custom-call(s32[8]{0:T(128)} %tiles_ref.5, s32[8]{0:T(128)} %assign_ref.5, bf16[8,8,4608]{2,1,0:T(8,128)(2,1)} %all_to_all.10.src_ref), custom_call_target="tpu_custom_call" | custom-call | tf_op jit(solution)/shard_map/pallas_call | solution.py:228
  21.3 4.8 %all-to-all-start.1 = ((bf16[16,8,3072]{2,1,0:T(8,128)(2,1)}), bf16[16,8,3072]{2,1,0:T(8,128)(2,1)}, u32[]{:S(2)}, u32[]{:S(2)}) async-start(bf16[16,8,3072]{2,1,0:T(8,128)(2,1)} %shard_map.46), calls=%async_computation.1 | async-start | bytes 1572864 | tf_op jit(solution)/shard_map/all_to_all | solution.py:235
  26.1 0.0 collective-permute-done.other_ref
  26.1 0.0 copy-done
  26.1 0.0 copy-done.1
  26.1 0.0 copy-done.2
  26.1 1.9 %shard_map.47 = (bf16[1536,384]{1,0:T(8,128)(2,1)S(1)}, bf16[1536,384]{1,0:T(8,128)(2,1)S(1)}) custom-call(s32[8]{0:T(128)S(1)} %copy-done.1, s32[8]{0:T(128)S(1)} %copy-done.2, bf16[4608,384]{1,0:T(8,128)(2,1)S(1)} %bitcast.47, bf16[4608,384]{1,0:T(8,128)(2,1)} %collective-permute-done.other_ref), custom_call_target="tpu_custom_call" | custom-call | tf_op jit(solution)/shard_map/pallas_call | solution.py:238
  28.0 0.0 copy-start.3
  28.0 1.0 copy-done.3
  29.1 1.0 copy-done.5
  30.1 12.3 %all-to-all-done.1 = bf16[16,8,3072]{2,1,0:T(8,128)(2,1)} async-done(((bf16[16,8,3072]{2,1,0:T(8,128)(2,1)}), bf16[16,8,3072]{2,1,0:T(8,128)(2,1)}, u32[]{:S(2)}, u32[]{:S(2)}) %all-to-all-start.1) | async-done | bytes 786464 | tf_op jit(solution)/shard_map/all_to_all | solution.py:235
  42.4 5.2 %collective-permute-start.1 = (bf16[16,8,3072]{2,1,0:T(8,128)(2,1)}, bf16[16,8,3072]{2,1,0:T(8,128)(2,1)S(1)}, u32[]{:S(2)}, u32[]{:S(2)}) collective-permute-start(bf16[16,8,3072]{2,1,0:T(8,128)(2,1)} %all-to-all-done.1), channel_id=1, source_target_pairs={{0,1},{1,2},{2,3},{3,4},{4,5},{5,6},{6,7},{7,0},{32,39},{33,32},{3... | collective-permute-start | bytes 2359304 | tf_op jit(solution)/shard_map/ppermute | solution.py:254
  47.5 1.2 slice_select_fusion.1.refs_0_
  48.7 0.5 collective-permute-start.2
  49.2 7.7 %collective-permute-done.2.refs_3_ = bf16[8,8,3072]{2,1,0:T(8,128)(2,1)S(1)} collective-permute-done((bf16[8,8,3072]{2,1,0:T(8,128)(2,1)S(1)}, bf16[8,8,3072]{2,1,0:T(8,128)(2,1)S(1)}, u32[]{:S(2)}, u32[]{:S(2)}) %collective-permute-start.2) | collective-permute-done | bytes 393248 | tf_op jit(solution)/shard_map/ppermute | solution.py:257
  56.9 0.0 collective-permute-done.1.refs_1_
  56.9 2.9 %collective-permute-start.3 = (bf16[16,8,3072]{2,1,0:T(8,128)(2,1)S(1)}, bf16[16,8,3072]{2,1,0:T(8,128)(2,1)S(1)}, u32[]{:S(2)}, u32[]{:S(2)}) collective-permute-start(bf16[16,8,3072]{2,1,0:T(8,128)(2,1)S(1)} %collective-permute-done.1.refs_1_), channel_id=1, source_target_pairs={{0,1},{1,2},{2,3},{3,4},{4,5},{5,6},{6,7},{7,0},{32,39},{33,32},{3... | collective-permute-start | bytes 2359304 | tf_op jit(solution)/shard_map/ppermute | solution.py:254
  59.8 0.4 collective-permute-start.4
  60.2 0.0 collective-permute-start.7
  60.2 0.0 copy-done.4
  60.2 2.7 %collective-permute-start.8 = (bf16[1536,384]{1,0:T(8,128)(2,1)S(1)}, bf16[1536,384]{1,0:T(8,128)(2,1)S(1)}, u32[]{:S(2)}, u32[]{:S(2)}) collective-permute-start(bf16[1536,384]{1,0:T(8,128)(2,1)S(1)} %copy-done.4), channel_id=1, source_target_pairs={{0,192},{32,224},{64,0},{96,32},{128,64},{160,96},{192,128},{224,1... | collective-permute-start | bytes 3538952 | tf_op jit(solution)/shard_map/ppermute | solution.py:248
  62.9 5.9 %collective-permute-done.3.refs_2_ = bf16[16,8,3072]{2,1,0:T(8,128)(2,1)S(1)} collective-permute-done((bf16[16,8,3072]{2,1,0:T(8,128)(2,1)S(1)}, bf16[16,8,3072]{2,1,0:T(8,128)(2,1)S(1)}, u32[]{:S(2)}, u32[]{:S(2)}) %collective-permute-start.3) | collective-permute-done | bytes 786464 | tf_op jit(solution)/shard_map/ppermute | solution.py:254
  68.7 3.4 %collective-permute-done.4.refs_4_ = bf16[16,8,3072]{2,1,0:T(8,128)(2,1)S(1)} collective-permute-done((bf16[16,8,3072]{2,1,0:T(8,128)(2,1)S(1)}, bf16[16,8,3072]{2,1,0:T(8,128)(2,1)S(1)}, u32[]{:S(2)}, u32[]{:S(2)}) %collective-permute-start.4) | collective-permute-done | bytes 786464 | tf_op jit(solution)/shard_map/ppermute | solution.py:257
  72.2 0.0 collective-permute-start.5
  72.2 0.4 collective-permute-start.6
  72.6 15.6 %collective-permute-done.7.fl_ref = bf16[1536,384]{1,0:T(8,128)(2,1)S(1)} collective-permute-done((bf16[1536,384]{1,0:T(8,128)(2,1)}, bf16[1536,384]{1,0:T(8,128)(2,1)S(1)}, u32[]{:S(2)}, u32[]{:S(2)}) %collective-permute-start.7) | collective-permute-done | bytes 1179680 | tf_op jit(solution)/shard_map/ppermute | solution.py:247
  88.1 0.0 collective-permute-done.8.fr_ref
  88.1 2.7 %shard_map.48.refs_6_.refs_4_ = bf16[1536,384]{1,0:T(8,128)(2,1)S(1)} custom-call(s32[8]{0:T(128)S(1)} %copy-done.1, s32[8]{0:T(128)S(1)} %copy-done.2, bf16[4608,384]{1,0:T(8,128)(2,1)S(1)} %bitcast.48, bf16[4608,384]{1,0:T(8,128)(2,1)} %collective-permute-done.other_ref, bf16[1536,384]{1,0:T(8,128)(2,1)S(1)} %collective-permute-done.7.fl_ref, ...), custom_call_target="tpu_custom_call" | custom-call | tf_op jit(solution)/shard_map/pallas_call | solution.py:266
  90.9 0.1 collective-permute-start.9
  91.0 0.0 collective-permute-done.5.refs_0_
  91.0 0.0 collective-permute-done.6.refs_5_
  91.0 2.4 %collective-permute-start.14 = (bf16[8,8,3072]{2,1,0:T(8,128)(2,1)S(1)}, bf16[8,8,3072]{2,1,0:T(8,128)(2,1)S(1)}, u32[]{:S(2)}, u32[]{:S(2)}) collective-permute-start(bf16[8,8,3072]{2,1,0:T(8,128)(2,1)S(1)} %slice_select_fusion), channel_id=1, source_target_pairs={{0,1},{1,2},{2,3},{3,4},{4,5},{5,6},{6,7},{7,0},{32,39},{33,32},{3... | collective-permute-start | bytes 1179656 | tf_op jit(solution)/shard_map/ppermute | solution.py:254
  93.4 0.3 collective-permute-start.15
  93.7 0.1 collective-permute-done.9.refs_7_.refs_5_
  93.8 2.2 %shard_map.49 = f32[4,160,384]{2,1,0:T(8,128)S(1)} custom-call(bf16[8,8,3072]{2,1,0:T(8,128)(2,1)S(1)} %slice_select_fusion.1.refs_0_, bf16[16,8,3072]{2,1,0:T(8,128)(2,1)S(1)} %collective-permute-done.1.refs_1_, bf16[16,8,3072]{2,1,0:T(8,128)(2,1)S(1)} %collective-permute-done.3.refs_2_, bf16[8,8,3072]{2,1,0:T(8,128)(2,1)S(1)} %collective-permute-done.2.refs_3_, ...), custom_call_target="tpu_custom_call" | custom-call | tf_op jit(solution)/shard_map/pallas_call | solution.py:278
  96.0 2.1 %collective-permute-done.14.refs_1_ = bf16[8,8,3072]{2,1,0:T(8,128)(2,1)S(1)} collective-permute-done((bf16[8,8,3072]{2,1,0:T(8,128)(2,1)S(1)}, bf16[8,8,3072]{2,1,0:T(8,128)(2,1)S(1)}, u32[]{:S(2)}, u32[]{:S(2)}) %collective-permute-start.14) | collective-permute-done | bytes 393248 | tf_op jit(solution)/shard_map/ppermute | solution.py:254
  98.1 2.2 %collective-permute-start.16 = (bf16[8,8,3072]{2,1,0:T(8,128)(2,1)S(1)}, bf16[8,8,3072]{2,1,0:T(8,128)(2,1)S(1)}, u32[]{:S(2)}, u32[]{:S(2)}) collective-permute-start(bf16[8,8,3072]{2,1,0:T(8,128)(2,1)S(1)} %collective-permute-done.14.refs_1_), channel_id=1, source_target_pairs={{0,24},{8,0},{16,8},{24,16},{32,40},{40,48},{48,56},{56,32},{64,88... | collective-permute-start | bytes 1179656 | tf_op jit(solution)/shard_map/ppermute | solution.py:257
  100.4 0.1 collective-permute-start.10
  100.5 2.7 %collective-permute-start.12 = (f32[160,384]{1,0:T(8,128)S(1)}, f32[160,384]{1,0:T(8,128)S(1)}, u32[]{:S(2)}, u32[]{:S(2)}) collective-permute-start(f32[160,384]{1,0:T(8,128)S(1)} %pad_maximum_fusion.2), channel_id=1, source_target_pairs={{0,192},{32,224},{64,0},{96,32},{128,64},{160,96},{192,128},{224,1... | collective-permute-start | bytes 737288 | tf_op jit(solution)/shard_map/ppermute | solution.py:200
  103.3 6.4 %collective-permute-done.16.refs_3_ = bf16[8,8,3072]{2,1,0:T(8,128)(2,1)S(1)} collective-permute-done((bf16[8,8,3072]{2,1,0:T(8,128)(2,1)S(1)}, bf16[8,8,3072]{2,1,0:T(8,128)(2,1)S(1)}, u32[]{:S(2)}, u32[]{:S(2)}) %collective-permute-start.16) | collective-permute-done | bytes 393248 | tf_op jit(solution)/shard_map/ppermute | solution.py:257
  109.7 0.0 collective-permute-done.15.refs_2_
  109.7 1.4 %shard_map.50 = f32[4,96,384]{2,1,0:T(8,128)S(1)} custom-call(bf16[16,8,3072]{2,1,0:T(8,128)(2,1)S(1)} %collective-permute-done.5.refs_0_, bf16[8,8,3072]{2,1,0:T(8,128)(2,1)S(1)} %collective-permute-done.14.refs_1_, bf16[16,8,3072]{2,1,0:T(8,128)(2,1)S(1)} %collective-permute-done.15.refs_2_, bf16[8,8,3072]{2,1,0:T(8,128)(2,1)S(1)} %collective-permute-done.16.refs_3_, ...), custom_call_target="tpu_custom_call" | custom-call | tf_op jit(solution)/shard_map/pallas_call | solution.py:278
  111.1 0.1 collective-permute-start.17
  111.2 2.7 %collective-permute-start.19 = (f32[96,384]{1,0:T(8,128)S(1)}, f32[96,384]{1,0:T(8,128)S(1)}, u32[]{:S(2)}, u32[]{:S(2)}) collective-permute-start(f32[96,384]{1,0:T(8,128)S(1)} %pad_maximum_fusion.4), channel_id=1, source_target_pairs={{0,192},{32,224},{64,0},{96,32},{128,64},{160,96},{192,128},{224,1... | collective-permute-start | bytes 442376 | tf_op jit(solution)/shard_map/ppermute | solution.py:200
  114.0 0.0 collective-permute-done.10
  114.0 0.0 collective-permute-done.12
  114.0 0.1 collective-permute-start.11
  114.1 2.7 %collective-permute-start.13 = (f32[80,384]{1,0:T(8,128)S(1)}, f32[80,384]{1,0:T(8,128)S(1)}, u32[]{:S(2)}, u32[]{:S(2)}) collective-permute-start(f32[80,384]{1,0:T(8,128)S(1)} %get-tuple-element.27), channel_id=1, source_target_pairs={{0,192},{32,224},{64,0},{96,32},{128,64},{160,96},{192,128},{224,1... | collective-permute-start | bytes 368648 | tf_op jit(solution)/shard_map/ppermute | solution.py:202
  116.8 0.5 collective-permute-done.17
  117.2 0.0 collective-permute-done.19
  117.3 1.8 %collective-permute-start.18 = (f32[48,384]{1,0:T(8,128)S(1)}, f32[48,384]{1,0:T(8,128)S(1)}, u32[]{:S(2)}, u32[]{:S(2)}) collective-permute-start(f32[48,384]{1,0:T(8,128)S(1)} %get-tuple-element.34), channel_id=1, source_target_pairs={{0,64},{32,96},{64,128},{96,160},{128,192},{160,224},{192,0},{224,... | collective-permute-start | bytes 221192 | tf_op jit(solution)/shard_map/ppermute | solution.py:201
  119.1 1.4 %collective-permute-start.20 = (f32[48,384]{1,0:T(8,128)S(1)}, f32[48,384]{1,0:T(8,128)S(1)}, u32[]{:S(2)}, u32[]{:S(2)}) collective-permute-start(f32[48,384]{1,0:T(8,128)S(1)} %get-tuple-element.33), channel_id=1, source_target_pairs={{0,192},{32,224},{64,0},{96,32},{128,64},{160,96},{192,128},{224,1... | collective-permute-start | bytes 221192 | tf_op jit(solution)/shard_map/ppermute | solution.py:202
  120.5 0.0 collective-permute-done.11
  120.5 0.0 collective-permute-done.13
  120.5 0.1 fusion.1
  120.5 2.3 %collective-permute-done.18 = f32[48,384]{1,0:T(8,128)S(1)} collective-permute-done((f32[48,384]{1,0:T(8,128)S(1)}, f32[48,384]{1,0:T(8,128)S(1)}, u32[]{:S(2)}, u32[]{:S(2)}) %collective-permute-start.18) | collective-permute-done | bytes 73760 | tf_op jit(solution)/shard_map/ppermute | solution.py:201
  122.8 0.3 collective-permute-done.20
  123.2 0.8 collective-permute-start.21
  124.0 1.3 %collective-permute-done.21.other_ref = f32[256,384]{1,0:T(8,128)S(1)} collective-permute-done((f32[256,384]{1,0:T(8,128)S(1)}, f32[256,384]{1,0:T(8,128)S(1)}, u32[]{:S(2)}, u32[]{:S(2)}) %collective-permute-start.21) | collective-permute-done | bytes 393248 | tf_op jit(solution)/shard_map/ppermute | solution.py:295
  125.3 0.0 copy-done.6
  125.3 0.7 copy-done.7
  126.1 1.9 %shard_map.51 = f32[256,384]{1,0:T(8,128)} custom-call(f32[256,384]{1,0:T(8,128)} %copy-done.6, f32[256,384]{1,0:T(8,128)} %copy-done.7), custom_call_target="tpu_custom_call" | custom-call | tf_op jit(solution)/shard_map/pallas_call | solution.py:290
  (18 shorter events, 0.3 us)
Async XLA Ops:
  0.0 26.1 %collective-permute-start = (bf16[4608,384]{1,0:T(8,128)(2,1)}, bf16[4608,384]{1,0:T(8,128)(2,1)}, u32[]{:S(2)}, u32[]{:S(2)}) collective-permute-start(bf16[4608,384]{1,0:T(8,128)(2,1)} %bitcast.46), channel_id=1, source_target_pairs={{0,32},{32,0},{64,96},{96,64},{128,160},{160,128},{192,224},{224,1... | collective-permute-start | bytes 10616840 | tf_op jit(solution)/shard_map/ppermute | solution.py:226
  3.2 22.8 %copy-start = (bf16[1,4608,384]{2,1,0:T(8,128)(2,1)S(1)}, bf16[1,4608,384]{2,1,0:T(8,128)(2,1)}, u32[]{:S(2)}) copy-start(bf16[1,4608,384]{2,1,0:T(8,128)(2,1)} %param.5) | copy-start | bytes 10616836
  18.0 8.1 %copy-start.1 = (s32[8]{0:T(128)S(1)}, s32[8]{0:T(128)}, u32[]{:S(2)}) copy-start(s32[8]{0:T(128)} %tiles_ref.5) | copy-start | bytes 100
  18.0 8.1 %copy-start.2 = (s32[8]{0:T(128)S(1)}, s32[8]{0:T(128)}, u32[]{:S(2)}) copy-start(s32[8]{0:T(128)} %assign_ref.5) | copy-start | bytes 100
  21.3 21.1 %all-to-all-start.1 = ((bf16[16,8,3072]{2,1,0:T(8,128)(2,1)}), bf16[16,8,3072]{2,1,0:T(8,128)(2,1)}, u32[]{:S(2)}, u32[]{:S(2)}) async-start(bf16[16,8,3072]{2,1,0:T(8,128)(2,1)} %shard_map.46), calls=%async_computation.1 | async-start | bytes 1572864 | tf_op jit(solution)/shard_map/all_to_all | solution.py:235
  28.0 1.0 copy-start.3
  29.1 1.0 copy-start.5
  42.4 17.9 %copy-start.4 = (bf16[1536,384]{1,0:T(8,128)(2,1)S(1)}, bf16[1536,384]{1,0:T(8,128)(2,1)}, u32[]{:S(2)}) copy-start(bf16[1536,384]{1,0:T(8,128)(2,1)} %copy-done.3) | copy-start | bytes 3538948
  42.4 14.6 %collective-permute-start.1 = (bf16[16,8,3072]{2,1,0:T(8,128)(2,1)}, bf16[16,8,3072]{2,1,0:T(8,128)(2,1)S(1)}, u32[]{:S(2)}, u32[]{:S(2)}) collective-permute-start(bf16[16,8,3072]{2,1,0:T(8,128)(2,1)} %all-to-all-done.1), channel_id=1, source_target_pairs={{0,1},{1,2},{2,3},{3,4},{4,5},{5,6},{6,7},{7,0},{32,39},{33,32},{3... | collective-permute-start | bytes 2359304 | tf_op jit(solution)/shard_map/ppermute | solution.py:254
  48.7 8.2 %collective-permute-start.2 = (bf16[8,8,3072]{2,1,0:T(8,128)(2,1)S(1)}, bf16[8,8,3072]{2,1,0:T(8,128)(2,1)S(1)}, u32[]{:S(2)}, u32[]{:S(2)}) collective-permute-start(bf16[8,8,3072]{2,1,0:T(8,128)(2,1)S(1)} %slice_select_fusion.1.refs_0_), channel_id=1, source_target_pairs={{0,24},{8,0},{16,8},{24,16},{32,40},{40,48},{48,56},{56,32},{64,88... | collective-permute-start | bytes 1179656 | tf_op jit(solution)/shard_map/ppermute | solution.py:257
  56.9 11.8 %collective-permute-start.3 = (bf16[16,8,3072]{2,1,0:T(8,128)(2,1)S(1)}, bf16[16,8,3072]{2,1,0:T(8,128)(2,1)S(1)}, u32[]{:S(2)}, u32[]{:S(2)}) collective-permute-start(bf16[16,8,3072]{2,1,0:T(8,128)(2,1)S(1)} %collective-permute-done.1.refs_1_), channel_id=1, source_target_pairs={{0,1},{1,2},{2,3},{3,4},{4,5},{5,6},{6,7},{7,0},{32,39},{33,32},{3... | collective-permute-start | bytes 2359304 | tf_op jit(solution)/shard_map/ppermute | solution.py:254
  59.8 12.3 %collective-permute-start.4 = (bf16[16,8,3072]{2,1,0:T(8,128)(2,1)S(1)}, bf16[16,8,3072]{2,1,0:T(8,128)(2,1)S(1)}, u32[]{:S(2)}, u32[]{:S(2)}) collective-permute-start(bf16[16,8,3072]{2,1,0:T(8,128)(2,1)S(1)} %collective-permute-done.1.refs_1_), channel_id=1, source_target_pairs={{0,24},{8,0},{16,8},{24,16},{32,40},{40,48},{48,56},{56,32},{64,88... | collective-permute-start | bytes 2359304 | tf_op jit(solution)/shard_map/ppermute | solution.py:257
  60.2 27.9 %collective-permute-start.7 = (bf16[1536,384]{1,0:T(8,128)(2,1)}, bf16[1536,384]{1,0:T(8,128)(2,1)S(1)}, u32[]{:S(2)}, u32[]{:S(2)}) collective-permute-start(bf16[1536,384]{1,0:T(8,128)(2,1)} %copy-done.5), channel_id=1, source_target_pairs={{0,64},{32,96},{64,128},{96,160},{128,192},{160,224},{192,0},{224,... | collective-permute-start | bytes 3538952 | tf_op jit(solution)/shard_map/ppermute | solution.py:247
  60.2 27.9 %collective-permute-start.8 = (bf16[1536,384]{1,0:T(8,128)(2,1)S(1)}, bf16[1536,384]{1,0:T(8,128)(2,1)S(1)}, u32[]{:S(2)}, u32[]{:S(2)}) collective-permute-start(bf16[1536,384]{1,0:T(8,128)(2,1)S(1)} %copy-done.4), channel_id=1, source_target_pairs={{0,192},{32,224},{64,0},{96,32},{128,64},{160,96},{192,128},{224,1... | collective-permute-start | bytes 3538952 | tf_op jit(solution)/shard_map/ppermute | solution.py:248
  72.2 18.8 %collective-permute-start.5 = (bf16[16,8,3072]{2,1,0:T(8,128)(2,1)S(1)}, bf16[16,8,3072]{2,1,0:T(8,128)(2,1)S(1)}, u32[]{:S(2)}, u32[]{:S(2)}) collective-permute-start(bf16[16,8,3072]{2,1,0:T(8,128)(2,1)S(1)} %collective-permute-done.3.refs_2_), channel_id=1, source_target_pairs={{0,1},{1,2},{2,3},{3,4},{4,5},{5,6},{6,7},{7,0},{32,39},{33,32},{3... | collective-permute-start | bytes 2359304 | tf_op jit(solution)/shard_map/ppermute | solution.py:254
  72.2 18.8 %collective-permute-start.6 = (bf16[16,8,3072]{2,1,0:T(8,128)(2,1)S(1)}, bf16[16,8,3072]{2,1,0:T(8,128)(2,1)S(1)}, u32[]{:S(2)}, u32[]{:S(2)}) collective-permute-start(bf16[16,8,3072]{2,1,0:T(8,128)(2,1)S(1)} %collective-permute-done.3.refs_2_), channel_id=1, source_target_pairs={{0,24},{8,0},{16,8},{24,16},{32,40},{40,48},{48,56},{56,32},{64,88... | collective-permute-start | bytes 2359304 | tf_op jit(solution)/shard_map/ppermute | solution.py:257
  90.9 2.9 %collective-permute-start.9 = (bf16[1536,384]{1,0:T(8,128)(2,1)S(1)}, bf16[1536,384]{1,0:T(8,128)(2,1)S(1)}, u32[]{:S(2)}, u32[]{:S(2)}) collective-permute-start(bf16[1536,384]{1,0:T(8,128)(2,1)S(1)} %shard_map.48.refs_6_.refs_4_), channel_id=1, source_target_pairs={{0,32},{32,0},{64,96},{96,64},{128,160},{160,128},{192,224},{224,1... | collective-permute-start | bytes 3538952 | tf_op jit(solution)/shard_map/ppermute | solution.py:274
  91.0 7.1 %collective-permute-start.14 = (bf16[8,8,3072]{2,1,0:T(8,128)(2,1)S(1)}, bf16[8,8,3072]{2,1,0:T(8,128)(2,1)S(1)}, u32[]{:S(2)}, u32[]{:S(2)}) collective-permute-start(bf16[8,8,3072]{2,1,0:T(8,128)(2,1)S(1)} %slice_select_fusion), channel_id=1, source_target_pairs={{0,1},{1,2},{2,3},{3,4},{4,5},{5,6},{6,7},{7,0},{32,39},{33,32},{3... | collective-permute-start | bytes 1179656 | tf_op jit(solution)/shard_map/ppermute | solution.py:254
  93.4 16.3 %collective-permute-start.15 = (bf16[16,8,3072]{2,1,0:T(8,128)(2,1)S(1)}, bf16[16,8,3072]{2,1,0:T(8,128)(2,1)S(1)}, u32[]{:S(2)}, u32[]{:S(2)}) collective-permute-start(bf16[16,8,3072]{2,1,0:T(8,128)(2,1)S(1)} %collective-permute-done.5.refs_0_), channel_id=1, source_target_pairs={{0,24},{8,0},{16,8},{24,16},{32,40},{40,48},{48,56},{56,32},{64,88... | collective-permute-start | bytes 2359304 | tf_op jit(solution)/shard_map/ppermute | solution.py:257
  98.1 11.5 %collective-permute-start.16 = (bf16[8,8,3072]{2,1,0:T(8,128)(2,1)S(1)}, bf16[8,8,3072]{2,1,0:T(8,128)(2,1)S(1)}, u32[]{:S(2)}, u32[]{:S(2)}) collective-permute-start(bf16[8,8,3072]{2,1,0:T(8,128)(2,1)S(1)} %collective-permute-done.14.refs_1_), channel_id=1, source_target_pairs={{0,24},{8,0},{16,8},{24,16},{32,40},{40,48},{48,56},{56,32},{64,88... | collective-permute-start | bytes 1179656 | tf_op jit(solution)/shard_map/ppermute | solution.py:257
  100.4 13.6 %collective-permute-start.10 = (f32[160,384]{1,0:T(8,128)S(1)}, f32[160,384]{1,0:T(8,128)S(1)}, u32[]{:S(2)}, u32[]{:S(2)}) collective-permute-start(f32[160,384]{1,0:T(8,128)S(1)} %pad_maximum_fusion.1), channel_id=1, source_target_pairs={{0,64},{32,96},{64,128},{96,160},{128,192},{160,224},{192,0},{224,... | collective-permute-start | bytes 737288 | tf_op jit(solution)/shard_map/ppermute | solution.py:199
  100.5 13.4 %collective-permute-start.12 = (f32[160,384]{1,0:T(8,128)S(1)}, f32[160,384]{1,0:T(8,128)S(1)}, u32[]{:S(2)}, u32[]{:S(2)}) collective-permute-start(f32[160,384]{1,0:T(8,128)S(1)} %pad_maximum_fusion.2), channel_id=1, source_target_pairs={{0,192},{32,224},{64,0},{96,32},{128,64},{160,96},{192,128},{224,1... | collective-permute-start | bytes 737288 | tf_op jit(solution)/shard_map/ppermute | solution.py:200
  111.1 6.1 %collective-permute-start.17 = (f32[96,384]{1,0:T(8,128)S(1)}, f32[96,384]{1,0:T(8,128)S(1)}, u32[]{:S(2)}, u32[]{:S(2)}) collective-permute-start(f32[96,384]{1,0:T(8,128)S(1)} %pad_maximum_fusion.3), channel_id=1, source_target_pairs={{0,64},{32,96},{64,128},{96,160},{128,192},{160,224},{192,0},{224,... | collective-permute-start | bytes 442376 | tf_op jit(solution)/shard_map/ppermute | solution.py:199
  111.2 6.0 %collective-permute-start.19 = (f32[96,384]{1,0:T(8,128)S(1)}, f32[96,384]{1,0:T(8,128)S(1)}, u32[]{:S(2)}, u32[]{:S(2)}) collective-permute-start(f32[96,384]{1,0:T(8,128)S(1)} %pad_maximum_fusion.4), channel_id=1, source_target_pairs={{0,192},{32,224},{64,0},{96,32},{128,64},{160,96},{192,128},{224,1... | collective-permute-start | bytes 442376 | tf_op jit(solution)/shard_map/ppermute | solution.py:200
  114.0 6.5 %collective-permute-start.11 = (f32[80,384]{1,0:T(8,128)S(1)}, f32[80,384]{1,0:T(8,128)S(1)}, u32[]{:S(2)}, u32[]{:S(2)}) collective-permute-start(f32[80,384]{1,0:T(8,128)S(1)} %get-tuple-element.28), channel_id=1, source_target_pairs={{0,64},{32,96},{64,128},{96,160},{128,192},{160,224},{192,0},{224,... | collective-permute-start | bytes 368648 | tf_op jit(solution)/shard_map/ppermute | solution.py:201
  114.1 6.4 %collective-permute-start.13 = (f32[80,384]{1,0:T(8,128)S(1)}, f32[80,384]{1,0:T(8,128)S(1)}, u32[]{:S(2)}, u32[]{:S(2)}) collective-permute-start(f32[80,384]{1,0:T(8,128)S(1)} %get-tuple-element.27), channel_id=1, source_target_pairs={{0,192},{32,224},{64,0},{96,32},{128,64},{160,96},{192,128},{224,1... | collective-permute-start | bytes 368648 | tf_op jit(solution)/shard_map/ppermute | solution.py:202
  117.3 5.5 %collective-permute-start.18 = (f32[48,384]{1,0:T(8,128)S(1)}, f32[48,384]{1,0:T(8,128)S(1)}, u32[]{:S(2)}, u32[]{:S(2)}) collective-permute-start(f32[48,384]{1,0:T(8,128)S(1)} %get-tuple-element.34), channel_id=1, source_target_pairs={{0,64},{32,96},{64,128},{96,160},{128,192},{160,224},{192,0},{224,... | collective-permute-start | bytes 221192 | tf_op jit(solution)/shard_map/ppermute | solution.py:201
  119.1 4.1 %collective-permute-start.20 = (f32[48,384]{1,0:T(8,128)S(1)}, f32[48,384]{1,0:T(8,128)S(1)}, u32[]{:S(2)}, u32[]{:S(2)}) collective-permute-start(f32[48,384]{1,0:T(8,128)S(1)} %get-tuple-element.33), channel_id=1, source_target_pairs={{0,192},{32,224},{64,0},{96,32},{128,64},{160,96},{192,128},{224,1... | collective-permute-start | bytes 221192 | tf_op jit(solution)/shard_map/ppermute | solution.py:202
  123.2 2.1 %copy-start.6 = (f32[256,384]{1,0:T(8,128)}, f32[256,384]{1,0:T(8,128)S(1)}, u32[]{:S(2)}) copy-start(f32[256,384]{1,0:T(8,128)S(1)} %pad_maximum_fusion.mine_ref) | copy-start | bytes 1179652
  123.2 2.1 %collective-permute-start.21 = (f32[256,384]{1,0:T(8,128)S(1)}, f32[256,384]{1,0:T(8,128)S(1)}, u32[]{:S(2)}, u32[]{:S(2)}) collective-permute-start(f32[256,384]{1,0:T(8,128)S(1)} %pad_maximum_fusion.mine_ref), channel_id=1, source_target_pairs={{0,32},{32,0},{64,96},{96,64},{128,160},{160,128},{192,224},{224,1... | collective-permute-start | bytes 1179656 | tf_op jit(solution)/shard_map/ppermute | solution.py:295
  125.3 0.8 copy-start.7
where the time goes:
time: 128 us
  waiting for transfers between devices  57.9 us (45%)
  starting transfers between devices  37.3 us (29%)
  blocking collectives  14.8 us (12%)
  Pallas kernels  13.4 us (10%)
  local copies, waits for them, and re-layouts  2.87 us (2%)
  other arithmetic  1.44 us (1%)
    ppermute x5, waiting for transfers between devices, y_step(): return lax.ppermute(block, ('grp', 'row'), beside)  17.6 us
    ppermute x1, waiting for transfers between devices, body(): from_left = lax.ppermute(to_right, 'grp', up)  15.6 us
    all_to_all x1, blocking collectives, body(): lax.all_to_all(amplitudes[0].reshape(groups, octet, cap), 'grp', 0, 0, ti...  14.8 us
    all_to_all x1, waiting for transfers between devices, body(): lax.all_to_all(packed, ('grp', 'row'), 0, 0, axis_index_groups=pairs, til...  12.3 us
    ppermute x4, starting transfers between devices, z_step(): return lax.ppermute(block, ('grp', 'col'), along)  10.5 us
    ppermute x4, waiting for transfers between devices, z_step(): return lax.ppermute(block, ('grp', 'col'), along)  8 us
    ppermute x2, starting transfers between devices, reduce_x(): b = lax.ppermute(jnp.concatenate([p[2, h:], p[3, :h]]), 'grp', down)  5.47 us
    all_to_all x1, starting transfers between devices, body(): lax.all_to_all(packed, ('grp', 'row'), 0, 0, axis_index_groups=pairs, til...  4.77 us
  transfers between devices with their start and end apart: 23, of which 12 were waited for; matrix products, arithmetic and copies ran while one was open for 1% of the time, Pallas kernels for 9%

commit v1 on v0

v1 whole, which is shorter than its diff:
```python
import functools

import jax
import jax.numpy as jnp
from jax import lax
from jax.experimental import pallas as pl
from jax.experimental.pallas import tpu as pltpu
from jax.sharding import PartitionSpec as P

TP = 128
ANY = pl.BlockSpec(memory_space=pl.ANY)
SMEM = pl.BlockSpec(memory_space=pltpu.SMEM)
VMEM = pl.BlockSpec(memory_space=pltpu.VMEM)


def balance(tiles_ref, assign_ref, held_ref, block_ref, groups):
    for b in range(groups):
        held_ref[assign_ref[b]] = tiles_ref[b]
        block_ref[assign_ref[b]] = b
    chips = groups // 2
    held = [held_ref[s] for s in range(groups)]
    total = [held[2 * x] + held[2 * x + 1] for x in range(chips)]
    share = 0
    for x in range(chips):
        share = share + total[x]
    share = share // chips
    running, prefix = 0, []
    for x in range(chips):
        running = running + total[x] - share
        prefix.append(running)
    high = functools.reduce(jnp.maximum, prefix)
    low = functools.reduce(jnp.minimum, prefix)
    middle = lax.shift_right_arithmetic(high + low, jnp.int32(1))
    flow = [p - middle for p in prefix]
    right = [jnp.maximum(flow[x], 0) for x in range(chips)]
    left = [jnp.maximum(-flow[(x - 1) % chips], 0) for x in range(chips)]
    return held, total, right, left


def pick(values, index):
    out = values[0]
    for i in range(1, len(values)):
        out = jnp.where(index == i, values[i], out)
    return out


def runs_of(x, total, right, left, chips):
    if isinstance(x, int):
        xl, xr = (x - 1) % chips, (x + 1) % chips
        n, m, t, k = right[xl], left[xr], total[xl], left[x]
    else:
        xl, xr = lax.rem(x + chips - 1, chips), lax.rem(x + 1, chips)
        n, m, t, k = pick(right, xl), pick(left, xr), pick(total, xl), pick(left, x)
    return (xl, t - n, n), (xr, 0, m), (x, k, None)


def pack_amplitudes(groups, share, tiles_ref, assign_ref, src_ref, out_ref, held_ref, block_ref):
    held, total, right, left = balance(tiles_ref, assign_ref, held_ref, block_ref, groups)
    blocks = [block_ref[s] for s in range(groups)]
    for x in range(groups // 2):
        place = 0
        for chip, start, count in runs_of(x, total, right, left, groups // 2):
            if count is None:
                count = share - place
            n0 = jnp.clip(held[2 * chip] - start, 0, count)
            second = jnp.maximum(start - held[2 * chip], 0)
            for block, tile, many in ((blocks[2 * chip], start, n0), (blocks[2 * chip + 1], second, count - n0)):

                def move(i, carry, block=block, tile=tile, place=place):
                    data = src_ref[block, :, pl.ds(pl.multiple_of((tile + i) * TP, TP), TP)]
                    into = pl.ds(pl.multiple_of((place + i) * TP, TP), TP)
                    out_ref[2 * x, :, into] = data
                    out_ref[2 * x + 1, :, into] = data
                    return carry

                lax.fori_loop(0, many, move, 0)
                place = place + many


def tile_rows(index):
    return pl.ds(pl.multiple_of(index * TP, TP), TP)


def run_copies(jobs, out_ref, sems):
    for phase in range(2):
        for source, tile, many, place in jobs:

            def move(i, carry, source=source, tile=tile, place=place):
                copy = pltpu.make_async_copy(source.at[tile_rows(tile + i)], out_ref.at[tile_rows(place + i)], sems.at[place + i])
                copy.start() if phase == 0 else copy.wait()
                return carry

            lax.fori_loop(0, many, move, 0)


def own_tiles(border, core, start, count, mine_ref, other_ref, place):
    lower = jnp.clip(border - start, 0, count)
    jobs = []
    for upper, tile, many, at in ((0, start, lower, place), (1, jnp.maximum(start - border, 0), count - lower, place + lower)):
        jobs.append((mine_ref, tile, jnp.where(core == upper, many, 0), at))
        jobs.append((other_ref, tile, jnp.where(core != upper, many, 0), at))
    return jobs


def send_tiles(groups, share, tiles_ref, assign_ref, mine_ref, other_ref, out_ref, held_ref, block_ref, sems):
    held, total, right, left = balance(tiles_ref, assign_ref, held_ref, block_ref, groups)
    group = lax.axis_index("grp")
    x, core = lax.div(group, 2), lax.rem(group, 2)
    go_right, go_left = pick(right, x), pick(left, x)
    start = jnp.where(core == 0, pick(total, x) - go_right, 0)
    count = jnp.where(core == 0, go_right, go_left)
    run_copies(own_tiles(pick(held[0::2], x), core, start, count, mine_ref, other_ref, 0), out_ref, sems)


def join_tiles(groups, share, tiles_ref, assign_ref, mine_ref, other_ref, got_ref, *refs):
    *their_refs, out_ref, held_ref, block_ref, sems = refs
    held, total, right, left = balance(tiles_ref, assign_ref, held_ref, block_ref, groups)
    group = lax.axis_index("grp")
    x, core = lax.div(group, 2), lax.rem(group, 2)
    (_, _, n), (_, _, m), (_, start, _) = runs_of(x, total, right, left, groups // 2)
    jobs = [
        (got_ref, 0, jnp.where(core == 0, n, 0), 0),
        (got_ref, 0, jnp.where(core == 0, 0, m), n),
    ]
    each = share // len(their_refs)
    for i, ref in enumerate(their_refs):
        jobs.append((ref, 0, jnp.clip(jnp.where(core == 0, m, n) - i * each, 0, each), jnp.where(core == 0, n, 0) + i * each))
    jobs += own_tiles(pick(held[0::2], x), core, start, share - n - m, mine_ref, other_ref, n + m)
    run_copies(jobs, out_ref, sems)


def multiply(ny, *refs):
    refs, (b_ref, out_ref, a_ref) = refs[:-3], refs[-3:]
    group, y = lax.axis_index("grp"), lax.axis_index("row")
    x, core = lax.div(group, 2), lax.rem(group, 2)
    near = jnp.where(core == 0, 1, ny - 1)
    at = 0
    for ref in refs:
        n, octet, wide = ref.shape
        a_ref[at : at + n * octet, :] = ref[...].reshape(n * octet, wide)
        at += n * octet
    out = jnp.dot(a_ref[...], b_ref[...], preferred_element_type=jnp.float32)
    at = row = 0
    for i, ref in enumerate(refs):
        n = ref.shape[0] * ref.shape[1]
        d = lax.rem(y + (0, 2, near, near + 2)[i % 4] - x + 2 * ny, ny)
        out_ref[d, row : row + n, :] = out[at : at + n]
        at += n
        row += n if i % 4 == 3 else 0


def finish(nz, rows, mine_ref, other_ref, out_ref):
    core, z = lax.rem(lax.axis_index("grp"), 2), lax.axis_index("col")
    h = rows // 2
    last = nz // 2 * rows - h
    for q in range(nz // 2):
        r = lax.rem(core * (nz // 2) + q - z + nz, nz)
        ends = jnp.logical_or(r == 0, r == nz // 2)
        above = r < nz // 2
        step = jnp.where(above, r, nz - r)
        for part in range(2):
            start = jnp.where(r == 0, 0, jnp.where(r == nz // 2, last, h + rows * (step - 1) + part * h))
            holder = jnp.where(ends, part, jnp.where(above, 1, 0))
            rows_in = pl.ds(pl.multiple_of(start, h), h)
            for ref, here in ((mine_ref, holder == core), (other_ref, holder != core)):

                @pl.when(here)
                def _(ref=ref, q=q, part=part, rows_in=rows_in):
                    out_ref[q * rows + part * h : q * rows + (part + 1) * h, :] = ref[rows_in, :]


def near_chips(p, up, down):
    h = p.shape[1] // 2
    a = lax.ppermute(jnp.concatenate([p[2, :h], p[1, h:]]), "grp", up)
    return a, lax.ppermute(jnp.concatenate([p[2, h:], p[3, :h]]), "grp", down)


def passed_on(p, a, b, up, down):
    h = p.shape[1] // 2
    return lax.ppermute(p[1, :h] + a[:h], "grp", up), lax.ppermute(p[3, h:] + b[:h], "grp", down)


def total_of(p, a, b, a2, b2):
    h = p.shape[1] // 2
    return p[0] + jnp.concatenate([a2, a[h:]]) + jnp.concatenate([b[h:], b2])


def body(amplitudes, integrals, block_tiles, assign):
    groups = assign.shape[0]
    _, rows, cap = amplitudes.shape
    cols = integrals.shape[2]
    ny, nz = lax.axis_size("row"), lax.axis_size("col")
    share = 24
    wide = share * TP
    octet = rows // groups
    small = [pltpu.SMEM((groups,), jnp.int32)] * 2
    swap = [(g, g ^ 1) for g in range(groups)]
    up = [(g, (g + 2) % groups) for g in range(groups)]
    down = [(g, (g - 2) % groups) for g in range(groups)]
    apart = [(g, (g + 2 - 4 * (g % 2)) % groups) for g in range(groups)]
    along = [(g * nz + z, g * nz + (z + 1 - 2 * (g % 2)) % nz) for g in range(groups) for z in range(nz)]
    beside = [(g * ny + y, g * ny + (y - 1 + 2 * (g % 2)) % ny) for g in range(groups) for y in range(ny)]
    across = [(y, (y + 2) % ny) for y in range(ny)]
    limit = pltpu.CompilerParams(vmem_limit_bytes=32 * 2**20)
    core = lax.rem(lax.axis_index("grp"), 2)
    barrier = lax.optimization_barrier

    mine = integrals[0]
    other = lax.ppermute(mine, "grp", swap)
    moved = lax.all_to_all(amplitudes[0].reshape(groups, octet, cap), "grp", 0, 0, tiled=True)
    moved, other = barrier((moved, other))
    packed = pl.pallas_call(
        functools.partial(pack_amplitudes, groups, share),
        out_shape=jax.ShapeDtypeStruct((groups, octet, wide), jnp.bfloat16),
        in_specs=[SMEM, SMEM, VMEM],
        out_specs=VMEM,
        scratch_shapes=small,
    )(block_tiles, assign, moved)
    piece = lax.all_to_all(packed, "grp", 0, 0, tiled=True)

    tiles = jax.ShapeDtypeStruct((wide, cols), jnp.bfloat16)
    scratch = small + [pltpu.SemaphoreType.DMA((share,))]
    sent = pl.pallas_call(
        functools.partial(send_tiles, groups, share),
        out_shape=tiles,
        in_specs=[SMEM, SMEM, ANY, ANY],
        out_specs=VMEM,
        scratch_shapes=scratch,
        compiler_params=limit,
    )(block_tiles, assign, mine, other)
    got = lax.ppermute(sent, "grp", apart)
    def half_of(block):
        h = block.shape[0] // 2
        return jnp.where(core == 0, block[:h], block[h:])

    def z_step(block):
        return lax.ppermute(block, ("grp", "col"), along)

    def y_step(block):
        return lax.ppermute(block, ("grp", "row"), beside)

    chains = [piece, lax.ppermute(piece, "row", across)]
    order = []
    for s in range(nz // 2 - 1):
        here, beside_here = [], []
        for i, block in enumerate(chains):
            kept = half_of(block) if s == 0 else block
            chains[i], other_y = barrier((z_step(block), y_step(kept)))
            here.append(kept)
            beside_here.append(other_y)
        order.append(here + beside_here)
    ends = [z_step(half_of(block)) for block in chains]
    order.append(chains + [y_step(block) for block in chains])

    theirs = [lax.ppermute(part, "grp", swap) for part in jnp.split(got, 2)]
    held = pl.pallas_call(
        functools.partial(join_tiles, groups, share),
        out_shape=tiles,
        in_specs=[SMEM, SMEM] + [ANY] * (3 + len(theirs)),
        out_specs=VMEM,
        scratch_shapes=scratch,
        compiler_params=limit,
    )(block_tiles, assign, mine, other, got, *theirs)

    def sums(steps):
        parts = [part for step in steps for part in step]
        n = sum(part.shape[0] for part in parts) * octet
        return pl.pallas_call(
            functools.partial(multiply, ny),
            out_shape=jax.ShapeDtypeStruct((ny, n // 4, cols), jnp.float32),
            in_specs=[VMEM] * (len(parts) + 1),
            out_specs=VMEM,
            scratch_shapes=[pltpu.VMEM((n, wide), jnp.bfloat16)],
            compiler_params=limit,
        )(*parts, held)

    p = sums(order[:3])
    a, b = near_chips(p, up, down)
    *ends, a, b = barrier((*ends, a, b))
    *beside_ends, a2, b2 = barrier((*map(y_step, ends), *passed_on(p, a, b, up, down)))
    early = total_of(p, a, b, a2, b2)
    p = sums(order[3:] + [ends + beside_ends])
    a, b = near_chips(p, up, down)
    late = total_of(p, a, b, *passed_on(p, a, b, up, down))
    done = jnp.concatenate([early, late])
    return pl.pallas_call(
        functools.partial(finish, nz, rows),
        out_shape=jax.ShapeDtypeStruct((nz // 2 * rows, cols), jnp.float32),
        in_specs=[VMEM, VMEM],
        out_specs=VMEM,
    )(done, lax.ppermute(done, "grp", swap))


def solution(mesh):
    in_specs = (P("grp", ("row", "col"), None), P("grp", None, ("row", "col")), P(), P())
    out_specs = P("grp", ("row", "col"))
    return jax.shard_map(body, mesh=mesh, in_specs=in_specs, out_specs=out_specs, check_vma=False)
```

time: 128 us -> 152 us (1.19)
  starting transfers between devices: 37.3 us -> 62 us
  waiting for transfers between devices: 57.9 us -> 51.3 us
  local copies, waits for them, and re-layouts: 2.87 us -> 6.02 us
  Pallas kernels: 13.4 us -> 15.6 us
    ppermute x4 -> x8, starting transfers between devices: 10.5 us -> 23.4 us  [z_step(): return lax.ppermute(block, ('grp', 'col'), along)]
    all_to_all x1, waiting for transfers between devices: 12.3 us -> 23.9 us  [body(): piece = lax.all_to_all(packed, 'grp', 0, 0, tiled=True)]
    ppermute x5 -> x10, waiting for transfers between devices: 17.6 us -> 8.81 us  [y_step(): return lax.ppermute(block, ('grp', 'row'), beside)]
    ppermute x1, starting transfers between devices: 0.75 us -> 6.68 us  [body(): lax.ppermute(done, 'grp', swap)]
    ppermute x4 -> x8, waiting for transfers between devices: 8 us -> 2.88 us  [z_step(): return lax.ppermute(block, ('grp', 'col'), along)]
    ppermute x5 -> x10, starting transfers between devices: 3.74 us -> 8.48 us  [y_step(): return lax.ppermute(block, ('grp', 'row'), beside)]
    ppermute x11 -> x12, waiting for transfers between devices: 18.8 us -> 14.4 us  [the longest x2 6.73 us: passed_on(): lax.ppermute(p[1, :h] + a[:h], 'grp', up)]
    pallas_call x5, Pallas kernels: 11.5 us -> 13.6 us  [the longest x1 3.82 us: body(): pl.pallas_call(functools.partial(send_tiles, groups, share), out_shape=ti...]
  transfers between devices with their start and end apart: 23 -> 33, of which waited for: 12 -> 16; matrix products, arithmetic and copies ran while one was open for 1% -> 2% of each run, Pallas kernels for 9% -> 6%
where the time goes in v1:
time: 152 us; the launch traced here: 151 us
  starting transfers between devices  62 us (41%)
  waiting for transfers between devices  51.3 us (34%)
  Pallas kernels  15.6 us (10%)
  blocking collectives  14.5 us (10%)
  local copies, waits for them, and re-layouts  6.02 us (4%)
    all_to_all x1, waiting for transfers between devices, body(): piece = lax.all_to_all(packed, 'grp', 0, 0, tiled=True)  23.9 us
    ppermute x8, starting transfers between devices, z_step(): return lax.ppermute(block, ('grp', 'col'), along)  23.4 us
    all_to_all x1, blocking collectives, body(): lax.all_to_all(amplitudes[0].reshape(groups, octet, cap), 'grp', 0, 0, ti...  14.5 us
    ppermute x10, waiting for transfers between devices, y_step(): return lax.ppermute(block, ('grp', 'row'), beside)  8.81 us
    ppermute x10, starting transfers between devices, y_step(): return lax.ppermute(block, ('grp', 'row'), beside)  8.48 us
    ppermute x2, waiting for transfers between devices, passed_on(): lax.ppermute(p[1, :h] + a[:h], 'grp', up)  6.73 us
    ppermute x1, starting transfers between devices, body(): lax.ppermute(done, 'grp', swap)  6.68 us
    all_to_all x1, starting transfers between devices, body(): piece = lax.all_to_all(packed, 'grp', 0, 0, tiled=True)  5.41 us
  transfers between devices with their start and end apart: 33, of which 16 were waited for; matrix products, arithmetic and copies ran while one was open for 2% of the time, Pallas kernels for 6%

profile of v1, /device:TPU:1, one launch (start us, length us, event | category | flops | bytes accessed | tf_op | source)
XLA Modules:
  0.0 151.0 jit_solution(15306661587742889000)
XLA Ops:
  0.0 3.2 %collective-permute-start = (bf16[4608,384]{1,0:T(8,128)(2,1)}, bf16[4608,384]{1,0:T(8,128)(2,1)S(1)}, u32[]{:S(2)}, u32[]{:S(2)}) collective-permute-start(bf16[4608,384]{1,0:T(8,128)(2,1)} %bitcast.46), channel_id=1, source_target_pairs={{0,32},{32,0},{64,96},{96,64},{128,160},{160,128},{192,224},{224,1... | collective-permute-start | bytes 10616840 | tf_op jit(solution)/shard_map/ppermute | solution.py:209
  3.2 14.5 %all_to_all.10.src_ref = bf16[8,8,4608]{2,1,0:T(8,128)(2,1)} all-to-all(bf16[8,8,4608]{2,1,0:T(8,128)(2,1)} %bitcast.49), channel_id=1, replica_groups=mesh['grp'=8,'row'=4,'col'=8] {'grp'}, dimensions={0} | all-to-all | bytes 1179648 | tf_op jit(solution)/shard_map/all_to_all | solution.py:210
  17.8 0.0 collective-permute-done.other_ref
  17.8 2.0 %copy-done = bf16[1,4608,384]{2,1,0:T(8,128)(2,1)S(1)} copy-done((bf16[1,4608,384]{2,1,0:T(8,128)(2,1)S(1)}, bf16[1,4608,384]{2,1,0:T(8,128)(2,1)}, u32[]{:S(2)}) %copy-start) | copy-done | bytes 3538968
  19.8 0.7 copy-done.2
  20.4 0.7 copy-done.4
  21.1 3.8 %shard_map.47 = bf16[3072,384]{1,0:T(8,128)(2,1)} custom-call(s32[8]{0:T(128)S(1)} %copy-done.2, s32[8]{0:T(128)S(1)} %copy-done.4, bf16[4608,384]{1,0:T(8,128)(2,1)S(1)} %bitcast.47, bf16[4608,384]{1,0:T(8,128)(2,1)S(1)} %collective-permute-done.other_ref), custom_call_target="tpu_custom_call" | custom-call | tf_op jit(solution)/shard_map/pallas_call | solution.py:223
  24.9 0.1 collective-permute-start.14
  25.0 2.7 %shard_map.46 = bf16[8,8,3072]{2,1,0:T(8,128)(2,1)} custom-call(s32[8]{0:T(128)} %tiles_ref.5, s32[8]{0:T(128)} %assign_ref.5, bf16[8,8,4608]{2,1,0:T(8,128)(2,1)} %all_to_all.10.src_ref), custom_call_target="tpu_custom_call" | custom-call | tf_op jit(solution)/shard_map/pallas_call | solution.py:212
  27.7 5.4 %all-to-all-start.1 = ((bf16[8,8,3072]{2,1,0:T(8,128)(2,1)}), bf16[8,8,3072]{2,1,0:T(8,128)(2,1)}, u32[]{:S(2)}, u32[]{:S(2)}) async-start(bf16[8,8,3072]{2,1,0:T(8,128)(2,1)} %shard_map.46), calls=%async_computation.1 | async-start | bytes 786432 | tf_op jit(solution)/shard_map/all_to_all | solution.py:219
  33.1 23.9 %all-to-all-done.1 = bf16[8,8,3072]{2,1,0:T(8,128)(2,1)} async-done(((bf16[8,8,3072]{2,1,0:T(8,128)(2,1)}), bf16[8,8,3072]{2,1,0:T(8,128)(2,1)}, u32[]{:S(2)}, u32[]{:S(2)}) %all-to-all-start.1) | async-done | bytes 393248 | tf_op jit(solution)/shard_map/all_to_all | solution.py:219
  57.1 1.5 %collective-permute-start.1 = (bf16[8,8,3072]{2,1,0:T(8,128)(2,1)}, bf16[8,8,3072]{2,1,0:T(8,128)(2,1)S(1)}, u32[]{:S(2)}, u32[]{:S(2)}) collective-permute-start(bf16[8,8,3072]{2,1,0:T(8,128)(2,1)} %all-to-all-done.1), channel_id=1, source_target_pairs={{0,16},{8,24},{16,0},{24,8},{1,17},{9,25},{17,1},{25,9},{2,18},{10... | collective-permute-start | bytes 1179656 | tf_op jit(solution)/shard_map/ppermute | solution.py:242
  58.6 1.0 slice_select_fusion.1.refs_0_
  59.6 0.5 collective-permute-start.3
  60.1 5.6 %collective-permute-start.2 = (bf16[8,8,3072]{2,1,0:T(8,128)(2,1)}, bf16[8,8,3072]{2,1,0:T(8,128)(2,1)S(1)}, u32[]{:S(2)}, u32[]{:S(2)}) collective-permute-start(bf16[8,8,3072]{2,1,0:T(8,128)(2,1)} %all-to-all-done.1), channel_id=1, source_target_pairs={{0,1},{1,2},{2,3},{3,4},{4,5},{5,6},{6,7},{7,0},{32,39},{33,32},{3... | collective-permute-start | bytes 1179656 | tf_op jit(solution)/shard_map/ppermute | solution.py:237
  65.7 2.0 %collective-permute-done.1 = bf16[8,8,3072]{2,1,0:T(8,128)(2,1)S(1)} collective-permute-done((bf16[8,8,3072]{2,1,0:T(8,128)(2,1)}, bf16[8,8,3072]{2,1,0:T(8,128)(2,1)S(1)}, u32[]{:S(2)}, u32[]{:S(2)}) %collective-permute-start.1) | collective-permute-done | bytes 393248 | tf_op jit(solution)/shard_map/ppermute | solution.py:242
  67.7 4.2 %collective-permute-start.4 = (bf16[8,8,3072]{2,1,0:T(8,128)(2,1)S(1)}, bf16[8,8,3072]{2,1,0:T(8,128)(2,1)S(1)}, u32[]{:S(2)}, u32[]{:S(2)}) collective-permute-start(bf16[8,8,3072]{2,1,0:T(8,128)(2,1)S(1)} %collective-permute-done.1), channel_id=1, source_target_pairs={{0,1},{1,2},{2,3},{3,4},{4,5},{5,6},{6,7},{7,0},{32,39},{33,32},{3... | collective-permute-start | bytes 1179656 | tf_op jit(solution)/shard_map/ppermute | solution.py:237
  71.9 0.0 copy-start.1
  71.9 0.0 copy-start.3
  71.9 0.0 copy-start.5
  71.9 1.4 collective-permute-start.5
  73.3 2.7 %collective-permute-start.6 = (bf16[8,8,3072]{2,1,0:T(8,128)(2,1)S(1)}, bf16[8,8,3072]{2,1,0:T(8,128)(2,1)S(1)}, u32[]{:S(2)}, u32[]{:S(2)}) collective-permute-start(bf16[8,8,3072]{2,1,0:T(8,128)(2,1)S(1)} %collective-permute-done.2.refs_4_), channel_id=1, source_target_pairs={{0,1},{1,2},{2,3},{3,4},{4,5},{5,6},{6,7},{7,0},{32,39},{33,32},{3... | collective-permute-start | bytes 1179656 | tf_op jit(solution)/shard_map/ppermute | solution.py:237
  76.0 1.5 collective-permute-start.7
  77.5 0.6 collective-permute-done.5.refs_3_
  78.1 1.6 %collective-permute-start.8 = (bf16[8,8,3072]{2,1,0:T(8,128)(2,1)S(1)}, bf16[8,8,3072]{2,1,0:T(8,128)(2,1)S(1)}, u32[]{:S(2)}, u32[]{:S(2)}) collective-permute-start(bf16[8,8,3072]{2,1,0:T(8,128)(2,1)S(1)} %collective-permute-done.4.refs_5_), channel_id=1, source_target_pairs={{0,1},{1,2},{2,3},{3,4},{4,5},{5,6},{6,7},{7,0},{32,39},{33,32},{3... | collective-permute-start | bytes 1179656 | tf_op jit(solution)/shard_map/ppermute | solution.py:237
  79.7 1.9 %fusion.6 = (bf16[1536,384]{1,0:T(8,128)(2,1)S(1)}, bf16[1536,384]{1,0:T(8,128)(2,1)S(1)}) fusion(bf16[3072,384]{1,0:T(8,128)(2,1)} %collective-permute-done.14.got_ref), kind=kLoop, calls=%fused_computation.31 | loop fusion | bytes 4718592 | tf_op jit(solution)/shard_map/split | solution.py:255
  81.6 3.0 %collective-permute-start.15 = (bf16[1536,384]{1,0:T(8,128)(2,1)S(1)}, bf16[1536,384]{1,0:T(8,128)(2,1)S(1)}, u32[]{:S(2)}, u32[]{:S(2)}) collective-permute-start(bf16[1536,384]{1,0:T(8,128)(2,1)S(1)} %get-tuple-element.50), channel_id=1, source_target_pairs={{0,32},{32,0},{64,96},{96,64},{128,160},{160,128},{192,224},{224,1... | collective-permute-start | bytes 3538952 | tf_op jit(solution)/shard_map/ppermute | solution.py:255
  84.6 0.1 collective-permute-start.16
  84.7 3.0 %collective-permute-start.10 = (bf16[8,8,3072]{2,1,0:T(8,128)(2,1)S(1)}, bf16[8,8,3072]{2,1,0:T(8,128)(2,1)S(1)}, u32[]{:S(2)}, u32[]{:S(2)}) collective-permute-start(bf16[8,8,3072]{2,1,0:T(8,128)(2,1)S(1)} %collective-permute-done.6.refs_8_), channel_id=1, source_target_pairs={{0,1},{1,2},{2,3},{3,4},{4,5},{5,6},{6,7},{7,0},{32,39},{33,32},{3... | collective-permute-start | bytes 1179656 | tf_op jit(solution)/shard_map/ppermute | solution.py:237
  87.8 2.6 %collective-permute-start.11 = (bf16[8,8,3072]{2,1,0:T(8,128)(2,1)S(1)}, bf16[8,8,3072]{2,1,0:T(8,128)(2,1)S(1)}, u32[]{:S(2)}, u32[]{:S(2)}) collective-permute-start(bf16[8,8,3072]{2,1,0:T(8,128)(2,1)S(1)} %collective-permute-done.6.refs_8_), channel_id=1, source_target_pairs={{0,24},{8,0},{16,8},{24,16},{32,40},{40,48},{48,56},{56,32},{64,88... | collective-permute-start | bytes 1179656 | tf_op jit(solution)/shard_map/ppermute | solution.py:240
  90.4 2.5 %collective-permute-done.9.refs_7_ = bf16[8,8,3072]{2,1,0:T(8,128)(2,1)S(1)} collective-permute-done((bf16[8,8,3072]{2,1,0:T(8,128)(2,1)S(1)}, bf16[8,8,3072]{2,1,0:T(8,128)(2,1)S(1)}, u32[]{:S(2)}, u32[]{:S(2)}) %collective-permute-start.9) | collective-permute-done | bytes 393248 | tf_op jit(solution)/shard_map/ppermute | solution.py:240
  92.9 2.7 %collective-permute-start.12 = (bf16[8,8,3072]{2,1,0:T(8,128)(2,1)S(1)}, bf16[8,8,3072]{2,1,0:T(8,128)(2,1)S(1)}, u32[]{:S(2)}, u32[]{:S(2)}) collective-permute-start(bf16[8,8,3072]{2,1,0:T(8,128)(2,1)S(1)} %collective-permute-done.8.refs_9_), channel_id=1, source_target_pairs={{0,1},{1,2},{2,3},{3,4},{4,5},{5,6},{6,7},{7,0},{32,39},{33,32},{3... | collective-permute-start | bytes 1179656 | tf_op jit(solution)/shard_map/ppermute | solution.py:237
  95.5 1.3 collective-permute-done.11.refs_10_
  96.8 3.0 %collective-permute-start.17 = (bf16[4,8,3072]{2,1,0:T(8,128)(2,1)S(1)}, bf16[4,8,3072]{2,1,0:T(8,128)(2,1)S(1)}, u32[]{:S(2)}, u32[]{:S(2)}) collective-permute-start(bf16[4,8,3072]{2,1,0:T(8,128)(2,1)S(1)} %slice_select_fusion.3), channel_id=1, source_target_pairs={{0,1},{1,2},{2,3},{3,4},{4,5},{5,6},{6,7},{7,0},{32,39},{33,32},{3... | collective-permute-start | bytes 589832 | tf_op jit(solution)/shard_map/ppermute | solution.py:237
  99.8 0.4 collective-permute-done.12.refs_1_
  100.3 3.1 %collective-permute-done.13.refs_11_ = bf16[8,8,3072]{2,1,0:T(8,128)(2,1)S(1)} collective-permute-done((bf16[8,8,3072]{2,1,0:T(8,128)(2,1)S(1)}, bf16[8,8,3072]{2,1,0:T(8,128)(2,1)S(1)}, u32[]{:S(2)}, u32[]{:S(2)}) %collective-permute-start.13) | collective-permute-done | bytes 393248 | tf_op jit(solution)/shard_map/ppermute | solution.py:240
  103.4 3.5 %shard_map.48.refs_12_.refs_8_ = bf16[3072,384]{1,0:T(8,128)(2,1)S(1)} custom-call(s32[8]{0:T(128)S(1)} %copy-done.3, s32[8]{0:T(128)S(1)} %copy-done.5, bf16[4608,384]{1,0:T(8,128)(2,1)S(1)} %bitcast.48, bf16[4608,384]{1,0:T(8,128)(2,1)S(1)} %collective-permute-done.other_ref, bf16[3072,384]{1,0:T(8,128)(2,1)} %collective-permute-done.14.got_ref, ...), custom_call_target="tpu_custom_call" | custom-call | tf_op jit(solution)/shard_map/pallas_call | solution.py:256
  106.9 2.2 %shard_map.49 = f32[4,160,384]{2,1,0:T(8,128)S(1)} custom-call(bf16[4,8,3072]{2,1,0:T(8,128)(2,1)S(1)} %slice_select_fusion.1.refs_0_, bf16[4,8,3072]{2,1,0:T(8,128)(2,1)S(1)} %slice_select_fusion.refs_1_, bf16[4,8,3072]{2,1,0:T(8,128)(2,1)S(1)} %collective-permute-done.3.refs_2_, bf16[4,8,3072]{2,1,0:T(8,128)(2,1)S(1)} %collective-permute-done.5.refs_3_, ...), custom_call_target="tpu_custom_call" | custom-call | tf_op jit(solution)/shard_map/pallas_call | solution.py:268
  109.2 0.6 collective-permute-start.20
  109.7 1.1 collective-permute-start.19
  110.8 0.7 collective-permute-start.18
  111.5 1.2 collective-permute-start.25
  112.7 0.6 collective-permute-start.26
  113.3 2.5 %collective-permute-done.18.refs_5_ = bf16[4,8,3072]{2,1,0:T(8,128)(2,1)S(1)} collective-permute-done((bf16[4,8,3072]{2,1,0:T(8,128)(2,1)S(1)}, bf16[4,8,3072]{2,1,0:T(8,128)(2,1)S(1)}, u32[]{:S(2)}, u32[]{:S(2)}) %collective-permute-start.18) | collective-permute-done | bytes 196640 | tf_op jit(solution)/shard_map/ppermute | solution.py:237
  115.7 0.7 collective-permute-done.19
  116.4 0.1 fusion.4
  116.4 0.8 collective-permute-start.23
  117.3 0.8 collective-permute-start.22
  118.0 4.4 %collective-permute-done.23 = f32[80,384]{1,0:T(8,128)S(1)} collective-permute-done((f32[80,384]{1,0:T(8,128)S(1)}, f32[80,384]{1,0:T(8,128)S(1)}, u32[]{:S(2)}, u32[]{:S(2)}) %collective-permute-start.23) | collective-permute-done | bytes 122912 | tf_op jit(solution)/shard_map/ppermute | solution.py:180
  122.4 1.8 %collective-permute-start.24 = (f32[80,384]{1,0:T(8,128)S(1)}, f32[80,384]{1,0:T(8,128)S(1)}, u32[]{:S(2)}, u32[]{:S(2)}) collective-permute-start(f32[80,384]{1,0:T(8,128)S(1)} %get-tuple-element.51), channel_id=1, source_target_pairs={{0,192},{32,224},{64,0},{96,32},{128,64},{160,96},{192,128},{224,1... | collective-permute-start | bytes 368648 | tf_op jit(solution)/shard_map/ppermute | solution.py:180
  124.2 2.3 %collective-permute-done.24 = f32[80,384]{1,0:T(8,128)S(1)} collective-permute-done((f32[80,384]{1,0:T(8,128)S(1)}, f32[80,384]{1,0:T(8,128)S(1)}, u32[]{:S(2)}, u32[]{:S(2)}) %collective-permute-start.24) | collective-permute-done | bytes 122912 | tf_op jit(solution)/shard_map/ppermute | solution.py:180
  126.4 1.3 collective-permute-done.22.refs_7_
  127.8 1.4 shard_map.50
  129.2 1.5 collective-permute-start.27
  130.7 1.6 %collective-permute-start.29 = (f32[96,384]{1,0:T(8,128)S(1)}, f32[96,384]{1,0:T(8,128)S(1)}, u32[]{:S(2)}, u32[]{:S(2)}) collective-permute-start(f32[96,384]{1,0:T(8,128)S(1)} %pad_maximum_fusion.4), channel_id=1, source_target_pairs={{0,192},{32,224},{64,0},{96,32},{128,64},{160,96},{192,128},{224,1... | collective-permute-start | bytes 442376 | tf_op jit(solution)/shard_map/ppermute | solution.py:175
  132.3 2.2 %collective-permute-done.27 = f32[96,384]{1,0:T(8,128)S(1)} collective-permute-done((f32[96,384]{1,0:T(8,128)S(1)}, f32[96,384]{1,0:T(8,128)S(1)}, u32[]{:S(2)}, u32[]{:S(2)}) %collective-permute-start.27) | collective-permute-done | bytes 147488 | tf_op jit(solution)/shard_map/ppermute | solution.py:174
  134.5 0.5 collective-permute-done.29
  135.0 1.8 %collective-permute-start.28 = (f32[48,384]{1,0:T(8,128)S(1)}, f32[48,384]{1,0:T(8,128)S(1)}, u32[]{:S(2)}, u32[]{:S(2)}) collective-permute-start(f32[48,384]{1,0:T(8,128)S(1)} %get-tuple-element.58), channel_id=1, source_target_pairs={{0,64},{32,96},{64,128},{96,160},{128,192},{160,224},{192,0},{224,... | collective-permute-start | bytes 221192 | tf_op jit(solution)/shard_map/ppermute | solution.py:180
  136.8 0.9 collective-permute-start.30
  137.8 2.4 %collective-permute-done.28 = f32[48,384]{1,0:T(8,128)S(1)} collective-permute-done((f32[48,384]{1,0:T(8,128)S(1)}, f32[48,384]{1,0:T(8,128)S(1)}, u32[]{:S(2)}, u32[]{:S(2)}) %collective-permute-start.28) | collective-permute-done | bytes 73760 | tf_op jit(solution)/shard_map/ppermute | solution.py:180
  140.2 6.7 %collective-permute-start.31 = (f32[256,384]{1,0:T(8,128)S(1)}, f32[256,384]{1,0:T(8,128)S(1)}, u32[]{:S(2)}, u32[]{:S(2)}) collective-permute-start(f32[256,384]{1,0:T(8,128)S(1)} %pad_maximum_fusion.mine_ref), channel_id=1, source_target_pairs={{0,32},{32,0},{64,96},{96,64},{128,160},{160,128},{192,224},{224,1... | collective-permute-start | bytes 1179656 | tf_op jit(solution)/shard_map/ppermute | solution.py:291
  146.9 1.3 collective-permute-done.31.other_ref
  148.3 0.8 copy-done.7
  149.0 1.9 %shard_map.51 = f32[256,384]{1,0:T(8,128)} custom-call(f32[256,384]{1,0:T(8,128)} %copy-done.6, f32[256,384]{1,0:T(8,128)} %copy-done.7), custom_call_target="tpu_custom_call" | custom-call | tf_op jit(solution)/shard_map/pallas_call | solution.py:286
  (41 shorter events, 0.4 us)
Async XLA Ops:
  0.0 17.8 %collective-permute-start = (bf16[4608,384]{1,0:T(8,128)(2,1)}, bf16[4608,384]{1,0:T(8,128)(2,1)S(1)}, u32[]{:S(2)}, u32[]{:S(2)}) collective-permute-start(bf16[4608,384]{1,0:T(8,128)(2,1)} %bitcast.46), channel_id=1, source_target_pairs={{0,32},{32,0},{64,96},{96,64},{128,160},{160,128},{192,224},{224,1... | collective-permute-start | bytes 10616840 | tf_op jit(solution)/shard_map/ppermute | solution.py:209
  17.8 2.0 %copy-start = (bf16[1,4608,384]{2,1,0:T(8,128)(2,1)S(1)}, bf16[1,4608,384]{2,1,0:T(8,128)(2,1)}, u32[]{:S(2)}) copy-start(bf16[1,4608,384]{2,1,0:T(8,128)(2,1)} %param.5) | copy-start | bytes 10616836
  19.8 0.7 copy-start.2
  20.4 0.7 copy-start.4
  24.9 54.8 %collective-permute-start.14 = (bf16[3072,384]{1,0:T(8,128)(2,1)}, bf16[3072,384]{1,0:T(8,128)(2,1)}, u32[]{:S(2)}, u32[]{:S(2)}) collective-permute-start(bf16[3072,384]{1,0:T(8,128)(2,1)} %shard_map.47), channel_id=1, source_target_pairs={{0,64},{32,224},{64,128},{96,32},{128,192},{160,96},{192,0},{224,1... | collective-permute-start | bytes 7077896 | tf_op jit(solution)/shard_map/ppermute | solution.py:231
  27.7 29.3 %all-to-all-start.1 = ((bf16[8,8,3072]{2,1,0:T(8,128)(2,1)}), bf16[8,8,3072]{2,1,0:T(8,128)(2,1)}, u32[]{:S(2)}, u32[]{:S(2)}) async-start(bf16[8,8,3072]{2,1,0:T(8,128)(2,1)} %shard_map.46), calls=%async_computation.1 | async-start | bytes 786432 | tf_op jit(solution)/shard_map/all_to_all | solution.py:219
  57.1 10.6 %collective-permute-start.1 = (bf16[8,8,3072]{2,1,0:T(8,128)(2,1)}, bf16[8,8,3072]{2,1,0:T(8,128)(2,1)S(1)}, u32[]{:S(2)}, u32[]{:S(2)}) collective-permute-start(bf16[8,8,3072]{2,1,0:T(8,128)(2,1)} %all-to-all-done.1), channel_id=1, source_target_pairs={{0,16},{8,24},{16,0},{24,8},{1,17},{9,25},{17,1},{25,9},{2,18},{10... | collective-permute-start | bytes 1179656 | tf_op jit(solution)/shard_map/ppermute | solution.py:242
  59.6 13.7 %collective-permute-start.3 = (bf16[4,8,3072]{2,1,0:T(8,128)(2,1)S(1)}, bf16[4,8,3072]{2,1,0:T(8,128)(2,1)S(1)}, u32[]{:S(2)}, u32[]{:S(2)}) collective-permute-start(bf16[4,8,3072]{2,1,0:T(8,128)(2,1)S(1)} %slice_select_fusion.1.refs_0_), channel_id=1, source_target_pairs={{0,24},{8,0},{16,8},{24,16},{32,40},{40,48},{48,56},{56,32},{64,88... | collective-permute-start | bytes 589832 | tf_op jit(solution)/shard_map/ppermute | solution.py:240
  60.1 13.2 %collective-permute-start.2 = (bf16[8,8,3072]{2,1,0:T(8,128)(2,1)}, bf16[8,8,3072]{2,1,0:T(8,128)(2,1)S(1)}, u32[]{:S(2)}, u32[]{:S(2)}) collective-permute-start(bf16[8,8,3072]{2,1,0:T(8,128)(2,1)} %all-to-all-done.1), channel_id=1, source_target_pairs={{0,1},{1,2},{2,3},{3,4},{4,5},{5,6},{6,7},{7,0},{32,39},{33,32},{3... | collective-permute-start | bytes 1179656 | tf_op jit(solution)/shard_map/ppermute | solution.py:237
  67.7 10.4 %collective-permute-start.4 = (bf16[8,8,3072]{2,1,0:T(8,128)(2,1)S(1)}, bf16[8,8,3072]{2,1,0:T(8,128)(2,1)S(1)}, u32[]{:S(2)}, u32[]{:S(2)}) collective-permute-start(bf16[8,8,3072]{2,1,0:T(8,128)(2,1)S(1)} %collective-permute-done.1), channel_id=1, source_target_pairs={{0,1},{1,2},{2,3},{3,4},{4,5},{5,6},{6,7},{7,0},{32,39},{33,32},{3... | collective-permute-start | bytes 1179656 | tf_op jit(solution)/shard_map/ppermute | solution.py:237
  71.9 31.5 %copy-start.1 = (bf16[1,4608,384]{2,1,0:T(8,128)(2,1)S(1)}, bf16[1,4608,384]{2,1,0:T(8,128)(2,1)}, u32[]{:S(2)}) copy-start(bf16[1,4608,384]{2,1,0:T(8,128)(2,1)} %param.5) | copy-start | bytes 10616836
  71.9 31.5 %copy-start.3 = (s32[8]{0:T(128)S(1)}, s32[8]{0:T(128)}, u32[]{:S(2)}) copy-start(s32[8]{0:T(128)} %tiles_ref.5) | copy-start | bytes 100
  71.9 31.5 %copy-start.5 = (s32[8]{0:T(128)S(1)}, s32[8]{0:T(128)}, u32[]{:S(2)}) copy-start(s32[8]{0:T(128)} %assign_ref.5) | copy-start | bytes 100
  71.9 6.2 %collective-permute-start.5 = (bf16[4,8,3072]{2,1,0:T(8,128)(2,1)S(1)}, bf16[4,8,3072]{2,1,0:T(8,128)(2,1)S(1)}, u32[]{:S(2)}, u32[]{:S(2)}) collective-permute-start(bf16[4,8,3072]{2,1,0:T(8,128)(2,1)S(1)} %slice_select_fusion.refs_1_), channel_id=1, source_target_pairs={{0,24},{8,0},{16,8},{24,16},{32,40},{40,48},{48,56},{56,32},{64,88... | collective-permute-start | bytes 589832 | tf_op jit(solution)/shard_map/ppermute | solution.py:240
  73.3 11.4 %collective-permute-start.6 = (bf16[8,8,3072]{2,1,0:T(8,128)(2,1)S(1)}, bf16[8,8,3072]{2,1,0:T(8,128)(2,1)S(1)}, u32[]{:S(2)}, u32[]{:S(2)}) collective-permute-start(bf16[8,8,3072]{2,1,0:T(8,128)(2,1)S(1)} %collective-permute-done.2.refs_4_), channel_id=1, source_target_pairs={{0,1},{1,2},{2,3},{3,4},{4,5},{5,6},{6,7},{7,0},{32,39},{33,32},{3... | collective-permute-start | bytes 1179656 | tf_op jit(solution)/shard_map/ppermute | solution.py:237
  76.0 8.7 %collective-permute-start.7 = (bf16[8,8,3072]{2,1,0:T(8,128)(2,1)S(1)}, bf16[8,8,3072]{2,1,0:T(8,128)(2,1)S(1)}, u32[]{:S(2)}, u32[]{:S(2)}) collective-permute-start(bf16[8,8,3072]{2,1,0:T(8,128)(2,1)S(1)} %collective-permute-done.2.refs_4_), channel_id=1, source_target_pairs={{0,24},{8,0},{16,8},{24,16},{32,40},{40,48},{48,56},{56,32},{64,88... | collective-permute-start | bytes 1179656 | tf_op jit(solution)/shard_map/ppermute | solution.py:240
  78.1 9.7 %collective-permute-start.8 = (bf16[8,8,3072]{2,1,0:T(8,128)(2,1)S(1)}, bf16[8,8,3072]{2,1,0:T(8,128)(2,1)S(1)}, u32[]{:S(2)}, u32[]{:S(2)}) collective-permute-start(bf16[8,8,3072]{2,1,0:T(8,128)(2,1)S(1)} %collective-permute-done.4.refs_5_), channel_id=1, source_target_pairs={{0,1},{1,2},{2,3},{3,4},{4,5},{5,6},{6,7},{7,0},{32,39},{33,32},{3... | collective-permute-start | bytes 1179656 | tf_op jit(solution)/shard_map/ppermute | solution.py:237
  81.6 21.8 %collective-permute-start.15 = (bf16[1536,384]{1,0:T(8,128)(2,1)S(1)}, bf16[1536,384]{1,0:T(8,128)(2,1)S(1)}, u32[]{:S(2)}, u32[]{:S(2)}) collective-permute-start(bf16[1536,384]{1,0:T(8,128)(2,1)S(1)} %get-tuple-element.50), channel_id=1, source_target_pairs={{0,32},{32,0},{64,96},{96,64},{128,160},{160,128},{192,224},{224,1... | collective-permute-start | bytes 3538952 | tf_op jit(solution)/shard_map/ppermute | solution.py:255
  84.6 18.7 %collective-permute-start.16 = (bf16[1536,384]{1,0:T(8,128)(2,1)S(1)}, bf16[1536,384]{1,0:T(8,128)(2,1)S(1)}, u32[]{:S(2)}, u32[]{:S(2)}) collective-permute-start(bf16[1536,384]{1,0:T(8,128)(2,1)S(1)} %get-tuple-element.49), channel_id=1, source_target_pairs={{0,32},{32,0},{64,96},{96,64},{128,160},{160,128},{192,224},{224,1... | collective-permute-start | bytes 3538952 | tf_op jit(solution)/shard_map/ppermute | solution.py:255
  84.7 8.1 %collective-permute-start.9 = (bf16[8,8,3072]{2,1,0:T(8,128)(2,1)S(1)}, bf16[8,8,3072]{2,1,0:T(8,128)(2,1)S(1)}, u32[]{:S(2)}, u32[]{:S(2)}) collective-permute-start(bf16[8,8,3072]{2,1,0:T(8,128)(2,1)S(1)} %collective-permute-done.4.refs_5_), channel_id=1, source_target_pairs={{0,24},{8,0},{16,8},{24,16},{32,40},{40,48},{48,56},{56,32},{64,88... | collective-permute-start | bytes 1179656 | tf_op jit(solution)/shard_map/ppermute | solution.py:240
  84.7 10.8 %collective-permute-start.10 = (bf16[8,8,3072]{2,1,0:T(8,128)(2,1)S(1)}, bf16[8,8,3072]{2,1,0:T(8,128)(2,1)S(1)}, u32[]{:S(2)}, u32[]{:S(2)}) collective-permute-start(bf16[8,8,3072]{2,1,0:T(8,128)(2,1)S(1)} %collective-permute-done.6.refs_8_), channel_id=1, source_target_pairs={{0,1},{1,2},{2,3},{3,4},{4,5},{5,6},{6,7},{7,0},{32,39},{33,32},{3... | collective-permute-start | bytes 1179656 | tf_op jit(solution)/shard_map/ppermute | solution.py:237
  87.8 9.0 %collective-permute-start.11 = (bf16[8,8,3072]{2,1,0:T(8,128)(2,1)S(1)}, bf16[8,8,3072]{2,1,0:T(8,128)(2,1)S(1)}, u32[]{:S(2)}, u32[]{:S(2)}) collective-permute-start(bf16[8,8,3072]{2,1,0:T(8,128)(2,1)S(1)} %collective-permute-done.6.refs_8_), channel_id=1, source_target_pairs={{0,24},{8,0},{16,8},{24,16},{32,40},{40,48},{48,56},{56,32},{64,88... | collective-permute-start | bytes 1179656 | tf_op jit(solution)/shard_map/ppermute | solution.py:240
  92.9 7.4 %collective-permute-start.12 = (bf16[8,8,3072]{2,1,0:T(8,128)(2,1)S(1)}, bf16[8,8,3072]{2,1,0:T(8,128)(2,1)S(1)}, u32[]{:S(2)}, u32[]{:S(2)}) collective-permute-start(bf16[8,8,3072]{2,1,0:T(8,128)(2,1)S(1)} %collective-permute-done.8.refs_9_), channel_id=1, source_target_pairs={{0,1},{1,2},{2,3},{3,4},{4,5},{5,6},{6,7},{7,0},{32,39},{33,32},{3... | collective-permute-start | bytes 1179656 | tf_op jit(solution)/shard_map/ppermute | solution.py:237
  95.5 7.8 %collective-permute-start.13 = (bf16[8,8,3072]{2,1,0:T(8,128)(2,1)S(1)}, bf16[8,8,3072]{2,1,0:T(8,128)(2,1)S(1)}, u32[]{:S(2)}, u32[]{:S(2)}) collective-permute-start(bf16[8,8,3072]{2,1,0:T(8,128)(2,1)S(1)} %collective-permute-done.8.refs_9_), channel_id=1, source_target_pairs={{0,24},{8,0},{16,8},{24,16},{32,40},{40,48},{48,56},{56,32},{64,88... | collective-permute-start | bytes 1179656 | tf_op jit(solution)/shard_map/ppermute | solution.py:240
  96.8 15.9 %collective-permute-start.17 = (bf16[4,8,3072]{2,1,0:T(8,128)(2,1)S(1)}, bf16[4,8,3072]{2,1,0:T(8,128)(2,1)S(1)}, u32[]{:S(2)}, u32[]{:S(2)}) collective-permute-start(bf16[4,8,3072]{2,1,0:T(8,128)(2,1)S(1)} %slice_select_fusion.3), channel_id=1, source_target_pairs={{0,1},{1,2},{2,3},{3,4},{4,5},{5,6},{6,7},{7,0},{32,39},{33,32},{3... | collective-permute-start | bytes 589832 | tf_op jit(solution)/shard_map/ppermute | solution.py:237
  109.2 6.6 %collective-permute-start.20 = (f32[160,384]{1,0:T(8,128)S(1)}, f32[160,384]{1,0:T(8,128)S(1)}, u32[]{:S(2)}, u32[]{:S(2)}) collective-permute-start(f32[160,384]{1,0:T(8,128)S(1)} %pad_maximum_fusion.2), channel_id=1, source_target_pairs={{0,192},{32,224},{64,0},{96,32},{128,64},{160,96},{192,128},{224,1... | collective-permute-start | bytes 737288 | tf_op jit(solution)/shard_map/ppermute | solution.py:175
  109.7 6.6 %collective-permute-start.19 = (f32[160,384]{1,0:T(8,128)S(1)}, f32[160,384]{1,0:T(8,128)S(1)}, u32[]{:S(2)}, u32[]{:S(2)}) collective-permute-start(f32[160,384]{1,0:T(8,128)S(1)} %pad_maximum_fusion.1), channel_id=1, source_target_pairs={{0,64},{32,96},{64,128},{96,160},{128,192},{160,224},{192,0},{224,... | collective-permute-start | bytes 737288 | tf_op jit(solution)/shard_map/ppermute | solution.py:174
  110.8 4.9 %collective-permute-start.18 = (bf16[4,8,3072]{2,1,0:T(8,128)(2,1)S(1)}, bf16[4,8,3072]{2,1,0:T(8,128)(2,1)S(1)}, u32[]{:S(2)}, u32[]{:S(2)}) collective-permute-start(bf16[4,8,3072]{2,1,0:T(8,128)(2,1)S(1)} %slice_select_fusion.2), channel_id=1, source_target_pairs={{0,1},{1,2},{2,3},{3,4},{4,5},{5,6},{6,7},{7,0},{32,39},{33,32},{3... | collective-permute-start | bytes 589832 | tf_op jit(solution)/shard_map/ppermute | solution.py:237
  111.5 16.3 %collective-permute-start.25 = (bf16[8,8,3072]{2,1,0:T(8,128)(2,1)S(1)}, bf16[8,8,3072]{2,1,0:T(8,128)(2,1)S(1)}, u32[]{:S(2)}, u32[]{:S(2)}) collective-permute-start(bf16[8,8,3072]{2,1,0:T(8,128)(2,1)S(1)} %collective-permute-done.10.refs_0_), channel_id=1, source_target_pairs={{0,24},{8,0},{16,8},{24,16},{32,40},{40,48},{48,56},{56,32},{64,88... | collective-permute-start | bytes 1179656 | tf_op jit(solution)/shard_map/ppermute | solution.py:240
  112.7 15.1 %collective-permute-start.26 = (bf16[8,8,3072]{2,1,0:T(8,128)(2,1)S(1)}, bf16[8,8,3072]{2,1,0:T(8,128)(2,1)S(1)}, u32[]{:S(2)}, u32[]{:S(2)}) collective-permute-start(bf16[8,8,3072]{2,1,0:T(8,128)(2,1)S(1)} %collective-permute-done.12.refs_1_), channel_id=1, source_target_pairs={{0,24},{8,0},{16,8},{24,16},{32,40},{40,48},{48,56},{56,32},{64,88... | collective-permute-start | bytes 1179656 | tf_op jit(solution)/shard_map/ppermute | solution.py:240
  116.4 6.0 %collective-permute-start.23 = (f32[80,384]{1,0:T(8,128)S(1)}, f32[80,384]{1,0:T(8,128)S(1)}, u32[]{:S(2)}, u32[]{:S(2)}) collective-permute-start(f32[80,384]{1,0:T(8,128)S(1)} %get-tuple-element.52), channel_id=1, source_target_pairs={{0,64},{32,96},{64,128},{96,160},{128,192},{160,224},{192,0},{224,... | collective-permute-start | bytes 368648 | tf_op jit(solution)/shard_map/ppermute | solution.py:180
  117.3 9.2 %collective-permute-start.21 = (bf16[4,8,3072]{2,1,0:T(8,128)(2,1)S(1)}, bf16[4,8,3072]{2,1,0:T(8,128)(2,1)S(1)}, u32[]{:S(2)}, u32[]{:S(2)}) collective-permute-start(bf16[4,8,3072]{2,1,0:T(8,128)(2,1)S(1)} %collective-permute-done.17.refs_4_), channel_id=1, source_target_pairs={{0,24},{8,0},{16,8},{24,16},{32,40},{40,48},{48,56},{56,32},{64,88... | collective-permute-start | bytes 589832 | tf_op jit(solution)/shard_map/ppermute | solution.py:240
  117.3 10.5 %collective-permute-start.22 = (bf16[4,8,3072]{2,1,0:T(8,128)(2,1)S(1)}, bf16[4,8,3072]{2,1,0:T(8,128)(2,1)S(1)}, u32[]{:S(2)}, u32[]{:S(2)}) collective-permute-start(bf16[4,8,3072]{2,1,0:T(8,128)(2,1)S(1)} %collective-permute-done.18.refs_5_), channel_id=1, source_target_pairs={{0,24},{8,0},{16,8},{24,16},{32,40},{40,48},{48,56},{56,32},{64,88... | collective-permute-start | bytes 589832 | tf_op jit(solution)/shard_map/ppermute | solution.py:240
  122.4 4.0 %collective-permute-start.24 = (f32[80,384]{1,0:T(8,128)S(1)}, f32[80,384]{1,0:T(8,128)S(1)}, u32[]{:S(2)}, u32[]{:S(2)}) collective-permute-start(f32[80,384]{1,0:T(8,128)S(1)} %get-tuple-element.51), channel_id=1, source_target_pairs={{0,192},{32,224},{64,0},{96,32},{128,64},{160,96},{192,128},{224,1... | collective-permute-start | bytes 368648 | tf_op jit(solution)/shard_map/ppermute | solution.py:180
  129.2 5.3 %collective-permute-start.27 = (f32[96,384]{1,0:T(8,128)S(1)}, f32[96,384]{1,0:T(8,128)S(1)}, u32[]{:S(2)}, u32[]{:S(2)}) collective-permute-start(f32[96,384]{1,0:T(8,128)S(1)} %pad_maximum_fusion.3), channel_id=1, source_target_pairs={{0,64},{32,96},{64,128},{96,160},{128,192},{160,224},{192,0},{224,... | collective-permute-start | bytes 442376 | tf_op jit(solution)/shard_map/ppermute | solution.py:174
  130.7 4.3 %collective-permute-start.29 = (f32[96,384]{1,0:T(8,128)S(1)}, f32[96,384]{1,0:T(8,128)S(1)}, u32[]{:S(2)}, u32[]{:S(2)}) collective-permute-start(f32[96,384]{1,0:T(8,128)S(1)} %pad_maximum_fusion.4), channel_id=1, source_target_pairs={{0,192},{32,224},{64,0},{96,32},{128,64},{160,96},{192,128},{224,1... | collective-permute-start | bytes 442376 | tf_op jit(solution)/shard_map/ppermute | solution.py:175
  135.0 5.2 %collective-permute-start.28 = (f32[48,384]{1,0:T(8,128)S(1)}, f32[48,384]{1,0:T(8,128)S(1)}, u32[]{:S(2)}, u32[]{:S(2)}) collective-permute-start(f32[48,384]{1,0:T(8,128)S(1)} %get-tuple-element.58), channel_id=1, source_target_pairs={{0,64},{32,96},{64,128},{96,160},{128,192},{160,224},{192,0},{224,... | collective-permute-start | bytes 221192 | tf_op jit(solution)/shard_map/ppermute | solution.py:180
  136.8 3.3 %collective-permute-start.30 = (f32[48,384]{1,0:T(8,128)S(1)}, f32[48,384]{1,0:T(8,128)S(1)}, u32[]{:S(2)}, u32[]{:S(2)}) collective-permute-start(f32[48,384]{1,0:T(8,128)S(1)} %get-tuple-element.57), channel_id=1, source_target_pairs={{0,192},{32,224},{64,0},{96,32},{128,64},{160,96},{192,128},{224,1... | collective-permute-start | bytes 221192 | tf_op jit(solution)/shard_map/ppermute | solution.py:180
  140.2 8.0 %copy-start.6 = (f32[256,384]{1,0:T(8,128)}, f32[256,384]{1,0:T(8,128)S(1)}, u32[]{:S(2)}) copy-start(f32[256,384]{1,0:T(8,128)S(1)} %pad_maximum_fusion.mine_ref) | copy-start | bytes 1179652
  140.2 8.0 %collective-permute-start.31 = (f32[256,384]{1,0:T(8,128)S(1)}, f32[256,384]{1,0:T(8,128)S(1)}, u32[]{:S(2)}, u32[]{:S(2)}) collective-permute-start(f32[256,384]{1,0:T(8,128)S(1)} %pad_maximum_fusion.mine_ref), channel_id=1, source_target_pairs={{0,32},{32,0},{64,96},{96,64},{128,160},{160,128},{192,224},{224,1... | collective-permute-start | bytes 1179656 | tf_op jit(solution)/shard_map/ppermute | solution.py:291
  148.3 0.8 copy-start.7

commit v2 on v1

--- a/solution.py
+++ b/solution.py
@@ -69,8 +69,8 @@
                 def move(i, carry, block=block, tile=tile, place=place):
                     data = src_ref[block, :, pl.ds(pl.multiple_of((tile + i) * TP, TP), TP)]
                     into = pl.ds(pl.multiple_of((place + i) * TP, TP), TP)
-                    out_ref[2 * x, :, into] = data
-                    out_ref[2 * x + 1, :, into] = data
+                    for copy in range(4):
+                        out_ref[4 * x + copy, :, into] = data
                     return carry
 
                 lax.fori_loop(0, many, move, 0)
@@ -131,9 +131,7 @@
 
 def multiply(ny, *refs):
     refs, (b_ref, out_ref, a_ref) = refs[:-3], refs[-3:]
-    group, y = lax.axis_index("grp"), lax.axis_index("row")
-    x, core = lax.div(group, 2), lax.rem(group, 2)
-    near = jnp.where(core == 0, 1, ny - 1)
+    x, y = lax.div(lax.axis_index("grp"), 2), lax.axis_index("row")
     at = 0
     for ref in refs:
         n, octet, wide = ref.shape
@@ -142,11 +140,14 @@
     out = jnp.dot(a_ref[...], b_ref[...], preferred_element_type=jnp.float32)
     at = row = 0
     for i, ref in enumerate(refs):
-        n = ref.shape[0] * ref.shape[1]
-        d = lax.rem(y + (0, 2, near, near + 2)[i % 4] - x + 2 * ny, ny)
-        out_ref[d, row : row + n, :] = out[at : at + n]
-        at += n
-        row += n if i % 4 == 3 else 0
+        n, octet, _ = ref.shape
+        for j in range(2):
+            d = lax.rem(lax.rem(y + i % 2, 2) + 2 * j - x + ny, ny)
+            for g in range(n // 2):
+                start = at + (2 * g + j) * octet
+                out_ref[d, row + g * octet : row + (g + 1) * octet, :] = out[start : start + octet]
+        at += n * octet
+        row += n // 2 * octet if i % 2 else 0
 
 
 def finish(nz, rows, mine_ref, other_ref, out_ref):
@@ -200,7 +201,7 @@
     apart = [(g, (g + 2 - 4 * (g % 2)) % groups) for g in range(groups)]
     along = [(g * nz + z, g * nz + (z + 1 - 2 * (g % 2)) % nz) for g in range(groups) for z in range(nz)]
     beside = [(g * ny + y, g * ny + (y - 1 + 2 * (g % 2)) % ny) for g in range(groups) for y in range(ny)]
-    across = [(y, (y + 2) % ny) for y in range(ny)]
+    pairs = [[g * ny + y for g in range(groups) for y in (p, p + 2)] for p in range(2)]
     limit = pltpu.CompilerParams(vmem_limit_bytes=32 * 2**20)
     core = lax.rem(lax.axis_index("grp"), 2)
     barrier = lax.optimization_barrier
@@ -208,15 +209,14 @@
     mine = integrals[0]
     other = lax.ppermute(mine, "grp", swap)
     moved = lax.all_to_all(amplitudes[0].reshape(groups, octet, cap), "grp", 0, 0, tiled=True)
-    moved, other = barrier((moved, other))
     packed = pl.pallas_call(
         functools.partial(pack_amplitudes, groups, share),
-        out_shape=jax.ShapeDtypeStruct((groups, octet, wide), jnp.bfloat16),
+        out_shape=jax.ShapeDtypeStruct((2 * groups, octet, wide), jnp.bfloat16),
         in_specs=[SMEM, SMEM, VMEM],
         out_specs=VMEM,
         scratch_shapes=small,
     )(block_tiles, assign, moved)
-    piece = lax.all_to_all(packed, "grp", 0, 0, tiled=True)
+    pair = lax.all_to_all(packed, ("grp", "row"), 0, 0, axis_index_groups=pairs, tiled=True)
 
     tiles = jax.ShapeDtypeStruct((wide, cols), jnp.bfloat16)
     scratch = small + [pltpu.SemaphoreType.DMA((share,))]
@@ -228,6 +228,7 @@
         scratch_shapes=scratch,
         compiler_params=limit,
     )(block_tiles, assign, mine, other)
+    pair, sent = barrier((pair, sent))
     got = lax.ppermute(sent, "grp", apart)
     def half_of(block):
         h = block.shape[0] // 2
@@ -239,20 +240,17 @@
     def y_step(block):
         return lax.ppermute(block, ("grp", "row"), beside)
 
-    chains = [piece, lax.ppermute(piece, "row", across)]
-    order = []
+    block, order = pair, []
     for s in range(nz // 2 - 1):
-        here, beside_here = [], []
-        for i, block in enumerate(chains):
-            kept = half_of(block) if s == 0 else block
-            chains[i], other_y = barrier((z_step(block), y_step(kept)))
-            here.append(kept)
-            beside_here.append(other_y)
-        order.append(here + beside_here)
-    ends = [z_step(half_of(block)) for block in chains]
-    order.append(chains + [y_step(block) for block in chains])
-
+        kept = half_of(block) if s == 0 else block
+        block, near = barrier((z_step(block), y_step(kept)))
+        if s == nz // 2 - 3:
+            block, near, got = barrier((block, near, got))
+        order += [kept, near]
     theirs = [lax.ppermute(part, "grp", swap) for part in jnp.split(got, 2)]
+    end = z_step(half_of(block))
+    order += [block, y_step(block), end, y_step(end)]
+
     held = pl.pallas_call(
         functools.partial(join_tiles, groups, share),
         out_shape=tiles,
@@ -262,8 +260,7 @@
         compiler_params=limit,
     )(block_tiles, assign, mine, other, got, *theirs)
 
-    def sums(steps):
-        parts = [part for step in steps for part in step]
+    def sums(parts):
         n = sum(part.shape[0] for part in parts) * octet
         return pl.pallas_call(
             functools.partial(multiply, ny),
@@ -274,14 +271,13 @@
             compiler_params=limit,
         )(*parts, held)
 
-    p = sums(order[:3])
-    a, b = near_chips(p, up, down)
-    *ends, a, b = barrier((*ends, a, b))
-    *beside_ends, a2, b2 = barrier((*map(y_step, ends), *passed_on(p, a, b, up, down)))
-    early = total_of(p, a, b, a2, b2)
-    p = sums(order[3:] + [ends + beside_ends])
-    a, b = near_chips(p, up, down)
-    late = total_of(p, a, b, *passed_on(p, a, b, up, down))
+    early, late = sums(order[:6]), order[6:]
+    a, b = near_chips(early, up, down)
+    *late, a, b = barrier((*late, a, b))
+    late = sums(late)
+    c, d = near_chips(late, up, down)
+    early = total_of(early, a, b, *passed_on(early, a, b, up, down))
+    late = total_of(late, c, d, *passed_on(late, c, d, up, down))
     done = jnp.concatenate([early, late])
     return pl.pallas_call(
         functools.partial(finish, nz, rows),

time: 152 us -> 126 us (0.83)
  starting transfers between devices: 62 us -> 35.3 us
  waiting for transfers between devices: 51.3 us -> 55.1 us
  Pallas kernels: 15.6 us -> 13.1 us
  local copies, waits for them, and re-layouts: 6.02 us -> 4.09 us
    ppermute x8 -> x4, waiting for transfers between devices: 2.88 us -> 16.2 us  [z_step(): return lax.ppermute(block, ('grp', 'col'), along)]
    all_to_all x1, waiting for transfers between devices: 23.9 us -> 12.5 us  [body(): lax.all_to_all(packed, ('grp', 'row'), 0, 0, axis_index_groups=pairs, til...]
    ppermute x8 -> x4, starting transfers between devices: 23.4 us -> 12.5 us  [z_step(): return lax.ppermute(block, ('grp', 'col'), along)]
    ppermute x10 -> x5, waiting for transfers between devices: 8.81 us -> 17.3 us  [y_step(): return lax.ppermute(block, ('grp', 'row'), beside)]
    ppermute x10 -> x5, starting transfers between devices: 8.48 us -> 1.28 us  [y_step(): return lax.ppermute(block, ('grp', 'row'), beside)]
    ppermute x2, waiting for transfers between devices: 6.73 us -> 1.74 us  [passed_on(): lax.ppermute(p[1, :h] + a[:h], 'grp', up)]
    ppermute x1, starting transfers between devices: 6.68 us -> 3.03 us  [body(): lax.ppermute(done, 'grp', swap)]
    ppermute x2, waiting for transfers between devices: 0.5 us -> 3.5 us  [near_chips(): return (a, lax.ppermute(jnp.concatenate([p[2, h:], p[3, :h]]), 'grp', down))]
  transfers between devices with their start and end apart: 33 -> 23, of which waited for: 16 -> 13; matrix products, arithmetic and copies ran while one was open for 2% -> 3% of each run, Pallas kernels for 6% -> 8%
where the time goes in v2:
time: 126 us; the launch traced here: 124 us
  waiting for transfers between devices  55.1 us (44%)
  starting transfers between devices  35.3 us (28%)
  blocking collectives  14.8 us (12%)
  Pallas kernels  13.1 us (10%)
  local copies, waits for them, and re-layouts  4.09 us (3%)
  other arithmetic  1.43 us (1%)
    ppermute x5, waiting for transfers between devices, y_step(): return lax.ppermute(block, ('grp', 'row'), beside)  17.3 us
    ppermute x4, waiting for transfers between devices, z_step(): return lax.ppermute(block, ('grp', 'col'), along)  16.2 us
    all_to_all x1, blocking collectives, body(): lax.all_to_all(amplitudes[0].reshape(groups, octet, cap), 'grp', 0, 0, ti...  14.8 us
    all_to_all x1, waiting for transfers between devices, body(): lax.all_to_all(packed, ('grp', 'row'), 0, 0, axis_index_groups=pairs, til...  12.5 us
    ppermute x4, starting transfers between devices, z_step(): return lax.ppermute(block, ('grp', 'col'), along)  12.5 us
    ppermute x2, starting transfers between devices, passed_on(): lax.ppermute(p[3, h:] + b[:h], 'grp', down)  5.33 us
    all_to_all x1, starting transfers between devices, body(): lax.all_to_all(packed, ('grp', 'row'), 0, 0, axis_index_groups=pairs, til...  4.77 us
    ppermute x2, starting transfers between devices, near_chips(): return (a, lax.ppermute(jnp.concatenate([p[2, h:], p[3, :h]]), 'grp', down))  3.7 us
  transfers between devices with their start and end apart: 23, of which 13 were waited for; matrix products, arithmetic and copies ran while one was open for 3% of the time, Pallas kernels for 8%

profile of v2, /device:TPU:1, one launch (start us, length us, event | category | flops | bytes accessed | tf_op | source)
XLA Modules:
  0.0 124.0 jit_solution(6223343930827924735)
XLA Ops:
  0.0 0.0 copy-start
  0.0 3.2 %collective-permute-start = (bf16[4608,384]{1,0:T(8,128)(2,1)}, bf16[4608,384]{1,0:T(8,128)(2,1)}, u32[]{:S(2)}, u32[]{:S(2)}) collective-permute-start(bf16[4608,384]{1,0:T(8,128)(2,1)} %bitcast.46), channel_id=1, source_target_pairs={{0,32},{32,0},{64,96},{96,64},{128,160},{160,128},{192,224},{224,1... | collective-permute-start | bytes 10616840 | tf_op jit(solution)/shard_map/ppermute | solution.py:210
  3.2 14.8 %all_to_all.10.src_ref = bf16[8,8,4608]{2,1,0:T(8,128)(2,1)} all-to-all(bf16[8,8,4608]{2,1,0:T(8,128)(2,1)} %bitcast.49), channel_id=1, replica_groups=mesh['grp'=8,'row'=4,'col'=8] {'grp'}, dimensions={0} | all-to-all | bytes 1179648 | tf_op jit(solution)/shard_map/all_to_all | solution.py:211
  18.1 2.9 %shard_map.46 = bf16[16,8,3072]{2,1,0:T(8,128)(2,1)} custom-call(s32[8]{0:T(128)} %tiles_ref.5, s32[8]{0:T(128)} %assign_ref.5, bf16[8,8,4608]{2,1,0:T(8,128)(2,1)} %all_to_all.10.src_ref), custom_call_target="tpu_custom_call" | custom-call | tf_op jit(solution)/shard_map/pallas_call | solution.py:212
  21.0 4.8 %all-to-all-start.1 = ((bf16[16,8,3072]{2,1,0:T(8,128)(2,1)}), bf16[16,8,3072]{2,1,0:T(8,128)(2,1)}, u32[]{:S(2)}, u32[]{:S(2)}) async-start(bf16[16,8,3072]{2,1,0:T(8,128)(2,1)} %shard_map.46), calls=%async_computation.1 | async-start | bytes 1572864 | tf_op jit(solution)/shard_map/all_to_all | solution.py:219
  25.7 0.0 collective-permute-done.other_ref
  25.7 0.0 copy-done
  25.7 0.0 copy-done.2
  25.8 0.0 copy-done.3
  25.8 2.3 %shard_map.47 = bf16[3072,384]{1,0:T(8,128)(2,1)S(1)} custom-call(s32[8]{0:T(128)S(1)} %copy-done.2, s32[8]{0:T(128)S(1)} %copy-done.3, bf16[4608,384]{1,0:T(8,128)(2,1)S(1)} %bitcast.47, bf16[4608,384]{1,0:T(8,128)(2,1)} %collective-permute-done.other_ref), custom_call_target="tpu_custom_call" | custom-call | tf_op jit(solution)/shard_map/pallas_call | solution.py:223
  28.1 0.0 copy-start.1
  28.1 1.4 %copy-done.1 = bf16[3072,384]{1,0:T(8,128)(2,1)} copy-done((bf16[3072,384]{1,0:T(8,128)(2,1)}, bf16[3072,384]{1,0:T(8,128)(2,1)S(1)}, u32[]{:S(2)}) %copy-start.1) | copy-done | bytes 2359320
  29.5 12.5 %all-to-all-done.1 = bf16[16,8,3072]{2,1,0:T(8,128)(2,1)} async-done(((bf16[16,8,3072]{2,1,0:T(8,128)(2,1)}), bf16[16,8,3072]{2,1,0:T(8,128)(2,1)}, u32[]{:S(2)}, u32[]{:S(2)}) %all-to-all-start.1) | async-done | bytes 786464 | tf_op jit(solution)/shard_map/all_to_all | solution.py:219
  42.0 0.0 collective-permute-start.5
  42.0 5.2 %collective-permute-start.1 = (bf16[16,8,3072]{2,1,0:T(8,128)(2,1)}, bf16[16,8,3072]{2,1,0:T(8,128)(2,1)S(1)}, u32[]{:S(2)}, u32[]{:S(2)}) collective-permute-start(bf16[16,8,3072]{2,1,0:T(8,128)(2,1)} %all-to-all-done.1), channel_id=1, source_target_pairs={{0,1},{1,2},{2,3},{3,4},{4,5},{5,6},{6,7},{7,0},{32,39},{33,32},{3... | collective-permute-start | bytes 2359304 | tf_op jit(solution)/shard_map/ppermute | solution.py:238
  47.2 1.2 slice_select_fusion.1.refs_0_
  48.3 0.5 collective-permute-start.2
  48.8 7.8 %collective-permute-done.2.refs_1_ = bf16[8,8,3072]{2,1,0:T(8,128)(2,1)S(1)} collective-permute-done((bf16[8,8,3072]{2,1,0:T(8,128)(2,1)S(1)}, bf16[8,8,3072]{2,1,0:T(8,128)(2,1)S(1)}, u32[]{:S(2)}, u32[]{:S(2)}) %collective-permute-start.2) | collective-permute-done | bytes 393248 | tf_op jit(solution)/shard_map/ppermute | solution.py:241
  56.7 0.0 collective-permute-done.1.refs_2_
  56.7 3.2 %collective-permute-start.3 = (bf16[16,8,3072]{2,1,0:T(8,128)(2,1)S(1)}, bf16[16,8,3072]{2,1,0:T(8,128)(2,1)S(1)}, u32[]{:S(2)}, u32[]{:S(2)}) collective-permute-start(bf16[16,8,3072]{2,1,0:T(8,128)(2,1)S(1)} %collective-permute-done.1.refs_2_), channel_id=1, source_target_pairs={{0,1},{1,2},{2,3},{3,4},{4,5},{5,6},{6,7},{7,0},{32,39},{33,32},{3... | collective-permute-start | bytes 2359304 | tf_op jit(solution)/shard_map/ppermute | solution.py:238
  59.9 0.4 collective-permute-start.4
  60.2 8.5 %collective-permute-done.3.refs_4_ = bf16[16,8,3072]{2,1,0:T(8,128)(2,1)S(1)} collective-permute-done((bf16[16,8,3072]{2,1,0:T(8,128)(2,1)S(1)}, bf16[16,8,3072]{2,1,0:T(8,128)(2,1)S(1)}, u32[]{:S(2)}, u32[]{:S(2)}) %collective-permute-start.3) | collective-permute-done | bytes 786464 | tf_op jit(solution)/shard_map/ppermute | solution.py:238
  68.8 3.4 %collective-permute-done.4.refs_3_ = bf16[16,8,3072]{2,1,0:T(8,128)(2,1)S(1)} collective-permute-done((bf16[16,8,3072]{2,1,0:T(8,128)(2,1)S(1)}, bf16[16,8,3072]{2,1,0:T(8,128)(2,1)S(1)}, u32[]{:S(2)}, u32[]{:S(2)}) %collective-permute-start.4) | collective-permute-done | bytes 786464 | tf_op jit(solution)/shard_map/ppermute | solution.py:241
  72.1 0.0 collective-permute-done.5.got_ref
  72.1 3.3 %collective-permute-start.6 = (bf16[16,8,3072]{2,1,0:T(8,128)(2,1)S(1)}, bf16[16,8,3072]{2,1,0:T(8,128)(2,1)S(1)}, u32[]{:S(2)}, u32[]{:S(2)}) collective-permute-start(bf16[16,8,3072]{2,1,0:T(8,128)(2,1)S(1)} %collective-permute-done.3.refs_4_), channel_id=1, source_target_pairs={{0,1},{1,2},{2,3},{3,4},{4,5},{5,6},{6,7},{7,0},{32,39},{33,32},{3... | collective-permute-start | bytes 2359304 | tf_op jit(solution)/shard_map/ppermute | solution.py:238
  75.5 0.4 collective-permute-start.7
  75.9 1.9 %fusion.6 = (bf16[1536,384]{1,0:T(8,128)(2,1)S(1)}, bf16[1536,384]{1,0:T(8,128)(2,1)S(1)}) fusion(bf16[3072,384]{1,0:T(8,128)(2,1)} %collective-permute-done.5.got_ref), kind=kLoop, calls=%fused_computation.29 | loop fusion | bytes 4718592 | tf_op jit(solution)/shard_map/split | solution.py:250
  77.8 0.1 collective-permute-start.8
  77.9 0.5 collective-permute-start.9
  78.4 6.1 %collective-permute-done.6.refs_0_ = bf16[16,8,3072]{2,1,0:T(8,128)(2,1)S(1)} collective-permute-done((bf16[16,8,3072]{2,1,0:T(8,128)(2,1)S(1)}, bf16[16,8,3072]{2,1,0:T(8,128)(2,1)S(1)}, u32[]{:S(2)}, u32[]{:S(2)}) %collective-permute-start.6) | collective-permute-done | bytes 786464 | tf_op jit(solution)/shard_map/ppermute | solution.py:238
  84.4 3.1 %collective-permute-done.7.refs_5_ = bf16[16,8,3072]{2,1,0:T(8,128)(2,1)S(1)} collective-permute-done((bf16[16,8,3072]{2,1,0:T(8,128)(2,1)S(1)}, bf16[16,8,3072]{2,1,0:T(8,128)(2,1)S(1)}, u32[]{:S(2)}, u32[]{:S(2)}) %collective-permute-start.7) | collective-permute-done | bytes 786464 | tf_op jit(solution)/shard_map/ppermute | solution.py:241
  87.6 0.8 collective-permute-start.11
  88.4 0.0 collective-permute-start.10
  88.4 0.0 collective-permute-done.8.refs_0_
  88.4 0.0 collective-permute-done.9.refs_1_
  88.4 2.4 %shard_map.48.refs_6_.refs_4_ = bf16[3072,384]{1,0:T(8,128)(2,1)S(1)} custom-call(s32[8]{0:T(128)S(1)} %copy-done.2, s32[8]{0:T(128)S(1)} %copy-done.3, bf16[4608,384]{1,0:T(8,128)(2,1)S(1)} %bitcast.48, bf16[4608,384]{1,0:T(8,128)(2,1)} %collective-permute-done.other_ref, bf16[3072,384]{1,0:T(8,128)(2,1)} %collective-permute-done.5.got_ref, ...), custom_call_target="tpu_custom_call" | custom-call | tf_op jit(solution)/shard_map/pallas_call | solution.py:254
  90.8 2.2 %shard_map.49 = f32[4,160,384]{2,1,0:T(8,128)S(1)} custom-call(bf16[8,8,3072]{2,1,0:T(8,128)(2,1)S(1)} %slice_select_fusion.1.refs_0_, bf16[8,8,3072]{2,1,0:T(8,128)(2,1)S(1)} %collective-permute-done.2.refs_1_, bf16[16,8,3072]{2,1,0:T(8,128)(2,1)S(1)} %collective-permute-done.1.refs_2_, bf16[16,8,3072]{2,1,0:T(8,128)(2,1)S(1)} %collective-permute-done.4.refs_3_, ...), custom_call_target="tpu_custom_call" | custom-call | tf_op jit(solution)/shard_map/pallas_call | solution.py:265
  93.0 1.6 %collective-permute-done.11.refs_2_ = bf16[8,8,3072]{2,1,0:T(8,128)(2,1)S(1)} collective-permute-done((bf16[8,8,3072]{2,1,0:T(8,128)(2,1)S(1)}, bf16[8,8,3072]{2,1,0:T(8,128)(2,1)S(1)}, u32[]{:S(2)}, u32[]{:S(2)}) %collective-permute-start.11) | collective-permute-done | bytes 393248 | tf_op jit(solution)/shard_map/ppermute | solution.py:238
  94.6 0.0 collective-permute-start.12
  94.6 1.0 collective-permute-start.14
  95.6 0.7 collective-permute-start.13
  96.3 3.5 %collective-permute-done.14 = f32[160,384]{1,0:T(8,128)S(1)} collective-permute-done((f32[160,384]{1,0:T(8,128)S(1)}, f32[160,384]{1,0:T(8,128)S(1)}, u32[]{:S(2)}, u32[]{:S(2)}) %collective-permute-start.14) | collective-permute-done | bytes 245792 | tf_op jit(solution)/shard_map/ppermute | solution.py:176
  99.8 2.2 %collective-permute-done.13 = f32[160,384]{1,0:T(8,128)S(1)} collective-permute-done((f32[160,384]{1,0:T(8,128)S(1)}, f32[160,384]{1,0:T(8,128)S(1)}, u32[]{:S(2)}, u32[]{:S(2)}) %collective-permute-start.13) | collective-permute-done | bytes 245792 | tf_op jit(solution)/shard_map/ppermute | solution.py:175
  102.0 3.0 %collective-permute-done.12.refs_3_ = bf16[8,8,3072]{2,1,0:T(8,128)(2,1)S(1)} collective-permute-done((bf16[8,8,3072]{2,1,0:T(8,128)(2,1)S(1)}, bf16[8,8,3072]{2,1,0:T(8,128)(2,1)S(1)}, u32[]{:S(2)}, u32[]{:S(2)}) %collective-permute-start.12) | collective-permute-done | bytes 393248 | tf_op jit(solution)/shard_map/ppermute | solution.py:241
  105.0 0.0 collective-permute-done.10.refs_1_
  105.0 1.4 %shard_map.50 = f32[4,96,384]{2,1,0:T(8,128)S(1)} custom-call(bf16[16,8,3072]{2,1,0:T(8,128)(2,1)S(1)} %collective-permute-done.6.refs_0_, bf16[16,8,3072]{2,1,0:T(8,128)(2,1)S(1)} %collective-permute-done.10.refs_1_, bf16[8,8,3072]{2,1,0:T(8,128)(2,1)S(1)} %collective-permute-done.11.refs_2_, bf16[8,8,3072]{2,1,0:T(8,128)(2,1)S(1)} %collective-permute-done.12.refs_3_, ...), custom_call_target="tpu_custom_call" | custom-call | tf_op jit(solution)/shard_map/pallas_call | solution.py:265
  106.4 0.1 collective-permute-start.17
  106.5 2.7 %collective-permute-start.19 = (f32[96,384]{1,0:T(8,128)S(1)}, f32[96,384]{1,0:T(8,128)S(1)}, u32[]{:S(2)}, u32[]{:S(2)}) collective-permute-start(f32[96,384]{1,0:T(8,128)S(1)} %pad_maximum_fusion.4), channel_id=1, source_target_pairs={{0,192},{32,224},{64,0},{96,32},{128,64},{160,96},{192,128},{224,1... | collective-permute-start | bytes 442376 | tf_op jit(solution)/shard_map/ppermute | solution.py:176
  109.3 0.1 collective-permute-start.15
  109.4 2.7 %collective-permute-start.16 = (f32[80,384]{1,0:T(8,128)S(1)}, f32[80,384]{1,0:T(8,128)S(1)}, u32[]{:S(2)}, u32[]{:S(2)}) collective-permute-start(f32[80,384]{1,0:T(8,128)S(1)} %get-tuple-element.41), channel_id=1, source_target_pairs={{0,192},{32,224},{64,0},{96,32},{128,64},{160,96},{192,128},{224,1... | collective-permute-start | bytes 368648 | tf_op jit(solution)/shard_map/ppermute | solution.py:181
  112.0 0.3 collective-permute-done.17
  112.3 0.0 collective-permute-done.19
  112.3 0.1 collective-permute-start.18
  112.4 2.7 %collective-permute-start.20 = (f32[48,384]{1,0:T(8,128)S(1)}, f32[48,384]{1,0:T(8,128)S(1)}, u32[]{:S(2)}, u32[]{:S(2)}) collective-permute-start(f32[48,384]{1,0:T(8,128)S(1)} %get-tuple-element.47), channel_id=1, source_target_pairs={{0,192},{32,224},{64,0},{96,32},{128,64},{160,96},{192,128},{224,1... | collective-permute-start | bytes 221192 | tf_op jit(solution)/shard_map/ppermute | solution.py:181
  115.1 0.0 collective-permute-done.15
  115.1 0.0 collective-permute-done.16
  115.1 1.7 %collective-permute-done.18 = f32[48,384]{1,0:T(8,128)S(1)} collective-permute-done((f32[48,384]{1,0:T(8,128)S(1)}, f32[48,384]{1,0:T(8,128)S(1)}, u32[]{:S(2)}, u32[]{:S(2)}) %collective-permute-start.18) | collective-permute-done | bytes 73760 | tf_op jit(solution)/shard_map/ppermute | solution.py:181
  116.9 0.0 collective-permute-done.20
  116.9 0.0 copy-start.4
  117.0 3.0 %collective-permute-start.21 = (f32[256,384]{1,0:T(8,128)S(1)}, f32[256,384]{1,0:T(8,128)S(1)}, u32[]{:S(2)}, u32[]{:S(2)}) collective-permute-start(f32[256,384]{1,0:T(8,128)S(1)} %pad_maximum_fusion.mine_ref), channel_id=1, source_target_pairs={{0,32},{32,0},{64,96},{96,64},{128,160},{160,128},{192,224},{224,1... | collective-permute-start | bytes 1179656 | tf_op jit(solution)/shard_map/ppermute | solution.py:287
  120.0 1.3 %collective-permute-done.21.other_ref = f32[256,384]{1,0:T(8,128)S(1)} collective-permute-done((f32[256,384]{1,0:T(8,128)S(1)}, f32[256,384]{1,0:T(8,128)S(1)}, u32[]{:S(2)}, u32[]{:S(2)}) %collective-permute-start.21) | collective-permute-done | bytes 393248 | tf_op jit(solution)/shard_map/ppermute | solution.py:287
  121.3 0.0 copy-done.4
  121.3 0.8 copy-done.5
  122.1 1.9 %shard_map.51 = f32[256,384]{1,0:T(8,128)} custom-call(f32[256,384]{1,0:T(8,128)} %copy-done.4, f32[256,384]{1,0:T(8,128)} %copy-done.5), custom_call_target="tpu_custom_call" | custom-call | tf_op jit(solution)/shard_map/pallas_call | solution.py:282
  (15 shorter events, 0.3 us)
Async XLA Ops:
  0.0 25.7 %copy-start = (bf16[1,4608,384]{2,1,0:T(8,128)(2,1)S(1)}, bf16[1,4608,384]{2,1,0:T(8,128)(2,1)}, u32[]{:S(2)}) copy-start(bf16[1,4608,384]{2,1,0:T(8,128)(2,1)} %param.5) | copy-start | bytes 10616836
  0.0 25.7 %copy-start.2 = (s32[8]{0:T(128)S(1)}, s32[8]{0:T(128)}, u32[]{:S(2)}) copy-start(s32[8]{0:T(128)} %tiles_ref.5) | copy-start | bytes 100
  0.0 25.8 %copy-start.3 = (s32[8]{0:T(128)S(1)}, s32[8]{0:T(128)}, u32[]{:S(2)}) copy-start(s32[8]{0:T(128)} %assign_ref.5) | copy-start | bytes 100
  0.0 25.7 %collective-permute-start = (bf16[4608,384]{1,0:T(8,128)(2,1)}, bf16[4608,384]{1,0:T(8,128)(2,1)}, u32[]{:S(2)}, u32[]{:S(2)}) collective-permute-start(bf16[4608,384]{1,0:T(8,128)(2,1)} %bitcast.46), channel_id=1, source_target_pairs={{0,32},{32,0},{64,96},{96,64},{128,160},{160,128},{192,224},{224,1... | collective-permute-start | bytes 10616840 | tf_op jit(solution)/shard_map/ppermute | solution.py:210
  21.0 21.0 %all-to-all-start.1 = ((bf16[16,8,3072]{2,1,0:T(8,128)(2,1)}), bf16[16,8,3072]{2,1,0:T(8,128)(2,1)}, u32[]{:S(2)}, u32[]{:S(2)}) async-start(bf16[16,8,3072]{2,1,0:T(8,128)(2,1)} %shard_map.46), calls=%async_computation.1 | async-start | bytes 1572864 | tf_op jit(solution)/shard_map/all_to_all | solution.py:219
  28.1 1.4 %copy-start.1 = (bf16[3072,384]{1,0:T(8,128)(2,1)}, bf16[3072,384]{1,0:T(8,128)(2,1)S(1)}, u32[]{:S(2)}) copy-start(bf16[3072,384]{1,0:T(8,128)(2,1)S(1)} %shard_map.47) | copy-start | bytes 7077892
  42.0 30.1 %collective-permute-start.5 = (bf16[3072,384]{1,0:T(8,128)(2,1)}, bf16[3072,384]{1,0:T(8,128)(2,1)}, u32[]{:S(2)}, u32[]{:S(2)}) collective-permute-start(bf16[3072,384]{1,0:T(8,128)(2,1)} %copy-done.1), channel_id=1, source_target_pairs={{0,64},{32,224},{64,128},{96,32},{128,192},{160,96},{192,0},{224,1... | collective-permute-start | bytes 7077896 | tf_op jit(solution)/shard_map/ppermute | solution.py:232
  42.0 14.7 %collective-permute-start.1 = (bf16[16,8,3072]{2,1,0:T(8,128)(2,1)}, bf16[16,8,3072]{2,1,0:T(8,128)(2,1)S(1)}, u32[]{:S(2)}, u32[]{:S(2)}) collective-permute-start(bf16[16,8,3072]{2,1,0:T(8,128)(2,1)} %all-to-all-done.1), channel_id=1, source_target_pairs={{0,1},{1,2},{2,3},{3,4},{4,5},{5,6},{6,7},{7,0},{32,39},{33,32},{3... | collective-permute-start | bytes 2359304 | tf_op jit(solution)/shard_map/ppermute | solution.py:238
  48.3 8.3 %collective-permute-start.2 = (bf16[8,8,3072]{2,1,0:T(8,128)(2,1)S(1)}, bf16[8,8,3072]{2,1,0:T(8,128)(2,1)S(1)}, u32[]{:S(2)}, u32[]{:S(2)}) collective-permute-start(bf16[8,8,3072]{2,1,0:T(8,128)(2,1)S(1)} %slice_select_fusion.1.refs_0_), channel_id=1, source_target_pairs={{0,24},{8,0},{16,8},{24,16},{32,40},{40,48},{48,56},{56,32},{64,88... | collective-permute-start | bytes 1179656 | tf_op jit(solution)/shard_map/ppermute | solution.py:241
  56.7 12.1 %collective-permute-start.3 = (bf16[16,8,3072]{2,1,0:T(8,128)(2,1)S(1)}, bf16[16,8,3072]{2,1,0:T(8,128)(2,1)S(1)}, u32[]{:S(2)}, u32[]{:S(2)}) collective-permute-start(bf16[16,8,3072]{2,1,0:T(8,128)(2,1)S(1)} %collective-permute-done.1.refs_2_), channel_id=1, source_target_pairs={{0,1},{1,2},{2,3},{3,4},{4,5},{5,6},{6,7},{7,0},{32,39},{33,32},{3... | collective-permute-start | bytes 2359304 | tf_op jit(solution)/shard_map/ppermute | solution.py:238
  59.9 12.3 %collective-permute-start.4 = (bf16[16,8,3072]{2,1,0:T(8,128)(2,1)S(1)}, bf16[16,8,3072]{2,1,0:T(8,128)(2,1)S(1)}, u32[]{:S(2)}, u32[]{:S(2)}) collective-permute-start(bf16[16,8,3072]{2,1,0:T(8,128)(2,1)S(1)} %collective-permute-done.1.refs_2_), channel_id=1, source_target_pairs={{0,24},{8,0},{16,8},{24,16},{32,40},{40,48},{48,56},{56,32},{64,88... | collective-permute-start | bytes 2359304 | tf_op jit(solution)/shard_map/ppermute | solution.py:241
  72.1 12.3 %collective-permute-start.6 = (bf16[16,8,3072]{2,1,0:T(8,128)(2,1)S(1)}, bf16[16,8,3072]{2,1,0:T(8,128)(2,1)S(1)}, u32[]{:S(2)}, u32[]{:S(2)}) collective-permute-start(bf16[16,8,3072]{2,1,0:T(8,128)(2,1)S(1)} %collective-permute-done.3.refs_4_), channel_id=1, source_target_pairs={{0,1},{1,2},{2,3},{3,4},{4,5},{5,6},{6,7},{7,0},{32,39},{33,32},{3... | collective-permute-start | bytes 2359304 | tf_op jit(solution)/shard_map/ppermute | solution.py:238
  75.5 12.1 %collective-permute-start.7 = (bf16[16,8,3072]{2,1,0:T(8,128)(2,1)S(1)}, bf16[16,8,3072]{2,1,0:T(8,128)(2,1)S(1)}, u32[]{:S(2)}, u32[]{:S(2)}) collective-permute-start(bf16[16,8,3072]{2,1,0:T(8,128)(2,1)S(1)} %collective-permute-done.3.refs_4_), channel_id=1, source_target_pairs={{0,24},{8,0},{16,8},{24,16},{32,40},{40,48},{48,56},{56,32},{64,88... | collective-permute-start | bytes 2359304 | tf_op jit(solution)/shard_map/ppermute | solution.py:241
  77.8 10.6 %collective-permute-start.8 = (bf16[1536,384]{1,0:T(8,128)(2,1)S(1)}, bf16[1536,384]{1,0:T(8,128)(2,1)S(1)}, u32[]{:S(2)}, u32[]{:S(2)}) collective-permute-start(bf16[1536,384]{1,0:T(8,128)(2,1)S(1)} %get-tuple-element.40), channel_id=1, source_target_pairs={{0,32},{32,0},{64,96},{96,64},{128,160},{160,128},{192,224},{224,1... | collective-permute-start | bytes 3538952 | tf_op jit(solution)/shard_map/ppermute | solution.py:250
  77.9 10.5 %collective-permute-start.9 = (bf16[1536,384]{1,0:T(8,128)(2,1)S(1)}, bf16[1536,384]{1,0:T(8,128)(2,1)S(1)}, u32[]{:S(2)}, u32[]{:S(2)}) collective-permute-start(bf16[1536,384]{1,0:T(8,128)(2,1)S(1)} %get-tuple-element.39), channel_id=1, source_target_pairs={{0,32},{32,0},{64,96},{96,64},{128,160},{160,128},{192,224},{224,1... | collective-permute-start | bytes 3538952 | tf_op jit(solution)/shard_map/ppermute | solution.py:250
  87.6 7.0 %collective-permute-start.11 = (bf16[8,8,3072]{2,1,0:T(8,128)(2,1)S(1)}, bf16[8,8,3072]{2,1,0:T(8,128)(2,1)S(1)}, u32[]{:S(2)}, u32[]{:S(2)}) collective-permute-start(bf16[8,8,3072]{2,1,0:T(8,128)(2,1)S(1)} %slice_select_fusion), channel_id=1, source_target_pairs={{0,1},{1,2},{2,3},{3,4},{4,5},{5,6},{6,7},{7,0},{32,39},{33,32},{3... | collective-permute-start | bytes 1179656 | tf_op jit(solution)/shard_map/ppermute | solution.py:238
  88.4 16.6 %collective-permute-start.10 = (bf16[16,8,3072]{2,1,0:T(8,128)(2,1)S(1)}, bf16[16,8,3072]{2,1,0:T(8,128)(2,1)S(1)}, u32[]{:S(2)}, u32[]{:S(2)}) collective-permute-start(bf16[16,8,3072]{2,1,0:T(8,128)(2,1)S(1)} %collective-permute-done.6.refs_0_), channel_id=1, source_target_pairs={{0,24},{8,0},{16,8},{24,16},{32,40},{40,48},{48,56},{56,32},{64,88... | collective-permute-start | bytes 2359304 | tf_op jit(solution)/shard_map/ppermute | solution.py:241
  94.6 10.3 %collective-permute-start.12 = (bf16[8,8,3072]{2,1,0:T(8,128)(2,1)S(1)}, bf16[8,8,3072]{2,1,0:T(8,128)(2,1)S(1)}, u32[]{:S(2)}, u32[]{:S(2)}) collective-permute-start(bf16[8,8,3072]{2,1,0:T(8,128)(2,1)S(1)} %collective-permute-done.11.refs_2_), channel_id=1, source_target_pairs={{0,24},{8,0},{16,8},{24,16},{32,40},{40,48},{48,56},{56,32},{64,88... | collective-permute-start | bytes 1179656 | tf_op jit(solution)/shard_map/ppermute | solution.py:241
  94.6 5.1 %collective-permute-start.14 = (f32[160,384]{1,0:T(8,128)S(1)}, f32[160,384]{1,0:T(8,128)S(1)}, u32[]{:S(2)}, u32[]{:S(2)}) collective-permute-start(f32[160,384]{1,0:T(8,128)S(1)} %pad_maximum_fusion.2), channel_id=1, source_target_pairs={{0,192},{32,224},{64,0},{96,32},{128,64},{160,96},{192,128},{224,1... | collective-permute-start | bytes 737288 | tf_op jit(solution)/shard_map/ppermute | solution.py:176
  95.6 6.3 %collective-permute-start.13 = (f32[160,384]{1,0:T(8,128)S(1)}, f32[160,384]{1,0:T(8,128)S(1)}, u32[]{:S(2)}, u32[]{:S(2)}) collective-permute-start(f32[160,384]{1,0:T(8,128)S(1)} %pad_maximum_fusion.1), channel_id=1, source_target_pairs={{0,64},{32,96},{64,128},{96,160},{128,192},{160,224},{192,0},{224,... | collective-permute-start | bytes 737288 | tf_op jit(solution)/shard_map/ppermute | solution.py:175
  106.4 5.9 %collective-permute-start.17 = (f32[96,384]{1,0:T(8,128)S(1)}, f32[96,384]{1,0:T(8,128)S(1)}, u32[]{:S(2)}, u32[]{:S(2)}) collective-permute-start(f32[96,384]{1,0:T(8,128)S(1)} %pad_maximum_fusion.3), channel_id=1, source_target_pairs={{0,64},{32,96},{64,128},{96,160},{128,192},{160,224},{192,0},{224,... | collective-permute-start | bytes 442376 | tf_op jit(solution)/shard_map/ppermute | solution.py:175
  106.5 5.8 %collective-permute-start.19 = (f32[96,384]{1,0:T(8,128)S(1)}, f32[96,384]{1,0:T(8,128)S(1)}, u32[]{:S(2)}, u32[]{:S(2)}) collective-permute-start(f32[96,384]{1,0:T(8,128)S(1)} %pad_maximum_fusion.4), channel_id=1, source_target_pairs={{0,192},{32,224},{64,0},{96,32},{128,64},{160,96},{192,128},{224,1... | collective-permute-start | bytes 442376 | tf_op jit(solution)/shard_map/ppermute | solution.py:176
  109.3 5.8 %collective-permute-start.15 = (f32[80,384]{1,0:T(8,128)S(1)}, f32[80,384]{1,0:T(8,128)S(1)}, u32[]{:S(2)}, u32[]{:S(2)}) collective-permute-start(f32[80,384]{1,0:T(8,128)S(1)} %get-tuple-element.42), channel_id=1, source_target_pairs={{0,64},{32,96},{64,128},{96,160},{128,192},{160,224},{192,0},{224,... | collective-permute-start | bytes 368648 | tf_op jit(solution)/shard_map/ppermute | solution.py:181
  109.4 5.7 %collective-permute-start.16 = (f32[80,384]{1,0:T(8,128)S(1)}, f32[80,384]{1,0:T(8,128)S(1)}, u32[]{:S(2)}, u32[]{:S(2)}) collective-permute-start(f32[80,384]{1,0:T(8,128)S(1)} %get-tuple-element.41), channel_id=1, source_target_pairs={{0,192},{32,224},{64,0},{96,32},{128,64},{160,96},{192,128},{224,1... | collective-permute-start | bytes 368648 | tf_op jit(solution)/shard_map/ppermute | solution.py:181
  112.3 4.6 %collective-permute-start.18 = (f32[48,384]{1,0:T(8,128)S(1)}, f32[48,384]{1,0:T(8,128)S(1)}, u32[]{:S(2)}, u32[]{:S(2)}) collective-permute-start(f32[48,384]{1,0:T(8,128)S(1)} %get-tuple-element.48), channel_id=1, source_target_pairs={{0,64},{32,96},{64,128},{96,160},{128,192},{160,224},{192,0},{224,... | collective-permute-start | bytes 221192 | tf_op jit(solution)/shard_map/ppermute | solution.py:181
  112.4 4.5 %collective-permute-start.20 = (f32[48,384]{1,0:T(8,128)S(1)}, f32[48,384]{1,0:T(8,128)S(1)}, u32[]{:S(2)}, u32[]{:S(2)}) collective-permute-start(f32[48,384]{1,0:T(8,128)S(1)} %get-tuple-element.47), channel_id=1, source_target_pairs={{0,192},{32,224},{64,0},{96,32},{128,64},{160,96},{192,128},{224,1... | collective-permute-start | bytes 221192 | tf_op jit(solution)/shard_map/ppermute | solution.py:181
  116.9 4.4 %copy-start.4 = (f32[256,384]{1,0:T(8,128)}, f32[256,384]{1,0:T(8,128)S(1)}, u32[]{:S(2)}) copy-start(f32[256,384]{1,0:T(8,128)S(1)} %pad_maximum_fusion.mine_ref) | copy-start | bytes 1179652
  117.0 4.4 %collective-permute-start.21 = (f32[256,384]{1,0:T(8,128)S(1)}, f32[256,384]{1,0:T(8,128)S(1)}, u32[]{:S(2)}, u32[]{:S(2)}) collective-permute-start(f32[256,384]{1,0:T(8,128)S(1)} %pad_maximum_fusion.mine_ref), channel_id=1, source_target_pairs={{0,32},{32,0},{64,96},{96,64},{128,160},{160,128},{192,224},{224,1... | collective-permute-start | bytes 1179656 | tf_op jit(solution)/shard_map/ppermute | solution.py:287
  121.3 0.8 copy-start.5

commit v3 on v2

--- a/solution.py
+++ b/solution.py
@@ -81,52 +81,59 @@
     return pl.ds(pl.multiple_of(index * TP, TP), TP)
 
 
-def run_copies(jobs, out_ref, sems):
+def run_copies(jobs, sems):
     for phase in range(2):
-        for source, tile, many, place in jobs:
-
-            def move(i, carry, source=source, tile=tile, place=place):
-                copy = pltpu.make_async_copy(source.at[tile_rows(tile + i)], out_ref.at[tile_rows(place + i)], sems.at[place + i])
+        for source, tile, many, out_ref, place, sem in jobs:
+
+            def move(i, carry, source=source, tile=tile, out_ref=out_ref, place=place, sem=sem):
+                copy = pltpu.make_async_copy(source.at[tile_rows(tile + i)], out_ref.at[tile_rows(place + i)], sems.at[sem + i])
                 copy.start() if phase == 0 else copy.wait()
                 return carry
 
             lax.fori_loop(0, many, move, 0)
 
 
-def own_tiles(border, core, start, count, mine_ref, other_ref, place):
+def own_tiles(border, core, start, count, mine_ref, other_ref, out_ref, place, sem):
     lower = jnp.clip(border - start, 0, count)
     jobs = []
-    for upper, tile, many, at in ((0, start, lower, place), (1, jnp.maximum(start - border, 0), count - lower, place + lower)):
-        jobs.append((mine_ref, tile, jnp.where(core == upper, many, 0), at))
-        jobs.append((other_ref, tile, jnp.where(core != upper, many, 0), at))
+    for upper, tile, many, at in ((0, start, lower, 0), (1, jnp.maximum(start - border, 0), count - lower, lower)):
+        jobs.append((mine_ref, tile, jnp.where(core == upper, many, 0), out_ref, place + at, sem + at))
+        jobs.append((other_ref, tile, jnp.where(core != upper, many, 0), out_ref, place + at, sem + at))
     return jobs
 
 
-def send_tiles(groups, share, tiles_ref, assign_ref, mine_ref, other_ref, out_ref, held_ref, block_ref, sems):
+def send_tiles(groups, share, tiles_ref, assign_ref, mine_ref, other_ref, *refs):
+    *out_refs, held_ref, block_ref, sems = refs
     held, total, right, left = balance(tiles_ref, assign_ref, held_ref, block_ref, groups)
     group = lax.axis_index("grp")
     x, core = lax.div(group, 2), lax.rem(group, 2)
     go_right, go_left = pick(right, x), pick(left, x)
     start = jnp.where(core == 0, pick(total, x) - go_right, 0)
     count = jnp.where(core == 0, go_right, go_left)
-    run_copies(own_tiles(pick(held[0::2], x), core, start, count, mine_ref, other_ref, 0), out_ref, sems)
-
-
-def join_tiles(groups, share, tiles_ref, assign_ref, mine_ref, other_ref, got_ref, *refs):
-    *their_refs, out_ref, held_ref, block_ref, sems = refs
+    each = share // len(out_refs)
+    jobs = []
+    for i, ref in enumerate(out_refs):
+        many = jnp.clip(count - i * each, 0, each)
+        jobs += own_tiles(pick(held[0::2], x), core, start + i * each, many, mine_ref, other_ref, ref, 0, i * each)
+    run_copies(jobs, sems)
+
+
+def join_tiles(groups, share, tiles_ref, assign_ref, mine_ref, other_ref, *refs):
+    *moved_refs, out_ref, held_ref, block_ref, sems = refs
     held, total, right, left = balance(tiles_ref, assign_ref, held_ref, block_ref, groups)
     group = lax.axis_index("grp")
     x, core = lax.div(group, 2), lax.rem(group, 2)
     (_, _, n), (_, _, m), (_, start, _) = runs_of(x, total, right, left, groups // 2)
-    jobs = [
-        (got_ref, 0, jnp.where(core == 0, n, 0), 0),
-        (got_ref, 0, jnp.where(core == 0, 0, m), n),
-    ]
-    each = share // len(their_refs)
-    for i, ref in enumerate(their_refs):
-        jobs.append((ref, 0, jnp.clip(jnp.where(core == 0, m, n) - i * each, 0, each), jnp.where(core == 0, n, 0) + i * each))
-    jobs += own_tiles(pick(held[0::2], x), core, start, share - n - m, mine_ref, other_ref, n + m)
-    run_copies(jobs, out_ref, sems)
+    halves = len(moved_refs) // 2
+    each = share // halves
+    jobs = []
+    for i, ref in enumerate(moved_refs):
+        h, below = i % halves, (core == 0) == (i < halves)
+        many = jnp.clip(jnp.where(below, n, m) - h * each, 0, each)
+        place = jnp.where(below, 0, n) + h * each
+        jobs.append((ref, 0, many, out_ref, place, place))
+    kept = own_tiles(pick(held[0::2], x), core, start, share - n - m, mine_ref, other_ref, out_ref, n + m, n + m)
+    run_copies(jobs + kept, sems)
 
 
 def multiply(ny, *refs):
@@ -150,24 +157,42 @@
         row += n // 2 * octet if i % 2 else 0
 
 
-def finish(nz, rows, mine_ref, other_ref, out_ref):
+def finish(nz, rows, mine_ref, other_ref, out_ref, sems):
     core, z = lax.rem(lax.axis_index("grp"), 2), lax.axis_index("col")
     h = rows // 2
     last = nz // 2 * rows - h
-    for q in range(nz // 2):
-        r = lax.rem(core * (nz // 2) + q - z + nz, nz)
-        ends = jnp.logical_or(r == 0, r == nz // 2)
-        above = r < nz // 2
-        step = jnp.where(above, r, nz - r)
-        for part in range(2):
-            start = jnp.where(r == 0, 0, jnp.where(r == nz // 2, last, h + rows * (step - 1) + part * h))
-            holder = jnp.where(ends, part, jnp.where(above, 1, 0))
-            rows_in = pl.ds(pl.multiple_of(start, h), h)
-            for ref, here in ((mine_ref, holder == core), (other_ref, holder != core)):
-
-                @pl.when(here)
-                def _(ref=ref, q=q, part=part, rows_in=rows_in):
-                    out_ref[q * rows + part * h : q * rows + (part + 1) * h, :] = ref[rows_in, :]
+    for phase in range(2):
+        for q in range(nz // 2):
+            r = lax.rem(core * (nz // 2) + q - z + nz, nz)
+            ends = jnp.logical_or(r == 0, r == nz // 2)
+            above = r < nz // 2
+            step = jnp.where(above, r, nz - r)
+            for part in range(2):
+                start = jnp.where(r == 0, 0, jnp.where(r == nz // 2, last, h + rows * (step - 1) + part * h))
+                holder = jnp.where(ends, part, jnp.where(above, 1, 0))
+                rows_in = pl.ds(pl.multiple_of(start, h), h)
+                i = 2 * q + part
+                for ref, here in ((mine_ref, holder == core), (other_ref, holder != core)):
+
+                    @pl.when(here)
+                    def _(ref=ref, i=i, rows_in=rows_in):
+                        copy = pltpu.make_async_copy(ref.at[rows_in], out_ref.at[pl.ds(i * h, h)], sems.at[i])
+                        copy.start() if phase == 0 else copy.wait()
+
+
+def nothing(in_ref, out_ref):
+    pass
+
+
+def collect(block):
+    return pl.pallas_call(
+        nothing,
+        out_shape=jax.ShapeDtypeStruct(block.shape, block.dtype),
+        in_specs=[ANY],
+        out_specs=ANY,
+        input_output_aliases={0: 0},
+        cost_estimate=pl.CostEstimate(flops=20_000_000_000, bytes_accessed=0, transcendentals=0),
+    )(block)
 
 
 def near_chips(p, up, down):
@@ -219,46 +244,47 @@
     pair = lax.all_to_all(packed, ("grp", "row"), 0, 0, axis_index_groups=pairs, tiled=True)
 
     tiles = jax.ShapeDtypeStruct((wide, cols), jnp.bfloat16)
+    half_tiles = jax.ShapeDtypeStruct((wide // 2, cols), jnp.bfloat16)
     scratch = small + [pltpu.SemaphoreType.DMA((share,))]
     sent = pl.pallas_call(
         functools.partial(send_tiles, groups, share),
+        out_shape=(half_tiles, half_tiles),
+        in_specs=[SMEM, SMEM, ANY, ANY],
+        out_specs=(VMEM, VMEM),
+        scratch_shapes=scratch,
+        compiler_params=limit,
+    )(block_tiles, assign, mine, other)
+    pair, *sent = barrier((pair, *sent))
+    got = [lax.ppermute(part, "grp", apart) for part in sent]
+    def half_of(block):
+        h = block.shape[0] // 2
+        return jnp.where(core == 0, block[:h], block[h:])
+
+    def z_step(block):
+        return lax.ppermute(block, ("grp", "col"), along)
+
+    def y_step(block):
+        return lax.ppermute(block, ("grp", "row"), beside)
+
+    blocks, near = [half_of(pair), z_step(pair)], [y_step(half_of(pair))]
+    for s in range(1, nz // 2):
+        near.append(y_step(blocks[s]))
+        beyond = z_step(half_of(blocks[s]) if s == nz // 2 - 1 else blocks[s])
+        beyond, near[s - 1] = barrier((beyond, collect(near[s - 1])))
+        if s < nz // 2 - 1:
+            beyond, got[s - 1] = barrier((beyond, got[s - 1]))
+        blocks.append(beyond)
+    near.append(y_step(blocks[-1]))
+    order = [part for both in zip(blocks, near) for part in both]
+    theirs = [lax.ppermute(part, "grp", swap) for part in got]
+    held = pl.pallas_call(
+        functools.partial(join_tiles, groups, share),
         out_shape=tiles,
-        in_specs=[SMEM, SMEM, ANY, ANY],
+        in_specs=[SMEM, SMEM] + [ANY] * (2 + len(got) + len(theirs)),
         out_specs=VMEM,
         scratch_shapes=scratch,
         compiler_params=limit,
-    )(block_tiles, assign, mine, other)
-    pair, sent = barrier((pair, sent))
-    got = lax.ppermute(sent, "grp", apart)
-    def half_of(block):
-        h = block.shape[0] // 2
-        return jnp.where(core == 0, block[:h], block[h:])
-
-    def z_step(block):
-        return lax.ppermute(block, ("grp", "col"), along)
-
-    def y_step(block):
-        return lax.ppermute(block, ("grp", "row"), beside)
-
-    block, order = pair, []
-    for s in range(nz // 2 - 1):
-        kept = half_of(block) if s == 0 else block
-        block, near = barrier((z_step(block), y_step(kept)))
-        if s == nz // 2 - 3:
-            block, near, got = barrier((block, near, got))
-        order += [kept, near]
-    theirs = [lax.ppermute(part, "grp", swap) for part in jnp.split(got, 2)]
-    end = z_step(half_of(block))
-    order += [block, y_step(block), end, y_step(end)]
-
-    held = pl.pallas_call(
-        functools.partial(join_tiles, groups, share),
-        out_shape=tiles,
-        in_specs=[SMEM, SMEM] + [ANY] * (3 + len(theirs)),
-        out_specs=VMEM,
-        scratch_shapes=scratch,
-        compiler_params=limit,
-    )(block_tiles, assign, mine, other, got, *theirs)
+    )(block_tiles, assign, mine, other, *got, *theirs)
 
     def sums(parts):
         n = sum(part.shape[0] for part in parts) * octet
@@ -282,8 +308,9 @@
     return pl.pallas_call(
         functools.partial(finish, nz, rows),
         out_shape=jax.ShapeDtypeStruct((nz // 2 * rows, cols), jnp.float32),
-        in_specs=[VMEM, VMEM],
-        out_specs=VMEM,
+        in_specs=[ANY, ANY],
+        out_specs=ANY,
+        scratch_shapes=[pltpu.SemaphoreType.DMA((nz,))],
     )(done, lax.ppermute(done, "grp", swap))
 
 

time: 126 us -> 145 us (1.15)
  Pallas kernels: 13.1 us -> 28 us
  starting transfers between devices: 35.3 us -> 41.6 us
  local copies, waits for them, and re-layouts: 4.09 us -> 1.57 us
  other arithmetic: 1.43 us -> 3.3 us
    ppermute x5, waiting for transfers between devices: 17.3 us -> 0.01 us  [y_step(): return lax.ppermute(block, ('grp', 'row'), beside)]
    ppermute x4, waiting for transfers between devices: 16.2 us -> 30.5 us  [z_step(): return lax.ppermute(block, ('grp', 'col'), along)]
    pallas_call x1, Pallas kernels: 1.95 us -> 13.1 us  [body(): pl.pallas_call(functools.partial(finish, nz, rows), out_shape=jax.ShapeDt...]
    ppermute x3 -> x4, starting transfers between devices: 0.59 us -> 4.51 us  [the longest x2 3.19 us: body(): theirs = [lax.ppermute(part, 'grp', swap) for part in got]]
    pallas_call x2, Pallas kernels: 3.56 us -> 6.99 us  [sums(): pl.pallas_call(functools.partial(multiply, ny), out_shape=jax.ShapeDtypeS...]
    ppermute x1, starting transfers between devices: 3.03 us -> 5.3 us  [body(): lax.ppermute(done, 'grp', swap)]
    split x1 -> x0, local copies, waits for them, and re-layouts: 1.86 us -> none  [body(): theirs = [lax.ppermute(part, 'grp', swap) for part in jnp.split(got, 2)]]
    select_n x2, other arithmetic: 1.2 us -> 3.06 us  [half_of(): return jnp.where(core == 0, block[:h], block[h:])]
  transfers between devices with their start and end apart: 23 -> 24, of which waited for: 13 -> 10; matrix products, arithmetic and copies ran while one was open for 3% -> 2% of each run, Pallas kernels for 8% -> 8%
where the time goes in v3:
time: 145 us; the launch traced here: 144 us
  waiting for transfers between devices  54.9 us (38%)
  starting transfers between devices  41.6 us (29%)
  Pallas kernels  28 us (19%)
  blocking collectives  14.8 us (10%)
  other arithmetic  3.3 us (2%)
  local copies, waits for them, and re-layouts  1.57 us (1%)
    ppermute x4, waiting for transfers between devices, z_step(): return lax.ppermute(block, ('grp', 'col'), along)  30.5 us
    all_to_all x1, blocking collectives, body(): lax.all_to_all(amplitudes[0].reshape(groups, octet, cap), 'grp', 0, 0, ti...  14.8 us
    all_to_all x1, waiting for transfers between devices, body(): lax.all_to_all(packed, ('grp', 'row'), 0, 0, axis_index_groups=pairs, til...  13.9 us
    pallas_call x1, Pallas kernels, body(): pl.pallas_call(functools.partial(finish, nz, rows), out_shape=jax.ShapeDt...  13.1 us
    ppermute x4, starting transfers between devices, z_step(): return lax.ppermute(block, ('grp', 'col'), along)  12 us
    pallas_call x2, Pallas kernels, sums(): pl.pallas_call(functools.partial(multiply, ny), out_shape=jax.ShapeDtypeS...  6.99 us
    ppermute x2, starting transfers between devices, passed_on(): lax.ppermute(p[3, h:] + b[:h], 'grp', down)  5.33 us
    ppermute x1, starting transfers between devices, body(): lax.ppermute(done, 'grp', swap)  5.3 us
  transfers between devices with their start and end apart: 24, of which 10 were waited for; matrix products, arithmetic and copies ran while one was open for 2% of the time, Pallas kernels for 8%

profile of v3, /device:TPU:1, one launch (start us, length us, event | category | flops | bytes accessed | tf_op | source)
XLA Modules:
  0.0 144.5 jit_solution(5264109588839098786)
XLA Ops:
  0.0 3.2 %collective-permute-start = (bf16[4608,384]{1,0:T(8,128)(2,1)}, bf16[4608,384]{1,0:T(8,128)(2,1)}, u32[]{:S(2)}, u32[]{:S(2)}) collective-permute-start(bf16[4608,384]{1,0:T(8,128)(2,1)} %bitcast.46), channel_id=1, source_target_pairs={{0,32},{32,0},{64,96},{96,64},{128,160},{160,128},{192,224},{224,1... | collective-permute-start | bytes 10616840 | tf_op jit(solution)/shard_map/ppermute | solution.py:235
  3.2 14.8 %all_to_all.10.src_ref = bf16[8,8,4608]{2,1,0:T(8,128)(2,1)} all-to-all(bf16[8,8,4608]{2,1,0:T(8,128)(2,1)} %bitcast.49), channel_id=1, replica_groups=mesh['grp'=8,'row'=4,'col'=8] {'grp'}, dimensions={0} | all-to-all | bytes 1179648 | tf_op jit(solution)/shard_map/all_to_all | solution.py:236
  18.0 3.0 %shard_map.46 = bf16[16,8,3072]{2,1,0:T(8,128)(2,1)} custom-call(s32[8]{0:T(128)} %tiles_ref.5, s32[8]{0:T(128)} %assign_ref.5, bf16[8,8,4608]{2,1,0:T(8,128)(2,1)} %all_to_all.10.src_ref), custom_call_target="tpu_custom_call" | custom-call | tf_op jit(solution)/shard_map/pallas_call | solution.py:237
  21.0 4.8 %all-to-all-start.1 = ((bf16[16,8,3072]{2,1,0:T(8,128)(2,1)}), bf16[16,8,3072]{2,1,0:T(8,128)(2,1)}, u32[]{:S(2)}, u32[]{:S(2)}) async-start(bf16[16,8,3072]{2,1,0:T(8,128)(2,1)} %shard_map.46), calls=%async_computation.1 | async-start | bytes 1572864 | tf_op jit(solution)/shard_map/all_to_all | solution.py:244
  25.8 0.0 collective-permute-done.other_ref
  25.8 0.0 copy-done
  25.8 0.0 copy-done.3
  25.8 0.0 copy-done.4
  25.8 2.3 %shard_map.47 = (bf16[1536,384]{1,0:T(8,128)(2,1)}, bf16[1536,384]{1,0:T(8,128)(2,1)}) custom-call(s32[8]{0:T(128)S(1)} %copy-done.3, s32[8]{0:T(128)S(1)} %copy-done.4, bf16[4608,384]{1,0:T(8,128)(2,1)S(1)} %bitcast.47, bf16[4608,384]{1,0:T(8,128)(2,1)} %collective-permute-done.other_ref), custom_call_target="tpu_custom_call" | custom-call | tf_op jit(solution)/shard_map/pallas_call | solution.py:249
  28.2 13.9 %all-to-all-done.1 = bf16[16,8,3072]{2,1,0:T(8,128)(2,1)} async-done(((bf16[16,8,3072]{2,1,0:T(8,128)(2,1)}), bf16[16,8,3072]{2,1,0:T(8,128)(2,1)}, u32[]{:S(2)}, u32[]{:S(2)}) %all-to-all-start.1) | async-done | bytes 786464 | tf_op jit(solution)/shard_map/all_to_all | solution.py:244
  42.1 5.2 %collective-permute-start.1 = (bf16[16,8,3072]{2,1,0:T(8,128)(2,1)}, bf16[16,8,3072]{2,1,0:T(8,128)(2,1)}, u32[]{:S(2)}, u32[]{:S(2)}) collective-permute-start(bf16[16,8,3072]{2,1,0:T(8,128)(2,1)} %all-to-all-done.1), channel_id=1, source_target_pairs={{0,1},{1,2},{2,3},{3,4},{4,5},{5,6},{6,7},{7,0},{32,39},{33,32},{3... | collective-permute-start | bytes 2359304 | tf_op jit(solution)/shard_map/ppermute | solution.py:264
  47.3 1.2 slice_select_fusion.1.refs_0_
  48.4 0.5 collective-permute-start.3
  48.9 0.7 copy-done.1
  49.7 0.0 collective-permute-start.4
  49.7 1.3 collective-permute-start.7
  51.0 5.5 %collective-permute-done.1.refs_2_ = bf16[16,8,3072]{2,1,0:T(8,128)(2,1)} collective-permute-done((bf16[16,8,3072]{2,1,0:T(8,128)(2,1)}, bf16[16,8,3072]{2,1,0:T(8,128)(2,1)}, u32[]{:S(2)}, u32[]{:S(2)}) %collective-permute-start.1) | collective-permute-done | bytes 786464 | tf_op jit(solution)/shard_map/ppermute | solution.py:264
  56.5 3.4 %collective-permute-start.2 = (bf16[16,8,3072]{2,1,0:T(8,128)(2,1)}, bf16[16,8,3072]{2,1,0:T(8,128)(2,1)}, u32[]{:S(2)}, u32[]{:S(2)}) collective-permute-start(bf16[16,8,3072]{2,1,0:T(8,128)(2,1)} %collective-permute-done.1.refs_2_), channel_id=1, source_target_pairs={{0,1},{1,2},{2,3},{3,4},{4,5},{5,6},{6,7},{7,0},{32,39},{33,32},{3... | collective-permute-start | bytes 2359304 | tf_op jit(solution)/shard_map/ppermute | solution.py:264
  59.9 0.4 collective-permute-start.6
  60.3 0.0 collective-permute-done.3.in_ref
  60.3 8.8 %collective-permute-done.2.refs_4_ = bf16[16,8,3072]{2,1,0:T(8,128)(2,1)} collective-permute-done((bf16[16,8,3072]{2,1,0:T(8,128)(2,1)}, bf16[16,8,3072]{2,1,0:T(8,128)(2,1)}, u32[]{:S(2)}, u32[]{:S(2)}) %collective-permute-start.2) | collective-permute-done | bytes 786464 | tf_op jit(solution)/shard_map/ppermute | solution.py:264
  69.2 0.0 collective-permute-done.4.refs_0_
  69.2 3.4 %collective-permute-start.5 = (bf16[16,8,3072]{2,1,0:T(8,128)(2,1)}, bf16[16,8,3072]{2,1,0:T(8,128)(2,1)}, u32[]{:S(2)}, u32[]{:S(2)}) collective-permute-start(bf16[16,8,3072]{2,1,0:T(8,128)(2,1)} %collective-permute-done.2.refs_4_), channel_id=1, source_target_pairs={{0,1},{1,2},{2,3},{3,4},{4,5},{5,6},{6,7},{7,0},{32,39},{33,32},{3... | collective-permute-start | bytes 2359304 | tf_op jit(solution)/shard_map/ppermute | solution.py:264
  72.6 0.4 collective-permute-start.9
  73.0 0.0 collective-permute-start.10
  73.0 0.0 collective-permute-done.6.in_ref
  73.0 8.8 %collective-permute-done.5.refs_0_ = bf16[16,8,3072]{2,1,0:T(8,128)(2,1)} collective-permute-done((bf16[16,8,3072]{2,1,0:T(8,128)(2,1)}, bf16[16,8,3072]{2,1,0:T(8,128)(2,1)}, u32[]{:S(2)}, u32[]{:S(2)}) %collective-permute-start.5) | collective-permute-done | bytes 786464 | tf_op jit(solution)/shard_map/ppermute | solution.py:264
  81.9 0.0 collective-permute-done.7.refs_1_
  81.9 3.2 %collective-permute-start.11 = (bf16[1536,384]{1,0:T(8,128)(2,1)}, bf16[1536,384]{1,0:T(8,128)(2,1)}, u32[]{:S(2)}, u32[]{:S(2)}) collective-permute-start(bf16[1536,384]{1,0:T(8,128)(2,1)} %collective-permute-done.7.refs_1_), channel_id=1, source_target_pairs={{0,32},{32,0},{64,96},{96,64},{128,160},{160,128},{192,224},{224,1... | collective-permute-start | bytes 3538952 | tf_op jit(solution)/shard_map/ppermute | solution.py:279
  85.1 0.4 collective-permute-start.12
  85.5 1.9 %slice_select_fusion = bf16[8,8,3072]{2,1,0:T(8,128)(2,1)} fusion(bf16[16,8,3072]{2,1,0:T(8,128)(2,1)} %collective-permute-done.5.refs_0_, pred[]{:T(512)S(6)} %eq.2), kind=kLoop, calls=%fused_computation.1 | loop fusion | flops 196608 | bytes 1179649 | tf_op jit(solution)/shard_map/jit(_where)/select_n | solution.py:261
  87.4 0.0 collective-permute-start.8
  87.4 0.0 collective-permute-done.9.in_ref
  87.4 7.2 %collective-permute-done.8.refs_2_ = bf16[8,8,3072]{2,1,0:T(8,128)(2,1)} collective-permute-done((bf16[8,8,3072]{2,1,0:T(8,128)(2,1)}, bf16[8,8,3072]{2,1,0:T(8,128)(2,1)}, u32[]{:S(2)}, u32[]{:S(2)}) %collective-permute-start.8) | collective-permute-done | bytes 393248 | tf_op jit(solution)/shard_map/ppermute | solution.py:264
  94.6 0.0 collective-permute-start.13
  94.6 0.0 collective-permute-done.10.refs_2_
  94.6 0.0 collective-permute-done.11.refs_3_
  94.6 2.5 %shard_map.51.refs_6_.refs_4_ = bf16[3072,384]{1,0:T(8,128)(2,1)S(1)} custom-call(s32[8]{0:T(128)S(1)} %copy-done.3, s32[8]{0:T(128)S(1)} %copy-done.4, bf16[4608,384]{1,0:T(8,128)(2,1)S(1)} %bitcast.48, bf16[4608,384]{1,0:T(8,128)(2,1)} %collective-permute-done.other_ref, bf16[1536,384]{1,0:T(8,128)(2,1)} %collective-permute-done.4.refs_0_, ...), custom_call_target="tpu_custom_call" | custom-call | tf_op jit(solution)/shard_map/pallas_call | solution.py:280
  97.2 4.2 %shard_map.52 = f32[4,160,384]{2,1,0:T(8,128)S(1)} custom-call(bf16[8,8,3072]{2,1,0:T(8,128)(2,1)S(1)} %copy-done.2, bf16[8,8,3072]{2,1,0:T(8,128)(2,1)} %shard_map.48.refs_1_, bf16[16,8,3072]{2,1,0:T(8,128)(2,1)} %collective-permute-done.1.refs_2_, bf16[16,8,3072]{2,1,0:T(8,128)(2,1)} %shard_map.49.refs_3_, ...), custom_call_target="tpu_custom_call" | custom-call | tf_op jit(solution)/shard_map/pallas_call | solution.py:291
  101.4 1.7 %collective-permute-start.15 = (f32[160,384]{1,0:T(8,128)S(1)}, f32[160,384]{1,0:T(8,128)S(1)}, u32[]{:S(2)}, u32[]{:S(2)}) collective-permute-start(f32[160,384]{1,0:T(8,128)S(1)} %pad_maximum_fusion.2), channel_id=1, source_target_pairs={{0,192},{32,224},{64,0},{96,32},{128,64},{160,96},{192,128},{224,1... | collective-permute-start | bytes 737288 | tf_op jit(solution)/shard_map/ppermute | solution.py:201
  103.1 0.1 collective-permute-start.14
  103.2 0.0 collective-permute-done.13.refs_3_
  103.2 0.0 collective-permute-done.12.refs_1_
  103.2 3.7 %collective-permute-done.15 = f32[160,384]{1,0:T(8,128)S(1)} collective-permute-done((f32[160,384]{1,0:T(8,128)S(1)}, f32[160,384]{1,0:T(8,128)S(1)}, u32[]{:S(2)}, u32[]{:S(2)}) %collective-permute-start.15) | collective-permute-done | bytes 245792 | tf_op jit(solution)/shard_map/ppermute | solution.py:201
  106.9 3.2 %collective-permute-done.14 = f32[160,384]{1,0:T(8,128)S(1)} collective-permute-done((f32[160,384]{1,0:T(8,128)S(1)}, f32[160,384]{1,0:T(8,128)S(1)}, u32[]{:S(2)}, u32[]{:S(2)}) %collective-permute-start.14) | collective-permute-done | bytes 245792 | tf_op jit(solution)/shard_map/ppermute | solution.py:200
  110.2 2.8 %shard_map.53 = f32[4,96,384]{2,1,0:T(8,128)S(1)} custom-call(bf16[16,8,3072]{2,1,0:T(8,128)(2,1)} %collective-permute-done.5.refs_0_, bf16[16,8,3072]{2,1,0:T(8,128)(2,1)} %collective-permute-done.12.refs_1_, bf16[8,8,3072]{2,1,0:T(8,128)(2,1)} %collective-permute-done.8.refs_2_, bf16[8,8,3072]{2,1,0:T(8,128)(2,1)S(1)} %collective-permute-done.13.refs_3_, ...), custom_call_target="tpu_custom_call" | custom-call | tf_op jit(solution)/shard_map/pallas_call | solution.py:291
  113.1 0.1 collective-permute-start.18
  113.2 2.7 %collective-permute-start.20 = (f32[96,384]{1,0:T(8,128)S(1)}, f32[96,384]{1,0:T(8,128)S(1)}, u32[]{:S(2)}, u32[]{:S(2)}) collective-permute-start(f32[96,384]{1,0:T(8,128)S(1)} %pad_maximum_fusion.4), channel_id=1, source_target_pairs={{0,192},{32,224},{64,0},{96,32},{128,64},{160,96},{192,128},{224,1... | collective-permute-start | bytes 442376 | tf_op jit(solution)/shard_map/ppermute | solution.py:201
  115.9 0.1 collective-permute-start.16
  116.0 2.7 %collective-permute-start.17 = (f32[80,384]{1,0:T(8,128)S(1)}, f32[80,384]{1,0:T(8,128)S(1)}, u32[]{:S(2)}, u32[]{:S(2)}) collective-permute-start(f32[80,384]{1,0:T(8,128)S(1)} %get-tuple-element.47), channel_id=1, source_target_pairs={{0,192},{32,224},{64,0},{96,32},{128,64},{160,96},{192,128},{224,1... | collective-permute-start | bytes 368648 | tf_op jit(solution)/shard_map/ppermute | solution.py:206
  118.7 0.0 collective-permute-done.18
  118.7 0.0 collective-permute-done.20
  118.7 0.1 collective-permute-start.19
  118.8 2.7 %collective-permute-start.21 = (f32[48,384]{1,0:T(8,128)S(1)}, f32[48,384]{1,0:T(8,128)S(1)}, u32[]{:S(2)}, u32[]{:S(2)}) collective-permute-start(f32[48,384]{1,0:T(8,128)S(1)} %get-tuple-element.53), channel_id=1, source_target_pairs={{0,192},{32,224},{64,0},{96,32},{128,64},{160,96},{192,128},{224,1... | collective-permute-start | bytes 221192 | tf_op jit(solution)/shard_map/ppermute | solution.py:206
  121.5 0.9 collective-permute-done.16
  122.4 0.0 collective-permute-done.17
  122.4 0.1 fusion.1
  122.5 1.3 collective-permute-done.19
  123.7 0.0 collective-permute-done.21
  123.8 0.0 copy-start.5
  123.8 5.3 %collective-permute-start.22 = (f32[256,384]{1,0:T(8,128)S(1)}, f32[256,384]{1,0:T(8,128)S(1)}, u32[]{:S(2)}, u32[]{:S(2)}) collective-permute-start(f32[256,384]{1,0:T(8,128)S(1)} %pad_maximum_fusion.mine_ref), channel_id=1, source_target_pairs={{0,32},{32,0},{64,96},{96,64},{128,160},{160,128},{192,224},{224,1... | collective-permute-start | bytes 1179656 | tf_op jit(solution)/shard_map/ppermute | solution.py:314
  129.1 1.3 collective-permute-done.22.other_ref
  130.5 0.7 copy-done.6
  131.2 13.1 %shard_map.54 = f32[256,384]{1,0:T(8,128)} custom-call(f32[256,384]{1,0:T(8,128)} %copy-done.5, f32[256,384]{1,0:T(8,128)} %copy-done.6), custom_call_target="tpu_custom_call" | custom-call | tf_op jit(solution)/shard_map/pallas_call | solution.py:308
  (21 shorter events, 0.3 us)
Async XLA Ops:
  0.0 25.8 %collective-permute-start = (bf16[4608,384]{1,0:T(8,128)(2,1)}, bf16[4608,384]{1,0:T(8,128)(2,1)}, u32[]{:S(2)}, u32[]{:S(2)}) collective-permute-start(bf16[4608,384]{1,0:T(8,128)(2,1)} %bitcast.46), channel_id=1, source_target_pairs={{0,32},{32,0},{64,96},{96,64},{128,160},{160,128},{192,224},{224,1... | collective-permute-start | bytes 10616840 | tf_op jit(solution)/shard_map/ppermute | solution.py:235
  3.2 22.6 %copy-start = (bf16[1,4608,384]{2,1,0:T(8,128)(2,1)S(1)}, bf16[1,4608,384]{2,1,0:T(8,128)(2,1)}, u32[]{:S(2)}) copy-start(bf16[1,4608,384]{2,1,0:T(8,128)(2,1)} %param.5) | copy-start | bytes 10616836
  18.0 7.8 %copy-start.3 = (s32[8]{0:T(128)S(1)}, s32[8]{0:T(128)}, u32[]{:S(2)}) copy-start(s32[8]{0:T(128)} %tiles_ref.5) | copy-start | bytes 100
  18.0 7.8 %copy-start.4 = (s32[8]{0:T(128)S(1)}, s32[8]{0:T(128)}, u32[]{:S(2)}) copy-start(s32[8]{0:T(128)} %assign_ref.5) | copy-start | bytes 100
  21.0 21.0 %all-to-all-start.1 = ((bf16[16,8,3072]{2,1,0:T(8,128)(2,1)}), bf16[16,8,3072]{2,1,0:T(8,128)(2,1)}, u32[]{:S(2)}, u32[]{:S(2)}) async-start(bf16[16,8,3072]{2,1,0:T(8,128)(2,1)} %shard_map.46), calls=%async_computation.1 | async-start | bytes 1572864 | tf_op jit(solution)/shard_map/all_to_all | solution.py:244
  42.1 14.5 %collective-permute-start.1 = (bf16[16,8,3072]{2,1,0:T(8,128)(2,1)}, bf16[16,8,3072]{2,1,0:T(8,128)(2,1)}, u32[]{:S(2)}, u32[]{:S(2)}) collective-permute-start(bf16[16,8,3072]{2,1,0:T(8,128)(2,1)} %all-to-all-done.1), channel_id=1, source_target_pairs={{0,1},{1,2},{2,3},{3,4},{4,5},{5,6},{6,7},{7,0},{32,39},{33,32},{3... | collective-permute-start | bytes 2359304 | tf_op jit(solution)/shard_map/ppermute | solution.py:264
  48.4 11.9 %collective-permute-start.3 = (bf16[8,8,3072]{2,1,0:T(8,128)(2,1)S(1)}, bf16[8,8,3072]{2,1,0:T(8,128)(2,1)}, u32[]{:S(2)}, u32[]{:S(2)}) collective-permute-start(bf16[8,8,3072]{2,1,0:T(8,128)(2,1)S(1)} %slice_select_fusion.1.refs_0_), channel_id=1, source_target_pairs={{0,24},{8,0},{16,8},{24,16},{32,40},{40,48},{48,56},{56,32},{64,88... | collective-permute-start | bytes 1179656 | tf_op jit(solution)/shard_map/ppermute | solution.py:267
  48.9 0.7 copy-start.1
  49.7 19.5 %collective-permute-start.4 = (bf16[1536,384]{1,0:T(8,128)(2,1)}, bf16[1536,384]{1,0:T(8,128)(2,1)}, u32[]{:S(2)}, u32[]{:S(2)}) collective-permute-start(bf16[1536,384]{1,0:T(8,128)(2,1)} %get-tuple-element.31), channel_id=1, source_target_pairs={{0,64},{32,224},{64,128},{96,32},{128,192},{160,96},{192,0},{224,1... | collective-permute-start | bytes 3538952 | tf_op jit(solution)/shard_map/ppermute | solution.py:258
  49.7 32.2 %collective-permute-start.7 = (bf16[1536,384]{1,0:T(8,128)(2,1)}, bf16[1536,384]{1,0:T(8,128)(2,1)}, u32[]{:S(2)}, u32[]{:S(2)}) collective-permute-start(bf16[1536,384]{1,0:T(8,128)(2,1)} %get-tuple-element.35), channel_id=1, source_target_pairs={{0,64},{32,224},{64,128},{96,32},{128,192},{160,96},{192,0},{224,1... | collective-permute-start | bytes 3538952 | tf_op jit(solution)/shard_map/ppermute | solution.py:258
  56.5 12.7 %collective-permute-start.2 = (bf16[16,8,3072]{2,1,0:T(8,128)(2,1)}, bf16[16,8,3072]{2,1,0:T(8,128)(2,1)}, u32[]{:S(2)}, u32[]{:S(2)}) collective-permute-start(bf16[16,8,3072]{2,1,0:T(8,128)(2,1)} %collective-permute-done.1.refs_2_), channel_id=1, source_target_pairs={{0,1},{1,2},{2,3},{3,4},{4,5},{5,6},{6,7},{7,0},{32,39},{33,32},{3... | collective-permute-start | bytes 2359304 | tf_op jit(solution)/shard_map/ppermute | solution.py:264
  59.9 13.1 %collective-permute-start.6 = (bf16[16,8,3072]{2,1,0:T(8,128)(2,1)}, bf16[16,8,3072]{2,1,0:T(8,128)(2,1)}, u32[]{:S(2)}, u32[]{:S(2)}) collective-permute-start(bf16[16,8,3072]{2,1,0:T(8,128)(2,1)} %collective-permute-done.1.refs_2_), channel_id=1, source_target_pairs={{0,24},{8,0},{16,8},{24,16},{32,40},{40,48},{48,56},{56,32},{64,88... | collective-permute-start | bytes 2359304 | tf_op jit(solution)/shard_map/ppermute | solution.py:267
  69.2 12.7 %collective-permute-start.5 = (bf16[16,8,3072]{2,1,0:T(8,128)(2,1)}, bf16[16,8,3072]{2,1,0:T(8,128)(2,1)}, u32[]{:S(2)}, u32[]{:S(2)}) collective-permute-start(bf16[16,8,3072]{2,1,0:T(8,128)(2,1)} %collective-permute-done.2.refs_4_), channel_id=1, source_target_pairs={{0,1},{1,2},{2,3},{3,4},{4,5},{5,6},{6,7},{7,0},{32,39},{33,32},{3... | collective-permute-start | bytes 2359304 | tf_op jit(solution)/shard_map/ppermute | solution.py:264
  72.6 14.7 %collective-permute-start.9 = (bf16[16,8,3072]{2,1,0:T(8,128)(2,1)}, bf16[16,8,3072]{2,1,0:T(8,128)(2,1)}, u32[]{:S(2)}, u32[]{:S(2)}) collective-permute-start(bf16[16,8,3072]{2,1,0:T(8,128)(2,1)} %collective-permute-done.2.refs_4_), channel_id=1, source_target_pairs={{0,24},{8,0},{16,8},{24,16},{32,40},{40,48},{48,56},{56,32},{64,88... | collective-permute-start | bytes 2359304 | tf_op jit(solution)/shard_map/ppermute | solution.py:267
  73.0 21.6 %collective-permute-start.10 = (bf16[1536,384]{1,0:T(8,128)(2,1)}, bf16[1536,384]{1,0:T(8,128)(2,1)}, u32[]{:S(2)}, u32[]{:S(2)}) collective-permute-start(bf16[1536,384]{1,0:T(8,128)(2,1)} %collective-permute-done.4.refs_0_), channel_id=1, source_target_pairs={{0,32},{32,0},{64,96},{96,64},{128,160},{160,128},{192,224},{224,1... | collective-permute-start | bytes 3538952 | tf_op jit(solution)/shard_map/ppermute | solution.py:279
  81.9 12.7 %collective-permute-start.11 = (bf16[1536,384]{1,0:T(8,128)(2,1)}, bf16[1536,384]{1,0:T(8,128)(2,1)}, u32[]{:S(2)}, u32[]{:S(2)}) collective-permute-start(bf16[1536,384]{1,0:T(8,128)(2,1)} %collective-permute-done.7.refs_1_), channel_id=1, source_target_pairs={{0,32},{32,0},{64,96},{96,64},{128,160},{160,128},{192,224},{224,1... | collective-permute-start | bytes 3538952 | tf_op jit(solution)/shard_map/ppermute | solution.py:279
  85.1 18.1 %collective-permute-start.12 = (bf16[16,8,3072]{2,1,0:T(8,128)(2,1)}, bf16[16,8,3072]{2,1,0:T(8,128)(2,1)}, u32[]{:S(2)}, u32[]{:S(2)}) collective-permute-start(bf16[16,8,3072]{2,1,0:T(8,128)(2,1)} %collective-permute-done.5.refs_0_), channel_id=1, source_target_pairs={{0,24},{8,0},{16,8},{24,16},{32,40},{40,48},{48,56},{56,32},{64,88... | collective-permute-start | bytes 2359304 | tf_op jit(solution)/shard_map/ppermute | solution.py:267
  87.4 7.2 %collective-permute-start.8 = (bf16[8,8,3072]{2,1,0:T(8,128)(2,1)}, bf16[8,8,3072]{2,1,0:T(8,128)(2,1)}, u32[]{:S(2)}, u32[]{:S(2)}) collective-permute-start(bf16[8,8,3072]{2,1,0:T(8,128)(2,1)} %slice_select_fusion), channel_id=1, source_target_pairs={{0,1},{1,2},{2,3},{3,4},{4,5},{5,6},{6,7},{7,0},{32,39},{33,32},{3... | collective-permute-start | bytes 1179656 | tf_op jit(solution)/shard_map/ppermute | solution.py:264
  87.4 9.8 %copy-start.2 = (bf16[8,8,3072]{2,1,0:T(8,128)(2,1)S(1)}, bf16[8,8,3072]{2,1,0:T(8,128)(2,1)}, u32[]{:S(2)}) copy-start(bf16[8,8,3072]{2,1,0:T(8,128)(2,1)} %copy-done.1) | copy-start | bytes 1179652
  94.6 8.6 %collective-permute-start.13 = (bf16[8,8,3072]{2,1,0:T(8,128)(2,1)}, bf16[8,8,3072]{2,1,0:T(8,128)(2,1)S(1)}, u32[]{:S(2)}, u32[]{:S(2)}) collective-permute-start(bf16[8,8,3072]{2,1,0:T(8,128)(2,1)} %collective-permute-done.8.refs_2_), channel_id=1, source_target_pairs={{0,24},{8,0},{16,8},{24,16},{32,40},{40,48},{48,56},{56,32},{64,88... | collective-permute-start | bytes 1179656 | tf_op jit(solution)/shard_map/ppermute | solution.py:267
  101.4 5.5 %collective-permute-start.15 = (f32[160,384]{1,0:T(8,128)S(1)}, f32[160,384]{1,0:T(8,128)S(1)}, u32[]{:S(2)}, u32[]{:S(2)}) collective-permute-start(f32[160,384]{1,0:T(8,128)S(1)} %pad_maximum_fusion.2), channel_id=1, source_target_pairs={{0,192},{32,224},{64,0},{96,32},{128,64},{160,96},{192,128},{224,1... | collective-permute-start | bytes 737288 | tf_op jit(solution)/shard_map/ppermute | solution.py:201
  103.1 7.1 %collective-permute-start.14 = (f32[160,384]{1,0:T(8,128)S(1)}, f32[160,384]{1,0:T(8,128)S(1)}, u32[]{:S(2)}, u32[]{:S(2)}) collective-permute-start(f32[160,384]{1,0:T(8,128)S(1)} %pad_maximum_fusion.1), channel_id=1, source_target_pairs={{0,64},{32,96},{64,128},{96,160},{128,192},{160,224},{192,0},{224,... | collective-permute-start | bytes 737288 | tf_op jit(solution)/shard_map/ppermute | solution.py:200
  113.1 5.6 %collective-permute-start.18 = (f32[96,384]{1,0:T(8,128)S(1)}, f32[96,384]{1,0:T(8,128)S(1)}, u32[]{:S(2)}, u32[]{:S(2)}) collective-permute-start(f32[96,384]{1,0:T(8,128)S(1)} %pad_maximum_fusion.3), channel_id=1, source_target_pairs={{0,64},{32,96},{64,128},{96,160},{128,192},{160,224},{192,0},{224,... | collective-permute-start | bytes 442376 | tf_op jit(solution)/shard_map/ppermute | solution.py:200
  113.2 5.5 %collective-permute-start.20 = (f32[96,384]{1,0:T(8,128)S(1)}, f32[96,384]{1,0:T(8,128)S(1)}, u32[]{:S(2)}, u32[]{:S(2)}) collective-permute-start(f32[96,384]{1,0:T(8,128)S(1)} %pad_maximum_fusion.4), channel_id=1, source_target_pairs={{0,192},{32,224},{64,0},{96,32},{128,64},{160,96},{192,128},{224,1... | collective-permute-start | bytes 442376 | tf_op jit(solution)/shard_map/ppermute | solution.py:201
  115.9 6.5 %collective-permute-start.16 = (f32[80,384]{1,0:T(8,128)S(1)}, f32[80,384]{1,0:T(8,128)S(1)}, u32[]{:S(2)}, u32[]{:S(2)}) collective-permute-start(f32[80,384]{1,0:T(8,128)S(1)} %get-tuple-element.48), channel_id=1, source_target_pairs={{0,64},{32,96},{64,128},{96,160},{128,192},{160,224},{192,0},{224,... | collective-permute-start | bytes 368648 | tf_op jit(solution)/shard_map/ppermute | solution.py:206
  116.0 6.4 %collective-permute-start.17 = (f32[80,384]{1,0:T(8,128)S(1)}, f32[80,384]{1,0:T(8,128)S(1)}, u32[]{:S(2)}, u32[]{:S(2)}) collective-permute-start(f32[80,384]{1,0:T(8,128)S(1)} %get-tuple-element.47), channel_id=1, source_target_pairs={{0,192},{32,224},{64,0},{96,32},{128,64},{160,96},{192,128},{224,1... | collective-permute-start | bytes 368648 | tf_op jit(solution)/shard_map/ppermute | solution.py:206
  118.7 5.0 %collective-permute-start.19 = (f32[48,384]{1,0:T(8,128)S(1)}, f32[48,384]{1,0:T(8,128)S(1)}, u32[]{:S(2)}, u32[]{:S(2)}) collective-permute-start(f32[48,384]{1,0:T(8,128)S(1)} %get-tuple-element.54), channel_id=1, source_target_pairs={{0,64},{32,96},{64,128},{96,160},{128,192},{160,224},{192,0},{224,... | collective-permute-start | bytes 221192 | tf_op jit(solution)/shard_map/ppermute | solution.py:206
  118.8 4.9 %collective-permute-start.21 = (f32[48,384]{1,0:T(8,128)S(1)}, f32[48,384]{1,0:T(8,128)S(1)}, u32[]{:S(2)}, u32[]{:S(2)}) collective-permute-start(f32[48,384]{1,0:T(8,128)S(1)} %get-tuple-element.53), channel_id=1, source_target_pairs={{0,192},{32,224},{64,0},{96,32},{128,64},{160,96},{192,128},{224,1... | collective-permute-start | bytes 221192 | tf_op jit(solution)/shard_map/ppermute | solution.py:206
  123.8 6.7 %copy-start.5 = (f32[256,384]{1,0:T(8,128)}, f32[256,384]{1,0:T(8,128)S(1)}, u32[]{:S(2)}) copy-start(f32[256,384]{1,0:T(8,128)S(1)} %pad_maximum_fusion.mine_ref) | copy-start | bytes 1179652
  123.8 6.6 %collective-permute-start.22 = (f32[256,384]{1,0:T(8,128)S(1)}, f32[256,384]{1,0:T(8,128)S(1)}, u32[]{:S(2)}, u32[]{:S(2)}) collective-permute-start(f32[256,384]{1,0:T(8,128)S(1)} %pad_maximum_fusion.mine_ref), channel_id=1, source_target_pairs={{0,32},{32,0},{64,96},{96,64},{128,160},{160,128},{192,224},{224,1... | collective-permute-start | bytes 1179656 | tf_op jit(solution)/shard_map/ppermute | solution.py:314
  130.5 0.8 copy-start.6

commit v4 on v2

--- a/solution.py
+++ b/solution.py
@@ -57,6 +57,7 @@
 def pack_amplitudes(groups, share, tiles_ref, assign_ref, src_ref, out_ref, held_ref, block_ref):
     held, total, right, left = balance(tiles_ref, assign_ref, held_ref, block_ref, groups)
     blocks = [block_ref[s] for s in range(groups)]
+    each = share // 2
     for x in range(groups // 2):
         place = 0
         for chip, start, count in runs_of(x, total, right, left, groups // 2):
@@ -68,9 +69,10 @@
 
                 def move(i, carry, block=block, tile=tile, place=place):
                     data = src_ref[block, :, pl.ds(pl.multiple_of((tile + i) * TP, TP), TP)]
-                    into = pl.ds(pl.multiple_of((place + i) * TP, TP), TP)
-                    for copy in range(4):
-                        out_ref[4 * x + copy, :, into] = data
+                    upper = (place + i >= each).astype(jnp.int32)
+                    into = pl.ds(pl.multiple_of((place + i - upper * each) * TP, TP), TP)
+                    for j in range(2):
+                        out_ref[4 * x + 2 * upper + j, :, into] = data
                     return carry
 
                 lax.fori_loop(0, many, move, 0)
@@ -131,16 +133,21 @@
 
 def multiply(ny, *refs):
     refs, (b_ref, out_ref, a_ref) = refs[:-3], refs[-3:]
-    x, y = lax.div(lax.axis_index("grp"), 2), lax.axis_index("row")
+    group, y = lax.axis_index("grp"), lax.axis_index("row")
+    x, core = lax.div(group, 2), lax.rem(group, 2)
     at = 0
     for ref in refs:
-        n, octet, wide = ref.shape
-        a_ref[at : at + n * octet, :] = ref[...].reshape(n * octet, wide)
+        _, n, octet, each = ref.shape
+        for k in range(2):
+            a_ref[at : at + n * octet, k * each : (k + 1) * each] = ref[k].reshape(n * octet, each)
         at += n * octet
-    out = jnp.dot(a_ref[...], b_ref[...], preferred_element_type=jnp.float32)
+    first = pl.ds(pl.multiple_of(core * each, each), each)
+    last = pl.ds(pl.multiple_of((1 - core) * each, each), each)
+    out = jnp.dot(a_ref[:, :each], b_ref[first, :], preferred_element_type=jnp.float32)
+    out += jnp.dot(a_ref[:, each:], b_ref[last, :], preferred_element_type=jnp.float32)
     at = row = 0
     for i, ref in enumerate(refs):
-        n, octet, _ = ref.shape
+        _, n, octet, _ = ref.shape
         for j in range(2):
             d = lax.rem(lax.rem(y + i % 2, 2) + 2 * j - x + ny, ny)
             for g in range(n // 2):
@@ -150,24 +157,27 @@
         row += n // 2 * octet if i % 2 else 0
 
 
-def finish(nz, rows, mine_ref, other_ref, out_ref):
+def finish(nz, rows, mine_ref, other_ref, out_ref, sems):
     core, z = lax.rem(lax.axis_index("grp"), 2), lax.axis_index("col")
     h = rows // 2
     last = nz // 2 * rows - h
-    for q in range(nz // 2):
-        r = lax.rem(core * (nz // 2) + q - z + nz, nz)
-        ends = jnp.logical_or(r == 0, r == nz // 2)
-        above = r < nz // 2
-        step = jnp.where(above, r, nz - r)
-        for part in range(2):
-            start = jnp.where(r == 0, 0, jnp.where(r == nz // 2, last, h + rows * (step - 1) + part * h))
-            holder = jnp.where(ends, part, jnp.where(above, 1, 0))
-            rows_in = pl.ds(pl.multiple_of(start, h), h)
-            for ref, here in ((mine_ref, holder == core), (other_ref, holder != core)):
-
-                @pl.when(here)
-                def _(ref=ref, q=q, part=part, rows_in=rows_in):
-                    out_ref[q * rows + part * h : q * rows + (part + 1) * h, :] = ref[rows_in, :]
+    for phase in range(2):
+        for q in range(nz // 2):
+            r = lax.rem(core * (nz // 2) + q - z + nz, nz)
+            ends = jnp.logical_or(r == 0, r == nz // 2)
+            above = r < nz // 2
+            step = jnp.where(above, r, nz - r)
+            for part in range(2):
+                start = jnp.where(r == 0, 0, jnp.where(r == nz // 2, last, h + rows * (step - 1) + part * h))
+                holder = jnp.where(ends, part, jnp.where(above, 1, 0))
+                rows_in = pl.ds(pl.multiple_of(start, h), h)
+                i = 2 * q + part
+                for ref, here in ((mine_ref, holder == core), (other_ref, holder != core)):
+
+                    @pl.when(here)
+                    def _(ref=ref, i=i, rows_in=rows_in):
+                        copy = pltpu.make_async_copy(ref.at[rows_in], out_ref.at[pl.ds(i * h, h)], sems.at[i])
+                        copy.start() if phase == 0 else copy.wait()
 
 
 def near_chips(p, up, down):
@@ -198,6 +208,7 @@
     swap = [(g, g ^ 1) for g in range(groups)]
     up = [(g, (g + 2) % groups) for g in range(groups)]
     down = [(g, (g - 2) % groups) for g in range(groups)]
+    opposite = [(g, (g + 4) % groups) for g in range(groups)]
     apart = [(g, (g + 2 - 4 * (g % 2)) % groups) for g in range(groups)]
     along = [(g * nz + z, g * nz + (z + 1 - 2 * (g % 2)) % nz) for g in range(groups) for z in range(nz)]
     beside = [(g * ny + y, g * ny + (y - 1 + 2 * (g % 2)) % ny) for g in range(groups) for y in range(ny)]
@@ -211,7 +222,7 @@
     moved = lax.all_to_all(amplitudes[0].reshape(groups, octet, cap), "grp", 0, 0, tiled=True)
     packed = pl.pallas_call(
         functools.partial(pack_amplitudes, groups, share),
-        out_shape=jax.ShapeDtypeStruct((2 * groups, octet, wide), jnp.bfloat16),
+        out_shape=jax.ShapeDtypeStruct((2 * groups, octet, wide // 2), jnp.bfloat16),
         in_specs=[SMEM, SMEM, VMEM],
         out_specs=VMEM,
         scratch_shapes=small,
@@ -231,8 +242,8 @@
     pair, sent = barrier((pair, sent))
     got = lax.ppermute(sent, "grp", apart)
     def half_of(block):
-        h = block.shape[0] // 2
-        return jnp.where(core == 0, block[:h], block[h:])
+        h = block.shape[1] // 2
+        return jnp.where(core == 0, block[:, :h], block[:, h:])
 
     def z_step(block):
         return lax.ppermute(block, ("grp", "col"), along)
@@ -240,13 +251,17 @@
     def y_step(block):
         return lax.ppermute(block, ("grp", "row"), beside)
 
-    block, order = pair, []
-    for s in range(nz // 2 - 1):
-        kept = half_of(block) if s == 0 else block
-        block, near = barrier((z_step(block), y_step(kept)))
+    pair_too = lax.ppermute(pair, "grp", swap)
+    block = half_of(jnp.stack([pair, pair_too]))
+    order = [block]
+    block, near = barrier((jnp.stack([z_step(pair), z_step(pair_too)]), y_step(block)))
+    order += [near]
+    for s in range(1, nz // 2 - 1):
+        order += [block]
+        block, near = barrier((z_step(block), y_step(block)))
         if s == nz // 2 - 3:
             block, near, got = barrier((block, near, got))
-        order += [kept, near]
+        order += [near]
     theirs = [lax.ppermute(part, "grp", swap) for part in jnp.split(got, 2)]
     end = z_step(half_of(block))
     order += [block, y_step(block), end, y_step(end)]
@@ -261,7 +276,7 @@
     )(block_tiles, assign, mine, other, got, *theirs)
 
     def sums(parts):
-        n = sum(part.shape[0] for part in parts) * octet
+        n = sum(part.shape[1] for part in parts) * octet
         return pl.pallas_call(
             functools.partial(multiply, ny),
             out_shape=jax.ShapeDtypeStruct((ny, n // 4, cols), jnp.float32),
@@ -275,15 +290,16 @@
     a, b = near_chips(early, up, down)
     *late, a, b = barrier((*late, a, b))
     late = sums(late)
-    c, d = near_chips(late, up, down)
+    ways = zip((1, 3, 2), (up, down, opposite))
+    late = sum([lax.ppermute(late[d], "grp", way) for d, way in ways], late[0])
     early = total_of(early, a, b, *passed_on(early, a, b, up, down))
-    late = total_of(late, c, d, *passed_on(late, c, d, up, down))
     done = jnp.concatenate([early, late])
     return pl.pallas_call(
         functools.partial(finish, nz, rows),
         out_shape=jax.ShapeDtypeStruct((nz // 2 * rows, cols), jnp.float32),
-        in_specs=[VMEM, VMEM],
+        in_specs=[ANY, ANY],
         out_specs=VMEM,
+        scratch_shapes=[pltpu.SemaphoreType.DMA((nz,))],
     )(done, lax.ppermute(done, "grp", swap))
 
 

time: 126 us -> 123 us (0.976)
  waiting for transfers between devices: 55.1 us -> 48.4 us
  Pallas kernels: 13.1 us -> 15.4 us
  local copies, waits for them, and re-layouts: 4.09 us -> 6.11 us
  starting transfers between devices: 35.3 us -> 33.7 us
  other arithmetic: 1.43 us -> 2.71 us
    ppermute x5, waiting for transfers between devices: 17.3 us -> 9.56 us  [y_step(): return lax.ppermute(block, ('grp', 'row'), beside)]
    all_to_all x1, waiting for transfers between devices: 12.5 us -> 5.01 us  [body(): lax.all_to_all(packed, ('grp', 'row'), 0, 0, axis_index_groups=pairs, til...]
    ppermute x0 -> x4, waiting for transfers between devices: none -> 6.77 us  [the longest x3 6.76 us: body(): late = sum([lax.ppermute(late[d], 'grp', way) for d, way in ways], late[0])]
    ppermute x4 -> x5, waiting for transfers between devices: 16.2 us -> 20.4 us  [z_step(): return lax.ppermute(block, ('grp', 'col'), along)]
    ppermute x2 -> x1, starting transfers between devices: 3.7 us -> 0.54 us  [near_chips(): return (a, lax.ppermute(jnp.concatenate([p[2, h:], p[3, :h]]), 'grp', down))]
    ppermute x0 -> x4, starting transfers between devices: none -> 2.75 us  [the longest x3 2.75 us: body(): late = sum([lax.ppermute(late[d], 'grp', way) for d, way in ways], late[0])]
    ppermute x2 -> x1, starting transfers between devices: 5.33 us -> 2.66 us  [passed_on(): lax.ppermute(p[3, h:] + b[:h], 'grp', down)]
    pallas_call x1, Pallas kernels: 2.36 us -> 4.74 us  [body(): pl.pallas_call(functools.partial(join_tiles, groups, share), out_shape=ti...]
  transfers between devices with their start and end apart: 23 -> 24, of which waited for: 13 -> 15; matrix products, arithmetic and copies ran while one was open for 3% -> 4% of each run, Pallas kernels for 8% -> 11%
where the time goes in v4:
time: 123 us; the launch traced here: 121 us
  waiting for transfers between devices  48.4 us (39%)
  starting transfers between devices  33.7 us (27%)
  Pallas kernels  15.4 us (13%)
  blocking collectives  14.7 us (12%)
  local copies, waits for them, and re-layouts  6.11 us (5%)
  other arithmetic  2.71 us (2%)
    ppermute x5, waiting for transfers between devices, z_step(): return lax.ppermute(block, ('grp', 'col'), along)  20.4 us
    all_to_all x1, blocking collectives, body(): lax.all_to_all(amplitudes[0].reshape(groups, octet, cap), 'grp', 0, 0, ti...  14.7 us
    ppermute x5, starting transfers between devices, z_step(): return lax.ppermute(block, ('grp', 'col'), along)  11.9 us
    ppermute x5, waiting for transfers between devices, y_step(): return lax.ppermute(block, ('grp', 'row'), beside)  9.56 us
    ppermute x3, waiting for transfers between devices, body(): late = sum([lax.ppermute(late[d], 'grp', way) for d, way in ways], late[0])  6.76 us
    all_to_all x1, waiting for transfers between devices, body(): lax.all_to_all(packed, ('grp', 'row'), 0, 0, axis_index_groups=pairs, til...  5.01 us
    pallas_call x1, Pallas kernels, body(): pl.pallas_call(functools.partial(join_tiles, groups, share), out_shape=ti...  4.74 us
    all_to_all x1, starting transfers between devices, body(): lax.all_to_all(packed, ('grp', 'row'), 0, 0, axis_index_groups=pairs, til...  4.69 us
  transfers between devices with their start and end apart: 24, of which 15 were waited for; matrix products, arithmetic and copies ran while one was open for 4% of the time, Pallas kernels for 11%

profile of v4, /device:TPU:1, one launch (start us, length us, event | category | flops | bytes accessed | tf_op | source)
XLA Modules:
  0.0 121.4 jit_solution(15948449893786639608)
XLA Ops:
  0.0 3.2 %collective-permute-start = (bf16[4608,384]{1,0:T(8,128)(2,1)}, bf16[4608,384]{1,0:T(8,128)(2,1)S(1)}, u32[]{:S(2)}, u32[]{:S(2)}) collective-permute-start(bf16[4608,384]{1,0:T(8,128)(2,1)} %bitcast.42), channel_id=1, source_target_pairs={{0,32},{32,0},{64,96},{96,64},{128,160},{160,128},{192,224},{224,1... | collective-permute-start | bytes 10616840 | tf_op jit(solution)/shard_map/ppermute | solution.py:221
  3.2 14.7 %all_to_all.10.src_ref = bf16[8,8,4608]{2,1,0:T(8,128)(2,1)} all-to-all(bf16[8,8,4608]{2,1,0:T(8,128)(2,1)} %bitcast.45), channel_id=1, replica_groups=mesh['grp'=8,'row'=4,'col'=8] {'grp'}, dimensions={0} | all-to-all | bytes 1179648 | tf_op jit(solution)/shard_map/all_to_all | solution.py:222
  17.9 3.0 %shard_map.46 = bf16[16,8,1536]{2,1,0:T(8,128)(2,1)} custom-call(s32[8]{0:T(128)} %tiles_ref.5, s32[8]{0:T(128)} %assign_ref.5, bf16[8,8,4608]{2,1,0:T(8,128)(2,1)} %all_to_all.10.src_ref), custom_call_target="tpu_custom_call" | custom-call | tf_op jit(solution)/shard_map/pallas_call | solution.py:223
  20.9 4.7 %all-to-all-start.1 = ((bf16[16,8,1536]{2,1,0:T(8,128)(2,1)}), bf16[16,8,1536]{2,1,0:T(8,128)(2,1)}, u32[]{:S(2)}, u32[]{:S(2)}) async-start(bf16[16,8,1536]{2,1,0:T(8,128)(2,1)} %shard_map.46), calls=%async_computation.1 | async-start | bytes 786432 | tf_op jit(solution)/shard_map/all_to_all | solution.py:230
  25.6 0.0 collective-permute-done.other_ref
  25.6 0.0 copy-start
  25.6 2.0 %copy-done = bf16[1,4608,384]{2,1,0:T(8,128)(2,1)S(1)} copy-done((bf16[1,4608,384]{2,1,0:T(8,128)(2,1)S(1)}, bf16[1,4608,384]{2,1,0:T(8,128)(2,1)}, u32[]{:S(2)}) %copy-start) | copy-done | bytes 3538968
  27.6 2.4 %shard_map.47 = bf16[3072,384]{1,0:T(8,128)(2,1)S(1)} custom-call(s32[8]{0:T(128)S(1)} %copy-done.3, s32[8]{0:T(128)S(1)} %copy-done.4, bf16[4608,384]{1,0:T(8,128)(2,1)S(1)} %bitcast.43, bf16[4608,384]{1,0:T(8,128)(2,1)S(1)} %collective-permute-done.other_ref), custom_call_target="tpu_custom_call" | custom-call | tf_op jit(solution)/shard_map/pallas_call | solution.py:234
  30.0 1.4 %copy-done.2 = bf16[3072,384]{1,0:T(8,128)(2,1)} copy-done((bf16[3072,384]{1,0:T(8,128)(2,1)}, bf16[3072,384]{1,0:T(8,128)(2,1)S(1)}, u32[]{:S(2)}) %copy-start.2) | copy-done | bytes 2359320
  31.4 5.0 %all-to-all-done.1 = bf16[16,8,1536]{2,1,0:T(8,128)(2,1)} async-done(((bf16[16,8,1536]{2,1,0:T(8,128)(2,1)}), bf16[16,8,1536]{2,1,0:T(8,128)(2,1)}, u32[]{:S(2)}, u32[]{:S(2)}) %all-to-all-start.1) | async-done | bytes 393248 | tf_op jit(solution)/shard_map/all_to_all | solution.py:230
  36.4 0.4 collective-permute-start.7
  36.8 0.0 collective-permute-start.1
  36.8 5.2 %collective-permute-start.2 = (bf16[16,8,1536]{2,1,0:T(8,128)(2,1)}, bf16[16,8,1536]{2,1,0:T(8,128)(2,1)}, u32[]{:S(2)}, u32[]{:S(2)}) collective-permute-start(bf16[16,8,1536]{2,1,0:T(8,128)(2,1)} %all-to-all-done.1), channel_id=1, source_target_pairs={{0,1},{1,2},{2,3},{3,4},{4,5},{5,6},{6,7},{7,0},{32,39},{33,32},{3... | collective-permute-start | bytes 1179656 | tf_op jit(solution)/shard_map/ppermute | solution.py:249
  42.1 0.0 collective-permute-done.1
  42.1 2.1 %collective-permute-start.3 = (bf16[16,8,1536]{2,1,0:T(8,128)(2,1)}, bf16[16,8,1536]{2,1,0:T(8,128)(2,1)}, u32[]{:S(2)}, u32[]{:S(2)}) collective-permute-start(bf16[16,8,1536]{2,1,0:T(8,128)(2,1)} %collective-permute-done.1), channel_id=1, source_target_pairs={{0,1},{1,2},{2,3},{3,4},{4,5},{5,6},{6,7},{7,0},{32,39},{33,32},{3... | collective-permute-start | bytes 1179656 | tf_op jit(solution)/shard_map/ppermute | solution.py:249
  44.1 1.3 %fusion.1.refs_0_ = bf16[2,8,8,1536]{3,2,1,0:T(8,128)(2,1)S(1)} fusion(bf16[1,16,8,1536]{3,2,1,0:T(8,128)(2,1)} %bitcast.2, bf16[1,16,8,1536]{3,2,1,0:T(8,128)(2,1)} %bitcast.3, pred[]{:T(512)S(6)} %eq.4), kind=kLoop, calls=%fused_computation.4 | loop fusion | flops 589824 | bytes 1179649 | tf_op jit(solution)/shard_map/jit(_where)/select_n | solution.py:246
  45.4 0.5 collective-permute-start.4
  45.9 1.2 collective-permute-done.2
  47.1 4.2 %collective-permute-done.3 = bf16[16,8,1536]{2,1,0:T(8,128)(2,1)} collective-permute-done((bf16[16,8,1536]{2,1,0:T(8,128)(2,1)}, bf16[16,8,1536]{2,1,0:T(8,128)(2,1)}, u32[]{:S(2)}, u32[]{:S(2)}) %collective-permute-start.3) | collective-permute-done | bytes 393248 | tf_op jit(solution)/shard_map/ppermute | solution.py:249
  51.3 1.2 pad_maximum_fusion.refs_2_
  52.5 0.0 copy-start.1
  52.5 1.2 %collective-permute-done.4.refs_1_ = bf16[2,8,8,1536]{3,2,1,0:T(8,128)(2,1)S(1)} collective-permute-done((bf16[2,8,8,1536]{3,2,1,0:T(8,128)(2,1)S(1)}, bf16[2,8,8,1536]{3,2,1,0:T(8,128)(2,1)S(1)}, u32[]{:S(2)}, u32[]{:S(2)}) %collective-permute-start.4) | collective-permute-done | bytes 393248 | tf_op jit(solution)/shard_map/ppermute | solution.py:252
  53.7 2.3 %collective-permute-start.5 = (bf16[2,16,8,1536]{3,2,1,0:T(8,128)(2,1)S(1)}, bf16[2,16,8,1536]{3,2,1,0:T(8,128)(2,1)S(1)}, u32[]{:S(2)}, u32[]{:S(2)}) collective-permute-start(bf16[2,16,8,1536]{3,2,1,0:T(8,128)(2,1)S(1)} %pad_maximum_fusion.refs_2_), channel_id=1, source_target_pairs={{0,1},{1,2},{2,3},{3,4},{4,5},{5,6},{6,7},{7,0},{32,39},{33,32},{3... | collective-permute-start | bytes 2359304 | tf_op jit(solution)/shard_map/ppermute | solution.py:249
  56.0 0.4 collective-permute-start.6
  56.4 8.6 %collective-permute-done.5.refs_4_ = bf16[2,16,8,1536]{3,2,1,0:T(8,128)(2,1)S(1)} collective-permute-done((bf16[2,16,8,1536]{3,2,1,0:T(8,128)(2,1)S(1)}, bf16[2,16,8,1536]{3,2,1,0:T(8,128)(2,1)S(1)}, u32[]{:S(2)}, u32[]{:S(2)}) %collective-permute-start.5) | collective-permute-done | bytes 786464 | tf_op jit(solution)/shard_map/ppermute | solution.py:249
  65.0 3.1 %collective-permute-done.6.refs_3_ = bf16[2,16,8,1536]{3,2,1,0:T(8,128)(2,1)S(1)} collective-permute-done((bf16[2,16,8,1536]{3,2,1,0:T(8,128)(2,1)S(1)}, bf16[2,16,8,1536]{3,2,1,0:T(8,128)(2,1)S(1)}, u32[]{:S(2)}, u32[]{:S(2)}) %collective-permute-start.6) | collective-permute-done | bytes 786464 | tf_op jit(solution)/shard_map/ppermute | solution.py:252
  68.1 0.0 collective-permute-done.7.got_ref
  68.1 1.8 %collective-permute-start.8 = (bf16[2,16,8,1536]{3,2,1,0:T(8,128)(2,1)S(1)}, bf16[2,16,8,1536]{3,2,1,0:T(8,128)(2,1)S(1)}, u32[]{:S(2)}, u32[]{:S(2)}) collective-permute-start(bf16[2,16,8,1536]{3,2,1,0:T(8,128)(2,1)S(1)} %collective-permute-done.5.refs_4_), channel_id=1, source_target_pairs={{0,1},{1,2},{2,3},{3,4},{4,5},{5,6},{6,7},{7,0},{32,39},{33,32},{3... | collective-permute-start | bytes 2359304 | tf_op jit(solution)/shard_map/ppermute | solution.py:249
  69.9 0.4 collective-permute-start.9
  70.3 1.9 %fusion.9 = (bf16[1536,384]{1,0:T(8,128)(2,1)S(1)}, bf16[1536,384]{1,0:T(8,128)(2,1)S(1)}) fusion(bf16[3072,384]{1,0:T(8,128)(2,1)} %collective-permute-done.7.got_ref), kind=kLoop, calls=%fused_computation.28 | loop fusion | bytes 4718592 | tf_op jit(solution)/shard_map/split | solution.py:265
  72.2 0.1 collective-permute-start.10
  72.3 0.5 collective-permute-start.11
  72.8 6.5 %collective-permute-done.8.refs_0_ = bf16[2,16,8,1536]{3,2,1,0:T(8,128)(2,1)S(1)} collective-permute-done((bf16[2,16,8,1536]{3,2,1,0:T(8,128)(2,1)S(1)}, bf16[2,16,8,1536]{3,2,1,0:T(8,128)(2,1)S(1)}, u32[]{:S(2)}, u32[]{:S(2)}) %collective-permute-start.8) | collective-permute-done | bytes 786464 | tf_op jit(solution)/shard_map/ppermute | solution.py:249
  79.2 3.0 %collective-permute-done.9.refs_5_ = bf16[2,16,8,1536]{3,2,1,0:T(8,128)(2,1)S(1)} collective-permute-done((bf16[2,16,8,1536]{3,2,1,0:T(8,128)(2,1)S(1)}, bf16[2,16,8,1536]{3,2,1,0:T(8,128)(2,1)S(1)}, u32[]{:S(2)}, u32[]{:S(2)}) %collective-permute-start.9) | collective-permute-done | bytes 786464 | tf_op jit(solution)/shard_map/ppermute | solution.py:252
  82.3 0.5 collective-permute-start.13
  82.8 0.0 collective-permute-start.12
  82.8 0.0 collective-permute-done.10.refs_0_
  82.8 0.0 collective-permute-done.11.refs_1_
  82.8 4.7 %shard_map.48.refs_6_.refs_4_ = bf16[3072,384]{1,0:T(8,128)(2,1)S(1)} custom-call(s32[8]{0:T(128)S(1)} %copy-done.3, s32[8]{0:T(128)S(1)} %copy-done.4, bf16[4608,384]{1,0:T(8,128)(2,1)S(1)} %bitcast.44, bf16[4608,384]{1,0:T(8,128)(2,1)S(1)} %collective-permute-done.other_ref, bf16[3072,384]{1,0:T(8,128)(2,1)} %collective-permute-done.7.got_ref, ...), custom_call_target="tpu_custom_call" | custom-call | tf_op jit(solution)/shard_map/pallas_call | solution.py:269
  87.6 2.2 %shard_map.49 = f32[4,160,384]{2,1,0:T(8,128)S(1)} custom-call(bf16[2,8,8,1536]{3,2,1,0:T(8,128)(2,1)S(1)} %fusion.1.refs_0_, bf16[2,8,8,1536]{3,2,1,0:T(8,128)(2,1)S(1)} %collective-permute-done.4.refs_1_, bf16[2,16,8,1536]{3,2,1,0:T(8,128)(2,1)S(1)} %pad_maximum_fusion.refs_2_, bf16[2,16,8,1536]{3,2,1,0:T(8,128)(2,1)S(1)} %collective-permute-done.6.refs_3_, ...), custom_call_target="tpu_custom_call" | custom-call | tf_op jit(solution)/shard_map/pallas_call | solution.py:280
  89.8 0.0 collective-permute-done.13.refs_2_
  89.8 0.1 collective-permute-start.14
  89.9 0.5 collective-permute-start.16
  90.5 1.1 collective-permute-start.15
  91.6 3.8 %collective-permute-done.16 = f32[160,384]{1,0:T(8,128)S(1)} collective-permute-done((f32[160,384]{1,0:T(8,128)S(1)}, f32[160,384]{1,0:T(8,128)S(1)}, u32[]{:S(2)}, u32[]{:S(2)}) %collective-permute-start.16) | collective-permute-done | bytes 245792 | tf_op jit(solution)/shard_map/ppermute | solution.py:186
  95.4 1.5 %collective-permute-done.15 = f32[160,384]{1,0:T(8,128)S(1)} collective-permute-done((f32[160,384]{1,0:T(8,128)S(1)}, f32[160,384]{1,0:T(8,128)S(1)}, u32[]{:S(2)}, u32[]{:S(2)}) %collective-permute-start.15) | collective-permute-done | bytes 245792 | tf_op jit(solution)/shard_map/ppermute | solution.py:185
  96.8 2.2 %collective-permute-done.14.refs_3_ = bf16[2,8,8,1536]{3,2,1,0:T(8,128)(2,1)S(1)} collective-permute-done((bf16[2,8,8,1536]{3,2,1,0:T(8,128)(2,1)S(1)}, bf16[2,8,8,1536]{3,2,1,0:T(8,128)(2,1)S(1)}, u32[]{:S(2)}, u32[]{:S(2)}) %collective-permute-start.14) | collective-permute-done | bytes 393248 | tf_op jit(solution)/shard_map/ppermute | solution.py:252
  99.1 0.0 collective-permute-done.12.refs_1_
  99.1 0.1 collective-permute-start.17
  99.2 2.7 %collective-permute-start.18 = (f32[80,384]{1,0:T(8,128)S(1)}, f32[80,384]{1,0:T(8,128)S(1)}, u32[]{:S(2)}, u32[]{:S(2)}) collective-permute-start(f32[80,384]{1,0:T(8,128)S(1)} %get-tuple-element.41), channel_id=1, source_target_pairs={{0,192},{32,224},{64,0},{96,32},{128,64},{160,96},{192,128},{224,1... | collective-permute-start | bytes 368648 | tf_op jit(solution)/shard_map/ppermute | solution.py:191
  101.9 1.4 %shard_map.50 = f32[4,96,384]{2,1,0:T(8,128)S(1)} custom-call(bf16[2,16,8,1536]{3,2,1,0:T(8,128)(2,1)S(1)} %collective-permute-done.8.refs_0_, bf16[2,16,8,1536]{3,2,1,0:T(8,128)(2,1)S(1)} %collective-permute-done.12.refs_1_, bf16[2,8,8,1536]{3,2,1,0:T(8,128)(2,1)S(1)} %collective-permute-done.13.refs_2_, ...), custom_call_target="tpu_custom_call" | custom-call | tf_op jit(solution)/shard_map/pallas_call | solution.py:280
  103.3 0.1 collective-permute-start.19
  103.4 2.7 %collective-permute-start.20 = (f32[96,384]{1,0:T(8,128)S(1)}, f32[96,384]{1,0:T(8,128)S(1)}, u32[]{:S(2)}, u32[]{:S(2)}) collective-permute-start(f32[96,384]{1,0:T(8,128)S(1)} %get-tuple-element.49), channel_id=1, source_target_pairs={{0,192},{32,224},{64,0},{96,32},{128,64},{160,96},{192,128},{224,1... | collective-permute-start | bytes 442376 | tf_op jit(solution)/shard_map/ppermute | solution.py:294
  106.0 0.0 collective-permute-start.21
  106.1 0.0 collective-permute-done.17
  106.1 0.0 collective-permute-done.18
  106.1 0.1 fusion.3
  106.1 3.4 %collective-permute-done.19 = f32[96,384]{1,0:T(8,128)S(1)} collective-permute-done((f32[96,384]{1,0:T(8,128)S(1)}, f32[96,384]{1,0:T(8,128)S(1)}, u32[]{:S(2)}, u32[]{:S(2)}) %collective-permute-start.19) | collective-permute-done | bytes 147488 | tf_op jit(solution)/shard_map/ppermute | solution.py:294
  109.5 1.4 %collective-permute-done.20 = f32[96,384]{1,0:T(8,128)S(1)} collective-permute-done((f32[96,384]{1,0:T(8,128)S(1)}, f32[96,384]{1,0:T(8,128)S(1)}, u32[]{:S(2)}, u32[]{:S(2)}) %collective-permute-start.20) | collective-permute-done | bytes 147488 | tf_op jit(solution)/shard_map/ppermute | solution.py:294
  111.0 1.9 %collective-permute-done.21 = f32[96,384]{1,0:T(8,128)S(1)} collective-permute-done((f32[96,384]{1,0:T(8,128)S(1)}, f32[96,384]{1,0:T(8,128)S(1)}, u32[]{:S(2)}, u32[]{:S(2)}) %collective-permute-start.21) | collective-permute-done | bytes 147488 | tf_op jit(solution)/shard_map/ppermute | solution.py:294
  113.0 4.4 %collective-permute-start.22 = (f32[256,384]{1,0:T(8,128)S(1)}, f32[256,384]{1,0:T(8,128)S(1)}, u32[]{:S(2)}, u32[]{:S(2)}) collective-permute-start(f32[256,384]{1,0:T(8,128)S(1)} %pad_maximum_fusion.2.mine_ref), channel_id=1, source_target_pairs={{0,32},{32,0},{64,96},{96,64},{128,160},{160,128},{192,224},{224,1... | collective-permute-start | bytes 1179656 | tf_op jit(solution)/shard_map/ppermute | solution.py:303
  117.4 1.3 %collective-permute-done.22.other_ref = f32[256,384]{1,0:T(8,128)S(1)} collective-permute-done((f32[256,384]{1,0:T(8,128)S(1)}, f32[256,384]{1,0:T(8,128)S(1)}, u32[]{:S(2)}, u32[]{:S(2)}) %collective-permute-start.22) | collective-permute-done | bytes 393248 | tf_op jit(solution)/shard_map/ppermute | solution.py:303
  118.7 0.8 copy-done.6
  119.5 1.8 %shard_map.51 = f32[256,384]{1,0:T(8,128)} custom-call(f32[256,384]{1,0:T(8,128)} %copy-done.5, f32[256,384]{1,0:T(8,128)} %copy-done.6), custom_call_target="tpu_custom_call" | custom-call | tf_op jit(solution)/shard_map/pallas_call | solution.py:297
  (17 shorter events, 0.3 us)
Async XLA Ops:
  0.0 25.6 %copy-start.3 = (s32[8]{0:T(128)S(1)}, s32[8]{0:T(128)}, u32[]{:S(2)}) copy-start(s32[8]{0:T(128)} %tiles_ref.5) | copy-start | bytes 100
  0.0 25.6 %copy-start.4 = (s32[8]{0:T(128)S(1)}, s32[8]{0:T(128)}, u32[]{:S(2)}) copy-start(s32[8]{0:T(128)} %assign_ref.5) | copy-start | bytes 100
  0.0 25.6 %collective-permute-start = (bf16[4608,384]{1,0:T(8,128)(2,1)}, bf16[4608,384]{1,0:T(8,128)(2,1)S(1)}, u32[]{:S(2)}, u32[]{:S(2)}) collective-permute-start(bf16[4608,384]{1,0:T(8,128)(2,1)} %bitcast.42), channel_id=1, source_target_pairs={{0,32},{32,0},{64,96},{96,64},{128,160},{160,128},{192,224},{224,1... | collective-permute-start | bytes 10616840 | tf_op jit(solution)/shard_map/ppermute | solution.py:221
  20.9 15.5 %all-to-all-start.1 = ((bf16[16,8,1536]{2,1,0:T(8,128)(2,1)}), bf16[16,8,1536]{2,1,0:T(8,128)(2,1)}, u32[]{:S(2)}, u32[]{:S(2)}) async-start(bf16[16,8,1536]{2,1,0:T(8,128)(2,1)} %shard_map.46), calls=%async_computation.1 | async-start | bytes 786432 | tf_op jit(solution)/shard_map/all_to_all | solution.py:230
  25.6 2.0 %copy-start = (bf16[1,4608,384]{2,1,0:T(8,128)(2,1)S(1)}, bf16[1,4608,384]{2,1,0:T(8,128)(2,1)}, u32[]{:S(2)}) copy-start(bf16[1,4608,384]{2,1,0:T(8,128)(2,1)} %param.5) | copy-start | bytes 10616836
  30.0 1.4 %copy-start.2 = (bf16[3072,384]{1,0:T(8,128)(2,1)}, bf16[3072,384]{1,0:T(8,128)(2,1)S(1)}, u32[]{:S(2)}) copy-start(bf16[3072,384]{1,0:T(8,128)(2,1)S(1)} %shard_map.47) | copy-start | bytes 7077892
  36.4 31.7 %collective-permute-start.7 = (bf16[3072,384]{1,0:T(8,128)(2,1)}, bf16[3072,384]{1,0:T(8,128)(2,1)}, u32[]{:S(2)}, u32[]{:S(2)}) collective-permute-start(bf16[3072,384]{1,0:T(8,128)(2,1)} %copy-done.2), channel_id=1, source_target_pairs={{0,64},{32,224},{64,128},{96,32},{128,192},{160,96},{192,0},{224,1... | collective-permute-start | bytes 7077896 | tf_op jit(solution)/shard_map/ppermute | solution.py:243
  36.8 5.2 %collective-permute-start.1 = (bf16[16,8,1536]{2,1,0:T(8,128)(2,1)}, bf16[16,8,1536]{2,1,0:T(8,128)(2,1)}, u32[]{:S(2)}, u32[]{:S(2)}) collective-permute-start(bf16[16,8,1536]{2,1,0:T(8,128)(2,1)} %all-to-all-done.1), channel_id=1, source_target_pairs={{0,32},{32,0},{64,96},{96,64},{128,160},{160,128},{192,224},{224,1... | collective-permute-start | bytes 1179656 | tf_op jit(solution)/shard_map/ppermute | solution.py:254
  36.8 10.3 %collective-permute-start.2 = (bf16[16,8,1536]{2,1,0:T(8,128)(2,1)}, bf16[16,8,1536]{2,1,0:T(8,128)(2,1)}, u32[]{:S(2)}, u32[]{:S(2)}) collective-permute-start(bf16[16,8,1536]{2,1,0:T(8,128)(2,1)} %all-to-all-done.1), channel_id=1, source_target_pairs={{0,1},{1,2},{2,3},{3,4},{4,5},{5,6},{6,7},{7,0},{32,39},{33,32},{3... | collective-permute-start | bytes 1179656 | tf_op jit(solution)/shard_map/ppermute | solution.py:249
  42.1 9.2 %collective-permute-start.3 = (bf16[16,8,1536]{2,1,0:T(8,128)(2,1)}, bf16[16,8,1536]{2,1,0:T(8,128)(2,1)}, u32[]{:S(2)}, u32[]{:S(2)}) collective-permute-start(bf16[16,8,1536]{2,1,0:T(8,128)(2,1)} %collective-permute-done.1), channel_id=1, source_target_pairs={{0,1},{1,2},{2,3},{3,4},{4,5},{5,6},{6,7},{7,0},{32,39},{33,32},{3... | collective-permute-start | bytes 1179656 | tf_op jit(solution)/shard_map/ppermute | solution.py:249
  45.4 8.3 %collective-permute-start.4 = (bf16[2,8,8,1536]{3,2,1,0:T(8,128)(2,1)S(1)}, bf16[2,8,8,1536]{3,2,1,0:T(8,128)(2,1)S(1)}, u32[]{:S(2)}, u32[]{:S(2)}) collective-permute-start(bf16[2,8,8,1536]{3,2,1,0:T(8,128)(2,1)S(1)} %fusion.1.refs_0_), channel_id=1, source_target_pairs={{0,24},{8,0},{16,8},{24,16},{32,40},{40,48},{48,56},{56,32},{64,88... | collective-permute-start | bytes 1179656 | tf_op jit(solution)/shard_map/ppermute | solution.py:252
  52.5 30.3 %copy-start.1 = (bf16[1,4608,384]{2,1,0:T(8,128)(2,1)S(1)}, bf16[1,4608,384]{2,1,0:T(8,128)(2,1)}, u32[]{:S(2)}) copy-start(bf16[1,4608,384]{2,1,0:T(8,128)(2,1)} %param.5) | copy-start | bytes 10616836
  53.7 11.2 %collective-permute-start.5 = (bf16[2,16,8,1536]{3,2,1,0:T(8,128)(2,1)S(1)}, bf16[2,16,8,1536]{3,2,1,0:T(8,128)(2,1)S(1)}, u32[]{:S(2)}, u32[]{:S(2)}) collective-permute-start(bf16[2,16,8,1536]{3,2,1,0:T(8,128)(2,1)S(1)} %pad_maximum_fusion.refs_2_), channel_id=1, source_target_pairs={{0,1},{1,2},{2,3},{3,4},{4,5},{5,6},{6,7},{7,0},{32,39},{33,32},{3... | collective-permute-start | bytes 2359304 | tf_op jit(solution)/shard_map/ppermute | solution.py:249
  56.0 12.1 %collective-permute-start.6 = (bf16[2,16,8,1536]{3,2,1,0:T(8,128)(2,1)S(1)}, bf16[2,16,8,1536]{3,2,1,0:T(8,128)(2,1)S(1)}, u32[]{:S(2)}, u32[]{:S(2)}) collective-permute-start(bf16[2,16,8,1536]{3,2,1,0:T(8,128)(2,1)S(1)} %pad_maximum_fusion.refs_2_), channel_id=1, source_target_pairs={{0,24},{8,0},{16,8},{24,16},{32,40},{40,48},{48,56},{56,32},{64,88... | collective-permute-start | bytes 2359304 | tf_op jit(solution)/shard_map/ppermute | solution.py:252
  68.1 11.1 %collective-permute-start.8 = (bf16[2,16,8,1536]{3,2,1,0:T(8,128)(2,1)S(1)}, bf16[2,16,8,1536]{3,2,1,0:T(8,128)(2,1)S(1)}, u32[]{:S(2)}, u32[]{:S(2)}) collective-permute-start(bf16[2,16,8,1536]{3,2,1,0:T(8,128)(2,1)S(1)} %collective-permute-done.5.refs_4_), channel_id=1, source_target_pairs={{0,1},{1,2},{2,3},{3,4},{4,5},{5,6},{6,7},{7,0},{32,39},{33,32},{3... | collective-permute-start | bytes 2359304 | tf_op jit(solution)/shard_map/ppermute | solution.py:249
  69.9 12.3 %collective-permute-start.9 = (bf16[2,16,8,1536]{3,2,1,0:T(8,128)(2,1)S(1)}, bf16[2,16,8,1536]{3,2,1,0:T(8,128)(2,1)S(1)}, u32[]{:S(2)}, u32[]{:S(2)}) collective-permute-start(bf16[2,16,8,1536]{3,2,1,0:T(8,128)(2,1)S(1)} %collective-permute-done.5.refs_4_), channel_id=1, source_target_pairs={{0,24},{8,0},{16,8},{24,16},{32,40},{40,48},{48,56},{56,32},{64,88... | collective-permute-start | bytes 2359304 | tf_op jit(solution)/shard_map/ppermute | solution.py:252
  72.2 10.6 %collective-permute-start.10 = (bf16[1536,384]{1,0:T(8,128)(2,1)S(1)}, bf16[1536,384]{1,0:T(8,128)(2,1)S(1)}, u32[]{:S(2)}, u32[]{:S(2)}) collective-permute-start(bf16[1536,384]{1,0:T(8,128)(2,1)S(1)} %get-tuple-element.40), channel_id=1, source_target_pairs={{0,32},{32,0},{64,96},{96,64},{128,160},{160,128},{192,224},{224,1... | collective-permute-start | bytes 3538952 | tf_op jit(solution)/shard_map/ppermute | solution.py:265
  72.3 10.5 %collective-permute-start.11 = (bf16[1536,384]{1,0:T(8,128)(2,1)S(1)}, bf16[1536,384]{1,0:T(8,128)(2,1)S(1)}, u32[]{:S(2)}, u32[]{:S(2)}) collective-permute-start(bf16[1536,384]{1,0:T(8,128)(2,1)S(1)} %get-tuple-element.39), channel_id=1, source_target_pairs={{0,32},{32,0},{64,96},{96,64},{128,160},{160,128},{192,224},{224,1... | collective-permute-start | bytes 3538952 | tf_op jit(solution)/shard_map/ppermute | solution.py:265
  82.3 7.5 %collective-permute-start.13 = (bf16[2,8,8,1536]{3,2,1,0:T(8,128)(2,1)S(1)}, bf16[2,8,8,1536]{3,2,1,0:T(8,128)(2,1)S(1)}, u32[]{:S(2)}, u32[]{:S(2)}) collective-permute-start(bf16[2,8,8,1536]{3,2,1,0:T(8,128)(2,1)S(1)} %slice_select_fusion), channel_id=1, source_target_pairs={{0,1},{1,2},{2,3},{3,4},{4,5},{5,6},{6,7},{7,0},{32,39},{33,32},{3... | collective-permute-start | bytes 1179656 | tf_op jit(solution)/shard_map/ppermute | solution.py:249
  82.8 16.3 %collective-permute-start.12 = (bf16[2,16,8,1536]{3,2,1,0:T(8,128)(2,1)S(1)}, bf16[2,16,8,1536]{3,2,1,0:T(8,128)(2,1)S(1)}, u32[]{:S(2)}, u32[]{:S(2)}) collective-permute-start(bf16[2,16,8,1536]{3,2,1,0:T(8,128)(2,1)S(1)} %collective-permute-done.8.refs_0_), channel_id=1, source_target_pairs={{0,24},{8,0},{16,8},{24,16},{32,40},{40,48},{48,56},{56,32},{64,88... | collective-permute-start | bytes 2359304 | tf_op jit(solution)/shard_map/ppermute | solution.py:252
  89.8 9.2 %collective-permute-start.14 = (bf16[2,8,8,1536]{3,2,1,0:T(8,128)(2,1)S(1)}, bf16[2,8,8,1536]{3,2,1,0:T(8,128)(2,1)S(1)}, u32[]{:S(2)}, u32[]{:S(2)}) collective-permute-start(bf16[2,8,8,1536]{3,2,1,0:T(8,128)(2,1)S(1)} %collective-permute-done.13.refs_2_), channel_id=1, source_target_pairs={{0,24},{8,0},{16,8},{24,16},{32,40},{40,48},{48,56},{56,32},{64,88... | collective-permute-start | bytes 1179656 | tf_op jit(solution)/shard_map/ppermute | solution.py:252
  89.9 5.4 %collective-permute-start.16 = (f32[160,384]{1,0:T(8,128)S(1)}, f32[160,384]{1,0:T(8,128)S(1)}, u32[]{:S(2)}, u32[]{:S(2)}) collective-permute-start(f32[160,384]{1,0:T(8,128)S(1)} %pad_maximum_fusion.4), channel_id=1, source_target_pairs={{0,192},{32,224},{64,0},{96,32},{128,64},{160,96},{192,128},{224,1... | collective-permute-start | bytes 737288 | tf_op jit(solution)/shard_map/ppermute | solution.py:186
  90.5 6.3 %collective-permute-start.15 = (f32[160,384]{1,0:T(8,128)S(1)}, f32[160,384]{1,0:T(8,128)S(1)}, u32[]{:S(2)}, u32[]{:S(2)}) collective-permute-start(f32[160,384]{1,0:T(8,128)S(1)} %pad_maximum_fusion.3), channel_id=1, source_target_pairs={{0,64},{32,96},{64,128},{96,160},{128,192},{160,224},{192,0},{224,... | collective-permute-start | bytes 737288 | tf_op jit(solution)/shard_map/ppermute | solution.py:185
  99.1 6.9 %collective-permute-start.17 = (f32[80,384]{1,0:T(8,128)S(1)}, f32[80,384]{1,0:T(8,128)S(1)}, u32[]{:S(2)}, u32[]{:S(2)}) collective-permute-start(f32[80,384]{1,0:T(8,128)S(1)} %get-tuple-element.42), channel_id=1, source_target_pairs={{0,64},{32,96},{64,128},{96,160},{128,192},{160,224},{192,0},{224,... | collective-permute-start | bytes 368648 | tf_op jit(solution)/shard_map/ppermute | solution.py:191
  99.2 6.8 %collective-permute-start.18 = (f32[80,384]{1,0:T(8,128)S(1)}, f32[80,384]{1,0:T(8,128)S(1)}, u32[]{:S(2)}, u32[]{:S(2)}) collective-permute-start(f32[80,384]{1,0:T(8,128)S(1)} %get-tuple-element.41), channel_id=1, source_target_pairs={{0,192},{32,224},{64,0},{96,32},{128,64},{160,96},{192,128},{224,1... | collective-permute-start | bytes 368648 | tf_op jit(solution)/shard_map/ppermute | solution.py:191
  103.3 6.2 %collective-permute-start.19 = (f32[96,384]{1,0:T(8,128)S(1)}, f32[96,384]{1,0:T(8,128)S(1)}, u32[]{:S(2)}, u32[]{:S(2)}) collective-permute-start(f32[96,384]{1,0:T(8,128)S(1)} %get-tuple-element.47), channel_id=1, source_target_pairs={{0,64},{32,96},{64,128},{96,160},{128,192},{160,224},{192,0},{224,... | collective-permute-start | bytes 442376 | tf_op jit(solution)/shard_map/ppermute | solution.py:294
  103.4 7.6 %collective-permute-start.20 = (f32[96,384]{1,0:T(8,128)S(1)}, f32[96,384]{1,0:T(8,128)S(1)}, u32[]{:S(2)}, u32[]{:S(2)}) collective-permute-start(f32[96,384]{1,0:T(8,128)S(1)} %get-tuple-element.49), channel_id=1, source_target_pairs={{0,192},{32,224},{64,0},{96,32},{128,64},{160,96},{192,128},{224,1... | collective-permute-start | bytes 442376 | tf_op jit(solution)/shard_map/ppermute | solution.py:294
  106.0 6.8 %collective-permute-start.21 = (f32[96,384]{1,0:T(8,128)S(1)}, f32[96,384]{1,0:T(8,128)S(1)}, u32[]{:S(2)}, u32[]{:S(2)}) collective-permute-start(f32[96,384]{1,0:T(8,128)S(1)} %get-tuple-element.48), channel_id=1, source_target_pairs={{0,128},{32,160},{64,192},{96,224},{128,0},{160,32},{192,64},{224,... | collective-permute-start | bytes 442376 | tf_op jit(solution)/shard_map/ppermute | solution.py:294
  112.9 5.8 %copy-start.5 = (f32[256,384]{1,0:T(8,128)}, f32[256,384]{1,0:T(8,128)S(1)}, u32[]{:S(2)}) copy-start(f32[256,384]{1,0:T(8,128)S(1)} %pad_maximum_fusion.2.mine_ref) | copy-start | bytes 1179652
  113.0 5.7 %collective-permute-start.22 = (f32[256,384]{1,0:T(8,128)S(1)}, f32[256,384]{1,0:T(8,128)S(1)}, u32[]{:S(2)}, u32[]{:S(2)}) collective-permute-start(f32[256,384]{1,0:T(8,128)S(1)} %pad_maximum_fusion.2.mine_ref), channel_id=1, source_target_pairs={{0,32},{32,0},{64,96},{96,64},{128,160},{160,128},{192,224},{224,1... | collective-permute-start | bytes 1179656 | tf_op jit(solution)/shard_map/ppermute | solution.py:303
  118.7 0.8 copy-start.6

commit v5 on v4

--- a/solution.py
+++ b/solution.py
@@ -157,43 +157,30 @@
         row += n // 2 * octet if i % 2 else 0
 
 
-def finish(nz, rows, mine_ref, other_ref, out_ref, sems):
+def finish(nz, rows, mine_ref, other_ref, out_ref):
     core, z = lax.rem(lax.axis_index("grp"), 2), lax.axis_index("col")
     h = rows // 2
     last = nz // 2 * rows - h
-    for phase in range(2):
-        for q in range(nz // 2):
-            r = lax.rem(core * (nz // 2) + q - z + nz, nz)
-            ends = jnp.logical_or(r == 0, r == nz // 2)
-            above = r < nz // 2
-            step = jnp.where(above, r, nz - r)
-            for part in range(2):
-                start = jnp.where(r == 0, 0, jnp.where(r == nz // 2, last, h + rows * (step - 1) + part * h))
-                holder = jnp.where(ends, part, jnp.where(above, 1, 0))
-                rows_in = pl.ds(pl.multiple_of(start, h), h)
-                i = 2 * q + part
-                for ref, here in ((mine_ref, holder == core), (other_ref, holder != core)):
-
-                    @pl.when(here)
-                    def _(ref=ref, i=i, rows_in=rows_in):
-                        copy = pltpu.make_async_copy(ref.at[rows_in], out_ref.at[pl.ds(i * h, h)], sems.at[i])
-                        copy.start() if phase == 0 else copy.wait()
+    for q in range(nz // 2):
+        r = lax.rem(core * (nz // 2) + q - z + nz, nz)
+        ends = jnp.logical_or(r == 0, r == nz // 2)
+        above = r < nz // 2
+        step = jnp.where(above, r, nz - r)
+        for part in range(2):
+            start = jnp.where(r == 0, 0, jnp.where(r == nz // 2, last, h + rows * (step - 1) + part * h))
+            holder = jnp.where(ends, part, jnp.where(above, 1, 0))
+            rows_in = pl.ds(pl.multiple_of(start, h), h)
+            for ref, here in ((mine_ref, holder == core), (other_ref, holder != core)):
+
+                @pl.when(here)
+                def _(ref=ref, q=q, part=part, rows_in=rows_in):
+                    out_ref[q * rows + part * h : q * rows + (part + 1) * h, :] = ref[rows_in, :]
 
 
 def near_chips(p, up, down):
     h = p.shape[1] // 2
     a = lax.ppermute(jnp.concatenate([p[2, :h], p[1, h:]]), "grp", up)
     return a, lax.ppermute(jnp.concatenate([p[2, h:], p[3, :h]]), "grp", down)
-
-
-def passed_on(p, a, b, up, down):
-    h = p.shape[1] // 2
-    return lax.ppermute(p[1, :h] + a[:h], "grp", up), lax.ppermute(p[3, h:] + b[:h], "grp", down)
-
-
-def total_of(p, a, b, a2, b2):
-    h = p.shape[1] // 2
-    return p[0] + jnp.concatenate([a2, a[h:]]) + jnp.concatenate([b[h:], b2])
 
 
 def body(amplitudes, integrals, block_tiles, assign):
@@ -226,6 +213,7 @@
         in_specs=[SMEM, SMEM, VMEM],
         out_specs=VMEM,
         scratch_shapes=small,
+        compiler_params=pltpu.CompilerParams(vmem_limit_bytes=8 * 2**20),
     )(block_tiles, assign, moved)
     pair = lax.all_to_all(packed, ("grp", "row"), 0, 0, axis_index_groups=pairs, tiled=True)
 
@@ -290,16 +278,18 @@
     a, b = near_chips(early, up, down)
     *late, a, b = barrier((*late, a, b))
     late = sums(late)
-    ways = zip((1, 3, 2), (up, down, opposite))
-    late = sum([lax.ppermute(late[d], "grp", way) for d, way in ways], late[0])
-    early = total_of(early, a, b, *passed_on(early, a, b, up, down))
-    done = jnp.concatenate([early, late])
+    h, n = early.shape[1] // 2, late.shape[1]
+    c = lax.ppermute(late[2], "grp", opposite)
+    a2 = lax.ppermute(jnp.concatenate([late[1], early[1, :h] + a[:h]]), "grp", up)
+    b2 = lax.ppermute(jnp.concatenate([late[3], early[3, h:] + b[:h]]), "grp", down)
+    early = early[0] + jnp.concatenate([a2[n:], a[h:]]) + jnp.concatenate([b[h:], b2[n:]])
+    done = jnp.concatenate([early, late[0] + a2[:n] + b2[:n] + c])
     return pl.pallas_call(
         functools.partial(finish, nz, rows),
         out_shape=jax.ShapeDtypeStruct((nz // 2 * rows, cols), jnp.float32),
-        in_specs=[ANY, ANY],
-        out_specs=VMEM,
-        scratch_shapes=[pltpu.SemaphoreType.DMA((nz,))],
+        in_specs=[VMEM, VMEM],
+        out_specs=VMEM,
+        compiler_params=pltpu.CompilerParams(vmem_limit_bytes=8 * 2**20),
     )(done, lax.ppermute(done, "grp", swap))
 
 

time: 123 us -> 118 us (0.959); the launches traced: 121 us -> 118 us
  starting transfers between devices: 33.7 us -> 31.2 us
  Pallas kernels: 15.4 us -> 14 us
  local copies, waits for them, and re-layouts: 6.11 us -> 7.42 us
    ppermute x5 -> x3, starting transfers between devices: 5.5 us -> 3.11 us  [the longest x1 2.73 us: body(): lax.ppermute(jnp.concatenate([late[3], early[3, h:] + b[:h]]), 'grp', down)]
    unnamed x14 -> x16, local copies, waits for them, and re-layouts: 4.18 us -> 5.48 us
    pallas_call x1, Pallas kernels: 2.96 us -> 1.73 us  [body(): pl.pallas_call(functools.partial(pack_amplitudes, groups, share), out_sha...]
    ppermute x5 -> x3, waiting for transfers between devices: 6.77 us -> 7.64 us  [the longest x1 3.46 us: body(): lax.ppermute(jnp.concatenate([late[1], early[1, :h] + a[:h]]), 'grp', up)]
  transfers between devices with their start and end apart: 24 -> 22, of which waited for: 15 -> 15; matrix products, arithmetic and copies ran while one was open for 4% -> 4% of each run, Pallas kernels for 11% -> 10%
where the time goes in v5:
time: 118 us
  waiting for transfers between devices  48.5 us (41%)
  starting transfers between devices  31.2 us (26%)
  Pallas kernels  14 us (12%)
  blocking collectives  13.9 us (12%)
  local copies, waits for them, and re-layouts  7.42 us (6%)
  other arithmetic  2.76 us (2%)
    ppermute x5, waiting for transfers between devices, z_step(): return lax.ppermute(block, ('grp', 'col'), along)  20.4 us
    all_to_all x1, blocking collectives, body(): lax.all_to_all(amplitudes[0].reshape(groups, octet, cap), 'grp', 0, 0, ti...  13.9 us
    ppermute x5, starting transfers between devices, z_step(): return lax.ppermute(block, ('grp', 'col'), along)  12.2 us
    ppermute x5, waiting for transfers between devices, y_step(): return lax.ppermute(block, ('grp', 'row'), beside)  9.56 us
    unnamed x16, local copies, waits for them, and re-layouts  5.48 us
    all_to_all x1, starting transfers between devices, body(): lax.all_to_all(packed, ('grp', 'row'), 0, 0, axis_index_groups=pairs, til...  4.97 us
    pallas_call x1, Pallas kernels, body(): pl.pallas_call(functools.partial(join_tiles, groups, share), out_shape=ti...  4.52 us
    all_to_all x1, waiting for transfers between devices, body(): lax.all_to_all(packed, ('grp', 'row'), 0, 0, axis_index_groups=pairs, til...  3.98 us
  transfers between devices with their start and end apart: 22, of which 15 were waited for; matrix products, arithmetic and copies ran while one was open for 4% of the time, Pallas kernels for 10%

profile of v5, /device:TPU:1, one launch (start us, length us, event | category | flops | bytes accessed | tf_op | source)
XLA Modules:
  0.0 118.0 jit_solution(11741730187126053468)
XLA Ops:
  0.0 3.2 %collective-permute-start = (bf16[4608,384]{1,0:T(8,128)(2,1)}, bf16[4608,384]{1,0:T(8,128)(2,1)S(1)}, u32[]{:S(2)}, u32[]{:S(2)}) collective-permute-start(bf16[4608,384]{1,0:T(8,128)(2,1)} %bitcast.38), channel_id=1, source_target_pairs={{0,32},{32,0},{64,96},{96,64},{128,160},{160,128},{192,224},{224,1... | collective-permute-start | bytes 10616840 | tf_op jit(solution)/shard_map/ppermute | solution.py:208
  3.2 13.9 %all_to_all.10.src_ref = bf16[8,8,4608]{2,1,0:T(8,128)(2,1)S(1)} all-to-all(bf16[8,8,4608]{2,1,0:T(8,128)(2,1)} %bitcast.41), channel_id=1, replica_groups=mesh['grp'=8,'row'=4,'col'=8] {'grp'}, dimensions={0} | all-to-all | bytes 1179648 | tf_op jit(solution)/shard_map/all_to_all | solution.py:209
  17.2 0.7 copy-done.4
  17.8 0.7 copy-done.6
  18.5 1.7 %shard_map.46 = bf16[16,8,1536]{2,1,0:T(8,128)(2,1)S(1)} custom-call(s32[8]{0:T(128)S(1)} %copy-done.4, s32[8]{0:T(128)S(1)} %copy-done.6, bf16[8,8,4608]{2,1,0:T(8,128)(2,1)S(1)} %all_to_all.10.src_ref), custom_call_target="tpu_custom_call" | custom-call | tf_op jit(solution)/shard_map/pallas_call | solution.py:210
  20.2 0.0 copy-start.3
  20.2 0.7 copy-done.3
  21.0 5.0 %all-to-all-start.1 = ((bf16[16,8,1536]{2,1,0:T(8,128)(2,1)}), bf16[16,8,1536]{2,1,0:T(8,128)(2,1)}, u32[]{:S(2)}, u32[]{:S(2)}) async-start(bf16[16,8,1536]{2,1,0:T(8,128)(2,1)} %copy-done.3), calls=%async_computation.1 | async-start | bytes 786432 | tf_op jit(solution)/shard_map/all_to_all | solution.py:218
  25.9 0.0 collective-permute-done.other_ref
  25.9 0.0 copy-done.5
  26.0 0.0 copy-start
  26.0 2.0 %copy-done = bf16[1,4608,384]{2,1,0:T(8,128)(2,1)S(1)} copy-done((bf16[1,4608,384]{2,1,0:T(8,128)(2,1)S(1)}, bf16[1,4608,384]{2,1,0:T(8,128)(2,1)}, u32[]{:S(2)}) %copy-start) | copy-done | bytes 3538968
  28.0 3.4 %shard_map.47 = bf16[3072,384]{1,0:T(8,128)(2,1)S(1)} custom-call(s32[8]{0:T(128)S(1)} %copy-done.5, s32[8]{0:T(128)S(1)} %copy-done.7, bf16[4608,384]{1,0:T(8,128)(2,1)S(1)} %bitcast.39, bf16[4608,384]{1,0:T(8,128)(2,1)S(1)} %collective-permute-done.other_ref), custom_call_target="tpu_custom_call" | custom-call | tf_op jit(solution)/shard_map/pallas_call | solution.py:222
  31.4 1.4 %copy-done.2 = bf16[3072,384]{1,0:T(8,128)(2,1)} copy-done((bf16[3072,384]{1,0:T(8,128)(2,1)}, bf16[3072,384]{1,0:T(8,128)(2,1)S(1)}, u32[]{:S(2)}) %copy-start.2) | copy-done | bytes 2359320
  32.8 4.0 %all-to-all-done.1 = bf16[16,8,1536]{2,1,0:T(8,128)(2,1)} async-done(((bf16[16,8,1536]{2,1,0:T(8,128)(2,1)}), bf16[16,8,1536]{2,1,0:T(8,128)(2,1)}, u32[]{:S(2)}, u32[]{:S(2)}) %all-to-all-start.1) | async-done | bytes 393248 | tf_op jit(solution)/shard_map/all_to_all | solution.py:218
  36.7 0.5 collective-permute-start.7
  37.2 0.0 collective-permute-start.1
  37.2 5.6 %collective-permute-start.2 = (bf16[16,8,1536]{2,1,0:T(8,128)(2,1)}, bf16[16,8,1536]{2,1,0:T(8,128)(2,1)}, u32[]{:S(2)}, u32[]{:S(2)}) collective-permute-start(bf16[16,8,1536]{2,1,0:T(8,128)(2,1)} %all-to-all-done.1), channel_id=1, source_target_pairs={{0,1},{1,2},{2,3},{3,4},{4,5},{5,6},{6,7},{7,0},{32,39},{33,32},{3... | collective-permute-start | bytes 1179656 | tf_op jit(solution)/shard_map/ppermute | solution.py:237
  42.8 0.0 collective-permute-done.1
  42.8 2.1 %collective-permute-start.3 = (bf16[16,8,1536]{2,1,0:T(8,128)(2,1)}, bf16[16,8,1536]{2,1,0:T(8,128)(2,1)}, u32[]{:S(2)}, u32[]{:S(2)}) collective-permute-start(bf16[16,8,1536]{2,1,0:T(8,128)(2,1)} %collective-permute-done.1), channel_id=1, source_target_pairs={{0,1},{1,2},{2,3},{3,4},{4,5},{5,6},{6,7},{7,0},{32,39},{33,32},{3... | collective-permute-start | bytes 1179656 | tf_op jit(solution)/shard_map/ppermute | solution.py:237
  44.9 1.3 %fusion.1.refs_0_ = bf16[2,8,8,1536]{3,2,1,0:T(8,128)(2,1)S(1)} fusion(bf16[1,16,8,1536]{3,2,1,0:T(8,128)(2,1)} %bitcast.2, bf16[1,16,8,1536]{3,2,1,0:T(8,128)(2,1)} %bitcast.3, pred[]{:T(512)S(6)} %eq.4), kind=kLoop, calls=%fused_computation.4 | loop fusion | flops 589824 | bytes 1179649 | tf_op jit(solution)/shard_map/jit(_where)/select_n | solution.py:234
  46.2 0.5 collective-permute-start.4
  46.6 1.2 %collective-permute-done.2 = bf16[16,8,1536]{2,1,0:T(8,128)(2,1)} collective-permute-done((bf16[16,8,1536]{2,1,0:T(8,128)(2,1)}, bf16[16,8,1536]{2,1,0:T(8,128)(2,1)}, u32[]{:S(2)}, u32[]{:S(2)}) %collective-permute-start.2) | collective-permute-done | bytes 393248 | tf_op jit(solution)/shard_map/ppermute | solution.py:237
  47.8 4.2 %collective-permute-done.3 = bf16[16,8,1536]{2,1,0:T(8,128)(2,1)} collective-permute-done((bf16[16,8,1536]{2,1,0:T(8,128)(2,1)}, bf16[16,8,1536]{2,1,0:T(8,128)(2,1)}, u32[]{:S(2)}, u32[]{:S(2)}) %collective-permute-start.3) | collective-permute-done | bytes 393248 | tf_op jit(solution)/shard_map/ppermute | solution.py:237
  52.1 1.2 %pad_maximum_fusion.refs_2_ = bf16[2,16,8,1536]{3,2,1,0:T(8,128)(2,1)S(1)} fusion(bf16[1,16,8,1536]{3,2,1,0:T(8,128)(2,1)} %bitcast.5, bf16[1,16,8,1536]{3,2,1,0:T(8,128)(2,1)} %bitcast.4), kind=kLoop, calls=%fused_computation.2 | loop fusion | flops 393216 | bytes 1572864 | tf_op jit(solution)/shard_map/stack | solution.py:245
  53.2 0.0 copy-start.1
  53.3 1.2 %collective-permute-done.4.refs_1_ = bf16[2,8,8,1536]{3,2,1,0:T(8,128)(2,1)S(1)} collective-permute-done((bf16[2,8,8,1536]{3,2,1,0:T(8,128)(2,1)S(1)}, bf16[2,8,8,1536]{3,2,1,0:T(8,128)(2,1)S(1)}, u32[]{:S(2)}, u32[]{:S(2)}) %collective-permute-start.4) | collective-permute-done | bytes 393248 | tf_op jit(solution)/shard_map/ppermute | solution.py:240
  54.5 2.3 %collective-permute-start.5 = (bf16[2,16,8,1536]{3,2,1,0:T(8,128)(2,1)S(1)}, bf16[2,16,8,1536]{3,2,1,0:T(8,128)(2,1)S(1)}, u32[]{:S(2)}, u32[]{:S(2)}) collective-permute-start(bf16[2,16,8,1536]{3,2,1,0:T(8,128)(2,1)S(1)} %pad_maximum_fusion.refs_2_), channel_id=1, source_target_pairs={{0,1},{1,2},{2,3},{3,4},{4,5},{5,6},{6,7},{7,0},{32,39},{33,32},{3... | collective-permute-start | bytes 2359304 | tf_op jit(solution)/shard_map/ppermute | solution.py:237
  56.8 0.4 collective-permute-start.6
  57.2 8.6 %collective-permute-done.5.refs_4_ = bf16[2,16,8,1536]{3,2,1,0:T(8,128)(2,1)S(1)} collective-permute-done((bf16[2,16,8,1536]{3,2,1,0:T(8,128)(2,1)S(1)}, bf16[2,16,8,1536]{3,2,1,0:T(8,128)(2,1)S(1)}, u32[]{:S(2)}, u32[]{:S(2)}) %collective-permute-start.5) | collective-permute-done | bytes 786464 | tf_op jit(solution)/shard_map/ppermute | solution.py:237
  65.7 3.1 %collective-permute-done.6.refs_3_ = bf16[2,16,8,1536]{3,2,1,0:T(8,128)(2,1)S(1)} collective-permute-done((bf16[2,16,8,1536]{3,2,1,0:T(8,128)(2,1)S(1)}, bf16[2,16,8,1536]{3,2,1,0:T(8,128)(2,1)S(1)}, u32[]{:S(2)}, u32[]{:S(2)}) %collective-permute-start.6) | collective-permute-done | bytes 786464 | tf_op jit(solution)/shard_map/ppermute | solution.py:240
  68.8 0.0 collective-permute-done.7.got_ref
  68.8 1.8 %collective-permute-start.8 = (bf16[2,16,8,1536]{3,2,1,0:T(8,128)(2,1)S(1)}, bf16[2,16,8,1536]{3,2,1,0:T(8,128)(2,1)S(1)}, u32[]{:S(2)}, u32[]{:S(2)}) collective-permute-start(bf16[2,16,8,1536]{3,2,1,0:T(8,128)(2,1)S(1)} %collective-permute-done.5.refs_4_), channel_id=1, source_target_pairs={{0,1},{1,2},{2,3},{3,4},{4,5},{5,6},{6,7},{7,0},{32,39},{33,32},{3... | collective-permute-start | bytes 2359304 | tf_op jit(solution)/shard_map/ppermute | solution.py:237
  70.6 0.4 collective-permute-start.9
  71.0 1.9 %fusion.7 = (bf16[1536,384]{1,0:T(8,128)(2,1)S(1)}, bf16[1536,384]{1,0:T(8,128)(2,1)S(1)}) fusion(bf16[3072,384]{1,0:T(8,128)(2,1)} %collective-permute-done.7.got_ref), kind=kLoop, calls=%fused_computation.30 | loop fusion | bytes 4718592 | tf_op jit(solution)/shard_map/split | solution.py:253
  72.9 0.1 collective-permute-start.10
  73.0 0.5 collective-permute-start.11
  73.5 6.5 %collective-permute-done.8.refs_0_ = bf16[2,16,8,1536]{3,2,1,0:T(8,128)(2,1)S(1)} collective-permute-done((bf16[2,16,8,1536]{3,2,1,0:T(8,128)(2,1)S(1)}, bf16[2,16,8,1536]{3,2,1,0:T(8,128)(2,1)S(1)}, u32[]{:S(2)}, u32[]{:S(2)}) %collective-permute-start.8) | collective-permute-done | bytes 786464 | tf_op jit(solution)/shard_map/ppermute | solution.py:237
  79.9 3.0 %collective-permute-done.9.refs_5_ = bf16[2,16,8,1536]{3,2,1,0:T(8,128)(2,1)S(1)} collective-permute-done((bf16[2,16,8,1536]{3,2,1,0:T(8,128)(2,1)S(1)}, bf16[2,16,8,1536]{3,2,1,0:T(8,128)(2,1)S(1)}, u32[]{:S(2)}, u32[]{:S(2)}) %collective-permute-start.9) | collective-permute-done | bytes 786464 | tf_op jit(solution)/shard_map/ppermute | solution.py:240
  83.0 0.5 collective-permute-start.13
  83.5 0.0 collective-permute-start.12
  83.5 0.0 collective-permute-done.10.refs_0_
  83.5 0.0 collective-permute-done.11.refs_1_
  83.6 4.5 %shard_map.48.refs_6_.refs_4_ = bf16[3072,384]{1,0:T(8,128)(2,1)S(1)} custom-call(s32[8]{0:T(128)S(1)} %copy-done.5, s32[8]{0:T(128)S(1)} %copy-done.7, bf16[4608,384]{1,0:T(8,128)(2,1)S(1)} %bitcast.40, bf16[4608,384]{1,0:T(8,128)(2,1)S(1)} %collective-permute-done.other_ref, bf16[3072,384]{1,0:T(8,128)(2,1)} %collective-permute-done.7.got_ref, ...), custom_call_target="tpu_custom_call" | custom-call | tf_op jit(solution)/shard_map/pallas_call | solution.py:257
  88.1 2.2 %shard_map.49 = f32[4,160,384]{2,1,0:T(8,128)S(1)} custom-call(bf16[2,8,8,1536]{3,2,1,0:T(8,128)(2,1)S(1)} %fusion.1.refs_0_, bf16[2,8,8,1536]{3,2,1,0:T(8,128)(2,1)S(1)} %collective-permute-done.4.refs_1_, bf16[2,16,8,1536]{3,2,1,0:T(8,128)(2,1)S(1)} %pad_maximum_fusion.refs_2_, bf16[2,16,8,1536]{3,2,1,0:T(8,128)(2,1)S(1)} %collective-permute-done.6.refs_3_, ...), custom_call_target="tpu_custom_call" | custom-call | tf_op jit(solution)/shard_map/pallas_call | solution.py:268
  90.3 0.0 collective-permute-done.13.refs_2_
  90.3 0.1 collective-permute-start.14
  90.5 0.8 collective-permute-start.16
  91.2 0.9 collective-permute-start.15
  92.1 3.8 %collective-permute-done.16 = f32[160,384]{1,0:T(8,128)S(1)} collective-permute-done((f32[160,384]{1,0:T(8,128)S(1)}, f32[160,384]{1,0:T(8,128)S(1)}, u32[]{:S(2)}, u32[]{:S(2)}) %collective-permute-start.16) | collective-permute-done | bytes 245792 | tf_op jit(solution)/shard_map/ppermute | solution.py:183
  95.9 1.7 %collective-permute-done.15 = f32[160,384]{1,0:T(8,128)S(1)} collective-permute-done((f32[160,384]{1,0:T(8,128)S(1)}, f32[160,384]{1,0:T(8,128)S(1)}, u32[]{:S(2)}, u32[]{:S(2)}) %collective-permute-start.15) | collective-permute-done | bytes 245792 | tf_op jit(solution)/shard_map/ppermute | solution.py:182
  97.6 2.2 %collective-permute-done.14.refs_3_ = bf16[2,8,8,1536]{3,2,1,0:T(8,128)(2,1)S(1)} collective-permute-done((bf16[2,8,8,1536]{3,2,1,0:T(8,128)(2,1)S(1)}, bf16[2,8,8,1536]{3,2,1,0:T(8,128)(2,1)S(1)}, u32[]{:S(2)}, u32[]{:S(2)}) %collective-permute-start.14) | collective-permute-done | bytes 393248 | tf_op jit(solution)/shard_map/ppermute | solution.py:240
  99.8 0.0 collective-permute-done.12.refs_1_
  99.8 1.4 %shard_map.50 = f32[4,96,384]{2,1,0:T(8,128)S(1)} custom-call(bf16[2,16,8,1536]{3,2,1,0:T(8,128)(2,1)S(1)} %collective-permute-done.8.refs_0_, bf16[2,16,8,1536]{3,2,1,0:T(8,128)(2,1)S(1)} %collective-permute-done.12.refs_1_, bf16[2,8,8,1536]{3,2,1,0:T(8,128)(2,1)S(1)} %collective-permute-done.13.refs_2_, ...), custom_call_target="tpu_custom_call" | custom-call | tf_op jit(solution)/shard_map/pallas_call | solution.py:268
  101.3 0.1 collective-permute-start.17
  101.4 2.7 %collective-permute-start.18 = (f32[176,384]{1,0:T(8,128)S(1)}, f32[176,384]{1,0:T(8,128)S(1)}, u32[]{:S(2)}, u32[]{:S(2)}) collective-permute-start(f32[176,384]{1,0:T(8,128)S(1)} %pad_maximum_fusion.4), channel_id=1, source_target_pairs={{0,192},{32,224},{64,0},{96,32},{128,64},{160,96},{192,128},{224,1... | collective-permute-start | bytes 811016 | tf_op jit(solution)/shard_map/ppermute | solution.py:284
  104.2 0.3 collective-permute-start.19
  104.4 3.5 %collective-permute-done.17 = f32[176,384]{1,0:T(8,128)S(1)} collective-permute-done((f32[176,384]{1,0:T(8,128)S(1)}, f32[176,384]{1,0:T(8,128)S(1)}, u32[]{:S(2)}, u32[]{:S(2)}) %collective-permute-start.17) | collective-permute-done | bytes 270368 | tf_op jit(solution)/shard_map/ppermute | solution.py:283
  107.9 1.4 %collective-permute-done.18 = f32[176,384]{1,0:T(8,128)S(1)} collective-permute-done((f32[176,384]{1,0:T(8,128)S(1)}, f32[176,384]{1,0:T(8,128)S(1)}, u32[]{:S(2)}, u32[]{:S(2)}) %collective-permute-start.18) | collective-permute-done | bytes 270368 | tf_op jit(solution)/shard_map/ppermute | solution.py:284
  109.3 0.1 fusion.3
  109.4 2.8 %collective-permute-done.19 = f32[96,384]{1,0:T(8,128)S(1)} collective-permute-done((f32[96,384]{1,0:T(8,128)S(1)}, f32[96,384]{1,0:T(8,128)S(1)}, u32[]{:S(2)}, u32[]{:S(2)}) %collective-permute-start.19) | collective-permute-done | bytes 147488 | tf_op jit(solution)/shard_map/ppermute | solution.py:282
  112.2 3.6 %collective-permute-start.20 = (f32[256,384]{1,0:T(8,128)S(1)}, f32[256,384]{1,0:T(8,128)S(1)}, u32[]{:S(2)}, u32[]{:S(2)}) collective-permute-start(f32[256,384]{1,0:T(8,128)S(1)} %pad_maximum_fusion.2.mine_ref), channel_id=1, source_target_pairs={{0,32},{32,0},{64,96},{96,64},{128,160},{160,128},{192,224},{224,1... | collective-permute-start | bytes 1179656 | tf_op jit(solution)/shard_map/ppermute | solution.py:293
  115.9 1.3 %collective-permute-done.20.other_ref = f32[256,384]{1,0:T(8,128)S(1)} collective-permute-done((f32[256,384]{1,0:T(8,128)S(1)}, f32[256,384]{1,0:T(8,128)S(1)}, u32[]{:S(2)}, u32[]{:S(2)}) %collective-permute-start.20) | collective-permute-done | bytes 393248 | tf_op jit(solution)/shard_map/ppermute | solution.py:293
  117.2 0.8 shard_map.51
  (19 shorter events, 0.3 us)
Async XLA Ops:
  0.0 25.9 %copy-start.5 = (s32[8]{0:T(128)S(1)}, s32[8]{0:T(128)}, u32[]{:S(2)}) copy-start(s32[8]{0:T(128)} %tiles_ref.5) | copy-start | bytes 100
  0.0 26.0 %copy-start.7 = (s32[8]{0:T(128)S(1)}, s32[8]{0:T(128)}, u32[]{:S(2)}) copy-start(s32[8]{0:T(128)} %assign_ref.5) | copy-start | bytes 100
  0.0 25.9 %collective-permute-start = (bf16[4608,384]{1,0:T(8,128)(2,1)}, bf16[4608,384]{1,0:T(8,128)(2,1)S(1)}, u32[]{:S(2)}, u32[]{:S(2)}) collective-permute-start(bf16[4608,384]{1,0:T(8,128)(2,1)} %bitcast.38), channel_id=1, source_target_pairs={{0,32},{32,0},{64,96},{96,64},{128,160},{160,128},{192,224},{224,1... | collective-permute-start | bytes 10616840 | tf_op jit(solution)/shard_map/ppermute | solution.py:208
  17.2 0.7 copy-start.4
  17.8 0.7 copy-start.6
  20.2 0.7 copy-start.3
  21.0 15.8 %all-to-all-start.1 = ((bf16[16,8,1536]{2,1,0:T(8,128)(2,1)}), bf16[16,8,1536]{2,1,0:T(8,128)(2,1)}, u32[]{:S(2)}, u32[]{:S(2)}) async-start(bf16[16,8,1536]{2,1,0:T(8,128)(2,1)} %copy-done.3), calls=%async_computation.1 | async-start | bytes 786432 | tf_op jit(solution)/shard_map/all_to_all | solution.py:218
  26.0 2.0 %copy-start = (bf16[1,4608,384]{2,1,0:T(8,128)(2,1)S(1)}, bf16[1,4608,384]{2,1,0:T(8,128)(2,1)}, u32[]{:S(2)}) copy-start(bf16[1,4608,384]{2,1,0:T(8,128)(2,1)} %param.5) | copy-start | bytes 10616836
  31.3 1.4 %copy-start.2 = (bf16[3072,384]{1,0:T(8,128)(2,1)}, bf16[3072,384]{1,0:T(8,128)(2,1)S(1)}, u32[]{:S(2)}) copy-start(bf16[3072,384]{1,0:T(8,128)(2,1)S(1)} %shard_map.47) | copy-start | bytes 7077892
  36.7 32.1 %collective-permute-start.7 = (bf16[3072,384]{1,0:T(8,128)(2,1)}, bf16[3072,384]{1,0:T(8,128)(2,1)}, u32[]{:S(2)}, u32[]{:S(2)}) collective-permute-start(bf16[3072,384]{1,0:T(8,128)(2,1)} %copy-done.2), channel_id=1, source_target_pairs={{0,64},{32,224},{64,128},{96,32},{128,192},{160,96},{192,0},{224,1... | collective-permute-start | bytes 7077896 | tf_op jit(solution)/shard_map/ppermute | solution.py:231
  37.2 5.6 %collective-permute-start.1 = (bf16[16,8,1536]{2,1,0:T(8,128)(2,1)}, bf16[16,8,1536]{2,1,0:T(8,128)(2,1)}, u32[]{:S(2)}, u32[]{:S(2)}) collective-permute-start(bf16[16,8,1536]{2,1,0:T(8,128)(2,1)} %all-to-all-done.1), channel_id=1, source_target_pairs={{0,32},{32,0},{64,96},{96,64},{128,160},{160,128},{192,224},{224,1... | collective-permute-start | bytes 1179656 | tf_op jit(solution)/shard_map/ppermute | solution.py:242
  37.2 10.6 %collective-permute-start.2 = (bf16[16,8,1536]{2,1,0:T(8,128)(2,1)}, bf16[16,8,1536]{2,1,0:T(8,128)(2,1)}, u32[]{:S(2)}, u32[]{:S(2)}) collective-permute-start(bf16[16,8,1536]{2,1,0:T(8,128)(2,1)} %all-to-all-done.1), channel_id=1, source_target_pairs={{0,1},{1,2},{2,3},{3,4},{4,5},{5,6},{6,7},{7,0},{32,39},{33,32},{3... | collective-permute-start | bytes 1179656 | tf_op jit(solution)/shard_map/ppermute | solution.py:237
  42.8 9.2 %collective-permute-start.3 = (bf16[16,8,1536]{2,1,0:T(8,128)(2,1)}, bf16[16,8,1536]{2,1,0:T(8,128)(2,1)}, u32[]{:S(2)}, u32[]{:S(2)}) collective-permute-start(bf16[16,8,1536]{2,1,0:T(8,128)(2,1)} %collective-permute-done.1), channel_id=1, source_target_pairs={{0,1},{1,2},{2,3},{3,4},{4,5},{5,6},{6,7},{7,0},{32,39},{33,32},{3... | collective-permute-start | bytes 1179656 | tf_op jit(solution)/shard_map/ppermute | solution.py:237
  46.2 8.3 %collective-permute-start.4 = (bf16[2,8,8,1536]{3,2,1,0:T(8,128)(2,1)S(1)}, bf16[2,8,8,1536]{3,2,1,0:T(8,128)(2,1)S(1)}, u32[]{:S(2)}, u32[]{:S(2)}) collective-permute-start(bf16[2,8,8,1536]{3,2,1,0:T(8,128)(2,1)S(1)} %fusion.1.refs_0_), channel_id=1, source_target_pairs={{0,24},{8,0},{16,8},{24,16},{32,40},{40,48},{48,56},{56,32},{64,88... | collective-permute-start | bytes 1179656 | tf_op jit(solution)/shard_map/ppermute | solution.py:240
  53.2 30.3 %copy-start.1 = (bf16[1,4608,384]{2,1,0:T(8,128)(2,1)S(1)}, bf16[1,4608,384]{2,1,0:T(8,128)(2,1)}, u32[]{:S(2)}) copy-start(bf16[1,4608,384]{2,1,0:T(8,128)(2,1)} %param.5) | copy-start | bytes 10616836
  54.5 11.2 %collective-permute-start.5 = (bf16[2,16,8,1536]{3,2,1,0:T(8,128)(2,1)S(1)}, bf16[2,16,8,1536]{3,2,1,0:T(8,128)(2,1)S(1)}, u32[]{:S(2)}, u32[]{:S(2)}) collective-permute-start(bf16[2,16,8,1536]{3,2,1,0:T(8,128)(2,1)S(1)} %pad_maximum_fusion.refs_2_), channel_id=1, source_target_pairs={{0,1},{1,2},{2,3},{3,4},{4,5},{5,6},{6,7},{7,0},{32,39},{33,32},{3... | collective-permute-start | bytes 2359304 | tf_op jit(solution)/shard_map/ppermute | solution.py:237
  56.8 12.1 %collective-permute-start.6 = (bf16[2,16,8,1536]{3,2,1,0:T(8,128)(2,1)S(1)}, bf16[2,16,8,1536]{3,2,1,0:T(8,128)(2,1)S(1)}, u32[]{:S(2)}, u32[]{:S(2)}) collective-permute-start(bf16[2,16,8,1536]{3,2,1,0:T(8,128)(2,1)S(1)} %pad_maximum_fusion.refs_2_), channel_id=1, source_target_pairs={{0,24},{8,0},{16,8},{24,16},{32,40},{40,48},{48,56},{56,32},{64,88... | collective-permute-start | bytes 2359304 | tf_op jit(solution)/shard_map/ppermute | solution.py:240
  68.8 11.1 %collective-permute-start.8 = (bf16[2,16,8,1536]{3,2,1,0:T(8,128)(2,1)S(1)}, bf16[2,16,8,1536]{3,2,1,0:T(8,128)(2,1)S(1)}, u32[]{:S(2)}, u32[]{:S(2)}) collective-permute-start(bf16[2,16,8,1536]{3,2,1,0:T(8,128)(2,1)S(1)} %collective-permute-done.5.refs_4_), channel_id=1, source_target_pairs={{0,1},{1,2},{2,3},{3,4},{4,5},{5,6},{6,7},{7,0},{32,39},{33,32},{3... | collective-permute-start | bytes 2359304 | tf_op jit(solution)/shard_map/ppermute | solution.py:237
  70.6 12.3 %collective-permute-start.9 = (bf16[2,16,8,1536]{3,2,1,0:T(8,128)(2,1)S(1)}, bf16[2,16,8,1536]{3,2,1,0:T(8,128)(2,1)S(1)}, u32[]{:S(2)}, u32[]{:S(2)}) collective-permute-start(bf16[2,16,8,1536]{3,2,1,0:T(8,128)(2,1)S(1)} %collective-permute-done.5.refs_4_), channel_id=1, source_target_pairs={{0,24},{8,0},{16,8},{24,16},{32,40},{40,48},{48,56},{56,32},{64,88... | collective-permute-start | bytes 2359304 | tf_op jit(solution)/shard_map/ppermute | solution.py:240
  72.9 10.6 %collective-permute-start.10 = (bf16[1536,384]{1,0:T(8,128)(2,1)S(1)}, bf16[1536,384]{1,0:T(8,128)(2,1)S(1)}, u32[]{:S(2)}, u32[]{:S(2)}) collective-permute-start(bf16[1536,384]{1,0:T(8,128)(2,1)S(1)} %get-tuple-element.40), channel_id=1, source_target_pairs={{0,32},{32,0},{64,96},{96,64},{128,160},{160,128},{192,224},{224,1... | collective-permute-start | bytes 3538952 | tf_op jit(solution)/shard_map/ppermute | solution.py:253
  73.0 10.5 %collective-permute-start.11 = (bf16[1536,384]{1,0:T(8,128)(2,1)S(1)}, bf16[1536,384]{1,0:T(8,128)(2,1)S(1)}, u32[]{:S(2)}, u32[]{:S(2)}) collective-permute-start(bf16[1536,384]{1,0:T(8,128)(2,1)S(1)} %get-tuple-element.39), channel_id=1, source_target_pairs={{0,32},{32,0},{64,96},{96,64},{128,160},{160,128},{192,224},{224,1... | collective-permute-start | bytes 3538952 | tf_op jit(solution)/shard_map/ppermute | solution.py:253
  83.0 7.3 %collective-permute-start.13 = (bf16[2,8,8,1536]{3,2,1,0:T(8,128)(2,1)S(1)}, bf16[2,8,8,1536]{3,2,1,0:T(8,128)(2,1)S(1)}, u32[]{:S(2)}, u32[]{:S(2)}) collective-permute-start(bf16[2,8,8,1536]{3,2,1,0:T(8,128)(2,1)S(1)} %slice_select_fusion), channel_id=1, source_target_pairs={{0,1},{1,2},{2,3},{3,4},{4,5},{5,6},{6,7},{7,0},{32,39},{33,32},{3... | collective-permute-start | bytes 1179656 | tf_op jit(solution)/shard_map/ppermute | solution.py:237
  83.5 16.3 %collective-permute-start.12 = (bf16[2,16,8,1536]{3,2,1,0:T(8,128)(2,1)S(1)}, bf16[2,16,8,1536]{3,2,1,0:T(8,128)(2,1)S(1)}, u32[]{:S(2)}, u32[]{:S(2)}) collective-permute-start(bf16[2,16,8,1536]{3,2,1,0:T(8,128)(2,1)S(1)} %collective-permute-done.8.refs_0_), channel_id=1, source_target_pairs={{0,24},{8,0},{16,8},{24,16},{32,40},{40,48},{48,56},{56,32},{64,88... | collective-permute-start | bytes 2359304 | tf_op jit(solution)/shard_map/ppermute | solution.py:240
  90.3 9.5 %collective-permute-start.14 = (bf16[2,8,8,1536]{3,2,1,0:T(8,128)(2,1)S(1)}, bf16[2,8,8,1536]{3,2,1,0:T(8,128)(2,1)S(1)}, u32[]{:S(2)}, u32[]{:S(2)}) collective-permute-start(bf16[2,8,8,1536]{3,2,1,0:T(8,128)(2,1)S(1)} %collective-permute-done.13.refs_2_), channel_id=1, source_target_pairs={{0,24},{8,0},{16,8},{24,16},{32,40},{40,48},{48,56},{56,32},{64,88... | collective-permute-start | bytes 1179656 | tf_op jit(solution)/shard_map/ppermute | solution.py:240
  90.5 5.4 %collective-permute-start.16 = (f32[160,384]{1,0:T(8,128)S(1)}, f32[160,384]{1,0:T(8,128)S(1)}, u32[]{:S(2)}, u32[]{:S(2)}) collective-permute-start(f32[160,384]{1,0:T(8,128)S(1)} %pad_maximum_fusion.6), channel_id=1, source_target_pairs={{0,192},{32,224},{64,0},{96,32},{128,64},{160,96},{192,128},{224,1... | collective-permute-start | bytes 737288 | tf_op jit(solution)/shard_map/ppermute | solution.py:183
  91.2 6.3 %collective-permute-start.15 = (f32[160,384]{1,0:T(8,128)S(1)}, f32[160,384]{1,0:T(8,128)S(1)}, u32[]{:S(2)}, u32[]{:S(2)}) collective-permute-start(f32[160,384]{1,0:T(8,128)S(1)} %pad_maximum_fusion.5), channel_id=1, source_target_pairs={{0,64},{32,96},{64,128},{96,160},{128,192},{160,224},{192,0},{224,... | collective-permute-start | bytes 737288 | tf_op jit(solution)/shard_map/ppermute | solution.py:182
  101.3 6.6 %collective-permute-start.17 = (f32[176,384]{1,0:T(8,128)S(1)}, f32[176,384]{1,0:T(8,128)S(1)}, u32[]{:S(2)}, u32[]{:S(2)}) collective-permute-start(f32[176,384]{1,0:T(8,128)S(1)} %pad_maximum_fusion.3), channel_id=1, source_target_pairs={{0,64},{32,96},{64,128},{96,160},{128,192},{160,224},{192,0},{224,... | collective-permute-start | bytes 811016 | tf_op jit(solution)/shard_map/ppermute | solution.py:283
  101.4 7.9 %collective-permute-start.18 = (f32[176,384]{1,0:T(8,128)S(1)}, f32[176,384]{1,0:T(8,128)S(1)}, u32[]{:S(2)}, u32[]{:S(2)}) collective-permute-start(f32[176,384]{1,0:T(8,128)S(1)} %pad_maximum_fusion.4), channel_id=1, source_target_pairs={{0,192},{32,224},{64,0},{96,32},{128,64},{160,96},{192,128},{224,1... | collective-permute-start | bytes 811016 | tf_op jit(solution)/shard_map/ppermute | solution.py:284
  104.2 8.0 %collective-permute-start.19 = (f32[96,384]{1,0:T(8,128)S(1)}, f32[96,384]{1,0:T(8,128)S(1)}, u32[]{:S(2)}, u32[]{:S(2)}) collective-permute-start(f32[96,384]{1,0:T(8,128)S(1)} %get-tuple-element.48), channel_id=1, source_target_pairs={{0,128},{32,160},{64,192},{96,224},{128,0},{160,32},{192,64},{224,... | collective-permute-start | bytes 442376 | tf_op jit(solution)/shard_map/ppermute | solution.py:282
  112.2 5.0 %collective-permute-start.20 = (f32[256,384]{1,0:T(8,128)S(1)}, f32[256,384]{1,0:T(8,128)S(1)}, u32[]{:S(2)}, u32[]{:S(2)}) collective-permute-start(f32[256,384]{1,0:T(8,128)S(1)} %pad_maximum_fusion.2.mine_ref), channel_id=1, source_target_pairs={{0,32},{32,0},{64,96},{96,64},{128,160},{160,128},{192,224},{224,1... | collective-permute-start | bytes 1179656 | tf_op jit(solution)/shard_map/ppermute | solution.py:293

commit v6 on v5

--- a/solution.py
+++ b/solution.py
@@ -13,10 +13,10 @@
 VMEM = pl.BlockSpec(memory_space=pltpu.VMEM)
 
 
-def balance(tiles_ref, assign_ref, held_ref, block_ref, groups):
+def balance(both_ref, held_ref, block_ref, groups):
     for b in range(groups):
-        held_ref[assign_ref[b]] = tiles_ref[b]
-        block_ref[assign_ref[b]] = b
+        held_ref[both_ref[1, b]] = both_ref[0, b]
+        block_ref[both_ref[1, b]] = b
     chips = groups // 2
     held = [held_ref[s] for s in range(groups)]
     total = [held[2 * x] + held[2 * x + 1] for x in range(chips)]
@@ -54,8 +54,8 @@
     return (xl, t - n, n), (xr, 0, m), (x, k, None)
 
 
-def pack_amplitudes(groups, share, tiles_ref, assign_ref, src_ref, out_ref, held_ref, block_ref):
-    held, total, right, left = balance(tiles_ref, assign_ref, held_ref, block_ref, groups)
+def pack_amplitudes(groups, share, both_ref, src_ref, out_ref, held_ref, block_ref):
+    held, total, right, left = balance(both_ref, held_ref, block_ref, groups)
     blocks = [block_ref[s] for s in range(groups)]
     each = share // 2
     for x in range(groups // 2):
@@ -104,8 +104,8 @@
     return jobs
 
 
-def send_tiles(groups, share, tiles_ref, assign_ref, mine_ref, other_ref, out_ref, held_ref, block_ref, sems):
-    held, total, right, left = balance(tiles_ref, assign_ref, held_ref, block_ref, groups)
+def send_tiles(groups, share, both_ref, mine_ref, other_ref, out_ref, held_ref, block_ref, sems):
+    held, total, right, left = balance(both_ref, held_ref, block_ref, groups)
     group = lax.axis_index("grp")
     x, core = lax.div(group, 2), lax.rem(group, 2)
     go_right, go_left = pick(right, x), pick(left, x)
@@ -114,9 +114,9 @@
     run_copies(own_tiles(pick(held[0::2], x), core, start, count, mine_ref, other_ref, 0), out_ref, sems)
 
 
-def join_tiles(groups, share, tiles_ref, assign_ref, mine_ref, other_ref, got_ref, *refs):
+def join_tiles(groups, share, both_ref, mine_ref, other_ref, got_ref, *refs):
     *their_refs, out_ref, held_ref, block_ref, sems = refs
-    held, total, right, left = balance(tiles_ref, assign_ref, held_ref, block_ref, groups)
+    held, total, right, left = balance(both_ref, held_ref, block_ref, groups)
     group = lax.axis_index("grp")
     x, core = lax.div(group, 2), lax.rem(group, 2)
     (_, _, n), (_, _, m), (_, start, _) = runs_of(x, total, right, left, groups // 2)
@@ -204,17 +204,18 @@
     core = lax.rem(lax.axis_index("grp"), 2)
     barrier = lax.optimization_barrier
 
+    both = jnp.stack([block_tiles, assign])
     mine = integrals[0]
     other = lax.ppermute(mine, "grp", swap)
     moved = lax.all_to_all(amplitudes[0].reshape(groups, octet, cap), "grp", 0, 0, tiled=True)
     packed = pl.pallas_call(
         functools.partial(pack_amplitudes, groups, share),
         out_shape=jax.ShapeDtypeStruct((2 * groups, octet, wide // 2), jnp.bfloat16),
-        in_specs=[SMEM, SMEM, VMEM],
+        in_specs=[SMEM, VMEM],
         out_specs=VMEM,
         scratch_shapes=small,
         compiler_params=pltpu.CompilerParams(vmem_limit_bytes=8 * 2**20),
-    )(block_tiles, assign, moved)
+    )(both, moved)
     pair = lax.all_to_all(packed, ("grp", "row"), 0, 0, axis_index_groups=pairs, tiled=True)
 
     tiles = jax.ShapeDtypeStruct((wide, cols), jnp.bfloat16)
@@ -222,11 +223,11 @@
     sent = pl.pallas_call(
         functools.partial(send_tiles, groups, share),
         out_shape=tiles,
-        in_specs=[SMEM, SMEM, ANY, ANY],
+        in_specs=[SMEM, ANY, ANY],
         out_specs=VMEM,
         scratch_shapes=scratch,
         compiler_params=limit,
-    )(block_tiles, assign, mine, other)
+    )(both, mine, other)
     pair, sent = barrier((pair, sent))
     got = lax.ppermute(sent, "grp", apart)
     def half_of(block):
@@ -257,11 +258,11 @@
     held = pl.pallas_call(
         functools.partial(join_tiles, groups, share),
         out_shape=tiles,
-        in_specs=[SMEM, SMEM] + [ANY] * (3 + len(theirs)),
+        in_specs=[SMEM] + [ANY] * (3 + len(theirs)),
         out_specs=VMEM,
         scratch_shapes=scratch,
         compiler_params=limit,
-    )(block_tiles, assign, mine, other, got, *theirs)
+    )(both, mine, other, got, *theirs)
 
     def sums(parts):
         n = sum(part.shape[1] for part in parts) * octet

time: 118 us -> 118 us (level)
  blocking collectives: 13.9 us -> 0 us
  waiting for transfers between devices: 48.5 us -> 59.5 us
  starting transfers between devices: 31.2 us -> 34.8 us
  local copies, waits for them, and re-layouts: 7.42 us -> 6.1 us
    all_to_all x1 -> x0, blocking collectives: 13.9 us -> none  [body(): lax.all_to_all(amplitudes[0].reshape(groups, octet, cap), 'grp', 0, 0, ti...]
    all_to_all x0 -> x1, waiting for transfers between devices: none -> 9.55 us  [body(): lax.all_to_all(amplitudes[0].reshape(groups, octet, cap), 'grp', 0, 0, ti...]
    all_to_all x0 -> x1, starting transfers between devices: none -> 4.15 us  [body(): lax.all_to_all(amplitudes[0].reshape(groups, octet, cap), 'grp', 0, 0, ti...]
    all_to_all x1, waiting for transfers between devices: 3.98 us -> 5.59 us  [body(): lax.all_to_all(packed, ('grp', 'row'), 0, 0, axis_index_groups=pairs, til...]
    pallas_call x1, Pallas kernels: 3.36 us -> 1.82 us  [body(): pl.pallas_call(functools.partial(send_tiles, groups, share), out_shape=ti...]
    unnamed x16 -> x8, local copies, waits for them, and re-layouts: 5.48 us -> 4.15 us
  transfers between devices with their start and end apart: 22 -> 23, of which waited for: 15 -> 16; matrix products, arithmetic and copies ran while one was open for 4% -> 4% of each run, Pallas kernels for 10% -> 9%
where the time goes in v6:
time: 118 us; the launch traced here: 117 us
  waiting for transfers between devices  59.5 us (50%)
  starting transfers between devices  34.8 us (29%)
  Pallas kernels  13.2 us (11%)
  local copies, waits for them, and re-layouts  6.1 us (5%)
  other arithmetic  3.45 us (3%)
    ppermute x5, waiting for transfers between devices, z_step(): return lax.ppermute(block, ('grp', 'col'), along)  20.4 us
    ppermute x5, starting transfers between devices, z_step(): return lax.ppermute(block, ('grp', 'col'), along)  12 us
    ppermute x5, waiting for transfers between devices, y_step(): return lax.ppermute(block, ('grp', 'row'), beside)  9.56 us
    all_to_all x1, waiting for transfers between devices, body(): lax.all_to_all(amplitudes[0].reshape(groups, octet, cap), 'grp', 0, 0, ti...  9.55 us
    all_to_all x1, waiting for transfers between devices, body(): lax.all_to_all(packed, ('grp', 'row'), 0, 0, axis_index_groups=pairs, til...  5.59 us
    all_to_all x1, starting transfers between devices, body(): lax.all_to_all(packed, ('grp', 'row'), 0, 0, axis_index_groups=pairs, til...  4.83 us
    pallas_call x1, Pallas kernels, body(): pl.pallas_call(functools.partial(join_tiles, groups, share), out_shape=ti...  4.74 us
    unnamed x8, local copies, waits for them, and re-layouts  4.15 us
  transfers between devices with their start and end apart: 23, of which 16 were waited for; matrix products, arithmetic and copies ran while one was open for 4% of the time, Pallas kernels for 9%

profile of v6, /device:TPU:1, one launch (start us, length us, event | category | flops | bytes accessed | tf_op | source)
XLA Modules:
  0.0 117.2 jit_solution(869695583120680492)
XLA Ops:
  0.0 3.2 %collective-permute-start = (bf16[4608,384]{1,0:T(8,128)(2,1)}, bf16[4608,384]{1,0:T(8,128)(2,1)S(1)}, u32[]{:S(2)}, u32[]{:S(2)}) collective-permute-start(bf16[4608,384]{1,0:T(8,128)(2,1)} %bitcast.40), channel_id=1, source_target_pairs={{0,32},{32,0},{64,96},{96,64},{128,160},{160,128},{192,224},{224,1... | collective-permute-start | bytes 10616840 | tf_op jit(solution)/shard_map/ppermute | solution.py:209
  3.2 4.1 %all-to-all-start = ((bf16[8,8,4608]{2,1,0:T(8,128)(2,1)}), bf16[8,8,4608]{2,1,0:T(8,128)(2,1)}, u32[]{:S(2)}, u32[]{:S(2)}) async-start(bf16[8,8,4608]{2,1,0:T(8,128)(2,1)} %bitcast.43), calls=%async_computation | async-start | bytes 1179648 | tf_op jit(solution)/shard_map/all_to_all | solution.py:210
  7.4 0.7 pad_add_fusion.both_ref
  8.1 9.6 %all-to-all-done.src_ref = bf16[8,8,4608]{2,1,0:T(8,128)(2,1)} async-done(((bf16[8,8,4608]{2,1,0:T(8,128)(2,1)}), bf16[8,8,4608]{2,1,0:T(8,128)(2,1)}, u32[]{:S(2)}, u32[]{:S(2)}) %all-to-all-start) | async-done | bytes 589856 | tf_op jit(solution)/shard_map/all_to_all | solution.py:210
  17.6 2.2 %shard_map.46 = bf16[16,8,1536]{2,1,0:T(8,128)(2,1)S(1)} custom-call(s32[2,8]{1,0:T(2,128)S(1)} %pad_add_fusion.both_ref, bf16[8,8,4608]{2,1,0:T(8,128)(2,1)} %all-to-all-done.src_ref), custom_call_target="tpu_custom_call" | custom-call | tf_op jit(solution)/shard_map/pallas_call | solution.py:211
  19.8 0.0 copy-start.3
  19.9 0.7 copy-done.3
  20.6 4.8 %all-to-all-start.1 = ((bf16[16,8,1536]{2,1,0:T(8,128)(2,1)}), bf16[16,8,1536]{2,1,0:T(8,128)(2,1)}, u32[]{:S(2)}, u32[]{:S(2)}) async-start(bf16[16,8,1536]{2,1,0:T(8,128)(2,1)} %copy-done.3), calls=%async_computation.1 | async-start | bytes 786432 | tf_op jit(solution)/shard_map/all_to_all | solution.py:219
  25.4 0.0 collective-permute-done.other_ref
  25.4 0.0 copy-start
  25.4 2.0 %copy-done = bf16[1,4608,384]{2,1,0:T(8,128)(2,1)S(1)} copy-done((bf16[1,4608,384]{2,1,0:T(8,128)(2,1)S(1)}, bf16[1,4608,384]{2,1,0:T(8,128)(2,1)}, u32[]{:S(2)}) %copy-start) | copy-done | bytes 3538968
  27.4 1.8 %shard_map.47 = bf16[3072,384]{1,0:T(8,128)(2,1)S(1)} custom-call(s32[2,8]{1,0:T(2,128)S(1)} %pad_add_fusion.both_ref, bf16[4608,384]{1,0:T(8,128)(2,1)S(1)} %bitcast.41, bf16[4608,384]{1,0:T(8,128)(2,1)S(1)} %collective-permute-done.other_ref), custom_call_target="tpu_custom_call" | custom-call | tf_op jit(solution)/shard_map/pallas_call | solution.py:223
  29.3 0.0 copy-start.2
  29.3 1.4 %copy-done.2 = bf16[3072,384]{1,0:T(8,128)(2,1)} copy-done((bf16[3072,384]{1,0:T(8,128)(2,1)}, bf16[3072,384]{1,0:T(8,128)(2,1)S(1)}, u32[]{:S(2)}) %copy-start.2) | copy-done | bytes 2359320
  30.7 5.6 %all-to-all-done.1 = bf16[16,8,1536]{2,1,0:T(8,128)(2,1)} async-done(((bf16[16,8,1536]{2,1,0:T(8,128)(2,1)}), bf16[16,8,1536]{2,1,0:T(8,128)(2,1)}, u32[]{:S(2)}, u32[]{:S(2)}) %all-to-all-start.1) | async-done | bytes 393248 | tf_op jit(solution)/shard_map/all_to_all | solution.py:219
  36.3 0.4 collective-permute-start.7
  36.7 0.0 collective-permute-start.1
  36.7 5.3 %collective-permute-start.2 = (bf16[16,8,1536]{2,1,0:T(8,128)(2,1)}, bf16[16,8,1536]{2,1,0:T(8,128)(2,1)}, u32[]{:S(2)}, u32[]{:S(2)}) collective-permute-start(bf16[16,8,1536]{2,1,0:T(8,128)(2,1)} %all-to-all-done.1), channel_id=1, source_target_pairs={{0,1},{1,2},{2,3},{3,4},{4,5},{5,6},{6,7},{7,0},{32,39},{33,32},{3... | collective-permute-start | bytes 1179656 | tf_op jit(solution)/shard_map/ppermute | solution.py:238
  42.0 0.0 collective-permute-done.1
  42.0 2.1 %collective-permute-start.3 = (bf16[16,8,1536]{2,1,0:T(8,128)(2,1)}, bf16[16,8,1536]{2,1,0:T(8,128)(2,1)}, u32[]{:S(2)}, u32[]{:S(2)}) collective-permute-start(bf16[16,8,1536]{2,1,0:T(8,128)(2,1)} %collective-permute-done.1), channel_id=1, source_target_pairs={{0,1},{1,2},{2,3},{3,4},{4,5},{5,6},{6,7},{7,0},{32,39},{33,32},{3... | collective-permute-start | bytes 1179656 | tf_op jit(solution)/shard_map/ppermute | solution.py:238
  44.0 1.3 %fusion.1.refs_0_ = bf16[2,8,8,1536]{3,2,1,0:T(8,128)(2,1)S(1)} fusion(bf16[1,16,8,1536]{3,2,1,0:T(8,128)(2,1)} %bitcast.4, bf16[1,16,8,1536]{3,2,1,0:T(8,128)(2,1)} %bitcast.5, pred[]{:T(512)S(6)} %eq.4), kind=kLoop, calls=%fused_computation.4 | loop fusion | flops 589824 | bytes 1179649 | tf_op jit(solution)/shard_map/jit(_where)/select_n | solution.py:235
  45.3 0.5 collective-permute-start.4
  45.8 1.2 %collective-permute-done.2 = bf16[16,8,1536]{2,1,0:T(8,128)(2,1)} collective-permute-done((bf16[16,8,1536]{2,1,0:T(8,128)(2,1)}, bf16[16,8,1536]{2,1,0:T(8,128)(2,1)}, u32[]{:S(2)}, u32[]{:S(2)}) %collective-permute-start.2) | collective-permute-done | bytes 393248 | tf_op jit(solution)/shard_map/ppermute | solution.py:238
  47.0 4.2 %collective-permute-done.3 = bf16[16,8,1536]{2,1,0:T(8,128)(2,1)} collective-permute-done((bf16[16,8,1536]{2,1,0:T(8,128)(2,1)}, bf16[16,8,1536]{2,1,0:T(8,128)(2,1)}, u32[]{:S(2)}, u32[]{:S(2)}) %collective-permute-start.3) | collective-permute-done | bytes 393248 | tf_op jit(solution)/shard_map/ppermute | solution.py:238
  51.2 1.2 %pad_maximum_fusion.refs_2_ = bf16[2,16,8,1536]{3,2,1,0:T(8,128)(2,1)S(1)} fusion(bf16[1,16,8,1536]{3,2,1,0:T(8,128)(2,1)} %bitcast.7, bf16[1,16,8,1536]{3,2,1,0:T(8,128)(2,1)} %bitcast.6), kind=kLoop, calls=%fused_computation.2 | loop fusion | flops 393216 | bytes 1572864 | tf_op jit(solution)/shard_map/stack | solution.py:246
  52.4 0.0 copy-start.1
  52.4 1.2 %collective-permute-done.4.refs_1_ = bf16[2,8,8,1536]{3,2,1,0:T(8,128)(2,1)S(1)} collective-permute-done((bf16[2,8,8,1536]{3,2,1,0:T(8,128)(2,1)S(1)}, bf16[2,8,8,1536]{3,2,1,0:T(8,128)(2,1)S(1)}, u32[]{:S(2)}, u32[]{:S(2)}) %collective-permute-start.4) | collective-permute-done | bytes 393248 | tf_op jit(solution)/shard_map/ppermute | solution.py:241
  53.6 2.3 %collective-permute-start.5 = (bf16[2,16,8,1536]{3,2,1,0:T(8,128)(2,1)S(1)}, bf16[2,16,8,1536]{3,2,1,0:T(8,128)(2,1)S(1)}, u32[]{:S(2)}, u32[]{:S(2)}) collective-permute-start(bf16[2,16,8,1536]{3,2,1,0:T(8,128)(2,1)S(1)} %pad_maximum_fusion.refs_2_), channel_id=1, source_target_pairs={{0,1},{1,2},{2,3},{3,4},{4,5},{5,6},{6,7},{7,0},{32,39},{33,32},{3... | collective-permute-start | bytes 2359304 | tf_op jit(solution)/shard_map/ppermute | solution.py:238
  55.9 0.4 collective-permute-start.6
  56.3 8.6 %collective-permute-done.5.refs_4_ = bf16[2,16,8,1536]{3,2,1,0:T(8,128)(2,1)S(1)} collective-permute-done((bf16[2,16,8,1536]{3,2,1,0:T(8,128)(2,1)S(1)}, bf16[2,16,8,1536]{3,2,1,0:T(8,128)(2,1)S(1)}, u32[]{:S(2)}, u32[]{:S(2)}) %collective-permute-start.5) | collective-permute-done | bytes 786464 | tf_op jit(solution)/shard_map/ppermute | solution.py:238
  64.9 3.1 %collective-permute-done.6.refs_3_ = bf16[2,16,8,1536]{3,2,1,0:T(8,128)(2,1)S(1)} collective-permute-done((bf16[2,16,8,1536]{3,2,1,0:T(8,128)(2,1)S(1)}, bf16[2,16,8,1536]{3,2,1,0:T(8,128)(2,1)S(1)}, u32[]{:S(2)}, u32[]{:S(2)}) %collective-permute-start.6) | collective-permute-done | bytes 786464 | tf_op jit(solution)/shard_map/ppermute | solution.py:241
  68.0 0.0 collective-permute-done.7.got_ref
  68.0 1.8 %collective-permute-start.8 = (bf16[2,16,8,1536]{3,2,1,0:T(8,128)(2,1)S(1)}, bf16[2,16,8,1536]{3,2,1,0:T(8,128)(2,1)S(1)}, u32[]{:S(2)}, u32[]{:S(2)}) collective-permute-start(bf16[2,16,8,1536]{3,2,1,0:T(8,128)(2,1)S(1)} %collective-permute-done.5.refs_4_), channel_id=1, source_target_pairs={{0,1},{1,2},{2,3},{3,4},{4,5},{5,6},{6,7},{7,0},{32,39},{33,32},{3... | collective-permute-start | bytes 2359304 | tf_op jit(solution)/shard_map/ppermute | solution.py:238
  69.8 0.4 collective-permute-start.9
  70.2 1.9 %fusion.7 = (bf16[1536,384]{1,0:T(8,128)(2,1)S(1)}, bf16[1536,384]{1,0:T(8,128)(2,1)S(1)}) fusion(bf16[3072,384]{1,0:T(8,128)(2,1)} %collective-permute-done.7.got_ref), kind=kLoop, calls=%fused_computation.31 | loop fusion | bytes 4718592 | tf_op jit(solution)/shard_map/split | solution.py:254
  72.1 0.1 collective-permute-start.10
  72.2 0.5 collective-permute-start.11
  72.7 6.5 %collective-permute-done.8.refs_0_ = bf16[2,16,8,1536]{3,2,1,0:T(8,128)(2,1)S(1)} collective-permute-done((bf16[2,16,8,1536]{3,2,1,0:T(8,128)(2,1)S(1)}, bf16[2,16,8,1536]{3,2,1,0:T(8,128)(2,1)S(1)}, u32[]{:S(2)}, u32[]{:S(2)}) %collective-permute-start.8) | collective-permute-done | bytes 786464 | tf_op jit(solution)/shard_map/ppermute | solution.py:238
  79.1 3.0 %collective-permute-done.9.refs_5_ = bf16[2,16,8,1536]{3,2,1,0:T(8,128)(2,1)S(1)} collective-permute-done((bf16[2,16,8,1536]{3,2,1,0:T(8,128)(2,1)S(1)}, bf16[2,16,8,1536]{3,2,1,0:T(8,128)(2,1)S(1)}, u32[]{:S(2)}, u32[]{:S(2)}) %collective-permute-start.9) | collective-permute-done | bytes 786464 | tf_op jit(solution)/shard_map/ppermute | solution.py:241
  82.2 0.5 collective-permute-start.13
  82.7 0.0 collective-permute-start.12
  82.7 0.0 collective-permute-done.10.refs_0_
  82.7 0.0 collective-permute-done.11.refs_1_
  82.7 4.7 %shard_map.48.refs_6_.refs_4_ = bf16[3072,384]{1,0:T(8,128)(2,1)S(1)} custom-call(s32[2,8]{1,0:T(2,128)S(1)} %pad_add_fusion.both_ref, bf16[4608,384]{1,0:T(8,128)(2,1)S(1)} %bitcast.42, bf16[4608,384]{1,0:T(8,128)(2,1)S(1)} %collective-permute-done.other_ref, bf16[3072,384]{1,0:T(8,128)(2,1)} %collective-permute-done.7.got_ref, ...), custom_call_target="tpu_custom_call" | custom-call | tf_op jit(solution)/shard_map/pallas_call | solution.py:258
  87.5 2.2 %shard_map.49 = f32[4,160,384]{2,1,0:T(8,128)S(1)} custom-call(bf16[2,8,8,1536]{3,2,1,0:T(8,128)(2,1)S(1)} %fusion.1.refs_0_, bf16[2,8,8,1536]{3,2,1,0:T(8,128)(2,1)S(1)} %collective-permute-done.4.refs_1_, bf16[2,16,8,1536]{3,2,1,0:T(8,128)(2,1)S(1)} %pad_maximum_fusion.refs_2_, bf16[2,16,8,1536]{3,2,1,0:T(8,128)(2,1)S(1)} %collective-permute-done.6.refs_3_, ...), custom_call_target="tpu_custom_call" | custom-call | tf_op jit(solution)/shard_map/pallas_call | solution.py:269
  89.7 0.0 collective-permute-done.13.refs_2_
  89.7 0.1 collective-permute-start.14
  89.9 0.5 collective-permute-start.16
  90.4 1.1 collective-permute-start.15
  91.5 3.8 %collective-permute-done.16 = f32[160,384]{1,0:T(8,128)S(1)} collective-permute-done((f32[160,384]{1,0:T(8,128)S(1)}, f32[160,384]{1,0:T(8,128)S(1)}, u32[]{:S(2)}, u32[]{:S(2)}) %collective-permute-start.16) | collective-permute-done | bytes 245792 | tf_op jit(solution)/shard_map/ppermute | solution.py:183
  95.3 1.5 %collective-permute-done.15 = f32[160,384]{1,0:T(8,128)S(1)} collective-permute-done((f32[160,384]{1,0:T(8,128)S(1)}, f32[160,384]{1,0:T(8,128)S(1)}, u32[]{:S(2)}, u32[]{:S(2)}) %collective-permute-start.15) | collective-permute-done | bytes 245792 | tf_op jit(solution)/shard_map/ppermute | solution.py:182
  96.8 2.2 %collective-permute-done.14.refs_3_ = bf16[2,8,8,1536]{3,2,1,0:T(8,128)(2,1)S(1)} collective-permute-done((bf16[2,8,8,1536]{3,2,1,0:T(8,128)(2,1)S(1)}, bf16[2,8,8,1536]{3,2,1,0:T(8,128)(2,1)S(1)}, u32[]{:S(2)}, u32[]{:S(2)}) %collective-permute-start.14) | collective-permute-done | bytes 393248 | tf_op jit(solution)/shard_map/ppermute | solution.py:241
  99.0 0.0 collective-permute-done.12.refs_1_
  99.0 1.4 %shard_map.50 = f32[4,96,384]{2,1,0:T(8,128)S(1)} custom-call(bf16[2,16,8,1536]{3,2,1,0:T(8,128)(2,1)S(1)} %collective-permute-done.8.refs_0_, bf16[2,16,8,1536]{3,2,1,0:T(8,128)(2,1)S(1)} %collective-permute-done.12.refs_1_, bf16[2,8,8,1536]{3,2,1,0:T(8,128)(2,1)S(1)} %collective-permute-done.13.refs_2_, ...), custom_call_target="tpu_custom_call" | custom-call | tf_op jit(solution)/shard_map/pallas_call | solution.py:269
  100.5 0.1 collective-permute-start.17
  100.6 2.7 %collective-permute-start.18 = (f32[176,384]{1,0:T(8,128)S(1)}, f32[176,384]{1,0:T(8,128)S(1)}, u32[]{:S(2)}, u32[]{:S(2)}) collective-permute-start(f32[176,384]{1,0:T(8,128)S(1)} %pad_maximum_fusion.4), channel_id=1, source_target_pairs={{0,192},{32,224},{64,0},{96,32},{128,64},{160,96},{192,128},{224,1... | collective-permute-start | bytes 811016 | tf_op jit(solution)/shard_map/ppermute | solution.py:285
  103.3 0.3 collective-permute-start.19
  103.6 3.5 %collective-permute-done.17 = f32[176,384]{1,0:T(8,128)S(1)} collective-permute-done((f32[176,384]{1,0:T(8,128)S(1)}, f32[176,384]{1,0:T(8,128)S(1)}, u32[]{:S(2)}, u32[]{:S(2)}) %collective-permute-start.17) | collective-permute-done | bytes 270368 | tf_op jit(solution)/shard_map/ppermute | solution.py:284
  107.1 1.4 %collective-permute-done.18 = f32[176,384]{1,0:T(8,128)S(1)} collective-permute-done((f32[176,384]{1,0:T(8,128)S(1)}, f32[176,384]{1,0:T(8,128)S(1)}, u32[]{:S(2)}, u32[]{:S(2)}) %collective-permute-start.18) | collective-permute-done | bytes 270368 | tf_op jit(solution)/shard_map/ppermute | solution.py:285
  108.5 0.1 fusion.3
  108.5 2.9 %collective-permute-done.19 = f32[96,384]{1,0:T(8,128)S(1)} collective-permute-done((f32[96,384]{1,0:T(8,128)S(1)}, f32[96,384]{1,0:T(8,128)S(1)}, u32[]{:S(2)}, u32[]{:S(2)}) %collective-permute-start.19) | collective-permute-done | bytes 147488 | tf_op jit(solution)/shard_map/ppermute | solution.py:283
  111.6 3.5 %collective-permute-start.20 = (f32[256,384]{1,0:T(8,128)S(1)}, f32[256,384]{1,0:T(8,128)S(1)}, u32[]{:S(2)}, u32[]{:S(2)}) collective-permute-start(f32[256,384]{1,0:T(8,128)S(1)} %pad_maximum_fusion.2.mine_ref), channel_id=1, source_target_pairs={{0,32},{32,0},{64,96},{96,64},{128,160},{160,128},{192,224},{224,1... | collective-permute-start | bytes 1179656 | tf_op jit(solution)/shard_map/ppermute | solution.py:294
  115.0 1.3 %collective-permute-done.20.other_ref = f32[256,384]{1,0:T(8,128)S(1)} collective-permute-done((f32[256,384]{1,0:T(8,128)S(1)}, f32[256,384]{1,0:T(8,128)S(1)}, u32[]{:S(2)}, u32[]{:S(2)}) %collective-permute-start.20) | collective-permute-done | bytes 393248 | tf_op jit(solution)/shard_map/ppermute | solution.py:294
  116.4 0.8 shard_map.51
  (13 shorter events, 0.3 us)
Async XLA Ops:
  0.0 25.4 %collective-permute-start = (bf16[4608,384]{1,0:T(8,128)(2,1)}, bf16[4608,384]{1,0:T(8,128)(2,1)S(1)}, u32[]{:S(2)}, u32[]{:S(2)}) collective-permute-start(bf16[4608,384]{1,0:T(8,128)(2,1)} %bitcast.40), channel_id=1, source_target_pairs={{0,32},{32,0},{64,96},{96,64},{128,160},{160,128},{192,224},{224,1... | collective-permute-start | bytes 10616840 | tf_op jit(solution)/shard_map/ppermute | solution.py:209
  3.2 14.4 %all-to-all-start = ((bf16[8,8,4608]{2,1,0:T(8,128)(2,1)}), bf16[8,8,4608]{2,1,0:T(8,128)(2,1)}, u32[]{:S(2)}, u32[]{:S(2)}) async-start(bf16[8,8,4608]{2,1,0:T(8,128)(2,1)} %bitcast.43), calls=%async_computation | async-start | bytes 1179648 | tf_op jit(solution)/shard_map/all_to_all | solution.py:210
  19.8 0.7 copy-start.3
  20.6 15.7 %all-to-all-start.1 = ((bf16[16,8,1536]{2,1,0:T(8,128)(2,1)}), bf16[16,8,1536]{2,1,0:T(8,128)(2,1)}, u32[]{:S(2)}, u32[]{:S(2)}) async-start(bf16[16,8,1536]{2,1,0:T(8,128)(2,1)} %copy-done.3), calls=%async_computation.1 | async-start | bytes 786432 | tf_op jit(solution)/shard_map/all_to_all | solution.py:219
  25.4 2.0 %copy-start = (bf16[1,4608,384]{2,1,0:T(8,128)(2,1)S(1)}, bf16[1,4608,384]{2,1,0:T(8,128)(2,1)}, u32[]{:S(2)}) copy-start(bf16[1,4608,384]{2,1,0:T(8,128)(2,1)} %param.5) | copy-start | bytes 10616836
  29.3 1.4 %copy-start.2 = (bf16[3072,384]{1,0:T(8,128)(2,1)}, bf16[3072,384]{1,0:T(8,128)(2,1)S(1)}, u32[]{:S(2)}) copy-start(bf16[3072,384]{1,0:T(8,128)(2,1)S(1)} %shard_map.47) | copy-start | bytes 7077892
  36.3 31.7 %collective-permute-start.7 = (bf16[3072,384]{1,0:T(8,128)(2,1)}, bf16[3072,384]{1,0:T(8,128)(2,1)}, u32[]{:S(2)}, u32[]{:S(2)}) collective-permute-start(bf16[3072,384]{1,0:T(8,128)(2,1)} %copy-done.2), channel_id=1, source_target_pairs={{0,64},{32,224},{64,128},{96,32},{128,192},{160,96},{192,0},{224,1... | collective-permute-start | bytes 7077896 | tf_op jit(solution)/shard_map/ppermute | solution.py:232
  36.7 5.3 %collective-permute-start.1 = (bf16[16,8,1536]{2,1,0:T(8,128)(2,1)}, bf16[16,8,1536]{2,1,0:T(8,128)(2,1)}, u32[]{:S(2)}, u32[]{:S(2)}) collective-permute-start(bf16[16,8,1536]{2,1,0:T(8,128)(2,1)} %all-to-all-done.1), channel_id=1, source_target_pairs={{0,32},{32,0},{64,96},{96,64},{128,160},{160,128},{192,224},{224,1... | collective-permute-start | bytes 1179656 | tf_op jit(solution)/shard_map/ppermute | solution.py:243
  36.7 10.3 %collective-permute-start.2 = (bf16[16,8,1536]{2,1,0:T(8,128)(2,1)}, bf16[16,8,1536]{2,1,0:T(8,128)(2,1)}, u32[]{:S(2)}, u32[]{:S(2)}) collective-permute-start(bf16[16,8,1536]{2,1,0:T(8,128)(2,1)} %all-to-all-done.1), channel_id=1, source_target_pairs={{0,1},{1,2},{2,3},{3,4},{4,5},{5,6},{6,7},{7,0},{32,39},{33,32},{3... | collective-permute-start | bytes 1179656 | tf_op jit(solution)/shard_map/ppermute | solution.py:238
  42.0 9.2 %collective-permute-start.3 = (bf16[16,8,1536]{2,1,0:T(8,128)(2,1)}, bf16[16,8,1536]{2,1,0:T(8,128)(2,1)}, u32[]{:S(2)}, u32[]{:S(2)}) collective-permute-start(bf16[16,8,1536]{2,1,0:T(8,128)(2,1)} %collective-permute-done.1), channel_id=1, source_target_pairs={{0,1},{1,2},{2,3},{3,4},{4,5},{5,6},{6,7},{7,0},{32,39},{33,32},{3... | collective-permute-start | bytes 1179656 | tf_op jit(solution)/shard_map/ppermute | solution.py:238
  45.3 8.3 %collective-permute-start.4 = (bf16[2,8,8,1536]{3,2,1,0:T(8,128)(2,1)S(1)}, bf16[2,8,8,1536]{3,2,1,0:T(8,128)(2,1)S(1)}, u32[]{:S(2)}, u32[]{:S(2)}) collective-permute-start(bf16[2,8,8,1536]{3,2,1,0:T(8,128)(2,1)S(1)} %fusion.1.refs_0_), channel_id=1, source_target_pairs={{0,24},{8,0},{16,8},{24,16},{32,40},{40,48},{48,56},{56,32},{64,88... | collective-permute-start | bytes 1179656 | tf_op jit(solution)/shard_map/ppermute | solution.py:241
  52.4 30.3 %copy-start.1 = (bf16[1,4608,384]{2,1,0:T(8,128)(2,1)S(1)}, bf16[1,4608,384]{2,1,0:T(8,128)(2,1)}, u32[]{:S(2)}) copy-start(bf16[1,4608,384]{2,1,0:T(8,128)(2,1)} %param.5) | copy-start | bytes 10616836
  53.6 11.2 %collective-permute-start.5 = (bf16[2,16,8,1536]{3,2,1,0:T(8,128)(2,1)S(1)}, bf16[2,16,8,1536]{3,2,1,0:T(8,128)(2,1)S(1)}, u32[]{:S(2)}, u32[]{:S(2)}) collective-permute-start(bf16[2,16,8,1536]{3,2,1,0:T(8,128)(2,1)S(1)} %pad_maximum_fusion.refs_2_), channel_id=1, source_target_pairs={{0,1},{1,2},{2,3},{3,4},{4,5},{5,6},{6,7},{7,0},{32,39},{33,32},{3... | collective-permute-start | bytes 2359304 | tf_op jit(solution)/shard_map/ppermute | solution.py:238
  55.9 12.1 %collective-permute-start.6 = (bf16[2,16,8,1536]{3,2,1,0:T(8,128)(2,1)S(1)}, bf16[2,16,8,1536]{3,2,1,0:T(8,128)(2,1)S(1)}, u32[]{:S(2)}, u32[]{:S(2)}) collective-permute-start(bf16[2,16,8,1536]{3,2,1,0:T(8,128)(2,1)S(1)} %pad_maximum_fusion.refs_2_), channel_id=1, source_target_pairs={{0,24},{8,0},{16,8},{24,16},{32,40},{40,48},{48,56},{56,32},{64,88... | collective-permute-start | bytes 2359304 | tf_op jit(solution)/shard_map/ppermute | solution.py:241
  68.0 11.1 %collective-permute-start.8 = (bf16[2,16,8,1536]{3,2,1,0:T(8,128)(2,1)S(1)}, bf16[2,16,8,1536]{3,2,1,0:T(8,128)(2,1)S(1)}, u32[]{:S(2)}, u32[]{:S(2)}) collective-permute-start(bf16[2,16,8,1536]{3,2,1,0:T(8,128)(2,1)S(1)} %collective-permute-done.5.refs_4_), channel_id=1, source_target_pairs={{0,1},{1,2},{2,3},{3,4},{4,5},{5,6},{6,7},{7,0},{32,39},{33,32},{3... | collective-permute-start | bytes 2359304 | tf_op jit(solution)/shard_map/ppermute | solution.py:238
  69.8 12.3 %collective-permute-start.9 = (bf16[2,16,8,1536]{3,2,1,0:T(8,128)(2,1)S(1)}, bf16[2,16,8,1536]{3,2,1,0:T(8,128)(2,1)S(1)}, u32[]{:S(2)}, u32[]{:S(2)}) collective-permute-start(bf16[2,16,8,1536]{3,2,1,0:T(8,128)(2,1)S(1)} %collective-permute-done.5.refs_4_), channel_id=1, source_target_pairs={{0,24},{8,0},{16,8},{24,16},{32,40},{40,48},{48,56},{56,32},{64,88... | collective-permute-start | bytes 2359304 | tf_op jit(solution)/shard_map/ppermute | solution.py:241
  72.1 10.6 %collective-permute-start.10 = (bf16[1536,384]{1,0:T(8,128)(2,1)S(1)}, bf16[1536,384]{1,0:T(8,128)(2,1)S(1)}, u32[]{:S(2)}, u32[]{:S(2)}) collective-permute-start(bf16[1536,384]{1,0:T(8,128)(2,1)S(1)} %get-tuple-element.40), channel_id=1, source_target_pairs={{0,32},{32,0},{64,96},{96,64},{128,160},{160,128},{192,224},{224,1... | collective-permute-start | bytes 3538952 | tf_op jit(solution)/shard_map/ppermute | solution.py:254
  72.2 10.5 %collective-permute-start.11 = (bf16[1536,384]{1,0:T(8,128)(2,1)S(1)}, bf16[1536,384]{1,0:T(8,128)(2,1)S(1)}, u32[]{:S(2)}, u32[]{:S(2)}) collective-permute-start(bf16[1536,384]{1,0:T(8,128)(2,1)S(1)} %get-tuple-element.39), channel_id=1, source_target_pairs={{0,32},{32,0},{64,96},{96,64},{128,160},{160,128},{192,224},{224,1... | collective-permute-start | bytes 3538952 | tf_op jit(solution)/shard_map/ppermute | solution.py:254
  82.2 7.5 %collective-permute-start.13 = (bf16[2,8,8,1536]{3,2,1,0:T(8,128)(2,1)S(1)}, bf16[2,8,8,1536]{3,2,1,0:T(8,128)(2,1)S(1)}, u32[]{:S(2)}, u32[]{:S(2)}) collective-permute-start(bf16[2,8,8,1536]{3,2,1,0:T(8,128)(2,1)S(1)} %slice_select_fusion), channel_id=1, source_target_pairs={{0,1},{1,2},{2,3},{3,4},{4,5},{5,6},{6,7},{7,0},{32,39},{33,32},{3... | collective-permute-start | bytes 1179656 | tf_op jit(solution)/shard_map/ppermute | solution.py:238
  82.7 16.3 %collective-permute-start.12 = (bf16[2,16,8,1536]{3,2,1,0:T(8,128)(2,1)S(1)}, bf16[2,16,8,1536]{3,2,1,0:T(8,128)(2,1)S(1)}, u32[]{:S(2)}, u32[]{:S(2)}) collective-permute-start(bf16[2,16,8,1536]{3,2,1,0:T(8,128)(2,1)S(1)} %collective-permute-done.8.refs_0_), channel_id=1, source_target_pairs={{0,24},{8,0},{16,8},{24,16},{32,40},{40,48},{48,56},{56,32},{64,88... | collective-permute-start | bytes 2359304 | tf_op jit(solution)/shard_map/ppermute | solution.py:241
  89.7 9.2 %collective-permute-start.14 = (bf16[2,8,8,1536]{3,2,1,0:T(8,128)(2,1)S(1)}, bf16[2,8,8,1536]{3,2,1,0:T(8,128)(2,1)S(1)}, u32[]{:S(2)}, u32[]{:S(2)}) collective-permute-start(bf16[2,8,8,1536]{3,2,1,0:T(8,128)(2,1)S(1)} %collective-permute-done.13.refs_2_), channel_id=1, source_target_pairs={{0,24},{8,0},{16,8},{24,16},{32,40},{40,48},{48,56},{56,32},{64,88... | collective-permute-start | bytes 1179656 | tf_op jit(solution)/shard_map/ppermute | solution.py:241
  89.9 5.4 %collective-permute-start.16 = (f32[160,384]{1,0:T(8,128)S(1)}, f32[160,384]{1,0:T(8,128)S(1)}, u32[]{:S(2)}, u32[]{:S(2)}) collective-permute-start(f32[160,384]{1,0:T(8,128)S(1)} %pad_maximum_fusion.6), channel_id=1, source_target_pairs={{0,192},{32,224},{64,0},{96,32},{128,64},{160,96},{192,128},{224,1... | collective-permute-start | bytes 737288 | tf_op jit(solution)/shard_map/ppermute | solution.py:183
  90.4 6.3 %collective-permute-start.15 = (f32[160,384]{1,0:T(8,128)S(1)}, f32[160,384]{1,0:T(8,128)S(1)}, u32[]{:S(2)}, u32[]{:S(2)}) collective-permute-start(f32[160,384]{1,0:T(8,128)S(1)} %pad_maximum_fusion.5), channel_id=1, source_target_pairs={{0,64},{32,96},{64,128},{96,160},{128,192},{160,224},{192,0},{224,... | collective-permute-start | bytes 737288 | tf_op jit(solution)/shard_map/ppermute | solution.py:182
  100.5 6.6 %collective-permute-start.17 = (f32[176,384]{1,0:T(8,128)S(1)}, f32[176,384]{1,0:T(8,128)S(1)}, u32[]{:S(2)}, u32[]{:S(2)}) collective-permute-start(f32[176,384]{1,0:T(8,128)S(1)} %pad_maximum_fusion.3), channel_id=1, source_target_pairs={{0,64},{32,96},{64,128},{96,160},{128,192},{160,224},{192,0},{224,... | collective-permute-start | bytes 811016 | tf_op jit(solution)/shard_map/ppermute | solution.py:284
  100.6 7.9 %collective-permute-start.18 = (f32[176,384]{1,0:T(8,128)S(1)}, f32[176,384]{1,0:T(8,128)S(1)}, u32[]{:S(2)}, u32[]{:S(2)}) collective-permute-start(f32[176,384]{1,0:T(8,128)S(1)} %pad_maximum_fusion.4), channel_id=1, source_target_pairs={{0,192},{32,224},{64,0},{96,32},{128,64},{160,96},{192,128},{224,1... | collective-permute-start | bytes 811016 | tf_op jit(solution)/shard_map/ppermute | solution.py:285
  103.3 8.1 %collective-permute-start.19 = (f32[96,384]{1,0:T(8,128)S(1)}, f32[96,384]{1,0:T(8,128)S(1)}, u32[]{:S(2)}, u32[]{:S(2)}) collective-permute-start(f32[96,384]{1,0:T(8,128)S(1)} %get-tuple-element.48), channel_id=1, source_target_pairs={{0,128},{32,160},{64,192},{96,224},{128,0},{160,32},{192,64},{224,... | collective-permute-start | bytes 442376 | tf_op jit(solution)/shard_map/ppermute | solution.py:283
  111.6 4.8 %collective-permute-start.20 = (f32[256,384]{1,0:T(8,128)S(1)}, f32[256,384]{1,0:T(8,128)S(1)}, u32[]{:S(2)}, u32[]{:S(2)}) collective-permute-start(f32[256,384]{1,0:T(8,128)S(1)} %pad_maximum_fusion.2.mine_ref), channel_id=1, source_target_pairs={{0,32},{32,0},{64,96},{96,64},{128,160},{160,128},{192,224},{224,1... | collective-permute-start | bytes 1179656 | tf_op jit(solution)/shard_map/ppermute | solution.py:294

commit v7 on v6

--- a/solution.py
+++ b/solution.py
@@ -177,12 +177,6 @@
                     out_ref[q * rows + part * h : q * rows + (part + 1) * h, :] = ref[rows_in, :]
 
 
-def near_chips(p, up, down):
-    h = p.shape[1] // 2
-    a = lax.ppermute(jnp.concatenate([p[2, :h], p[1, h:]]), "grp", up)
-    return a, lax.ppermute(jnp.concatenate([p[2, h:], p[3, :h]]), "grp", down)
-
-
 def body(amplitudes, integrals, block_tiles, assign):
     groups = assign.shape[0]
     _, rows, cap = amplitudes.shape
@@ -247,7 +241,9 @@
     order += [near]
     for s in range(1, nz // 2 - 1):
         order += [block]
-        block, near = barrier((z_step(block), y_step(block)))
+        block, near = z_step(block), y_step(block)
+        if s < nz // 2 - 2:
+            block, near = barrier((block, near))
         if s == nz // 2 - 3:
             block, near, got = barrier((block, near, got))
         order += [near]
@@ -275,16 +271,14 @@
             compiler_params=limit,
         )(*parts, held)
 
+    def to_chips(p):
+        return [lax.ppermute(p[d], "grp", way) for d, way in ((2, opposite), (1, up), (3, down))]
+
     early, late = sums(order[:6]), order[6:]
-    a, b = near_chips(early, up, down)
-    *late, a, b = barrier((*late, a, b))
+    arrived = to_chips(early)
+    *late, arrived[1], arrived[2] = barrier((*late, *arrived[1:]))
     late = sums(late)
-    h, n = early.shape[1] // 2, late.shape[1]
-    c = lax.ppermute(late[2], "grp", opposite)
-    a2 = lax.ppermute(jnp.concatenate([late[1], early[1, :h] + a[:h]]), "grp", up)
-    b2 = lax.ppermute(jnp.concatenate([late[3], early[3, h:] + b[:h]]), "grp", down)
-    early = early[0] + jnp.concatenate([a2[n:], a[h:]]) + jnp.concatenate([b[h:], b2[n:]])
-    done = jnp.concatenate([early, late[0] + a2[:n] + b2[:n] + c])
+    done = jnp.concatenate([sum(arrived, early[0]), sum(to_chips(late), late[0])])
     return pl.pallas_call(
         functools.partial(finish, nz, rows),
         out_shape=jax.ShapeDtypeStruct((nz // 2 * rows, cols), jnp.float32),

time: 118 us -> 119 us (level)
  starting transfers between devices: 34.8 us -> 42.9 us
  waiting for transfers between devices: 59.5 us -> 52.6 us
  Pallas kernels: 13.2 us -> 12 us
    ppermute x5, waiting for transfers between devices: 9.56 us -> 5.01 us  [y_step(): return lax.ppermute(block, ('grp', 'row'), beside)]
    ppermute x1, starting transfers between devices: 3.48 us -> 6.85 us  [body(): lax.ppermute(done, 'grp', swap)]
    ppermute x5 -> x6, waiting for transfers between devices: 13 us -> 9.71 us  [to_chips(): lax.ppermute(p[d], 'grp', way)]
    ppermute x5, starting transfers between devices: 12 us -> 14.3 us  [z_step(): return lax.ppermute(block, ('grp', 'col'), along)]
    ppermute x5 -> x6, starting transfers between devices: 4.73 us -> 6.77 us  [to_chips(): lax.ppermute(p[d], 'grp', way)]
  transfers between devices with their start and end apart: 23 -> 24, of which waited for: 16 -> 15; matrix products, arithmetic and copies ran while one was open for 4% -> 4% of each run, Pallas kernels for 9% -> 9%
where the time goes in v7:
time: 119 us; the launch traced here: 117 us
  waiting for transfers between devices  52.6 us (44%)
  starting transfers between devices  42.9 us (36%)
  Pallas kernels  12 us (10%)
  local copies, waits for them, and re-layouts  6.09 us (5%)
  other arithmetic  3.32 us (3%)
    ppermute x5, waiting for transfers between devices, z_step(): return lax.ppermute(block, ('grp', 'col'), along)  20.4 us
    ppermute x5, starting transfers between devices, z_step(): return lax.ppermute(block, ('grp', 'col'), along)  14.3 us
    ppermute x6, waiting for transfers between devices, to_chips(): lax.ppermute(p[d], 'grp', way)  9.71 us
    all_to_all x1, waiting for transfers between devices, body(): lax.all_to_all(amplitudes[0].reshape(groups, octet, cap), 'grp', 0, 0, ti...  9.55 us
    ppermute x1, starting transfers between devices, body(): lax.ppermute(done, 'grp', swap)  6.85 us
    ppermute x6, starting transfers between devices, to_chips(): lax.ppermute(p[d], 'grp', way)  6.77 us
    all_to_all x1, waiting for transfers between devices, body(): lax.all_to_all(packed, ('grp', 'row'), 0, 0, axis_index_groups=pairs, til...  6.55 us
    ppermute x5, waiting for transfers between devices, y_step(): return lax.ppermute(block, ('grp', 'row'), beside)  5.01 us
  transfers between devices with their start and end apart: 24, of which 15 were waited for; matrix products, arithmetic and copies ran while one was open for 4% of the time, Pallas kernels for 9%

profile of v7, /device:TPU:1, one launch (start us, length us, event | category | flops | bytes accessed | tf_op | source)
XLA Modules:
  0.0 117.1 jit_solution(17396787189231037657)
XLA Ops:
  0.0 3.2 %collective-permute-start = (bf16[4608,384]{1,0:T(8,128)(2,1)}, bf16[4608,384]{1,0:T(8,128)(2,1)S(1)}, u32[]{:S(2)}, u32[]{:S(2)}) collective-permute-start(bf16[4608,384]{1,0:T(8,128)(2,1)} %bitcast.36), channel_id=1, source_target_pairs={{0,32},{32,0},{64,96},{96,64},{128,160},{160,128},{192,224},{224,1... | collective-permute-start | bytes 10616840 | tf_op jit(solution)/shard_map/ppermute | solution.py:203
  3.2 4.1 %all-to-all-start = ((bf16[8,8,4608]{2,1,0:T(8,128)(2,1)}), bf16[8,8,4608]{2,1,0:T(8,128)(2,1)}, u32[]{:S(2)}, u32[]{:S(2)}) async-start(bf16[8,8,4608]{2,1,0:T(8,128)(2,1)} %bitcast.39), calls=%async_computation | async-start | bytes 1179648 | tf_op jit(solution)/shard_map/all_to_all | solution.py:204
  7.4 0.7 pad_add_fusion.both_ref
  8.1 9.6 %all-to-all-done.src_ref = bf16[8,8,4608]{2,1,0:T(8,128)(2,1)} async-done(((bf16[8,8,4608]{2,1,0:T(8,128)(2,1)}), bf16[8,8,4608]{2,1,0:T(8,128)(2,1)}, u32[]{:S(2)}, u32[]{:S(2)}) %all-to-all-start) | async-done | bytes 589856 | tf_op jit(solution)/shard_map/all_to_all | solution.py:204
  17.6 2.2 %shard_map.46 = bf16[16,8,1536]{2,1,0:T(8,128)(2,1)S(1)} custom-call(s32[2,8]{1,0:T(2,128)S(1)} %pad_add_fusion.both_ref, bf16[8,8,4608]{2,1,0:T(8,128)(2,1)} %all-to-all-done.src_ref), custom_call_target="tpu_custom_call" | custom-call | tf_op jit(solution)/shard_map/pallas_call | solution.py:205
  19.9 0.0 copy-start.3
  19.9 0.7 copy-done.3
  20.6 4.8 %all-to-all-start.1 = ((bf16[16,8,1536]{2,1,0:T(8,128)(2,1)}), bf16[16,8,1536]{2,1,0:T(8,128)(2,1)}, u32[]{:S(2)}, u32[]{:S(2)}) async-start(bf16[16,8,1536]{2,1,0:T(8,128)(2,1)} %copy-done.3), calls=%async_computation.1 | async-start | bytes 786432 | tf_op jit(solution)/shard_map/all_to_all | solution.py:213
  25.5 0.0 collective-permute-done.other_ref
  25.5 0.0 copy-start
  25.5 2.0 %copy-done = bf16[1,4608,384]{2,1,0:T(8,128)(2,1)S(1)} copy-done((bf16[1,4608,384]{2,1,0:T(8,128)(2,1)S(1)}, bf16[1,4608,384]{2,1,0:T(8,128)(2,1)}, u32[]{:S(2)}) %copy-start) | copy-done | bytes 3538968
  27.5 0.9 shard_map.47
  28.3 1.4 %copy-done.2 = bf16[3072,384]{1,0:T(8,128)(2,1)} copy-done((bf16[3072,384]{1,0:T(8,128)(2,1)}, bf16[3072,384]{1,0:T(8,128)(2,1)S(1)}, u32[]{:S(2)}) %copy-start.2) | copy-done | bytes 2359320
  29.7 6.5 %all-to-all-done.1 = bf16[16,8,1536]{2,1,0:T(8,128)(2,1)} async-done(((bf16[16,8,1536]{2,1,0:T(8,128)(2,1)}), bf16[16,8,1536]{2,1,0:T(8,128)(2,1)}, u32[]{:S(2)}, u32[]{:S(2)}) %all-to-all-start.1) | async-done | bytes 393248 | tf_op jit(solution)/shard_map/all_to_all | solution.py:213
  36.3 0.4 collective-permute-start.7
  36.7 0.0 collective-permute-start.1
  36.7 5.3 %collective-permute-start.2 = (bf16[16,8,1536]{2,1,0:T(8,128)(2,1)}, bf16[16,8,1536]{2,1,0:T(8,128)(2,1)}, u32[]{:S(2)}, u32[]{:S(2)}) collective-permute-start(bf16[16,8,1536]{2,1,0:T(8,128)(2,1)} %all-to-all-done.1), channel_id=1, source_target_pairs={{0,1},{1,2},{2,3},{3,4},{4,5},{5,6},{6,7},{7,0},{32,39},{33,32},{3... | collective-permute-start | bytes 1179656 | tf_op jit(solution)/shard_map/ppermute | solution.py:232
  42.0 2.1 %collective-permute-start.3 = (bf16[16,8,1536]{2,1,0:T(8,128)(2,1)}, bf16[16,8,1536]{2,1,0:T(8,128)(2,1)}, u32[]{:S(2)}, u32[]{:S(2)}) collective-permute-start(bf16[16,8,1536]{2,1,0:T(8,128)(2,1)} %collective-permute-done.1), channel_id=1, source_target_pairs={{0,1},{1,2},{2,3},{3,4},{4,5},{5,6},{6,7},{7,0},{32,39},{33,32},{3... | collective-permute-start | bytes 1179656 | tf_op jit(solution)/shard_map/ppermute | solution.py:232
  44.1 1.3 %fusion.1.refs_0_ = bf16[2,8,8,1536]{3,2,1,0:T(8,128)(2,1)S(1)} fusion(bf16[1,16,8,1536]{3,2,1,0:T(8,128)(2,1)} %bitcast.4, bf16[1,16,8,1536]{3,2,1,0:T(8,128)(2,1)} %bitcast.5, pred[]{:T(512)S(6)} %eq.4), kind=kLoop, calls=%fused_computation.4 | loop fusion | flops 589824 | bytes 1179649 | tf_op jit(solution)/shard_map/jit(_where)/select_n | solution.py:229
  45.4 0.5 collective-permute-start.4
  45.8 1.2 %collective-permute-done.2 = bf16[16,8,1536]{2,1,0:T(8,128)(2,1)} collective-permute-done((bf16[16,8,1536]{2,1,0:T(8,128)(2,1)}, bf16[16,8,1536]{2,1,0:T(8,128)(2,1)}, u32[]{:S(2)}, u32[]{:S(2)}) %collective-permute-start.2) | collective-permute-done | bytes 393248 | tf_op jit(solution)/shard_map/ppermute | solution.py:232
  47.1 4.2 %collective-permute-done.3 = bf16[16,8,1536]{2,1,0:T(8,128)(2,1)} collective-permute-done((bf16[16,8,1536]{2,1,0:T(8,128)(2,1)}, bf16[16,8,1536]{2,1,0:T(8,128)(2,1)}, u32[]{:S(2)}, u32[]{:S(2)}) %collective-permute-start.3) | collective-permute-done | bytes 393248 | tf_op jit(solution)/shard_map/ppermute | solution.py:232
  51.3 1.2 %pad_maximum_fusion.refs_2_ = bf16[2,16,8,1536]{3,2,1,0:T(8,128)(2,1)S(1)} fusion(bf16[1,16,8,1536]{3,2,1,0:T(8,128)(2,1)} %bitcast.7, bf16[1,16,8,1536]{3,2,1,0:T(8,128)(2,1)} %bitcast.6), kind=kLoop, calls=%fused_computation.2 | loop fusion | flops 393216 | bytes 1572864 | tf_op jit(solution)/shard_map/stack | solution.py:240
  52.5 0.0 copy-start.1
  52.5 1.2 %collective-permute-done.4.refs_1_ = bf16[2,8,8,1536]{3,2,1,0:T(8,128)(2,1)S(1)} collective-permute-done((bf16[2,8,8,1536]{3,2,1,0:T(8,128)(2,1)S(1)}, bf16[2,8,8,1536]{3,2,1,0:T(8,128)(2,1)S(1)}, u32[]{:S(2)}, u32[]{:S(2)}) %collective-permute-start.4) | collective-permute-done | bytes 393248 | tf_op jit(solution)/shard_map/ppermute | solution.py:235
  53.7 2.3 %collective-permute-start.5 = (bf16[2,16,8,1536]{3,2,1,0:T(8,128)(2,1)S(1)}, bf16[2,16,8,1536]{3,2,1,0:T(8,128)(2,1)S(1)}, u32[]{:S(2)}, u32[]{:S(2)}) collective-permute-start(bf16[2,16,8,1536]{3,2,1,0:T(8,128)(2,1)S(1)} %pad_maximum_fusion.refs_2_), channel_id=1, source_target_pairs={{0,1},{1,2},{2,3},{3,4},{4,5},{5,6},{6,7},{7,0},{32,39},{33,32},{3... | collective-permute-start | bytes 2359304 | tf_op jit(solution)/shard_map/ppermute | solution.py:232
  56.0 0.4 collective-permute-start.6
  56.4 8.6 %collective-permute-done.5.refs_4_ = bf16[2,16,8,1536]{3,2,1,0:T(8,128)(2,1)S(1)} collective-permute-done((bf16[2,16,8,1536]{3,2,1,0:T(8,128)(2,1)S(1)}, bf16[2,16,8,1536]{3,2,1,0:T(8,128)(2,1)S(1)}, u32[]{:S(2)}, u32[]{:S(2)}) %collective-permute-start.5) | collective-permute-done | bytes 786464 | tf_op jit(solution)/shard_map/ppermute | solution.py:232
  64.9 3.1 %collective-permute-done.6.refs_3_ = bf16[2,16,8,1536]{3,2,1,0:T(8,128)(2,1)S(1)} collective-permute-done((bf16[2,16,8,1536]{3,2,1,0:T(8,128)(2,1)S(1)}, bf16[2,16,8,1536]{3,2,1,0:T(8,128)(2,1)S(1)}, u32[]{:S(2)}, u32[]{:S(2)}) %collective-permute-start.6) | collective-permute-done | bytes 786464 | tf_op jit(solution)/shard_map/ppermute | solution.py:235
  68.0 1.8 %collective-permute-start.12 = (bf16[2,16,8,1536]{3,2,1,0:T(8,128)(2,1)S(1)}, bf16[2,16,8,1536]{3,2,1,0:T(8,128)(2,1)S(1)}, u32[]{:S(2)}, u32[]{:S(2)}) collective-permute-start(bf16[2,16,8,1536]{3,2,1,0:T(8,128)(2,1)S(1)} %collective-permute-done.5.refs_4_), channel_id=1, source_target_pairs={{0,1},{1,2},{2,3},{3,4},{4,5},{5,6},{6,7},{7,0},{32,39},{33,32},{3... | collective-permute-start | bytes 2359304 | tf_op jit(solution)/shard_map/ppermute | solution.py:232
  69.8 1.9 %fusion.8 = (bf16[1536,384]{1,0:T(8,128)(2,1)S(1)}, bf16[1536,384]{1,0:T(8,128)(2,1)S(1)}) fusion(bf16[3072,384]{1,0:T(8,128)(2,1)} %collective-permute-done.7.got_ref), kind=kLoop, calls=%fused_computation.23 | loop fusion | bytes 4718592 | tf_op jit(solution)/shard_map/split | solution.py:250
  71.7 0.1 collective-permute-start.10
  71.8 0.5 collective-permute-start.9
  72.3 0.4 collective-permute-start.8
  72.7 6.5 %collective-permute-done.12.refs_0_ = bf16[2,16,8,1536]{3,2,1,0:T(8,128)(2,1)S(1)} collective-permute-done((bf16[2,16,8,1536]{3,2,1,0:T(8,128)(2,1)S(1)}, bf16[2,16,8,1536]{3,2,1,0:T(8,128)(2,1)S(1)}, u32[]{:S(2)}, u32[]{:S(2)}) %collective-permute-start.12) | collective-permute-done | bytes 786464 | tf_op jit(solution)/shard_map/ppermute | solution.py:232
  79.2 2.8 %collective-permute-start.14 = (bf16[2,8,8,1536]{3,2,1,0:T(8,128)(2,1)S(1)}, bf16[2,8,8,1536]{3,2,1,0:T(8,128)(2,1)S(1)}, u32[]{:S(2)}, u32[]{:S(2)}) collective-permute-start(bf16[2,8,8,1536]{3,2,1,0:T(8,128)(2,1)S(1)} %slice_select_fusion), channel_id=1, source_target_pairs={{0,1},{1,2},{2,3},{3,4},{4,5},{5,6},{6,7},{7,0},{32,39},{33,32},{3... | collective-permute-start | bytes 1179656 | tf_op jit(solution)/shard_map/ppermute | solution.py:232
  82.0 0.4 collective-permute-start.13
  82.4 0.0 collective-permute-done.10.refs_1_
  82.4 0.0 collective-permute-done.9.refs_0_
  82.4 4.4 %shard_map.48.refs_6_.refs_4_ = bf16[3072,384]{1,0:T(8,128)(2,1)S(1)} custom-call(s32[2,8]{1,0:T(2,128)S(1)} %pad_add_fusion.both_ref, bf16[4608,384]{1,0:T(8,128)(2,1)S(1)} %bitcast.38, bf16[4608,384]{1,0:T(8,128)(2,1)S(1)} %collective-permute-done.other_ref, bf16[3072,384]{1,0:T(8,128)(2,1)} %collective-permute-done.7.got_ref, ...), custom_call_target="tpu_custom_call" | custom-call | tf_op jit(solution)/shard_map/pallas_call | solution.py:254
  86.9 0.0 collective-permute-done.8.refs_5_
  86.9 2.2 %shard_map.49 = f32[4,160,384]{2,1,0:T(8,128)S(1)} custom-call(bf16[2,8,8,1536]{3,2,1,0:T(8,128)(2,1)S(1)} %fusion.1.refs_0_, bf16[2,8,8,1536]{3,2,1,0:T(8,128)(2,1)S(1)} %collective-permute-done.4.refs_1_, bf16[2,16,8,1536]{3,2,1,0:T(8,128)(2,1)S(1)} %pad_maximum_fusion.refs_2_, bf16[2,16,8,1536]{3,2,1,0:T(8,128)(2,1)S(1)} %collective-permute-done.6.refs_3_, ...), custom_call_target="tpu_custom_call" | custom-call | tf_op jit(solution)/shard_map/pallas_call | solution.py:265
  89.1 0.0 collective-permute-done.14.refs_2_
  89.1 0.1 collective-permute-start.15
  89.2 0.1 slice_bitcast_fusion.2
  89.3 0.1 collective-permute-start.16
  89.4 2.7 %collective-permute-start.17 = (f32[160,384]{1,0:T(8,128)S(1)}, f32[160,384]{1,0:T(8,128)S(1)}, u32[]{:S(2)}, u32[]{:S(2)}) collective-permute-start(f32[160,384]{1,0:T(8,128)S(1)} %get-tuple-element.38), channel_id=1, source_target_pairs={{0,192},{32,224},{64,0},{96,32},{128,64},{160,96},{192,128},{224,1... | collective-permute-start | bytes 737288 | tf_op jit(solution)/shard_map/ppermute | solution.py:275
  92.0 0.2 collective-permute-start.11
  92.2 3.4 %collective-permute-done.16 = f32[160,384]{1,0:T(8,128)S(1)} collective-permute-done((f32[160,384]{1,0:T(8,128)S(1)}, f32[160,384]{1,0:T(8,128)S(1)}, u32[]{:S(2)}, u32[]{:S(2)}) %collective-permute-start.16) | collective-permute-done | bytes 245792 | tf_op jit(solution)/shard_map/ppermute | solution.py:275
  95.6 2.3 %collective-permute-done.17 = f32[160,384]{1,0:T(8,128)S(1)} collective-permute-done((f32[160,384]{1,0:T(8,128)S(1)}, f32[160,384]{1,0:T(8,128)S(1)}, u32[]{:S(2)}, u32[]{:S(2)}) %collective-permute-start.17) | collective-permute-done | bytes 245792 | tf_op jit(solution)/shard_map/ppermute | solution.py:275
  97.9 0.7 collective-permute-done.15.refs_3_
  98.6 0.0 collective-permute-done.13.refs_1_
  98.6 1.4 %shard_map.50 = f32[4,96,384]{2,1,0:T(8,128)S(1)} custom-call(bf16[2,16,8,1536]{3,2,1,0:T(8,128)(2,1)S(1)} %collective-permute-done.12.refs_0_, bf16[2,16,8,1536]{3,2,1,0:T(8,128)(2,1)S(1)} %collective-permute-done.13.refs_1_, bf16[2,8,8,1536]{3,2,1,0:T(8,128)(2,1)S(1)} %collective-permute-done.14.refs_2_, ...), custom_call_target="tpu_custom_call" | custom-call | tf_op jit(solution)/shard_map/pallas_call | solution.py:265
  100.0 1.0 collective-permute-start.18
  101.0 2.8 %collective-permute-start.19 = (f32[96,384]{1,0:T(8,128)S(1)}, f32[96,384]{1,0:T(8,128)S(1)}, u32[]{:S(2)}, u32[]{:S(2)}) collective-permute-start(f32[96,384]{1,0:T(8,128)S(1)} %get-tuple-element.42), channel_id=1, source_target_pairs={{0,64},{32,96},{64,128},{96,160},{128,192},{160,224},{192,0},{224,... | collective-permute-start | bytes 442376 | tf_op jit(solution)/shard_map/ppermute | solution.py:275
  103.8 0.0 collective-permute-start.20
  103.8 0.0 collective-permute-done.11
  103.8 0.1 fusion.4
  103.9 1.8 %collective-permute-done.18 = f32[96,384]{1,0:T(8,128)S(1)} collective-permute-done((f32[96,384]{1,0:T(8,128)S(1)}, f32[96,384]{1,0:T(8,128)S(1)}, u32[]{:S(2)}, u32[]{:S(2)}) %collective-permute-start.18) | collective-permute-done | bytes 147488 | tf_op jit(solution)/shard_map/ppermute | solution.py:275
  105.6 1.6 %collective-permute-done.19 = f32[96,384]{1,0:T(8,128)S(1)} collective-permute-done((f32[96,384]{1,0:T(8,128)S(1)}, f32[96,384]{1,0:T(8,128)S(1)}, u32[]{:S(2)}, u32[]{:S(2)}) %collective-permute-start.19) | collective-permute-done | bytes 147488 | tf_op jit(solution)/shard_map/ppermute | solution.py:275
  107.2 0.7 collective-permute-done.20
  108.0 6.9 %collective-permute-start.21 = (f32[256,384]{1,0:T(8,128)S(1)}, f32[256,384]{1,0:T(8,128)S(1)}, u32[]{:S(2)}, u32[]{:S(2)}) collective-permute-start(f32[256,384]{1,0:T(8,128)S(1)} %pad_maximum_fusion.2.mine_ref), channel_id=1, source_target_pairs={{0,32},{32,0},{64,96},{96,64},{128,160},{160,128},{192,224},{224,1... | collective-permute-start | bytes 1179656 | tf_op jit(solution)/shard_map/ppermute | solution.py:288
  114.9 1.3 %collective-permute-done.21.other_ref = f32[256,384]{1,0:T(8,128)S(1)} collective-permute-done((f32[256,384]{1,0:T(8,128)S(1)}, f32[256,384]{1,0:T(8,128)S(1)}, u32[]{:S(2)}, u32[]{:S(2)}) %collective-permute-start.21) | collective-permute-done | bytes 393248 | tf_op jit(solution)/shard_map/ppermute | solution.py:288
  116.2 0.8 shard_map.51
  (8 shorter events, 0.2 us)
Async XLA Ops:
  0.0 25.5 %collective-permute-start = (bf16[4608,384]{1,0:T(8,128)(2,1)}, bf16[4608,384]{1,0:T(8,128)(2,1)S(1)}, u32[]{:S(2)}, u32[]{:S(2)}) collective-permute-start(bf16[4608,384]{1,0:T(8,128)(2,1)} %bitcast.36), channel_id=1, source_target_pairs={{0,32},{32,0},{64,96},{96,64},{128,160},{160,128},{192,224},{224,1... | collective-permute-start | bytes 10616840 | tf_op jit(solution)/shard_map/ppermute | solution.py:203
  3.2 14.4 %all-to-all-start = ((bf16[8,8,4608]{2,1,0:T(8,128)(2,1)}), bf16[8,8,4608]{2,1,0:T(8,128)(2,1)}, u32[]{:S(2)}, u32[]{:S(2)}) async-start(bf16[8,8,4608]{2,1,0:T(8,128)(2,1)} %bitcast.39), calls=%async_computation | async-start | bytes 1179648 | tf_op jit(solution)/shard_map/all_to_all | solution.py:204
  19.9 0.7 copy-start.3
  20.6 15.7 %all-to-all-start.1 = ((bf16[16,8,1536]{2,1,0:T(8,128)(2,1)}), bf16[16,8,1536]{2,1,0:T(8,128)(2,1)}, u32[]{:S(2)}, u32[]{:S(2)}) async-start(bf16[16,8,1536]{2,1,0:T(8,128)(2,1)} %copy-done.3), calls=%async_computation.1 | async-start | bytes 786432 | tf_op jit(solution)/shard_map/all_to_all | solution.py:213
  25.5 2.0 %copy-start = (bf16[1,4608,384]{2,1,0:T(8,128)(2,1)S(1)}, bf16[1,4608,384]{2,1,0:T(8,128)(2,1)}, u32[]{:S(2)}) copy-start(bf16[1,4608,384]{2,1,0:T(8,128)(2,1)} %param.5) | copy-start | bytes 10616836
  28.3 1.4 %copy-start.2 = (bf16[3072,384]{1,0:T(8,128)(2,1)}, bf16[3072,384]{1,0:T(8,128)(2,1)S(1)}, u32[]{:S(2)}) copy-start(bf16[3072,384]{1,0:T(8,128)(2,1)S(1)} %shard_map.47) | copy-start | bytes 7077892
  36.3 31.7 %collective-permute-start.7 = (bf16[3072,384]{1,0:T(8,128)(2,1)}, bf16[3072,384]{1,0:T(8,128)(2,1)}, u32[]{:S(2)}, u32[]{:S(2)}) collective-permute-start(bf16[3072,384]{1,0:T(8,128)(2,1)} %copy-done.2), channel_id=1, source_target_pairs={{0,64},{32,224},{64,128},{96,32},{128,192},{160,96},{192,0},{224,1... | collective-permute-start | bytes 7077896 | tf_op jit(solution)/shard_map/ppermute | solution.py:226
  36.7 5.3 %collective-permute-start.1 = (bf16[16,8,1536]{2,1,0:T(8,128)(2,1)}, bf16[16,8,1536]{2,1,0:T(8,128)(2,1)}, u32[]{:S(2)}, u32[]{:S(2)}) collective-permute-start(bf16[16,8,1536]{2,1,0:T(8,128)(2,1)} %all-to-all-done.1), channel_id=1, source_target_pairs={{0,32},{32,0},{64,96},{96,64},{128,160},{160,128},{192,224},{224,1... | collective-permute-start | bytes 1179656 | tf_op jit(solution)/shard_map/ppermute | solution.py:237
  36.7 10.3 %collective-permute-start.2 = (bf16[16,8,1536]{2,1,0:T(8,128)(2,1)}, bf16[16,8,1536]{2,1,0:T(8,128)(2,1)}, u32[]{:S(2)}, u32[]{:S(2)}) collective-permute-start(bf16[16,8,1536]{2,1,0:T(8,128)(2,1)} %all-to-all-done.1), channel_id=1, source_target_pairs={{0,1},{1,2},{2,3},{3,4},{4,5},{5,6},{6,7},{7,0},{32,39},{33,32},{3... | collective-permute-start | bytes 1179656 | tf_op jit(solution)/shard_map/ppermute | solution.py:232
  42.0 9.2 %collective-permute-start.3 = (bf16[16,8,1536]{2,1,0:T(8,128)(2,1)}, bf16[16,8,1536]{2,1,0:T(8,128)(2,1)}, u32[]{:S(2)}, u32[]{:S(2)}) collective-permute-start(bf16[16,8,1536]{2,1,0:T(8,128)(2,1)} %collective-permute-done.1), channel_id=1, source_target_pairs={{0,1},{1,2},{2,3},{3,4},{4,5},{5,6},{6,7},{7,0},{32,39},{33,32},{3... | collective-permute-start | bytes 1179656 | tf_op jit(solution)/shard_map/ppermute | solution.py:232
  45.4 8.3 %collective-permute-start.4 = (bf16[2,8,8,1536]{3,2,1,0:T(8,128)(2,1)S(1)}, bf16[2,8,8,1536]{3,2,1,0:T(8,128)(2,1)S(1)}, u32[]{:S(2)}, u32[]{:S(2)}) collective-permute-start(bf16[2,8,8,1536]{3,2,1,0:T(8,128)(2,1)S(1)} %fusion.1.refs_0_), channel_id=1, source_target_pairs={{0,24},{8,0},{16,8},{24,16},{32,40},{40,48},{48,56},{56,32},{64,88... | collective-permute-start | bytes 1179656 | tf_op jit(solution)/shard_map/ppermute | solution.py:235
  52.5 30.0 %copy-start.1 = (bf16[1,4608,384]{2,1,0:T(8,128)(2,1)S(1)}, bf16[1,4608,384]{2,1,0:T(8,128)(2,1)}, u32[]{:S(2)}) copy-start(bf16[1,4608,384]{2,1,0:T(8,128)(2,1)} %param.5) | copy-start | bytes 10616836
  53.7 11.2 %collective-permute-start.5 = (bf16[2,16,8,1536]{3,2,1,0:T(8,128)(2,1)S(1)}, bf16[2,16,8,1536]{3,2,1,0:T(8,128)(2,1)S(1)}, u32[]{:S(2)}, u32[]{:S(2)}) collective-permute-start(bf16[2,16,8,1536]{3,2,1,0:T(8,128)(2,1)S(1)} %pad_maximum_fusion.refs_2_), channel_id=1, source_target_pairs={{0,1},{1,2},{2,3},{3,4},{4,5},{5,6},{6,7},{7,0},{32,39},{33,32},{3... | collective-permute-start | bytes 2359304 | tf_op jit(solution)/shard_map/ppermute | solution.py:232
  56.0 12.1 %collective-permute-start.6 = (bf16[2,16,8,1536]{3,2,1,0:T(8,128)(2,1)S(1)}, bf16[2,16,8,1536]{3,2,1,0:T(8,128)(2,1)S(1)}, u32[]{:S(2)}, u32[]{:S(2)}) collective-permute-start(bf16[2,16,8,1536]{3,2,1,0:T(8,128)(2,1)S(1)} %pad_maximum_fusion.refs_2_), channel_id=1, source_target_pairs={{0,24},{8,0},{16,8},{24,16},{32,40},{40,48},{48,56},{56,32},{64,88... | collective-permute-start | bytes 2359304 | tf_op jit(solution)/shard_map/ppermute | solution.py:235
  68.0 11.1 %collective-permute-start.12 = (bf16[2,16,8,1536]{3,2,1,0:T(8,128)(2,1)S(1)}, bf16[2,16,8,1536]{3,2,1,0:T(8,128)(2,1)S(1)}, u32[]{:S(2)}, u32[]{:S(2)}) collective-permute-start(bf16[2,16,8,1536]{3,2,1,0:T(8,128)(2,1)S(1)} %collective-permute-done.5.refs_4_), channel_id=1, source_target_pairs={{0,1},{1,2},{2,3},{3,4},{4,5},{5,6},{6,7},{7,0},{32,39},{33,32},{3... | collective-permute-start | bytes 2359304 | tf_op jit(solution)/shard_map/ppermute | solution.py:232
  71.7 10.7 %collective-permute-start.10 = (bf16[1536,384]{1,0:T(8,128)(2,1)S(1)}, bf16[1536,384]{1,0:T(8,128)(2,1)S(1)}, u32[]{:S(2)}, u32[]{:S(2)}) collective-permute-start(bf16[1536,384]{1,0:T(8,128)(2,1)S(1)} %get-tuple-element.35), channel_id=1, source_target_pairs={{0,32},{32,0},{64,96},{96,64},{128,160},{160,128},{192,224},{224,1... | collective-permute-start | bytes 3538952 | tf_op jit(solution)/shard_map/ppermute | solution.py:250
  71.8 10.6 %collective-permute-start.9 = (bf16[1536,384]{1,0:T(8,128)(2,1)S(1)}, bf16[1536,384]{1,0:T(8,128)(2,1)S(1)}, u32[]{:S(2)}, u32[]{:S(2)}) collective-permute-start(bf16[1536,384]{1,0:T(8,128)(2,1)S(1)} %get-tuple-element.36), channel_id=1, source_target_pairs={{0,32},{32,0},{64,96},{96,64},{128,160},{160,128},{192,224},{224,1... | collective-permute-start | bytes 3538952 | tf_op jit(solution)/shard_map/ppermute | solution.py:250
  72.3 14.6 %collective-permute-start.8 = (bf16[2,16,8,1536]{3,2,1,0:T(8,128)(2,1)S(1)}, bf16[2,16,8,1536]{3,2,1,0:T(8,128)(2,1)S(1)}, u32[]{:S(2)}, u32[]{:S(2)}) collective-permute-start(bf16[2,16,8,1536]{3,2,1,0:T(8,128)(2,1)S(1)} %collective-permute-done.5.refs_4_), channel_id=1, source_target_pairs={{0,24},{8,0},{16,8},{24,16},{32,40},{40,48},{48,56},{56,32},{64,88... | collective-permute-start | bytes 2359304 | tf_op jit(solution)/shard_map/ppermute | solution.py:235
  79.2 9.9 %collective-permute-start.14 = (bf16[2,8,8,1536]{3,2,1,0:T(8,128)(2,1)S(1)}, bf16[2,8,8,1536]{3,2,1,0:T(8,128)(2,1)S(1)}, u32[]{:S(2)}, u32[]{:S(2)}) collective-permute-start(bf16[2,8,8,1536]{3,2,1,0:T(8,128)(2,1)S(1)} %slice_select_fusion), channel_id=1, source_target_pairs={{0,1},{1,2},{2,3},{3,4},{4,5},{5,6},{6,7},{7,0},{32,39},{33,32},{3... | collective-permute-start | bytes 1179656 | tf_op jit(solution)/shard_map/ppermute | solution.py:232
  82.0 16.6 %collective-permute-start.13 = (bf16[2,16,8,1536]{3,2,1,0:T(8,128)(2,1)S(1)}, bf16[2,16,8,1536]{3,2,1,0:T(8,128)(2,1)S(1)}, u32[]{:S(2)}, u32[]{:S(2)}) collective-permute-start(bf16[2,16,8,1536]{3,2,1,0:T(8,128)(2,1)S(1)} %collective-permute-done.12.refs_0_), channel_id=1, source_target_pairs={{0,24},{8,0},{16,8},{24,16},{32,40},{40,48},{48,56},{56,32},{64,88... | collective-permute-start | bytes 2359304 | tf_op jit(solution)/shard_map/ppermute | solution.py:235
  89.1 9.5 %collective-permute-start.15 = (bf16[2,8,8,1536]{3,2,1,0:T(8,128)(2,1)S(1)}, bf16[2,8,8,1536]{3,2,1,0:T(8,128)(2,1)S(1)}, u32[]{:S(2)}, u32[]{:S(2)}) collective-permute-start(bf16[2,8,8,1536]{3,2,1,0:T(8,128)(2,1)S(1)} %collective-permute-done.14.refs_2_), channel_id=1, source_target_pairs={{0,24},{8,0},{16,8},{24,16},{32,40},{40,48},{48,56},{56,32},{64,88... | collective-permute-start | bytes 1179656 | tf_op jit(solution)/shard_map/ppermute | solution.py:235
  89.3 6.3 %collective-permute-start.16 = (f32[160,384]{1,0:T(8,128)S(1)}, f32[160,384]{1,0:T(8,128)S(1)}, u32[]{:S(2)}, u32[]{:S(2)}) collective-permute-start(f32[160,384]{1,0:T(8,128)S(1)} %get-tuple-element.39), channel_id=1, source_target_pairs={{0,64},{32,96},{64,128},{96,160},{128,192},{160,224},{192,0},{224,... | collective-permute-start | bytes 737288 | tf_op jit(solution)/shard_map/ppermute | solution.py:275
  89.4 8.5 %collective-permute-start.17 = (f32[160,384]{1,0:T(8,128)S(1)}, f32[160,384]{1,0:T(8,128)S(1)}, u32[]{:S(2)}, u32[]{:S(2)}) collective-permute-start(f32[160,384]{1,0:T(8,128)S(1)} %get-tuple-element.38), channel_id=1, source_target_pairs={{0,192},{32,224},{64,0},{96,32},{128,64},{160,96},{192,128},{224,1... | collective-permute-start | bytes 737288 | tf_op jit(solution)/shard_map/ppermute | solution.py:275
  92.0 11.8 %collective-permute-start.11 = (f32[160,384]{1,0:T(8,128)S(1)}, f32[160,384]{1,0:T(8,128)S(1)}, u32[]{:S(2)}, u32[]{:S(2)}) collective-permute-start(f32[160,384]{1,0:T(8,128)S(1)} %get-tuple-element.37), channel_id=1, source_target_pairs={{0,128},{32,160},{64,192},{96,224},{128,0},{160,32},{192,64},{224,... | collective-permute-start | bytes 737288 | tf_op jit(solution)/shard_map/ppermute | solution.py:275
  100.0 5.6 %collective-permute-start.18 = (f32[96,384]{1,0:T(8,128)S(1)}, f32[96,384]{1,0:T(8,128)S(1)}, u32[]{:S(2)}, u32[]{:S(2)}) collective-permute-start(f32[96,384]{1,0:T(8,128)S(1)} %get-tuple-element.40), channel_id=1, source_target_pairs={{0,128},{32,160},{64,192},{96,224},{128,0},{160,32},{192,64},{224,... | collective-permute-start | bytes 442376 | tf_op jit(solution)/shard_map/ppermute | solution.py:275
  101.0 6.2 %collective-permute-start.19 = (f32[96,384]{1,0:T(8,128)S(1)}, f32[96,384]{1,0:T(8,128)S(1)}, u32[]{:S(2)}, u32[]{:S(2)}) collective-permute-start(f32[96,384]{1,0:T(8,128)S(1)} %get-tuple-element.42), channel_id=1, source_target_pairs={{0,64},{32,96},{64,128},{96,160},{128,192},{160,224},{192,0},{224,... | collective-permute-start | bytes 442376 | tf_op jit(solution)/shard_map/ppermute | solution.py:275
  103.8 4.1 %collective-permute-start.20 = (f32[96,384]{1,0:T(8,128)S(1)}, f32[96,384]{1,0:T(8,128)S(1)}, u32[]{:S(2)}, u32[]{:S(2)}) collective-permute-start(f32[96,384]{1,0:T(8,128)S(1)} %get-tuple-element.41), channel_id=1, source_target_pairs={{0,192},{32,224},{64,0},{96,32},{128,64},{160,96},{192,128},{224,1... | collective-permute-start | bytes 442376 | tf_op jit(solution)/shard_map/ppermute | solution.py:275
  108.0 8.2 %collective-permute-start.21 = (f32[256,384]{1,0:T(8,128)S(1)}, f32[256,384]{1,0:T(8,128)S(1)}, u32[]{:S(2)}, u32[]{:S(2)}) collective-permute-start(f32[256,384]{1,0:T(8,128)S(1)} %pad_maximum_fusion.2.mine_ref), channel_id=1, source_target_pairs={{0,32},{32,0},{64,96},{96,64},{128,160},{160,128},{192,224},{224,1... | collective-permute-start | bytes 1179656 | tf_op jit(solution)/shard_map/ppermute | solution.py:288

commit v8 on v6

--- a/solution.py
+++ b/solution.py
@@ -247,7 +247,9 @@
     order += [near]
     for s in range(1, nz // 2 - 1):
         order += [block]
-        block, near = barrier((z_step(block), y_step(block)))
+        block, near = z_step(block), y_step(block)
+        if s < nz // 2 - 2:
+            block, near = barrier((block, near))
         if s == nz // 2 - 3:
             block, near, got = barrier((block, near, got))
         order += [near]

time: 118 us -> 116 us (0.983)
  waiting for transfers between devices: 59.5 us -> 56.8 us
    ppermute x5, waiting for transfers between devices: 9.56 us -> 6.87 us  [y_step(): return lax.ppermute(block, ('grp', 'row'), beside)]
    ppermute x5, starting transfers between devices: 12 us -> 14.3 us  [z_step(): return lax.ppermute(block, ('grp', 'col'), along)]
    ppermute x1, starting transfers between devices: 3.48 us -> 1.59 us  [body(): lax.ppermute(done, 'grp', swap)]
  transfers between devices with their start and end apart: 23 -> 23, of which waited for: 16 -> 15; matrix products, arithmetic and copies ran while one was open for 4% -> 5% of each run, Pallas kernels for 9% -> 10%
where the time goes in v8:
time: 116 us
  waiting for transfers between devices  56.8 us (49%)
  starting transfers between devices  35.3 us (30%)
  Pallas kernels  14 us (12%)
  local copies, waits for them, and re-layouts  6.1 us (5%)
  other arithmetic  3.44 us (3%)
    ppermute x5, waiting for transfers between devices, z_step(): return lax.ppermute(block, ('grp', 'col'), along)  20.4 us
    ppermute x5, starting transfers between devices, z_step(): return lax.ppermute(block, ('grp', 'col'), along)  14.3 us
    all_to_all x1, waiting for transfers between devices, body(): lax.all_to_all(amplitudes[0].reshape(groups, octet, cap), 'grp', 0, 0, ti...  9.55 us
    ppermute x5, waiting for transfers between devices, y_step(): return lax.ppermute(block, ('grp', 'row'), beside)  6.87 us
    all_to_all x1, starting transfers between devices, body(): lax.all_to_all(packed, ('grp', 'row'), 0, 0, axis_index_groups=pairs, til...  4.83 us
    pallas_call x1, Pallas kernels, body(): pl.pallas_call(functools.partial(join_tiles, groups, share), out_shape=ti...  4.74 us
    all_to_all x1, waiting for transfers between devices, body(): lax.all_to_all(packed, ('grp', 'row'), 0, 0, axis_index_groups=pairs, til...  4.74 us
    ppermute x1, waiting for transfers between devices, body(): lax.ppermute(jnp.concatenate([late[1], early[1, :h] + a[:h]]), 'grp', up)  4.32 us
  transfers between devices with their start and end apart: 23, of which 15 were waited for; matrix products, arithmetic and copies ran while one was open for 5% of the time, Pallas kernels for 10%

profile of v8, /device:TPU:1, one launch (start us, length us, event | category | flops | bytes accessed | tf_op | source)
XLA Modules:
  0.0 115.8 jit_solution(1007732854160403662)
XLA Ops:
  0.0 3.2 %collective-permute-start = (bf16[4608,384]{1,0:T(8,128)(2,1)}, bf16[4608,384]{1,0:T(8,128)(2,1)S(1)}, u32[]{:S(2)}, u32[]{:S(2)}) collective-permute-start(bf16[4608,384]{1,0:T(8,128)(2,1)} %bitcast.40), channel_id=1, source_target_pairs={{0,32},{32,0},{64,96},{96,64},{128,160},{160,128},{192,224},{224,1... | collective-permute-start | bytes 10616840 | tf_op jit(solution)/shard_map/ppermute | solution.py:209
  3.2 4.1 %all-to-all-start = ((bf16[8,8,4608]{2,1,0:T(8,128)(2,1)}), bf16[8,8,4608]{2,1,0:T(8,128)(2,1)}, u32[]{:S(2)}, u32[]{:S(2)}) async-start(bf16[8,8,4608]{2,1,0:T(8,128)(2,1)} %bitcast.43), calls=%async_computation | async-start | bytes 1179648 | tf_op jit(solution)/shard_map/all_to_all | solution.py:210
  7.4 0.7 pad_add_fusion.both_ref
  8.1 9.6 %all-to-all-done.src_ref = bf16[8,8,4608]{2,1,0:T(8,128)(2,1)} async-done(((bf16[8,8,4608]{2,1,0:T(8,128)(2,1)}), bf16[8,8,4608]{2,1,0:T(8,128)(2,1)}, u32[]{:S(2)}, u32[]{:S(2)}) %all-to-all-start) | async-done | bytes 589856 | tf_op jit(solution)/shard_map/all_to_all | solution.py:210
  17.6 2.2 %shard_map.46 = bf16[16,8,1536]{2,1,0:T(8,128)(2,1)S(1)} custom-call(s32[2,8]{1,0:T(2,128)S(1)} %pad_add_fusion.both_ref, bf16[8,8,4608]{2,1,0:T(8,128)(2,1)} %all-to-all-done.src_ref), custom_call_target="tpu_custom_call" | custom-call | tf_op jit(solution)/shard_map/pallas_call | solution.py:211
  19.8 0.0 copy-start.3
  19.8 0.7 copy-done.3
  20.5 4.8 %all-to-all-start.1 = ((bf16[16,8,1536]{2,1,0:T(8,128)(2,1)}), bf16[16,8,1536]{2,1,0:T(8,128)(2,1)}, u32[]{:S(2)}, u32[]{:S(2)}) async-start(bf16[16,8,1536]{2,1,0:T(8,128)(2,1)} %copy-done.3), calls=%async_computation.1 | async-start | bytes 786432 | tf_op jit(solution)/shard_map/all_to_all | solution.py:219
  25.4 0.0 collective-permute-done.other_ref
  25.4 0.0 copy-start
  25.4 2.0 %copy-done = bf16[1,4608,384]{2,1,0:T(8,128)(2,1)S(1)} copy-done((bf16[1,4608,384]{2,1,0:T(8,128)(2,1)S(1)}, bf16[1,4608,384]{2,1,0:T(8,128)(2,1)}, u32[]{:S(2)}) %copy-start) | copy-done | bytes 3538968
  27.4 2.7 %shard_map.47 = bf16[3072,384]{1,0:T(8,128)(2,1)S(1)} custom-call(s32[2,8]{1,0:T(2,128)S(1)} %pad_add_fusion.both_ref, bf16[4608,384]{1,0:T(8,128)(2,1)S(1)} %bitcast.41, bf16[4608,384]{1,0:T(8,128)(2,1)S(1)} %collective-permute-done.other_ref), custom_call_target="tpu_custom_call" | custom-call | tf_op jit(solution)/shard_map/pallas_call | solution.py:223
  30.1 0.0 copy-start.2
  30.1 1.4 %copy-done.2 = bf16[3072,384]{1,0:T(8,128)(2,1)} copy-done((bf16[3072,384]{1,0:T(8,128)(2,1)}, bf16[3072,384]{1,0:T(8,128)(2,1)S(1)}, u32[]{:S(2)}) %copy-start.2) | copy-done | bytes 2359320
  31.5 4.7 %all-to-all-done.1 = bf16[16,8,1536]{2,1,0:T(8,128)(2,1)} async-done(((bf16[16,8,1536]{2,1,0:T(8,128)(2,1)}), bf16[16,8,1536]{2,1,0:T(8,128)(2,1)}, u32[]{:S(2)}, u32[]{:S(2)}) %all-to-all-start.1) | async-done | bytes 393248 | tf_op jit(solution)/shard_map/all_to_all | solution.py:219
  36.2 0.4 collective-permute-start.7
  36.6 0.0 collective-permute-start.1
  36.7 5.3 %collective-permute-start.2 = (bf16[16,8,1536]{2,1,0:T(8,128)(2,1)}, bf16[16,8,1536]{2,1,0:T(8,128)(2,1)}, u32[]{:S(2)}, u32[]{:S(2)}) collective-permute-start(bf16[16,8,1536]{2,1,0:T(8,128)(2,1)} %all-to-all-done.1), channel_id=1, source_target_pairs={{0,1},{1,2},{2,3},{3,4},{4,5},{5,6},{6,7},{7,0},{32,39},{33,32},{3... | collective-permute-start | bytes 1179656 | tf_op jit(solution)/shard_map/ppermute | solution.py:238
  41.9 0.0 collective-permute-done.1
  41.9 2.1 %collective-permute-start.3 = (bf16[16,8,1536]{2,1,0:T(8,128)(2,1)}, bf16[16,8,1536]{2,1,0:T(8,128)(2,1)}, u32[]{:S(2)}, u32[]{:S(2)}) collective-permute-start(bf16[16,8,1536]{2,1,0:T(8,128)(2,1)} %collective-permute-done.1), channel_id=1, source_target_pairs={{0,1},{1,2},{2,3},{3,4},{4,5},{5,6},{6,7},{7,0},{32,39},{33,32},{3... | collective-permute-start | bytes 1179656 | tf_op jit(solution)/shard_map/ppermute | solution.py:238
  44.0 1.3 %fusion.1.refs_0_ = bf16[2,8,8,1536]{3,2,1,0:T(8,128)(2,1)S(1)} fusion(bf16[1,16,8,1536]{3,2,1,0:T(8,128)(2,1)} %bitcast.4, bf16[1,16,8,1536]{3,2,1,0:T(8,128)(2,1)} %bitcast.5, pred[]{:T(512)S(6)} %eq.4), kind=kLoop, calls=%fused_computation.4 | loop fusion | flops 589824 | bytes 1179649 | tf_op jit(solution)/shard_map/jit(_where)/select_n | solution.py:235
  45.3 0.5 collective-permute-start.4
  45.8 1.2 %collective-permute-done.2 = bf16[16,8,1536]{2,1,0:T(8,128)(2,1)} collective-permute-done((bf16[16,8,1536]{2,1,0:T(8,128)(2,1)}, bf16[16,8,1536]{2,1,0:T(8,128)(2,1)}, u32[]{:S(2)}, u32[]{:S(2)}) %collective-permute-start.2) | collective-permute-done | bytes 393248 | tf_op jit(solution)/shard_map/ppermute | solution.py:238
  47.0 4.2 %collective-permute-done.3 = bf16[16,8,1536]{2,1,0:T(8,128)(2,1)} collective-permute-done((bf16[16,8,1536]{2,1,0:T(8,128)(2,1)}, bf16[16,8,1536]{2,1,0:T(8,128)(2,1)}, u32[]{:S(2)}, u32[]{:S(2)}) %collective-permute-start.3) | collective-permute-done | bytes 393248 | tf_op jit(solution)/shard_map/ppermute | solution.py:238
  51.2 1.2 %pad_maximum_fusion.refs_2_ = bf16[2,16,8,1536]{3,2,1,0:T(8,128)(2,1)S(1)} fusion(bf16[1,16,8,1536]{3,2,1,0:T(8,128)(2,1)} %bitcast.7, bf16[1,16,8,1536]{3,2,1,0:T(8,128)(2,1)} %bitcast.6), kind=kLoop, calls=%fused_computation.2 | loop fusion | flops 393216 | bytes 1572864 | tf_op jit(solution)/shard_map/stack | solution.py:246
  52.4 0.0 copy-start.1
  52.4 1.2 %collective-permute-done.4.refs_1_ = bf16[2,8,8,1536]{3,2,1,0:T(8,128)(2,1)S(1)} collective-permute-done((bf16[2,8,8,1536]{3,2,1,0:T(8,128)(2,1)S(1)}, bf16[2,8,8,1536]{3,2,1,0:T(8,128)(2,1)S(1)}, u32[]{:S(2)}, u32[]{:S(2)}) %collective-permute-start.4) | collective-permute-done | bytes 393248 | tf_op jit(solution)/shard_map/ppermute | solution.py:241
  53.6 2.3 %collective-permute-start.5 = (bf16[2,16,8,1536]{3,2,1,0:T(8,128)(2,1)S(1)}, bf16[2,16,8,1536]{3,2,1,0:T(8,128)(2,1)S(1)}, u32[]{:S(2)}, u32[]{:S(2)}) collective-permute-start(bf16[2,16,8,1536]{3,2,1,0:T(8,128)(2,1)S(1)} %pad_maximum_fusion.refs_2_), channel_id=1, source_target_pairs={{0,1},{1,2},{2,3},{3,4},{4,5},{5,6},{6,7},{7,0},{32,39},{33,32},{3... | collective-permute-start | bytes 2359304 | tf_op jit(solution)/shard_map/ppermute | solution.py:238
  55.9 0.4 collective-permute-start.6
  56.3 8.6 %collective-permute-done.5.refs_4_ = bf16[2,16,8,1536]{3,2,1,0:T(8,128)(2,1)S(1)} collective-permute-done((bf16[2,16,8,1536]{3,2,1,0:T(8,128)(2,1)S(1)}, bf16[2,16,8,1536]{3,2,1,0:T(8,128)(2,1)S(1)}, u32[]{:S(2)}, u32[]{:S(2)}) %collective-permute-start.5) | collective-permute-done | bytes 786464 | tf_op jit(solution)/shard_map/ppermute | solution.py:238
  64.8 3.1 %collective-permute-done.6.refs_3_ = bf16[2,16,8,1536]{3,2,1,0:T(8,128)(2,1)S(1)} collective-permute-done((bf16[2,16,8,1536]{3,2,1,0:T(8,128)(2,1)S(1)}, bf16[2,16,8,1536]{3,2,1,0:T(8,128)(2,1)S(1)}, u32[]{:S(2)}, u32[]{:S(2)}) %collective-permute-start.6) | collective-permute-done | bytes 786464 | tf_op jit(solution)/shard_map/ppermute | solution.py:241
  67.9 0.0 collective-permute-done.7.got_ref
  67.9 1.8 %collective-permute-start.11 = (bf16[2,16,8,1536]{3,2,1,0:T(8,128)(2,1)S(1)}, bf16[2,16,8,1536]{3,2,1,0:T(8,128)(2,1)S(1)}, u32[]{:S(2)}, u32[]{:S(2)}) collective-permute-start(bf16[2,16,8,1536]{3,2,1,0:T(8,128)(2,1)S(1)} %collective-permute-done.5.refs_4_), channel_id=1, source_target_pairs={{0,1},{1,2},{2,3},{3,4},{4,5},{5,6},{6,7},{7,0},{32,39},{33,32},{3... | collective-permute-start | bytes 2359304 | tf_op jit(solution)/shard_map/ppermute | solution.py:238
  69.8 1.9 %fusion.7 = (bf16[1536,384]{1,0:T(8,128)(2,1)S(1)}, bf16[1536,384]{1,0:T(8,128)(2,1)S(1)}) fusion(bf16[3072,384]{1,0:T(8,128)(2,1)} %collective-permute-done.7.got_ref), kind=kLoop, calls=%fused_computation.31 | loop fusion | bytes 4718592 | tf_op jit(solution)/shard_map/split | solution.py:256
  71.6 0.1 collective-permute-start.10
  71.7 0.5 collective-permute-start.9
  72.2 0.4 collective-permute-start.8
  72.6 6.5 %collective-permute-done.11.refs_0_ = bf16[2,16,8,1536]{3,2,1,0:T(8,128)(2,1)S(1)} collective-permute-done((bf16[2,16,8,1536]{3,2,1,0:T(8,128)(2,1)S(1)}, bf16[2,16,8,1536]{3,2,1,0:T(8,128)(2,1)S(1)}, u32[]{:S(2)}, u32[]{:S(2)}) %collective-permute-start.11) | collective-permute-done | bytes 786464 | tf_op jit(solution)/shard_map/ppermute | solution.py:238
  79.1 2.8 %collective-permute-start.13 = (bf16[2,8,8,1536]{3,2,1,0:T(8,128)(2,1)S(1)}, bf16[2,8,8,1536]{3,2,1,0:T(8,128)(2,1)S(1)}, u32[]{:S(2)}, u32[]{:S(2)}) collective-permute-start(bf16[2,8,8,1536]{3,2,1,0:T(8,128)(2,1)S(1)} %slice_select_fusion), channel_id=1, source_target_pairs={{0,1},{1,2},{2,3},{3,4},{4,5},{5,6},{6,7},{7,0},{32,39},{33,32},{3... | collective-permute-start | bytes 1179656 | tf_op jit(solution)/shard_map/ppermute | solution.py:238
  81.9 0.4 collective-permute-start.12
  82.3 0.0 collective-permute-done.10.refs_1_
  82.3 0.0 collective-permute-done.9.refs_0_
  82.3 4.7 %shard_map.48.refs_6_.refs_4_ = bf16[3072,384]{1,0:T(8,128)(2,1)S(1)} custom-call(s32[2,8]{1,0:T(2,128)S(1)} %pad_add_fusion.both_ref, bf16[4608,384]{1,0:T(8,128)(2,1)S(1)} %bitcast.42, bf16[4608,384]{1,0:T(8,128)(2,1)S(1)} %collective-permute-done.other_ref, bf16[3072,384]{1,0:T(8,128)(2,1)} %collective-permute-done.7.got_ref, ...), custom_call_target="tpu_custom_call" | custom-call | tf_op jit(solution)/shard_map/pallas_call | solution.py:260
  87.1 0.0 collective-permute-done.8.refs_5_
  87.1 2.2 %shard_map.49 = f32[4,160,384]{2,1,0:T(8,128)S(1)} custom-call(bf16[2,8,8,1536]{3,2,1,0:T(8,128)(2,1)S(1)} %fusion.1.refs_0_, bf16[2,8,8,1536]{3,2,1,0:T(8,128)(2,1)S(1)} %collective-permute-done.4.refs_1_, bf16[2,16,8,1536]{3,2,1,0:T(8,128)(2,1)S(1)} %pad_maximum_fusion.refs_2_, bf16[2,16,8,1536]{3,2,1,0:T(8,128)(2,1)S(1)} %collective-permute-done.6.refs_3_, ...), custom_call_target="tpu_custom_call" | custom-call | tf_op jit(solution)/shard_map/pallas_call | solution.py:271
  89.4 0.0 collective-permute-done.13.refs_2_
  89.4 0.1 collective-permute-start.14
  89.5 0.1 collective-permute-start.16
  89.6 1.5 %collective-permute-start.15 = (f32[160,384]{1,0:T(8,128)S(1)}, f32[160,384]{1,0:T(8,128)S(1)}, u32[]{:S(2)}, u32[]{:S(2)}) collective-permute-start(f32[160,384]{1,0:T(8,128)S(1)} %pad_maximum_fusion.5), channel_id=1, source_target_pairs={{0,64},{32,96},{64,128},{96,160},{128,192},{160,224},{192,0},{224,... | collective-permute-start | bytes 737288 | tf_op jit(solution)/shard_map/ppermute | solution.py:182
  91.1 3.8 %collective-permute-done.16 = f32[160,384]{1,0:T(8,128)S(1)} collective-permute-done((f32[160,384]{1,0:T(8,128)S(1)}, f32[160,384]{1,0:T(8,128)S(1)}, u32[]{:S(2)}, u32[]{:S(2)}) %collective-permute-start.16) | collective-permute-done | bytes 245792 | tf_op jit(solution)/shard_map/ppermute | solution.py:183
  94.9 1.0 collective-permute-done.15
  95.9 2.6 %collective-permute-done.14.refs_3_ = bf16[2,8,8,1536]{3,2,1,0:T(8,128)(2,1)S(1)} collective-permute-done((bf16[2,8,8,1536]{3,2,1,0:T(8,128)(2,1)S(1)}, bf16[2,8,8,1536]{3,2,1,0:T(8,128)(2,1)S(1)}, u32[]{:S(2)}, u32[]{:S(2)}) %collective-permute-start.14) | collective-permute-done | bytes 393248 | tf_op jit(solution)/shard_map/ppermute | solution.py:241
  98.5 0.0 collective-permute-done.12.refs_1_
  98.5 1.4 %shard_map.50 = f32[4,96,384]{2,1,0:T(8,128)S(1)} custom-call(bf16[2,16,8,1536]{3,2,1,0:T(8,128)(2,1)S(1)} %collective-permute-done.11.refs_0_, bf16[2,16,8,1536]{3,2,1,0:T(8,128)(2,1)S(1)} %collective-permute-done.12.refs_1_, bf16[2,8,8,1536]{3,2,1,0:T(8,128)(2,1)S(1)} %collective-permute-done.13.refs_2_, ...), custom_call_target="tpu_custom_call" | custom-call | tf_op jit(solution)/shard_map/pallas_call | solution.py:271
  100.0 0.1 collective-permute-start.17
  100.1 2.7 %collective-permute-start.18 = (f32[176,384]{1,0:T(8,128)S(1)}, f32[176,384]{1,0:T(8,128)S(1)}, u32[]{:S(2)}, u32[]{:S(2)}) collective-permute-start(f32[176,384]{1,0:T(8,128)S(1)} %pad_maximum_fusion.4), channel_id=1, source_target_pairs={{0,192},{32,224},{64,0},{96,32},{128,64},{160,96},{192,128},{224,1... | collective-permute-start | bytes 811016 | tf_op jit(solution)/shard_map/ppermute | solution.py:287
  102.9 0.0 collective-permute-start.19
  102.9 4.3 %collective-permute-done.17 = f32[176,384]{1,0:T(8,128)S(1)} collective-permute-done((f32[176,384]{1,0:T(8,128)S(1)}, f32[176,384]{1,0:T(8,128)S(1)}, u32[]{:S(2)}, u32[]{:S(2)}) %collective-permute-start.17) | collective-permute-done | bytes 270368 | tf_op jit(solution)/shard_map/ppermute | solution.py:286
  107.2 0.9 collective-permute-done.18
  108.1 0.1 fusion.3
  108.1 3.8 %collective-permute-done.19 = f32[96,384]{1,0:T(8,128)S(1)} collective-permute-done((f32[96,384]{1,0:T(8,128)S(1)}, f32[96,384]{1,0:T(8,128)S(1)}, u32[]{:S(2)}, u32[]{:S(2)}) %collective-permute-start.19) | collective-permute-done | bytes 147488 | tf_op jit(solution)/shard_map/ppermute | solution.py:285
  112.0 1.6 %collective-permute-start.20 = (f32[256,384]{1,0:T(8,128)S(1)}, f32[256,384]{1,0:T(8,128)S(1)}, u32[]{:S(2)}, u32[]{:S(2)}) collective-permute-start(f32[256,384]{1,0:T(8,128)S(1)} %pad_maximum_fusion.2.mine_ref), channel_id=1, source_target_pairs={{0,32},{32,0},{64,96},{96,64},{128,160},{160,128},{192,224},{224,1... | collective-permute-start | bytes 1179656 | tf_op jit(solution)/shard_map/ppermute | solution.py:296
  113.6 1.3 %collective-permute-done.20.other_ref = f32[256,384]{1,0:T(8,128)S(1)} collective-permute-done((f32[256,384]{1,0:T(8,128)S(1)}, f32[256,384]{1,0:T(8,128)S(1)}, u32[]{:S(2)}, u32[]{:S(2)}) %collective-permute-start.20) | collective-permute-done | bytes 393248 | tf_op jit(solution)/shard_map/ppermute | solution.py:296
  115.0 0.8 shard_map.51
  (13 shorter events, 0.3 us)
Async XLA Ops:
  0.0 25.4 %collective-permute-start = (bf16[4608,384]{1,0:T(8,128)(2,1)}, bf16[4608,384]{1,0:T(8,128)(2,1)S(1)}, u32[]{:S(2)}, u32[]{:S(2)}) collective-permute-start(bf16[4608,384]{1,0:T(8,128)(2,1)} %bitcast.40), channel_id=1, source_target_pairs={{0,32},{32,0},{64,96},{96,64},{128,160},{160,128},{192,224},{224,1... | collective-permute-start | bytes 10616840 | tf_op jit(solution)/shard_map/ppermute | solution.py:209
  3.2 14.4 %all-to-all-start = ((bf16[8,8,4608]{2,1,0:T(8,128)(2,1)}), bf16[8,8,4608]{2,1,0:T(8,128)(2,1)}, u32[]{:S(2)}, u32[]{:S(2)}) async-start(bf16[8,8,4608]{2,1,0:T(8,128)(2,1)} %bitcast.43), calls=%async_computation | async-start | bytes 1179648 | tf_op jit(solution)/shard_map/all_to_all | solution.py:210
  19.8 0.7 copy-start.3
  20.5 15.7 %all-to-all-start.1 = ((bf16[16,8,1536]{2,1,0:T(8,128)(2,1)}), bf16[16,8,1536]{2,1,0:T(8,128)(2,1)}, u32[]{:S(2)}, u32[]{:S(2)}) async-start(bf16[16,8,1536]{2,1,0:T(8,128)(2,1)} %copy-done.3), calls=%async_computation.1 | async-start | bytes 786432 | tf_op jit(solution)/shard_map/all_to_all | solution.py:219
  25.4 2.0 %copy-start = (bf16[1,4608,384]{2,1,0:T(8,128)(2,1)S(1)}, bf16[1,4608,384]{2,1,0:T(8,128)(2,1)}, u32[]{:S(2)}) copy-start(bf16[1,4608,384]{2,1,0:T(8,128)(2,1)} %param.5) | copy-start | bytes 10616836
  30.1 1.4 %copy-start.2 = (bf16[3072,384]{1,0:T(8,128)(2,1)}, bf16[3072,384]{1,0:T(8,128)(2,1)S(1)}, u32[]{:S(2)}) copy-start(bf16[3072,384]{1,0:T(8,128)(2,1)S(1)} %shard_map.47) | copy-start | bytes 7077892
  36.2 31.7 %collective-permute-start.7 = (bf16[3072,384]{1,0:T(8,128)(2,1)}, bf16[3072,384]{1,0:T(8,128)(2,1)}, u32[]{:S(2)}, u32[]{:S(2)}) collective-permute-start(bf16[3072,384]{1,0:T(8,128)(2,1)} %copy-done.2), channel_id=1, source_target_pairs={{0,64},{32,224},{64,128},{96,32},{128,192},{160,96},{192,0},{224,1... | collective-permute-start | bytes 7077896 | tf_op jit(solution)/shard_map/ppermute | solution.py:232
  36.6 5.3 %collective-permute-start.1 = (bf16[16,8,1536]{2,1,0:T(8,128)(2,1)}, bf16[16,8,1536]{2,1,0:T(8,128)(2,1)}, u32[]{:S(2)}, u32[]{:S(2)}) collective-permute-start(bf16[16,8,1536]{2,1,0:T(8,128)(2,1)} %all-to-all-done.1), channel_id=1, source_target_pairs={{0,32},{32,0},{64,96},{96,64},{128,160},{160,128},{192,224},{224,1... | collective-permute-start | bytes 1179656 | tf_op jit(solution)/shard_map/ppermute | solution.py:243
  36.7 10.3 %collective-permute-start.2 = (bf16[16,8,1536]{2,1,0:T(8,128)(2,1)}, bf16[16,8,1536]{2,1,0:T(8,128)(2,1)}, u32[]{:S(2)}, u32[]{:S(2)}) collective-permute-start(bf16[16,8,1536]{2,1,0:T(8,128)(2,1)} %all-to-all-done.1), channel_id=1, source_target_pairs={{0,1},{1,2},{2,3},{3,4},{4,5},{5,6},{6,7},{7,0},{32,39},{33,32},{3... | collective-permute-start | bytes 1179656 | tf_op jit(solution)/shard_map/ppermute | solution.py:238
  41.9 9.2 %collective-permute-start.3 = (bf16[16,8,1536]{2,1,0:T(8,128)(2,1)}, bf16[16,8,1536]{2,1,0:T(8,128)(2,1)}, u32[]{:S(2)}, u32[]{:S(2)}) collective-permute-start(bf16[16,8,1536]{2,1,0:T(8,128)(2,1)} %collective-permute-done.1), channel_id=1, source_target_pairs={{0,1},{1,2},{2,3},{3,4},{4,5},{5,6},{6,7},{7,0},{32,39},{33,32},{3... | collective-permute-start | bytes 1179656 | tf_op jit(solution)/shard_map/ppermute | solution.py:238
  45.3 8.3 %collective-permute-start.4 = (bf16[2,8,8,1536]{3,2,1,0:T(8,128)(2,1)S(1)}, bf16[2,8,8,1536]{3,2,1,0:T(8,128)(2,1)S(1)}, u32[]{:S(2)}, u32[]{:S(2)}) collective-permute-start(bf16[2,8,8,1536]{3,2,1,0:T(8,128)(2,1)S(1)} %fusion.1.refs_0_), channel_id=1, source_target_pairs={{0,24},{8,0},{16,8},{24,16},{32,40},{40,48},{48,56},{56,32},{64,88... | collective-permute-start | bytes 1179656 | tf_op jit(solution)/shard_map/ppermute | solution.py:241
  52.4 30.0 %copy-start.1 = (bf16[1,4608,384]{2,1,0:T(8,128)(2,1)S(1)}, bf16[1,4608,384]{2,1,0:T(8,128)(2,1)}, u32[]{:S(2)}) copy-start(bf16[1,4608,384]{2,1,0:T(8,128)(2,1)} %param.5) | copy-start | bytes 10616836
  53.6 11.2 %collective-permute-start.5 = (bf16[2,16,8,1536]{3,2,1,0:T(8,128)(2,1)S(1)}, bf16[2,16,8,1536]{3,2,1,0:T(8,128)(2,1)S(1)}, u32[]{:S(2)}, u32[]{:S(2)}) collective-permute-start(bf16[2,16,8,1536]{3,2,1,0:T(8,128)(2,1)S(1)} %pad_maximum_fusion.refs_2_), channel_id=1, source_target_pairs={{0,1},{1,2},{2,3},{3,4},{4,5},{5,6},{6,7},{7,0},{32,39},{33,32},{3... | collective-permute-start | bytes 2359304 | tf_op jit(solution)/shard_map/ppermute | solution.py:238
  55.9 12.1 %collective-permute-start.6 = (bf16[2,16,8,1536]{3,2,1,0:T(8,128)(2,1)S(1)}, bf16[2,16,8,1536]{3,2,1,0:T(8,128)(2,1)S(1)}, u32[]{:S(2)}, u32[]{:S(2)}) collective-permute-start(bf16[2,16,8,1536]{3,2,1,0:T(8,128)(2,1)S(1)} %pad_maximum_fusion.refs_2_), channel_id=1, source_target_pairs={{0,24},{8,0},{16,8},{24,16},{32,40},{40,48},{48,56},{56,32},{64,88... | collective-permute-start | bytes 2359304 | tf_op jit(solution)/shard_map/ppermute | solution.py:241
  67.9 11.1 %collective-permute-start.11 = (bf16[2,16,8,1536]{3,2,1,0:T(8,128)(2,1)S(1)}, bf16[2,16,8,1536]{3,2,1,0:T(8,128)(2,1)S(1)}, u32[]{:S(2)}, u32[]{:S(2)}) collective-permute-start(bf16[2,16,8,1536]{3,2,1,0:T(8,128)(2,1)S(1)} %collective-permute-done.5.refs_4_), channel_id=1, source_target_pairs={{0,1},{1,2},{2,3},{3,4},{4,5},{5,6},{6,7},{7,0},{32,39},{33,32},{3... | collective-permute-start | bytes 2359304 | tf_op jit(solution)/shard_map/ppermute | solution.py:238
  71.6 10.7 %collective-permute-start.10 = (bf16[1536,384]{1,0:T(8,128)(2,1)S(1)}, bf16[1536,384]{1,0:T(8,128)(2,1)S(1)}, u32[]{:S(2)}, u32[]{:S(2)}) collective-permute-start(bf16[1536,384]{1,0:T(8,128)(2,1)S(1)} %get-tuple-element.35), channel_id=1, source_target_pairs={{0,32},{32,0},{64,96},{96,64},{128,160},{160,128},{192,224},{224,1... | collective-permute-start | bytes 3538952 | tf_op jit(solution)/shard_map/ppermute | solution.py:256
  71.7 10.6 %collective-permute-start.9 = (bf16[1536,384]{1,0:T(8,128)(2,1)S(1)}, bf16[1536,384]{1,0:T(8,128)(2,1)S(1)}, u32[]{:S(2)}, u32[]{:S(2)}) collective-permute-start(bf16[1536,384]{1,0:T(8,128)(2,1)S(1)} %get-tuple-element.36), channel_id=1, source_target_pairs={{0,32},{32,0},{64,96},{96,64},{128,160},{160,128},{192,224},{224,1... | collective-permute-start | bytes 3538952 | tf_op jit(solution)/shard_map/ppermute | solution.py:256
  72.2 14.9 %collective-permute-start.8 = (bf16[2,16,8,1536]{3,2,1,0:T(8,128)(2,1)S(1)}, bf16[2,16,8,1536]{3,2,1,0:T(8,128)(2,1)S(1)}, u32[]{:S(2)}, u32[]{:S(2)}) collective-permute-start(bf16[2,16,8,1536]{3,2,1,0:T(8,128)(2,1)S(1)} %collective-permute-done.5.refs_4_), channel_id=1, source_target_pairs={{0,24},{8,0},{16,8},{24,16},{32,40},{40,48},{48,56},{56,32},{64,88... | collective-permute-start | bytes 2359304 | tf_op jit(solution)/shard_map/ppermute | solution.py:241
  79.1 10.2 %collective-permute-start.13 = (bf16[2,8,8,1536]{3,2,1,0:T(8,128)(2,1)S(1)}, bf16[2,8,8,1536]{3,2,1,0:T(8,128)(2,1)S(1)}, u32[]{:S(2)}, u32[]{:S(2)}) collective-permute-start(bf16[2,8,8,1536]{3,2,1,0:T(8,128)(2,1)S(1)} %slice_select_fusion), channel_id=1, source_target_pairs={{0,1},{1,2},{2,3},{3,4},{4,5},{5,6},{6,7},{7,0},{32,39},{33,32},{3... | collective-permute-start | bytes 1179656 | tf_op jit(solution)/shard_map/ppermute | solution.py:238
  81.9 16.6 %collective-permute-start.12 = (bf16[2,16,8,1536]{3,2,1,0:T(8,128)(2,1)S(1)}, bf16[2,16,8,1536]{3,2,1,0:T(8,128)(2,1)S(1)}, u32[]{:S(2)}, u32[]{:S(2)}) collective-permute-start(bf16[2,16,8,1536]{3,2,1,0:T(8,128)(2,1)S(1)} %collective-permute-done.11.refs_0_), channel_id=1, source_target_pairs={{0,24},{8,0},{16,8},{24,16},{32,40},{40,48},{48,56},{56,32},{64,88... | collective-permute-start | bytes 2359304 | tf_op jit(solution)/shard_map/ppermute | solution.py:241
  89.4 9.1 %collective-permute-start.14 = (bf16[2,8,8,1536]{3,2,1,0:T(8,128)(2,1)S(1)}, bf16[2,8,8,1536]{3,2,1,0:T(8,128)(2,1)S(1)}, u32[]{:S(2)}, u32[]{:S(2)}) collective-permute-start(bf16[2,8,8,1536]{3,2,1,0:T(8,128)(2,1)S(1)} %collective-permute-done.13.refs_2_), channel_id=1, source_target_pairs={{0,24},{8,0},{16,8},{24,16},{32,40},{40,48},{48,56},{56,32},{64,88... | collective-permute-start | bytes 1179656 | tf_op jit(solution)/shard_map/ppermute | solution.py:241
  89.5 5.4 %collective-permute-start.16 = (f32[160,384]{1,0:T(8,128)S(1)}, f32[160,384]{1,0:T(8,128)S(1)}, u32[]{:S(2)}, u32[]{:S(2)}) collective-permute-start(f32[160,384]{1,0:T(8,128)S(1)} %pad_maximum_fusion.6), channel_id=1, source_target_pairs={{0,192},{32,224},{64,0},{96,32},{128,64},{160,96},{192,128},{224,1... | collective-permute-start | bytes 737288 | tf_op jit(solution)/shard_map/ppermute | solution.py:183
  89.6 6.3 %collective-permute-start.15 = (f32[160,384]{1,0:T(8,128)S(1)}, f32[160,384]{1,0:T(8,128)S(1)}, u32[]{:S(2)}, u32[]{:S(2)}) collective-permute-start(f32[160,384]{1,0:T(8,128)S(1)} %pad_maximum_fusion.5), channel_id=1, source_target_pairs={{0,64},{32,96},{64,128},{96,160},{128,192},{160,224},{192,0},{224,... | collective-permute-start | bytes 737288 | tf_op jit(solution)/shard_map/ppermute | solution.py:182
  100.0 7.2 %collective-permute-start.17 = (f32[176,384]{1,0:T(8,128)S(1)}, f32[176,384]{1,0:T(8,128)S(1)}, u32[]{:S(2)}, u32[]{:S(2)}) collective-permute-start(f32[176,384]{1,0:T(8,128)S(1)} %pad_maximum_fusion.3), channel_id=1, source_target_pairs={{0,64},{32,96},{64,128},{96,160},{128,192},{160,224},{192,0},{224,... | collective-permute-start | bytes 811016 | tf_op jit(solution)/shard_map/ppermute | solution.py:286
  100.1 8.0 %collective-permute-start.18 = (f32[176,384]{1,0:T(8,128)S(1)}, f32[176,384]{1,0:T(8,128)S(1)}, u32[]{:S(2)}, u32[]{:S(2)}) collective-permute-start(f32[176,384]{1,0:T(8,128)S(1)} %pad_maximum_fusion.4), channel_id=1, source_target_pairs={{0,192},{32,224},{64,0},{96,32},{128,64},{160,96},{192,128},{224,1... | collective-permute-start | bytes 811016 | tf_op jit(solution)/shard_map/ppermute | solution.py:287
  102.9 9.1 %collective-permute-start.19 = (f32[96,384]{1,0:T(8,128)S(1)}, f32[96,384]{1,0:T(8,128)S(1)}, u32[]{:S(2)}, u32[]{:S(2)}) collective-permute-start(f32[96,384]{1,0:T(8,128)S(1)} %get-tuple-element.44), channel_id=1, source_target_pairs={{0,128},{32,160},{64,192},{96,224},{128,0},{160,32},{192,64},{224,... | collective-permute-start | bytes 442376 | tf_op jit(solution)/shard_map/ppermute | solution.py:285
  112.0 2.9 %collective-permute-start.20 = (f32[256,384]{1,0:T(8,128)S(1)}, f32[256,384]{1,0:T(8,128)S(1)}, u32[]{:S(2)}, u32[]{:S(2)}) collective-permute-start(f32[256,384]{1,0:T(8,128)S(1)} %pad_maximum_fusion.2.mine_ref), channel_id=1, source_target_pairs={{0,32},{32,0},{64,96},{96,64},{128,160},{160,128},{192,224},{224,1... | collective-permute-start | bytes 1179656 | tf_op jit(solution)/shard_map/ppermute | solution.py:296

commit v9 on v8

--- a/solution.py
+++ b/solution.py
@@ -54,81 +54,101 @@
     return (xl, t - n, n), (xr, 0, m), (x, k, None)
 
 
-def pack_amplitudes(groups, share, both_ref, src_ref, out_ref, held_ref, block_ref):
+def list_tiles(groups, share, shift, both_ref, out_ref, held_ref, block_ref):
     held, total, right, left = balance(both_ref, held_ref, block_ref, groups)
-    blocks = [block_ref[s] for s in range(groups)]
-    each = share // 2
+    blocks = [block_ref[s] << shift for s in range(groups)]
     for x in range(groups // 2):
-        place = 0
+        place = x * share
         for chip, start, count in runs_of(x, total, right, left, groups // 2):
             if count is None:
-                count = share - place
+                count = (x + 1) * share - place
             n0 = jnp.clip(held[2 * chip] - start, 0, count)
             second = jnp.maximum(start - held[2 * chip], 0)
-            for block, tile, many in ((blocks[2 * chip], start, n0), (blocks[2 * chip + 1], second, count - n0)):
-
-                def move(i, carry, block=block, tile=tile, place=place):
-                    data = src_ref[block, :, pl.ds(pl.multiple_of((tile + i) * TP, TP), TP)]
-                    upper = (place + i >= each).astype(jnp.int32)
-                    into = pl.ds(pl.multiple_of((place + i - upper * each) * TP, TP), TP)
-                    for j in range(2):
-                        out_ref[4 * x + 2 * upper + j, :, into] = data
+            for first, many in ((blocks[2 * chip] + start, n0), (blocks[2 * chip + 1] + second, count - n0)):
+
+                def note(i, carry, first=first, place=place):
+                    out_ref[place + i] = first + i
                     return carry
 
-                lax.fori_loop(0, many, move, 0)
+                lax.fori_loop(0, many, note, 0)
                 place = place + many
+
+
+def pack_amplitudes(groups, share, shift, list_ref, src_ref, out_ref, packed_ref, sems):
+    each = share // 2
+    copies = []
+    for x in range(groups // 2):
+        for p in range(share):
+            entry = list_ref[x * share + p]
+            tile = pl.multiple_of((entry & ((1 << shift) - 1)) * TP, TP)
+            data = src_ref[lax.shift_right_logical(entry, jnp.int32(shift)), :, pl.ds(tile, TP)]
+            at = p % each * TP
+            for j in range(2):
+                packed_ref[4 * x + p // each * 2 + j, :, at : at + TP] = data
+        part = pl.ds(4 * x, 4)
+        copies.append(pltpu.make_async_copy(packed_ref.at[part], out_ref.at[part], sems.at[x]))
+        copies[-1].start()
+    for copy in copies:
+        copy.wait()
 
 
 def tile_rows(index):
     return pl.ds(pl.multiple_of(index * TP, TP), TP)
 
 
-def run_copies(jobs, out_ref, sems):
+def run_copies(jobs, sems):
     for phase in range(2):
-        for source, tile, many, place in jobs:
-
-            def move(i, carry, source=source, tile=tile, place=place):
-                copy = pltpu.make_async_copy(source.at[tile_rows(tile + i)], out_ref.at[tile_rows(place + i)], sems.at[place + i])
+        for source, tile, many, out_ref, place, sem in jobs:
+
+            def move(i, carry, source=source, tile=tile, out_ref=out_ref, place=place, sem=sem):
+                copy = pltpu.make_async_copy(source.at[tile_rows(tile + i)], out_ref.at[tile_rows(place + i)], sems.at[sem + i])
                 copy.start() if phase == 0 else copy.wait()
                 return carry
 
             lax.fori_loop(0, many, move, 0)
 
 
-def own_tiles(border, core, start, count, mine_ref, other_ref, place):
+def own_tiles(border, core, start, count, mine_ref, other_ref, out_ref, place, sem):
     lower = jnp.clip(border - start, 0, count)
     jobs = []
-    for upper, tile, many, at in ((0, start, lower, place), (1, jnp.maximum(start - border, 0), count - lower, place + lower)):
-        jobs.append((mine_ref, tile, jnp.where(core == upper, many, 0), at))
-        jobs.append((other_ref, tile, jnp.where(core != upper, many, 0), at))
+    for upper, tile, many, at in ((0, start, lower, 0), (1, jnp.maximum(start - border, 0), count - lower, lower)):
+        jobs.append((mine_ref, tile, jnp.where(core == upper, many, 0), out_ref, place + at, sem + at))
+        jobs.append((other_ref, tile, jnp.where(core != upper, many, 0), out_ref, place + at, sem + at))
     return jobs
 
 
-def send_tiles(groups, share, both_ref, mine_ref, other_ref, out_ref, held_ref, block_ref, sems):
+def send_tiles(groups, share, both_ref, mine_ref, other_ref, *refs):
+    *out_refs, held_ref, block_ref, sems = refs
     held, total, right, left = balance(both_ref, held_ref, block_ref, groups)
     group = lax.axis_index("grp")
     x, core = lax.div(group, 2), lax.rem(group, 2)
     go_right, go_left = pick(right, x), pick(left, x)
     start = jnp.where(core == 0, pick(total, x) - go_right, 0)
     count = jnp.where(core == 0, go_right, go_left)
-    run_copies(own_tiles(pick(held[0::2], x), core, start, count, mine_ref, other_ref, 0), out_ref, sems)
-
-
-def join_tiles(groups, share, both_ref, mine_ref, other_ref, got_ref, *refs):
-    *their_refs, out_ref, held_ref, block_ref, sems = refs
+    each = share // len(out_refs)
+    jobs = []
+    for i, ref in enumerate(out_refs):
+        many = jnp.clip(count - i * each, 0, each)
+        jobs += own_tiles(pick(held[0::2], x), core, start + i * each, many, mine_ref, other_ref, ref, 0, i * each)
+    run_copies(jobs, sems)
+
+
+def join_tiles(groups, share, both_ref, mine_ref, other_ref, *refs):
+    *moved_refs, out_ref, held_ref, block_ref, sems = refs
     held, total, right, left = balance(both_ref, held_ref, block_ref, groups)
     group = lax.axis_index("grp")
     x, core = lax.div(group, 2), lax.rem(group, 2)
     (_, _, n), (_, _, m), (_, start, _) = runs_of(x, total, right, left, groups // 2)
-    jobs = [
-        (got_ref, 0, jnp.where(core == 0, n, 0), 0),
-        (got_ref, 0, jnp.where(core == 0, 0, m), n),
-    ]
-    each = share // len(their_refs)
-    for i, ref in enumerate(their_refs):
-        jobs.append((ref, 0, jnp.clip(jnp.where(core == 0, m, n) - i * each, 0, each), jnp.where(core == 0, n, 0) + i * each))
-    jobs += own_tiles(pick(held[0::2], x), core, start, share - n - m, mine_ref, other_ref, n + m)
-    run_copies(jobs, out_ref, sems)
+    halves = len(moved_refs) // 2
+    each = share // halves
+    jobs = []
+    for i, ref in enumerate(moved_refs):
+        h, below = i % halves, (core == 0) == (i < halves)
+        many = jnp.clip(jnp.where(below, n, m) - h * each, 0, each)
+        place = jnp.where(below, 0, n) + h * each
+        jobs.append((ref, 0, many, out_ref, place, place))
+    kept = own_tiles(pick(held[0::2], x), core, start, share - n - m, mine_ref, other_ref, out_ref, n + m, n + m)
+    run_copies(jobs + kept, sems)
 
 
 def multiply(ny, *refs):
@@ -208,28 +228,40 @@
     mine = integrals[0]
     other = lax.ppermute(mine, "grp", swap)
     moved = lax.all_to_all(amplitudes[0].reshape(groups, octet, cap), "grp", 0, 0, tiled=True)
+    shift = (cap // TP).bit_length()
+    little = pltpu.CompilerParams(vmem_limit_bytes=8 * 2**20)
+    listed = pl.pallas_call(
+        functools.partial(list_tiles, groups, share, shift),
+        out_shape=jax.ShapeDtypeStruct((groups // 2 * share,), jnp.int32),
+        in_specs=[SMEM],
+        out_specs=SMEM,
+        scratch_shapes=small,
+        compiler_params=little,
+    )(both)
+    packed = jax.ShapeDtypeStruct((2 * groups, octet, wide // 2), jnp.bfloat16)
     packed = pl.pallas_call(
-        functools.partial(pack_amplitudes, groups, share),
-        out_shape=jax.ShapeDtypeStruct((2 * groups, octet, wide // 2), jnp.bfloat16),
+        functools.partial(pack_amplitudes, groups, share, shift),
+        out_shape=packed,
         in_specs=[SMEM, VMEM],
-        out_specs=VMEM,
-        scratch_shapes=small,
-        compiler_params=pltpu.CompilerParams(vmem_limit_bytes=8 * 2**20),
-    )(both, moved)
+        out_specs=pl.BlockSpec(memory_space=pltpu.HBM),
+        scratch_shapes=[pltpu.VMEM(packed.shape, packed.dtype), pltpu.SemaphoreType.DMA((groups // 2,))],
+        compiler_params=little,
+    )(listed, moved)
     pair = lax.all_to_all(packed, ("grp", "row"), 0, 0, axis_index_groups=pairs, tiled=True)
 
     tiles = jax.ShapeDtypeStruct((wide, cols), jnp.bfloat16)
+    half_tiles = jax.ShapeDtypeStruct((wide // 2, cols), jnp.bfloat16)
     scratch = small + [pltpu.SemaphoreType.DMA((share,))]
     sent = pl.pallas_call(
         functools.partial(send_tiles, groups, share),
-        out_shape=tiles,
+        out_shape=(half_tiles, half_tiles),
         in_specs=[SMEM, ANY, ANY],
-        out_specs=VMEM,
+        out_specs=(VMEM, VMEM),
         scratch_shapes=scratch,
         compiler_params=limit,
     )(both, mine, other)
-    pair, sent = barrier((pair, sent))
-    got = lax.ppermute(sent, "grp", apart)
+    pair, *sent = barrier((pair, *sent))
+    got = [lax.ppermute(part, "grp", apart) for part in sent]
     def half_of(block):
         h = block.shape[1] // 2
         return jnp.where(core == 0, block[:, :h], block[:, h:])
@@ -244,6 +276,7 @@
     block = half_of(jnp.stack([pair, pair_too]))
     order = [block]
     block, near = barrier((jnp.stack([z_step(pair), z_step(pair_too)]), y_step(block)))
+    block, got[0] = barrier((block, got[0]))
     order += [near]
     for s in range(1, nz // 2 - 1):
         order += [block]
@@ -251,20 +284,20 @@
         if s < nz // 2 - 2:
             block, near = barrier((block, near))
         if s == nz // 2 - 3:
-            block, near, got = barrier((block, near, got))
+            block, near, got[1] = barrier((block, near, got[1]))
         order += [near]
-    theirs = [lax.ppermute(part, "grp", swap) for part in jnp.split(got, 2)]
+    theirs = [lax.ppermute(part, "grp", swap) for part in got]
     end = z_step(half_of(block))
-    order += [block, y_step(block), end, y_step(end)]
+    order += [block, y_step(block)]
 
     held = pl.pallas_call(
         functools.partial(join_tiles, groups, share),
         out_shape=tiles,
-        in_specs=[SMEM] + [ANY] * (3 + len(theirs)),
+        in_specs=[SMEM] + [ANY] * (2 + len(got) + len(theirs)),
         out_specs=VMEM,
         scratch_shapes=scratch,
         compiler_params=limit,
-    )(both, mine, other, got, *theirs)
+    )(both, mine, other, *got, *theirs)
 
     def sums(parts):
         n = sum(part.shape[1] for part in parts) * octet
@@ -277,7 +310,9 @@
             compiler_params=limit,
         )(*parts, held)
 
-    early, late = sums(order[:6]), order[6:]
+    early = sums(order[:6])
+    end, early = barrier((end, early))
+    late = order[6:] + [end, y_step(end)]
     a, b = near_chips(early, up, down)
     *late, a, b = barrier((*late, a, b))
     late = sums(late)

time: 116 us -> 116 us (level)
  waiting for transfers between devices: 56.8 us -> 58.3 us
  local copies, waits for them, and re-layouts: 6.1 us -> 4.87 us
    ppermute x3 -> x4, starting transfers between devices: 1.02 us -> 3.48 us  [the longest x2 2.97 us: body(): got = [lax.ppermute(part, 'grp', apart) for part in sent]]
    split x1 -> x0, local copies, waits for them, and re-layouts: 1.86 us -> none  [body(): theirs = [lax.ppermute(part, 'grp', swap) for part in jnp.split(got, 2)]]
    ppermute x1, starting transfers between devices: 0.08 us -> 1.37 us  [near_chips(): return (a, lax.ppermute(jnp.concatenate([p[2, h:], p[3, :h]]), 'grp', down))]
    ppermute x1, starting transfers between devices: 1.52 us -> 0.25 us  [near_chips(): a = lax.ppermute(jnp.concatenate([p[2, :h], p[1, h:]]), 'grp', up)]
    ppermute x1, waiting for transfers between devices: 1.03 us -> 2.3 us  [near_chips(): a = lax.ppermute(jnp.concatenate([p[2, :h], p[1, h:]]), 'grp', up)]
    all_to_all x1, waiting for transfers between devices: 9.55 us -> 8.32 us  [body(): lax.all_to_all(amplitudes[0].reshape(groups, octet, cap), 'grp', 0, 0, ti...]
    ppermute x5, starting transfers between devices: 14.3 us -> 13.1 us  [z_step(): return lax.ppermute(block, ('grp', 'col'), along)]
    unnamed x8 -> x14, local copies, waits for them, and re-layouts: 4.15 us -> 4.78 us
  transfers between devices with their start and end apart: 23 -> 24, of which waited for: 15 -> 14; matrix products, arithmetic and copies ran while one was open for 5% -> 2% of each run, Pallas kernels for 10% -> 10%
where the time goes in v9:
time: 116 us
  waiting for transfers between devices  58.3 us (50%)
  starting transfers between devices  36.2 us (31%)
  Pallas kernels  13.5 us (12%)
  local copies, waits for them, and re-layouts  4.87 us (4%)
  other arithmetic  2.91 us (3%)
    ppermute x5, waiting for transfers between devices, z_step(): return lax.ppermute(block, ('grp', 'col'), along)  21.2 us
    ppermute x5, starting transfers between devices, z_step(): return lax.ppermute(block, ('grp', 'col'), along)  13.1 us
    all_to_all x1, waiting for transfers between devices, body(): lax.all_to_all(amplitudes[0].reshape(groups, octet, cap), 'grp', 0, 0, ti...  8.32 us
    ppermute x5, waiting for transfers between devices, y_step(): return lax.ppermute(block, ('grp', 'row'), beside)  6.85 us
    all_to_all x1, waiting for transfers between devices, body(): lax.all_to_all(packed, ('grp', 'row'), 0, 0, axis_index_groups=pairs, til...  5.87 us
    all_to_all x1, starting transfers between devices, body(): lax.all_to_all(packed, ('grp', 'row'), 0, 0, axis_index_groups=pairs, til...  4.83 us
    unnamed x14, local copies, waits for them, and re-layouts  4.78 us
    ppermute x1, waiting for transfers between devices, body(): lax.ppermute(jnp.concatenate([late[1], early[1, :h] + a[:h]]), 'grp', up)  4.72 us
  transfers between devices with their start and end apart: 24, of which 14 were waited for; matrix products, arithmetic and copies ran while one was open for 2% of the time, Pallas kernels for 10%

profile of v9, /device:TPU:1, one launch (start us, length us, event | category | flops | bytes accessed | tf_op | source)
XLA Modules:
  0.0 116.0 jit_solution(10710366868900941192)
XLA Ops:
  0.0 3.2 %collective-permute-start = (bf16[4608,384]{1,0:T(8,128)(2,1)}, bf16[4608,384]{1,0:T(8,128)(2,1)S(1)}, u32[]{:S(2)}, u32[]{:S(2)}) collective-permute-start(bf16[4608,384]{1,0:T(8,128)(2,1)} %bitcast.32), channel_id=1, source_target_pairs={{0,32},{32,0},{64,96},{96,64},{128,160},{160,128},{192,224},{224,1... | collective-permute-start | bytes 10616840 | tf_op jit(solution)/shard_map/ppermute | solution.py:229
  3.2 4.2 %all-to-all-start = ((bf16[8,8,4608]{2,1,0:T(8,128)(2,1)}), bf16[8,8,4608]{2,1,0:T(8,128)(2,1)}, u32[]{:S(2)}, u32[]{:S(2)}) async-start(bf16[8,8,4608]{2,1,0:T(8,128)(2,1)} %bitcast.35), calls=%async_computation | async-start | bytes 1179648 | tf_op jit(solution)/shard_map/all_to_all | solution.py:230
  7.5 2.0 %shard_map.46.list_ref = s32[96]{0:T(128)S(1)} custom-call(s32[2,8]{1,0:T(2,128)S(1)} %pad_add_fusion.both_ref), custom_call_target="tpu_custom_call" | custom-call | tf_op jit(solution)/shard_map/pallas_call | solution.py:233
  9.5 8.3 %all-to-all-done.src_ref = bf16[8,8,4608]{2,1,0:T(8,128)(2,1)} async-done(((bf16[8,8,4608]{2,1,0:T(8,128)(2,1)}), bf16[8,8,4608]{2,1,0:T(8,128)(2,1)}, u32[]{:S(2)}, u32[]{:S(2)}) %all-to-all-start) | async-done | bytes 589856 | tf_op jit(solution)/shard_map/all_to_all | solution.py:230
  17.8 1.9 %shard_map.47 = bf16[16,8,1536]{2,1,0:T(8,128)(2,1)S(1)} custom-call(s32[96]{0:T(128)S(1)} %shard_map.46.list_ref, bf16[8,8,4608]{2,1,0:T(8,128)(2,1)} %all-to-all-done.src_ref), custom_call_target="tpu_custom_call" | custom-call | tf_op jit(solution)/shard_map/pallas_call | solution.py:242
  19.6 0.0 copy-start.2
  19.6 0.7 copy-done.2
  20.4 4.8 %all-to-all-start.1 = ((bf16[16,8,1536]{2,1,0:T(8,128)(2,1)}), bf16[16,8,1536]{2,1,0:T(8,128)(2,1)}, u32[]{:S(2)}, u32[]{:S(2)}) async-start(bf16[16,8,1536]{2,1,0:T(8,128)(2,1)} %copy-done.2), calls=%async_computation.1 | async-start | bytes 786432 | tf_op jit(solution)/shard_map/all_to_all | solution.py:250
  25.2 0.0 collective-permute-done.other_ref
  25.2 0.0 copy-start
  25.2 2.0 %copy-done = bf16[1,4608,384]{2,1,0:T(8,128)(2,1)S(1)} copy-done((bf16[1,4608,384]{2,1,0:T(8,128)(2,1)S(1)}, bf16[1,4608,384]{2,1,0:T(8,128)(2,1)}, u32[]{:S(2)}) %copy-start) | copy-done | bytes 3538968
  27.2 0.9 shard_map.48
  28.1 1.0 copy-done.3
  29.2 1.0 copy-done.4
  30.2 5.9 %all-to-all-done.1 = bf16[16,8,1536]{2,1,0:T(8,128)(2,1)} async-done(((bf16[16,8,1536]{2,1,0:T(8,128)(2,1)}), bf16[16,8,1536]{2,1,0:T(8,128)(2,1)}, u32[]{:S(2)}, u32[]{:S(2)}) %all-to-all-start.1) | async-done | bytes 393248 | tf_op jit(solution)/shard_map/all_to_all | solution.py:250
  36.1 0.4 collective-permute-start.5
  36.5 0.0 collective-permute-start.2
  36.5 5.2 %collective-permute-start.1 = (bf16[16,8,1536]{2,1,0:T(8,128)(2,1)}, bf16[16,8,1536]{2,1,0:T(8,128)(2,1)}, u32[]{:S(2)}, u32[]{:S(2)}) collective-permute-start(bf16[16,8,1536]{2,1,0:T(8,128)(2,1)} %all-to-all-done.1), channel_id=1, source_target_pairs={{0,1},{1,2},{2,3},{3,4},{4,5},{5,6},{6,7},{7,0},{32,39},{33,32},{3... | collective-permute-start | bytes 1179656 | tf_op jit(solution)/shard_map/ppermute | solution.py:270
  41.7 0.0 collective-permute-done.2
  41.7 2.1 %collective-permute-start.3 = (bf16[16,8,1536]{2,1,0:T(8,128)(2,1)}, bf16[16,8,1536]{2,1,0:T(8,128)(2,1)}, u32[]{:S(2)}, u32[]{:S(2)}) collective-permute-start(bf16[16,8,1536]{2,1,0:T(8,128)(2,1)} %collective-permute-done.2), channel_id=1, source_target_pairs={{0,1},{1,2},{2,3},{3,4},{4,5},{5,6},{6,7},{7,0},{32,39},{33,32},{3... | collective-permute-start | bytes 1179656 | tf_op jit(solution)/shard_map/ppermute | solution.py:270
  43.7 1.4 %fusion.1.refs_0_ = bf16[2,8,8,1536]{3,2,1,0:T(8,128)(2,1)S(1)} fusion(bf16[1,16,8,1536]{3,2,1,0:T(8,128)(2,1)} %bitcast.6, bf16[1,16,8,1536]{3,2,1,0:T(8,128)(2,1)} %bitcast.7, pred[]{:T(512)S(6)} %eq.4), kind=kLoop, calls=%fused_computation.4 | loop fusion | flops 589824 | bytes 1179649 | tf_op jit(solution)/shard_map/jit(_where)/select_n | solution.py:267
  45.2 0.5 collective-permute-start.4
  45.7 2.5 %collective-permute-start.8 = (bf16[1536,384]{1,0:T(8,128)(2,1)}, bf16[1536,384]{1,0:T(8,128)(2,1)S(1)}, u32[]{:S(2)}, u32[]{:S(2)}) collective-permute-start(bf16[1536,384]{1,0:T(8,128)(2,1)} %copy-done.3), channel_id=1, source_target_pairs={{0,64},{32,224},{64,128},{96,32},{128,192},{160,96},{192,0},{224,1... | collective-permute-start | bytes 3538952 | tf_op jit(solution)/shard_map/ppermute | solution.py:264
  48.2 0.0 collective-permute-done.1
  48.2 2.7 %collective-permute-done.3 = bf16[16,8,1536]{2,1,0:T(8,128)(2,1)} collective-permute-done((bf16[16,8,1536]{2,1,0:T(8,128)(2,1)}, bf16[16,8,1536]{2,1,0:T(8,128)(2,1)}, u32[]{:S(2)}, u32[]{:S(2)}) %collective-permute-start.3) | collective-permute-done | bytes 393248 | tf_op jit(solution)/shard_map/ppermute | solution.py:270
  50.9 1.2 %pad_maximum_fusion.refs_2_ = bf16[2,16,8,1536]{3,2,1,0:T(8,128)(2,1)S(1)} fusion(bf16[1,16,8,1536]{3,2,1,0:T(8,128)(2,1)} %bitcast.5, bf16[1,16,8,1536]{3,2,1,0:T(8,128)(2,1)} %bitcast.4), kind=kLoop, calls=%fused_computation | loop fusion | flops 393216 | bytes 1572864 | tf_op jit(solution)/shard_map/stack | solution.py:278
  52.1 1.4 %collective-permute-done.4.refs_1_ = bf16[2,8,8,1536]{3,2,1,0:T(8,128)(2,1)S(1)} collective-permute-done((bf16[2,8,8,1536]{3,2,1,0:T(8,128)(2,1)S(1)}, bf16[2,8,8,1536]{3,2,1,0:T(8,128)(2,1)S(1)}, u32[]{:S(2)}, u32[]{:S(2)}) %collective-permute-start.4) | collective-permute-done | bytes 393248 | tf_op jit(solution)/shard_map/ppermute | solution.py:273
  53.5 0.0 collective-permute-done.5.refs_0_
  53.5 3.4 %collective-permute-start.6 = (bf16[2,16,8,1536]{3,2,1,0:T(8,128)(2,1)S(1)}, bf16[2,16,8,1536]{3,2,1,0:T(8,128)(2,1)S(1)}, u32[]{:S(2)}, u32[]{:S(2)}) collective-permute-start(bf16[2,16,8,1536]{3,2,1,0:T(8,128)(2,1)S(1)} %pad_maximum_fusion.refs_2_), channel_id=1, source_target_pairs={{0,1},{1,2},{2,3},{3,4},{4,5},{5,6},{6,7},{7,0},{32,39},{33,32},{3... | collective-permute-start | bytes 2359304 | tf_op jit(solution)/shard_map/ppermute | solution.py:270
  56.9 0.4 collective-permute-start.7
  57.3 8.5 %collective-permute-done.6.refs_4_ = bf16[2,16,8,1536]{3,2,1,0:T(8,128)(2,1)S(1)} collective-permute-done((bf16[2,16,8,1536]{3,2,1,0:T(8,128)(2,1)S(1)}, bf16[2,16,8,1536]{3,2,1,0:T(8,128)(2,1)S(1)}, u32[]{:S(2)}, u32[]{:S(2)}) %collective-permute-start.6) | collective-permute-done | bytes 786464 | tf_op jit(solution)/shard_map/ppermute | solution.py:270
  65.8 3.4 %collective-permute-done.7.refs_3_ = bf16[2,16,8,1536]{3,2,1,0:T(8,128)(2,1)S(1)} collective-permute-done((bf16[2,16,8,1536]{3,2,1,0:T(8,128)(2,1)S(1)}, bf16[2,16,8,1536]{3,2,1,0:T(8,128)(2,1)S(1)}, u32[]{:S(2)}, u32[]{:S(2)}) %collective-permute-start.7) | collective-permute-done | bytes 786464 | tf_op jit(solution)/shard_map/ppermute | solution.py:273
  69.2 0.0 collective-permute-done.8.refs_1_
  69.2 0.7 collective-permute-start.9
  70.0 0.0 collective-permute-start.12
  70.0 0.5 collective-permute-start.13
  70.5 0.0 collective-permute-start.11
  70.5 9.9 %collective-permute-done.9.refs_0_ = bf16[2,16,8,1536]{3,2,1,0:T(8,128)(2,1)S(1)} collective-permute-done((bf16[2,16,8,1536]{3,2,1,0:T(8,128)(2,1)S(1)}, bf16[2,16,8,1536]{3,2,1,0:T(8,128)(2,1)S(1)}, u32[]{:S(2)}, u32[]{:S(2)}) %collective-permute-start.9) | collective-permute-done | bytes 786464 | tf_op jit(solution)/shard_map/ppermute | solution.py:270
  80.4 1.7 %collective-permute-start.10 = (bf16[2,8,8,1536]{3,2,1,0:T(8,128)(2,1)S(1)}, bf16[2,8,8,1536]{3,2,1,0:T(8,128)(2,1)S(1)}, u32[]{:S(2)}, u32[]{:S(2)}) collective-permute-start(bf16[2,8,8,1536]{3,2,1,0:T(8,128)(2,1)S(1)} %slice_select_fusion), channel_id=1, source_target_pairs={{0,1},{1,2},{2,3},{3,4},{4,5},{5,6},{6,7},{7,0},{32,39},{33,32},{3... | collective-permute-start | bytes 1179656 | tf_op jit(solution)/shard_map/ppermute | solution.py:270
  82.1 0.0 collective-permute-start.14
  82.1 0.0 collective-permute-done.12.refs_2_
  82.1 0.0 collective-permute-done.13.refs_3_
  82.1 4.4 %shard_map.49.refs_6_.refs_4_ = bf16[3072,384]{1,0:T(8,128)(2,1)S(1)} custom-call(s32[2,8]{1,0:T(2,128)S(1)} %pad_add_fusion.both_ref, bf16[4608,384]{1,0:T(8,128)(2,1)S(1)} %bitcast.34, bf16[4608,384]{1,0:T(8,128)(2,1)S(1)} %collective-permute-done.other_ref, bf16[1536,384]{1,0:T(8,128)(2,1)} %collective-permute-done.5.refs_0_, ...), custom_call_target="tpu_custom_call" | custom-call | tf_op jit(solution)/shard_map/pallas_call | solution.py:293
  86.5 0.0 collective-permute-done.11.refs_5_
  86.5 2.2 %shard_map.50 = f32[4,160,384]{2,1,0:T(8,128)S(1)} custom-call(bf16[2,8,8,1536]{3,2,1,0:T(8,128)(2,1)S(1)} %fusion.1.refs_0_, bf16[2,8,8,1536]{3,2,1,0:T(8,128)(2,1)S(1)} %collective-permute-done.4.refs_1_, bf16[2,16,8,1536]{3,2,1,0:T(8,128)(2,1)S(1)} %pad_maximum_fusion.refs_2_, bf16[2,16,8,1536]{3,2,1,0:T(8,128)(2,1)S(1)} %collective-permute-done.7.refs_3_, ...), custom_call_target="tpu_custom_call" | custom-call | tf_op jit(solution)/shard_map/pallas_call | solution.py:304
  88.7 0.0 collective-permute-done.10.refs_2_
  88.7 0.1 collective-permute-start.15
  88.9 1.4 %collective-permute-start.17 = (f32[160,384]{1,0:T(8,128)S(1)}, f32[160,384]{1,0:T(8,128)S(1)}, u32[]{:S(2)}, u32[]{:S(2)}) collective-permute-start(f32[160,384]{1,0:T(8,128)S(1)} %pad_maximum_fusion.6), channel_id=1, source_target_pairs={{0,192},{32,224},{64,0},{96,32},{128,64},{160,96},{192,128},{224,1... | collective-permute-start | bytes 737288 | tf_op jit(solution)/shard_map/ppermute | solution.py:203
  90.3 0.3 collective-permute-start.16
  90.5 3.8 %collective-permute-done.17 = f32[160,384]{1,0:T(8,128)S(1)} collective-permute-done((f32[160,384]{1,0:T(8,128)S(1)}, f32[160,384]{1,0:T(8,128)S(1)}, u32[]{:S(2)}, u32[]{:S(2)}) %collective-permute-start.17) | collective-permute-done | bytes 245792 | tf_op jit(solution)/shard_map/ppermute | solution.py:203
  94.3 2.3 %collective-permute-done.16 = f32[160,384]{1,0:T(8,128)S(1)} collective-permute-done((f32[160,384]{1,0:T(8,128)S(1)}, f32[160,384]{1,0:T(8,128)S(1)}, u32[]{:S(2)}, u32[]{:S(2)}) %collective-permute-start.16) | collective-permute-done | bytes 245792 | tf_op jit(solution)/shard_map/ppermute | solution.py:202
  96.6 2.1 %collective-permute-done.15.refs_3_ = bf16[2,8,8,1536]{3,2,1,0:T(8,128)(2,1)S(1)} collective-permute-done((bf16[2,8,8,1536]{3,2,1,0:T(8,128)(2,1)S(1)}, bf16[2,8,8,1536]{3,2,1,0:T(8,128)(2,1)S(1)}, u32[]{:S(2)}, u32[]{:S(2)}) %collective-permute-start.15) | collective-permute-done | bytes 393248 | tf_op jit(solution)/shard_map/ppermute | solution.py:273
  98.7 0.0 collective-permute-done.14.refs_1_
  98.7 1.4 %shard_map.51 = f32[4,96,384]{2,1,0:T(8,128)S(1)} custom-call(bf16[2,16,8,1536]{3,2,1,0:T(8,128)(2,1)S(1)} %collective-permute-done.9.refs_0_, bf16[2,16,8,1536]{3,2,1,0:T(8,128)(2,1)S(1)} %collective-permute-done.14.refs_1_, bf16[2,8,8,1536]{3,2,1,0:T(8,128)(2,1)S(1)} %collective-permute-done.10.refs_2_, ...), custom_call_target="tpu_custom_call" | custom-call | tf_op jit(solution)/shard_map/pallas_call | solution.py:304
  100.2 0.1 collective-permute-start.18
  100.3 2.7 %collective-permute-start.19 = (f32[176,384]{1,0:T(8,128)S(1)}, f32[176,384]{1,0:T(8,128)S(1)}, u32[]{:S(2)}, u32[]{:S(2)}) collective-permute-start(f32[176,384]{1,0:T(8,128)S(1)} %pad_maximum_fusion.4), channel_id=1, source_target_pairs={{0,192},{32,224},{64,0},{96,32},{128,64},{160,96},{192,128},{224,1... | collective-permute-start | bytes 811016 | tf_op jit(solution)/shard_map/ppermute | solution.py:322
  103.0 0.0 collective-permute-start.20
  103.0 4.7 %collective-permute-done.18 = f32[176,384]{1,0:T(8,128)S(1)} collective-permute-done((f32[176,384]{1,0:T(8,128)S(1)}, f32[176,384]{1,0:T(8,128)S(1)}, u32[]{:S(2)}, u32[]{:S(2)}) %collective-permute-start.18) | collective-permute-done | bytes 270368 | tf_op jit(solution)/shard_map/ppermute | solution.py:321
  107.8 0.9 collective-permute-done.19
  108.7 0.1 fusion.2
  108.7 3.0 %collective-permute-done.20 = f32[96,384]{1,0:T(8,128)S(1)} collective-permute-done((f32[96,384]{1,0:T(8,128)S(1)}, f32[96,384]{1,0:T(8,128)S(1)}, u32[]{:S(2)}, u32[]{:S(2)}) %collective-permute-start.20) | collective-permute-done | bytes 147488 | tf_op jit(solution)/shard_map/ppermute | solution.py:320
  111.8 2.0 %collective-permute-start.21 = (f32[256,384]{1,0:T(8,128)S(1)}, f32[256,384]{1,0:T(8,128)S(1)}, u32[]{:S(2)}, u32[]{:S(2)}) collective-permute-start(f32[256,384]{1,0:T(8,128)S(1)} %pad_maximum_fusion.2.mine_ref), channel_id=1, source_target_pairs={{0,32},{32,0},{64,96},{96,64},{128,160},{160,128},{192,224},{224,1... | collective-permute-start | bytes 1179656 | tf_op jit(solution)/shard_map/ppermute | solution.py:331
  113.8 1.3 %collective-permute-done.21.other_ref = f32[256,384]{1,0:T(8,128)S(1)} collective-permute-done((f32[256,384]{1,0:T(8,128)S(1)}, f32[256,384]{1,0:T(8,128)S(1)}, u32[]{:S(2)}, u32[]{:S(2)}) %collective-permute-start.21) | collective-permute-done | bytes 393248 | tf_op jit(solution)/shard_map/ppermute | solution.py:331
  115.2 0.8 shard_map.52
  (21 shorter events, 0.3 us)
Async XLA Ops:
  0.0 7.5 %copy-start.6 = (s32[8]{0:T(128)S(1)}, s32[8]{0:T(128)}, u32[]{:S(2)}) copy-start(s32[8]{0:T(128)} %param.6) | copy-start | bytes 100
  0.0 7.5 %copy-start.5 = (s32[8]{0:T(128)S(1)}, s32[8]{0:T(128)}, u32[]{:S(2)}) copy-start(s32[8]{0:T(128)} %param.7) | copy-start | bytes 100
  0.0 25.2 %collective-permute-start = (bf16[4608,384]{1,0:T(8,128)(2,1)}, bf16[4608,384]{1,0:T(8,128)(2,1)S(1)}, u32[]{:S(2)}, u32[]{:S(2)}) collective-permute-start(bf16[4608,384]{1,0:T(8,128)(2,1)} %bitcast.32), channel_id=1, source_target_pairs={{0,32},{32,0},{64,96},{96,64},{128,160},{160,128},{192,224},{224,1... | collective-permute-start | bytes 10616840 | tf_op jit(solution)/shard_map/ppermute | solution.py:229
  3.2 14.5 %all-to-all-start = ((bf16[8,8,4608]{2,1,0:T(8,128)(2,1)}), bf16[8,8,4608]{2,1,0:T(8,128)(2,1)}, u32[]{:S(2)}, u32[]{:S(2)}) async-start(bf16[8,8,4608]{2,1,0:T(8,128)(2,1)} %bitcast.35), calls=%async_computation | async-start | bytes 1179648 | tf_op jit(solution)/shard_map/all_to_all | solution.py:230
  19.6 0.7 copy-start.2
  20.4 15.7 %all-to-all-start.1 = ((bf16[16,8,1536]{2,1,0:T(8,128)(2,1)}), bf16[16,8,1536]{2,1,0:T(8,128)(2,1)}, u32[]{:S(2)}, u32[]{:S(2)}) async-start(bf16[16,8,1536]{2,1,0:T(8,128)(2,1)} %copy-done.2), calls=%async_computation.1 | async-start | bytes 786432 | tf_op jit(solution)/shard_map/all_to_all | solution.py:250
  25.2 2.0 %copy-start = (bf16[1,4608,384]{2,1,0:T(8,128)(2,1)S(1)}, bf16[1,4608,384]{2,1,0:T(8,128)(2,1)}, u32[]{:S(2)}) copy-start(bf16[1,4608,384]{2,1,0:T(8,128)(2,1)} %param.5) | copy-start | bytes 10616836
  28.1 1.0 copy-start.3
  29.2 1.0 copy-start.4
  36.1 17.4 %collective-permute-start.5 = (bf16[1536,384]{1,0:T(8,128)(2,1)}, bf16[1536,384]{1,0:T(8,128)(2,1)}, u32[]{:S(2)}, u32[]{:S(2)}) collective-permute-start(bf16[1536,384]{1,0:T(8,128)(2,1)} %copy-done.4), channel_id=1, source_target_pairs={{0,64},{32,224},{64,128},{96,32},{128,192},{160,96},{192,0},{224,1... | collective-permute-start | bytes 3538952 | tf_op jit(solution)/shard_map/ppermute | solution.py:264
  36.5 5.2 %collective-permute-start.2 = (bf16[16,8,1536]{2,1,0:T(8,128)(2,1)}, bf16[16,8,1536]{2,1,0:T(8,128)(2,1)}, u32[]{:S(2)}, u32[]{:S(2)}) collective-permute-start(bf16[16,8,1536]{2,1,0:T(8,128)(2,1)} %all-to-all-done.1), channel_id=1, source_target_pairs={{0,32},{32,0},{64,96},{96,64},{128,160},{160,128},{192,224},{224,1... | collective-permute-start | bytes 1179656 | tf_op jit(solution)/shard_map/ppermute | solution.py:275
  36.5 11.7 %collective-permute-start.1 = (bf16[16,8,1536]{2,1,0:T(8,128)(2,1)}, bf16[16,8,1536]{2,1,0:T(8,128)(2,1)}, u32[]{:S(2)}, u32[]{:S(2)}) collective-permute-start(bf16[16,8,1536]{2,1,0:T(8,128)(2,1)} %all-to-all-done.1), channel_id=1, source_target_pairs={{0,1},{1,2},{2,3},{3,4},{4,5},{5,6},{6,7},{7,0},{32,39},{33,32},{3... | collective-permute-start | bytes 1179656 | tf_op jit(solution)/shard_map/ppermute | solution.py:270
  41.7 9.2 %collective-permute-start.3 = (bf16[16,8,1536]{2,1,0:T(8,128)(2,1)}, bf16[16,8,1536]{2,1,0:T(8,128)(2,1)}, u32[]{:S(2)}, u32[]{:S(2)}) collective-permute-start(bf16[16,8,1536]{2,1,0:T(8,128)(2,1)} %collective-permute-done.2), channel_id=1, source_target_pairs={{0,1},{1,2},{2,3},{3,4},{4,5},{5,6},{6,7},{7,0},{32,39},{33,32},{3... | collective-permute-start | bytes 1179656 | tf_op jit(solution)/shard_map/ppermute | solution.py:270
  43.7 38.4 %copy-start.1 = (bf16[1,4608,384]{2,1,0:T(8,128)(2,1)S(1)}, bf16[1,4608,384]{2,1,0:T(8,128)(2,1)}, u32[]{:S(2)}) copy-start(bf16[1,4608,384]{2,1,0:T(8,128)(2,1)} %param.5) | copy-start | bytes 10616836
  45.2 8.3 %collective-permute-start.4 = (bf16[2,8,8,1536]{3,2,1,0:T(8,128)(2,1)S(1)}, bf16[2,8,8,1536]{3,2,1,0:T(8,128)(2,1)S(1)}, u32[]{:S(2)}, u32[]{:S(2)}) collective-permute-start(bf16[2,8,8,1536]{3,2,1,0:T(8,128)(2,1)S(1)} %fusion.1.refs_0_), channel_id=1, source_target_pairs={{0,24},{8,0},{16,8},{24,16},{32,40},{40,48},{48,56},{56,32},{64,88... | collective-permute-start | bytes 1179656 | tf_op jit(solution)/shard_map/ppermute | solution.py:273
  45.7 23.6 %collective-permute-start.8 = (bf16[1536,384]{1,0:T(8,128)(2,1)}, bf16[1536,384]{1,0:T(8,128)(2,1)S(1)}, u32[]{:S(2)}, u32[]{:S(2)}) collective-permute-start(bf16[1536,384]{1,0:T(8,128)(2,1)} %copy-done.3), channel_id=1, source_target_pairs={{0,64},{32,224},{64,128},{96,32},{128,192},{160,96},{192,0},{224,1... | collective-permute-start | bytes 3538952 | tf_op jit(solution)/shard_map/ppermute | solution.py:264
  53.5 12.3 %collective-permute-start.6 = (bf16[2,16,8,1536]{3,2,1,0:T(8,128)(2,1)S(1)}, bf16[2,16,8,1536]{3,2,1,0:T(8,128)(2,1)S(1)}, u32[]{:S(2)}, u32[]{:S(2)}) collective-permute-start(bf16[2,16,8,1536]{3,2,1,0:T(8,128)(2,1)S(1)} %pad_maximum_fusion.refs_2_), channel_id=1, source_target_pairs={{0,1},{1,2},{2,3},{3,4},{4,5},{5,6},{6,7},{7,0},{32,39},{33,32},{3... | collective-permute-start | bytes 2359304 | tf_op jit(solution)/shard_map/ppermute | solution.py:270
  56.9 12.3 %collective-permute-start.7 = (bf16[2,16,8,1536]{3,2,1,0:T(8,128)(2,1)S(1)}, bf16[2,16,8,1536]{3,2,1,0:T(8,128)(2,1)S(1)}, u32[]{:S(2)}, u32[]{:S(2)}) collective-permute-start(bf16[2,16,8,1536]{3,2,1,0:T(8,128)(2,1)S(1)} %pad_maximum_fusion.refs_2_), channel_id=1, source_target_pairs={{0,24},{8,0},{16,8},{24,16},{32,40},{40,48},{48,56},{56,32},{64,88... | collective-permute-start | bytes 2359304 | tf_op jit(solution)/shard_map/ppermute | solution.py:273
  69.2 11.1 %collective-permute-start.9 = (bf16[2,16,8,1536]{3,2,1,0:T(8,128)(2,1)S(1)}, bf16[2,16,8,1536]{3,2,1,0:T(8,128)(2,1)S(1)}, u32[]{:S(2)}, u32[]{:S(2)}) collective-permute-start(bf16[2,16,8,1536]{3,2,1,0:T(8,128)(2,1)S(1)} %collective-permute-done.6.refs_4_), channel_id=1, source_target_pairs={{0,1},{1,2},{2,3},{3,4},{4,5},{5,6},{6,7},{7,0},{32,39},{33,32},{3... | collective-permute-start | bytes 2359304 | tf_op jit(solution)/shard_map/ppermute | solution.py:270
  70.0 12.2 %collective-permute-start.12 = (bf16[1536,384]{1,0:T(8,128)(2,1)}, bf16[1536,384]{1,0:T(8,128)(2,1)S(1)}, u32[]{:S(2)}, u32[]{:S(2)}) collective-permute-start(bf16[1536,384]{1,0:T(8,128)(2,1)} %collective-permute-done.5.refs_0_), channel_id=1, source_target_pairs={{0,32},{32,0},{64,96},{96,64},{128,160},{160,128},{192,224},{224,1... | collective-permute-start | bytes 3538952 | tf_op jit(solution)/shard_map/ppermute | solution.py:289
  70.0 12.2 %collective-permute-start.13 = (bf16[1536,384]{1,0:T(8,128)(2,1)S(1)}, bf16[1536,384]{1,0:T(8,128)(2,1)S(1)}, u32[]{:S(2)}, u32[]{:S(2)}) collective-permute-start(bf16[1536,384]{1,0:T(8,128)(2,1)S(1)} %collective-permute-done.8.refs_1_), channel_id=1, source_target_pairs={{0,32},{32,0},{64,96},{96,64},{128,160},{160,128},{192,224},{224,1... | collective-permute-start | bytes 3538952 | tf_op jit(solution)/shard_map/ppermute | solution.py:289
  70.5 16.0 %collective-permute-start.11 = (bf16[2,16,8,1536]{3,2,1,0:T(8,128)(2,1)S(1)}, bf16[2,16,8,1536]{3,2,1,0:T(8,128)(2,1)S(1)}, u32[]{:S(2)}, u32[]{:S(2)}) collective-permute-start(bf16[2,16,8,1536]{3,2,1,0:T(8,128)(2,1)S(1)} %collective-permute-done.6.refs_4_), channel_id=1, source_target_pairs={{0,24},{8,0},{16,8},{24,16},{32,40},{40,48},{48,56},{56,32},{64,88... | collective-permute-start | bytes 2359304 | tf_op jit(solution)/shard_map/ppermute | solution.py:273
  80.4 8.3 %collective-permute-start.10 = (bf16[2,8,8,1536]{3,2,1,0:T(8,128)(2,1)S(1)}, bf16[2,8,8,1536]{3,2,1,0:T(8,128)(2,1)S(1)}, u32[]{:S(2)}, u32[]{:S(2)}) collective-permute-start(bf16[2,8,8,1536]{3,2,1,0:T(8,128)(2,1)S(1)} %slice_select_fusion), channel_id=1, source_target_pairs={{0,1},{1,2},{2,3},{3,4},{4,5},{5,6},{6,7},{7,0},{32,39},{33,32},{3... | collective-permute-start | bytes 1179656 | tf_op jit(solution)/shard_map/ppermute | solution.py:270
  82.1 16.6 %collective-permute-start.14 = (bf16[2,16,8,1536]{3,2,1,0:T(8,128)(2,1)S(1)}, bf16[2,16,8,1536]{3,2,1,0:T(8,128)(2,1)S(1)}, u32[]{:S(2)}, u32[]{:S(2)}) collective-permute-start(bf16[2,16,8,1536]{3,2,1,0:T(8,128)(2,1)S(1)} %collective-permute-done.9.refs_0_), channel_id=1, source_target_pairs={{0,24},{8,0},{16,8},{24,16},{32,40},{40,48},{48,56},{56,32},{64,88... | collective-permute-start | bytes 2359304 | tf_op jit(solution)/shard_map/ppermute | solution.py:273
  88.7 9.9 %collective-permute-start.15 = (bf16[2,8,8,1536]{3,2,1,0:T(8,128)(2,1)S(1)}, bf16[2,8,8,1536]{3,2,1,0:T(8,128)(2,1)S(1)}, u32[]{:S(2)}, u32[]{:S(2)}) collective-permute-start(bf16[2,8,8,1536]{3,2,1,0:T(8,128)(2,1)S(1)} %collective-permute-done.10.refs_2_), channel_id=1, source_target_pairs={{0,24},{8,0},{16,8},{24,16},{32,40},{40,48},{48,56},{56,32},{64,88... | collective-permute-start | bytes 1179656 | tf_op jit(solution)/shard_map/ppermute | solution.py:273
  88.9 5.4 %collective-permute-start.17 = (f32[160,384]{1,0:T(8,128)S(1)}, f32[160,384]{1,0:T(8,128)S(1)}, u32[]{:S(2)}, u32[]{:S(2)}) collective-permute-start(f32[160,384]{1,0:T(8,128)S(1)} %pad_maximum_fusion.6), channel_id=1, source_target_pairs={{0,192},{32,224},{64,0},{96,32},{128,64},{160,96},{192,128},{224,1... | collective-permute-start | bytes 737288 | tf_op jit(solution)/shard_map/ppermute | solution.py:203
  90.3 6.3 %collective-permute-start.16 = (f32[160,384]{1,0:T(8,128)S(1)}, f32[160,384]{1,0:T(8,128)S(1)}, u32[]{:S(2)}, u32[]{:S(2)}) collective-permute-start(f32[160,384]{1,0:T(8,128)S(1)} %pad_maximum_fusion.5), channel_id=1, source_target_pairs={{0,64},{32,96},{64,128},{96,160},{128,192},{160,224},{192,0},{224,... | collective-permute-start | bytes 737288 | tf_op jit(solution)/shard_map/ppermute | solution.py:202
  100.2 7.6 %collective-permute-start.18 = (f32[176,384]{1,0:T(8,128)S(1)}, f32[176,384]{1,0:T(8,128)S(1)}, u32[]{:S(2)}, u32[]{:S(2)}) collective-permute-start(f32[176,384]{1,0:T(8,128)S(1)} %pad_maximum_fusion.3), channel_id=1, source_target_pairs={{0,64},{32,96},{64,128},{96,160},{128,192},{160,224},{192,0},{224,... | collective-permute-start | bytes 811016 | tf_op jit(solution)/shard_map/ppermute | solution.py:321
  100.3 8.3 %collective-permute-start.19 = (f32[176,384]{1,0:T(8,128)S(1)}, f32[176,384]{1,0:T(8,128)S(1)}, u32[]{:S(2)}, u32[]{:S(2)}) collective-permute-start(f32[176,384]{1,0:T(8,128)S(1)} %pad_maximum_fusion.4), channel_id=1, source_target_pairs={{0,192},{32,224},{64,0},{96,32},{128,64},{160,96},{192,128},{224,1... | collective-permute-start | bytes 811016 | tf_op jit(solution)/shard_map/ppermute | solution.py:322
  103.0 8.7 %collective-permute-start.20 = (f32[96,384]{1,0:T(8,128)S(1)}, f32[96,384]{1,0:T(8,128)S(1)}, u32[]{:S(2)}, u32[]{:S(2)}) collective-permute-start(f32[96,384]{1,0:T(8,128)S(1)} %get-tuple-element.56), channel_id=1, source_target_pairs={{0,128},{32,160},{64,192},{96,224},{128,0},{160,32},{192,64},{224,... | collective-permute-start | bytes 442376 | tf_op jit(solution)/shard_map/ppermute | solution.py:320
  111.8 3.3 %collective-permute-start.21 = (f32[256,384]{1,0:T(8,128)S(1)}, f32[256,384]{1,0:T(8,128)S(1)}, u32[]{:S(2)}, u32[]{:S(2)}) collective-permute-start(f32[256,384]{1,0:T(8,128)S(1)} %pad_maximum_fusion.2.mine_ref), channel_id=1, source_target_pairs={{0,32},{32,0},{64,96},{96,64},{128,160},{160,128},{192,224},{224,1... | collective-permute-start | bytes 1179656 | tf_op jit(solution)/shard_map/ppermute | solution.py:331

commit v10 on v8

--- a/solution.py
+++ b/solution.py
@@ -54,29 +54,42 @@
     return (xl, t - n, n), (xr, 0, m), (x, k, None)
 
 
-def pack_amplitudes(groups, share, both_ref, src_ref, out_ref, held_ref, block_ref):
+def list_tiles(groups, share, shift, both_ref, out_ref, held_ref, block_ref):
     held, total, right, left = balance(both_ref, held_ref, block_ref, groups)
-    blocks = [block_ref[s] for s in range(groups)]
-    each = share // 2
+    blocks = [block_ref[s] << shift for s in range(groups)]
     for x in range(groups // 2):
-        place = 0
+        place = x * share
         for chip, start, count in runs_of(x, total, right, left, groups // 2):
             if count is None:
-                count = share - place
+                count = (x + 1) * share - place
             n0 = jnp.clip(held[2 * chip] - start, 0, count)
             second = jnp.maximum(start - held[2 * chip], 0)
-            for block, tile, many in ((blocks[2 * chip], start, n0), (blocks[2 * chip + 1], second, count - n0)):
-
-                def move(i, carry, block=block, tile=tile, place=place):
-                    data = src_ref[block, :, pl.ds(pl.multiple_of((tile + i) * TP, TP), TP)]
-                    upper = (place + i >= each).astype(jnp.int32)
-                    into = pl.ds(pl.multiple_of((place + i - upper * each) * TP, TP), TP)
-                    for j in range(2):
-                        out_ref[4 * x + 2 * upper + j, :, into] = data
+            for first, many in ((blocks[2 * chip] + start, n0), (blocks[2 * chip + 1] + second, count - n0)):
+
+                def note(i, carry, first=first, place=place):
+                    out_ref[place + i] = first + i
                     return carry
 
-                lax.fori_loop(0, many, move, 0)
+                lax.fori_loop(0, many, note, 0)
                 place = place + many
+
+
+def pack_amplitudes(groups, share, shift, list_ref, src_ref, out_ref, packed_ref, sems):
+    each = share // 2
+    copies = []
+    for x in range(groups // 2):
+        for p in range(share):
+            entry = list_ref[x * share + p]
+            tile = pl.multiple_of((entry & ((1 << shift) - 1)) * TP, TP)
+            data = src_ref[lax.shift_right_logical(entry, jnp.int32(shift)), :, pl.ds(tile, TP)]
+            at = p % each * TP
+            for j in range(2):
+                packed_ref[4 * x + p // each * 2 + j, :, at : at + TP] = data
+        part = pl.ds(4 * x, 4)
+        copies.append(pltpu.make_async_copy(packed_ref.at[part], out_ref.at[part], sems.at[x]))
+        copies[-1].start()
+    for copy in copies:
+        copy.wait()
 
 
 def tile_rows(index):
@@ -115,7 +128,7 @@
 
 
 def join_tiles(groups, share, both_ref, mine_ref, other_ref, got_ref, *refs):
-    *their_refs, out_ref, held_ref, block_ref, sems = refs
+    *their_refs, out_ref, held_ref, block_ref = refs
     held, total, right, left = balance(both_ref, held_ref, block_ref, groups)
     group = lax.axis_index("grp")
     x, core = lax.div(group, 2), lax.rem(group, 2)
@@ -128,7 +141,13 @@
     for i, ref in enumerate(their_refs):
         jobs.append((ref, 0, jnp.clip(jnp.where(core == 0, m, n) - i * each, 0, each), jnp.where(core == 0, n, 0) + i * each))
     jobs += own_tiles(pick(held[0::2], x), core, start, share - n - m, mine_ref, other_ref, n + m)
-    run_copies(jobs, out_ref, sems)
+    for source, tile, many, place in jobs:
+
+        def move(i, carry, source=source, tile=tile, place=place):
+            out_ref[tile_rows(place + i), :] = source[tile_rows(tile + i), :]
+            return carry
+
+        lax.fori_loop(0, many, move, 0)
 
 
 def multiply(ny, *refs):
@@ -208,14 +227,25 @@
     mine = integrals[0]
     other = lax.ppermute(mine, "grp", swap)
     moved = lax.all_to_all(amplitudes[0].reshape(groups, octet, cap), "grp", 0, 0, tiled=True)
+    shift = (cap // TP).bit_length()
+    little = pltpu.CompilerParams(vmem_limit_bytes=8 * 2**20)
+    listed = pl.pallas_call(
+        functools.partial(list_tiles, groups, share, shift),
+        out_shape=jax.ShapeDtypeStruct((groups // 2 * share,), jnp.int32),
+        in_specs=[SMEM],
+        out_specs=SMEM,
+        scratch_shapes=small,
+        compiler_params=little,
+    )(both)
+    packed = jax.ShapeDtypeStruct((2 * groups, octet, wide // 2), jnp.bfloat16)
     packed = pl.pallas_call(
-        functools.partial(pack_amplitudes, groups, share),
-        out_shape=jax.ShapeDtypeStruct((2 * groups, octet, wide // 2), jnp.bfloat16),
+        functools.partial(pack_amplitudes, groups, share, shift),
+        out_shape=packed,
         in_specs=[SMEM, VMEM],
-        out_specs=VMEM,
-        scratch_shapes=small,
-        compiler_params=pltpu.CompilerParams(vmem_limit_bytes=8 * 2**20),
-    )(both, moved)
+        out_specs=pl.BlockSpec(memory_space=pltpu.HBM),
+        scratch_shapes=[pltpu.VMEM(packed.shape, packed.dtype), pltpu.SemaphoreType.DMA((groups // 2,))],
+        compiler_params=little,
+    )(listed, moved)
     pair = lax.all_to_all(packed, ("grp", "row"), 0, 0, axis_index_groups=pairs, tiled=True)
 
     tiles = jax.ShapeDtypeStruct((wide, cols), jnp.bfloat16)
@@ -260,9 +290,9 @@
     held = pl.pallas_call(
         functools.partial(join_tiles, groups, share),
         out_shape=tiles,
-        in_specs=[SMEM] + [ANY] * (3 + len(theirs)),
+        in_specs=[SMEM] + [VMEM] * (3 + len(theirs)),
         out_specs=VMEM,
-        scratch_shapes=scratch,
+        scratch_shapes=small,
         compiler_params=limit,
     )(both, mine, other, got, *theirs)
 

time: 116 us -> 116 us (level)
  Pallas kernels: 14 us -> 12.1 us
  waiting for transfers between devices: 56.8 us -> 58.1 us
    pallas_call x1, Pallas kernels: 4.74 us -> 2.32 us  [body(): pl.pallas_call(functools.partial(join_tiles, groups, share), out_shape=ti...]
    all_to_all x1, waiting for transfers between devices: 9.55 us -> 7.58 us  [body(): lax.all_to_all(amplitudes[0].reshape(groups, octet, cap), 'grp', 0, 0, ti...]
    ppermute x1, starting transfers between devices: 0.08 us -> 1.76 us  [near_chips(): return (a, lax.ppermute(jnp.concatenate([p[2, h:], p[3, :h]]), 'grp', down))]
    pallas_call x1 -> x2, Pallas kernels: 2.15 us -> 3.82 us  [the longest x1 1.96 us: body(): pl.pallas_call(functools.partial(list_tiles, groups, share, shift), out_s...]
    ppermute x1, waiting for transfers between devices: 1.03 us -> 2.7 us  [near_chips(): a = lax.ppermute(jnp.concatenate([p[2, :h], p[1, h:]]), 'grp', up)]
    ppermute x1, starting transfers between devices: 1.52 us -> 0.08 us  [near_chips(): a = lax.ppermute(jnp.concatenate([p[2, :h], p[1, h:]]), 'grp', up)]
  transfers between devices with their start and end apart: 23 -> 23, of which waited for: 15 -> 15; matrix products, arithmetic and copies ran while one was open for 5% -> 5% of each run, Pallas kernels for 10% -> 9%
where the time goes in v10:
time: 116 us
  waiting for transfers between devices  58.1 us (50%)
  starting transfers between devices  35.5 us (31%)
  Pallas kernels  12.1 us (10%)
  local copies, waits for them, and re-layouts  6.1 us (5%)
  other arithmetic  3.44 us (3%)
    ppermute x5, waiting for transfers between devices, z_step(): return lax.ppermute(block, ('grp', 'col'), along)  20.4 us
    ppermute x5, starting transfers between devices, z_step(): return lax.ppermute(block, ('grp', 'col'), along)  14.3 us
    ppermute x5, waiting for transfers between devices, y_step(): return lax.ppermute(block, ('grp', 'row'), beside)  7.61 us
    all_to_all x1, waiting for transfers between devices, body(): lax.all_to_all(amplitudes[0].reshape(groups, octet, cap), 'grp', 0, 0, ti...  7.58 us
    all_to_all x1, waiting for transfers between devices, body(): lax.all_to_all(packed, ('grp', 'row'), 0, 0, axis_index_groups=pairs, til...  5.86 us
    all_to_all x1, starting transfers between devices, body(): lax.all_to_all(packed, ('grp', 'row'), 0, 0, axis_index_groups=pairs, til...  4.83 us
    ppermute x1, waiting for transfers between devices, body(): lax.ppermute(jnp.concatenate([late[1], early[1, :h] + a[:h]]), 'grp', up)  4.32 us
    unnamed x8, local copies, waits for them, and re-layouts  4.15 us
  transfers between devices with their start and end apart: 23, of which 15 were waited for; matrix products, arithmetic and copies ran while one was open for 5% of the time, Pallas kernels for 9%

profile of v10, /device:TPU:1, one launch (start us, length us, event | category | flops | bytes accessed | tf_op | source)
XLA Modules:
  0.0 115.5 jit_solution(11528008325074056601)
XLA Ops:
  0.0 3.2 %collective-permute-start = (bf16[4608,384]{1,0:T(8,128)(2,1)}, bf16[4608,384]{1,0:T(8,128)(2,1)S(1)}, u32[]{:S(2)}, u32[]{:S(2)}) collective-permute-start(bf16[4608,384]{1,0:T(8,128)(2,1)} %bitcast.40), channel_id=1, source_target_pairs={{0,32},{32,0},{64,96},{96,64},{128,160},{160,128},{192,224},{224,1... | collective-permute-start | bytes 10616840 | tf_op jit(solution)/shard_map/ppermute | solution.py:228
  3.2 4.1 %all-to-all-start = ((bf16[8,8,4608]{2,1,0:T(8,128)(2,1)}), bf16[8,8,4608]{2,1,0:T(8,128)(2,1)}, u32[]{:S(2)}, u32[]{:S(2)}) async-start(bf16[8,8,4608]{2,1,0:T(8,128)(2,1)} %bitcast.43), calls=%async_computation | async-start | bytes 1179648 | tf_op jit(solution)/shard_map/all_to_all | solution.py:229
  7.4 0.7 pad_add_fusion.both_ref
  8.1 2.0 %shard_map.46.list_ref = s32[96]{0:T(128)S(1)} custom-call(s32[2,8]{1,0:T(2,128)S(1)} %pad_add_fusion.both_ref), custom_call_target="tpu_custom_call" | custom-call | tf_op jit(solution)/shard_map/pallas_call | solution.py:232
  10.1 7.6 %all-to-all-done.src_ref = bf16[8,8,4608]{2,1,0:T(8,128)(2,1)} async-done(((bf16[8,8,4608]{2,1,0:T(8,128)(2,1)}), bf16[8,8,4608]{2,1,0:T(8,128)(2,1)}, u32[]{:S(2)}, u32[]{:S(2)}) %all-to-all-start) | async-done | bytes 589856 | tf_op jit(solution)/shard_map/all_to_all | solution.py:229
  17.6 1.9 %shard_map.47 = bf16[16,8,1536]{2,1,0:T(8,128)(2,1)S(1)} custom-call(s32[96]{0:T(128)S(1)} %shard_map.46.list_ref, bf16[8,8,4608]{2,1,0:T(8,128)(2,1)} %all-to-all-done.src_ref), custom_call_target="tpu_custom_call" | custom-call | tf_op jit(solution)/shard_map/pallas_call | solution.py:241
  19.5 0.0 copy-start.3
  19.5 0.7 copy-done.3
  20.2 4.8 %all-to-all-start.1 = ((bf16[16,8,1536]{2,1,0:T(8,128)(2,1)}), bf16[16,8,1536]{2,1,0:T(8,128)(2,1)}, u32[]{:S(2)}, u32[]{:S(2)}) async-start(bf16[16,8,1536]{2,1,0:T(8,128)(2,1)} %copy-done.3), calls=%async_computation.1 | async-start | bytes 786432 | tf_op jit(solution)/shard_map/all_to_all | solution.py:249
  25.1 0.0 collective-permute-done.other_ref
  25.1 0.0 copy-start
  25.1 2.0 %copy-done = bf16[1,4608,384]{2,1,0:T(8,128)(2,1)S(1)} copy-done((bf16[1,4608,384]{2,1,0:T(8,128)(2,1)S(1)}, bf16[1,4608,384]{2,1,0:T(8,128)(2,1)}, u32[]{:S(2)}) %copy-start) | copy-done | bytes 3538968
  27.1 1.5 %shard_map.48 = bf16[3072,384]{1,0:T(8,128)(2,1)S(1)} custom-call(s32[2,8]{1,0:T(2,128)S(1)} %pad_add_fusion.both_ref, bf16[4608,384]{1,0:T(8,128)(2,1)S(1)} %bitcast.41, bf16[4608,384]{1,0:T(8,128)(2,1)S(1)} %collective-permute-done.other_ref), custom_call_target="tpu_custom_call" | custom-call | tf_op jit(solution)/shard_map/pallas_call | solution.py:253
  28.7 1.4 %copy-done.2 = bf16[3072,384]{1,0:T(8,128)(2,1)} copy-done((bf16[3072,384]{1,0:T(8,128)(2,1)}, bf16[3072,384]{1,0:T(8,128)(2,1)S(1)}, u32[]{:S(2)}) %copy-start.2) | copy-done | bytes 2359320
  30.1 5.9 %all-to-all-done.1 = bf16[16,8,1536]{2,1,0:T(8,128)(2,1)} async-done(((bf16[16,8,1536]{2,1,0:T(8,128)(2,1)}), bf16[16,8,1536]{2,1,0:T(8,128)(2,1)}, u32[]{:S(2)}, u32[]{:S(2)}) %all-to-all-start.1) | async-done | bytes 393248 | tf_op jit(solution)/shard_map/all_to_all | solution.py:249
  35.9 0.4 collective-permute-start.7
  36.4 0.0 collective-permute-start.1
  36.4 5.3 %collective-permute-start.2 = (bf16[16,8,1536]{2,1,0:T(8,128)(2,1)}, bf16[16,8,1536]{2,1,0:T(8,128)(2,1)}, u32[]{:S(2)}, u32[]{:S(2)}) collective-permute-start(bf16[16,8,1536]{2,1,0:T(8,128)(2,1)} %all-to-all-done.1), channel_id=1, source_target_pairs={{0,1},{1,2},{2,3},{3,4},{4,5},{5,6},{6,7},{7,0},{32,39},{33,32},{3... | collective-permute-start | bytes 1179656 | tf_op jit(solution)/shard_map/ppermute | solution.py:268
  41.6 0.0 collective-permute-done.1
  41.6 2.1 %collective-permute-start.3 = (bf16[16,8,1536]{2,1,0:T(8,128)(2,1)}, bf16[16,8,1536]{2,1,0:T(8,128)(2,1)}, u32[]{:S(2)}, u32[]{:S(2)}) collective-permute-start(bf16[16,8,1536]{2,1,0:T(8,128)(2,1)} %collective-permute-done.1), channel_id=1, source_target_pairs={{0,1},{1,2},{2,3},{3,4},{4,5},{5,6},{6,7},{7,0},{32,39},{33,32},{3... | collective-permute-start | bytes 1179656 | tf_op jit(solution)/shard_map/ppermute | solution.py:268
  43.7 1.3 %fusion.1.refs_0_ = bf16[2,8,8,1536]{3,2,1,0:T(8,128)(2,1)S(1)} fusion(bf16[1,16,8,1536]{3,2,1,0:T(8,128)(2,1)} %bitcast.4, bf16[1,16,8,1536]{3,2,1,0:T(8,128)(2,1)} %bitcast.5, pred[]{:T(512)S(6)} %eq.4), kind=kLoop, calls=%fused_computation.4 | loop fusion | flops 589824 | bytes 1179649 | tf_op jit(solution)/shard_map/jit(_where)/select_n | solution.py:265
  45.0 0.5 collective-permute-start.4
  45.5 1.2 %collective-permute-done.2 = bf16[16,8,1536]{2,1,0:T(8,128)(2,1)} collective-permute-done((bf16[16,8,1536]{2,1,0:T(8,128)(2,1)}, bf16[16,8,1536]{2,1,0:T(8,128)(2,1)}, u32[]{:S(2)}, u32[]{:S(2)}) %collective-permute-start.2) | collective-permute-done | bytes 393248 | tf_op jit(solution)/shard_map/ppermute | solution.py:268
  46.7 4.2 %collective-permute-done.3 = bf16[16,8,1536]{2,1,0:T(8,128)(2,1)} collective-permute-done((bf16[16,8,1536]{2,1,0:T(8,128)(2,1)}, bf16[16,8,1536]{2,1,0:T(8,128)(2,1)}, u32[]{:S(2)}, u32[]{:S(2)}) %collective-permute-start.3) | collective-permute-done | bytes 393248 | tf_op jit(solution)/shard_map/ppermute | solution.py:268
  50.9 1.2 %pad_maximum_fusion.refs_2_ = bf16[2,16,8,1536]{3,2,1,0:T(8,128)(2,1)S(1)} fusion(bf16[1,16,8,1536]{3,2,1,0:T(8,128)(2,1)} %bitcast.7, bf16[1,16,8,1536]{3,2,1,0:T(8,128)(2,1)} %bitcast.6), kind=kLoop, calls=%fused_computation.2 | loop fusion | flops 393216 | bytes 1572864 | tf_op jit(solution)/shard_map/stack | solution.py:276
  52.1 0.0 copy-start.1
  52.1 1.2 %collective-permute-done.4.refs_1_ = bf16[2,8,8,1536]{3,2,1,0:T(8,128)(2,1)S(1)} collective-permute-done((bf16[2,8,8,1536]{3,2,1,0:T(8,128)(2,1)S(1)}, bf16[2,8,8,1536]{3,2,1,0:T(8,128)(2,1)S(1)}, u32[]{:S(2)}, u32[]{:S(2)}) %collective-permute-start.4) | collective-permute-done | bytes 393248 | tf_op jit(solution)/shard_map/ppermute | solution.py:271
  53.3 2.3 %collective-permute-start.5 = (bf16[2,16,8,1536]{3,2,1,0:T(8,128)(2,1)S(1)}, bf16[2,16,8,1536]{3,2,1,0:T(8,128)(2,1)S(1)}, u32[]{:S(2)}, u32[]{:S(2)}) collective-permute-start(bf16[2,16,8,1536]{3,2,1,0:T(8,128)(2,1)S(1)} %pad_maximum_fusion.refs_2_), channel_id=1, source_target_pairs={{0,1},{1,2},{2,3},{3,4},{4,5},{5,6},{6,7},{7,0},{32,39},{33,32},{3... | collective-permute-start | bytes 2359304 | tf_op jit(solution)/shard_map/ppermute | solution.py:268
  55.6 0.4 collective-permute-start.6
  56.0 8.6 %collective-permute-done.5.refs_4_ = bf16[2,16,8,1536]{3,2,1,0:T(8,128)(2,1)S(1)} collective-permute-done((bf16[2,16,8,1536]{3,2,1,0:T(8,128)(2,1)S(1)}, bf16[2,16,8,1536]{3,2,1,0:T(8,128)(2,1)S(1)}, u32[]{:S(2)}, u32[]{:S(2)}) %collective-permute-start.5) | collective-permute-done | bytes 786464 | tf_op jit(solution)/shard_map/ppermute | solution.py:268
  64.6 3.1 %collective-permute-done.6.refs_3_ = bf16[2,16,8,1536]{3,2,1,0:T(8,128)(2,1)S(1)} collective-permute-done((bf16[2,16,8,1536]{3,2,1,0:T(8,128)(2,1)S(1)}, bf16[2,16,8,1536]{3,2,1,0:T(8,128)(2,1)S(1)}, u32[]{:S(2)}, u32[]{:S(2)}) %collective-permute-start.6) | collective-permute-done | bytes 786464 | tf_op jit(solution)/shard_map/ppermute | solution.py:271
  67.6 0.0 collective-permute-done.7.got_ref
  67.6 1.8 %collective-permute-start.11 = (bf16[2,16,8,1536]{3,2,1,0:T(8,128)(2,1)S(1)}, bf16[2,16,8,1536]{3,2,1,0:T(8,128)(2,1)S(1)}, u32[]{:S(2)}, u32[]{:S(2)}) collective-permute-start(bf16[2,16,8,1536]{3,2,1,0:T(8,128)(2,1)S(1)} %collective-permute-done.5.refs_4_), channel_id=1, source_target_pairs={{0,1},{1,2},{2,3},{3,4},{4,5},{5,6},{6,7},{7,0},{32,39},{33,32},{3... | collective-permute-start | bytes 2359304 | tf_op jit(solution)/shard_map/ppermute | solution.py:268
  69.5 1.9 %fusion.7 = (bf16[1536,384]{1,0:T(8,128)(2,1)S(1)}, bf16[1536,384]{1,0:T(8,128)(2,1)S(1)}) fusion(bf16[3072,384]{1,0:T(8,128)(2,1)} %collective-permute-done.7.got_ref), kind=kLoop, calls=%fused_computation.31 | loop fusion | bytes 4718592 | tf_op jit(solution)/shard_map/split | solution.py:286
  71.3 0.1 collective-permute-start.10
  71.4 0.5 collective-permute-start.9
  71.9 0.4 collective-permute-start.8
  72.3 6.5 %collective-permute-done.11.refs_0_ = bf16[2,16,8,1536]{3,2,1,0:T(8,128)(2,1)S(1)} collective-permute-done((bf16[2,16,8,1536]{3,2,1,0:T(8,128)(2,1)S(1)}, bf16[2,16,8,1536]{3,2,1,0:T(8,128)(2,1)S(1)}, u32[]{:S(2)}, u32[]{:S(2)}) %collective-permute-start.11) | collective-permute-done | bytes 786464 | tf_op jit(solution)/shard_map/ppermute | solution.py:268
  78.8 2.8 %collective-permute-start.13 = (bf16[2,8,8,1536]{3,2,1,0:T(8,128)(2,1)S(1)}, bf16[2,8,8,1536]{3,2,1,0:T(8,128)(2,1)S(1)}, u32[]{:S(2)}, u32[]{:S(2)}) collective-permute-start(bf16[2,8,8,1536]{3,2,1,0:T(8,128)(2,1)S(1)} %slice_select_fusion), channel_id=1, source_target_pairs={{0,1},{1,2},{2,3},{3,4},{4,5},{5,6},{6,7},{7,0},{32,39},{33,32},{3... | collective-permute-start | bytes 1179656 | tf_op jit(solution)/shard_map/ppermute | solution.py:268
  81.6 0.4 collective-permute-start.12
  82.0 0.0 collective-permute-done.10.refs_1_
  82.0 0.0 collective-permute-done.9.refs_0_
  82.1 2.3 %shard_map.49.refs_6_.refs_4_ = bf16[3072,384]{1,0:T(8,128)(2,1)S(1)} custom-call(s32[2,8]{1,0:T(2,128)S(1)} %pad_add_fusion.both_ref, bf16[4608,384]{1,0:T(8,128)(2,1)S(1)} %bitcast.42, bf16[4608,384]{1,0:T(8,128)(2,1)S(1)} %collective-permute-done.other_ref, bf16[3072,384]{1,0:T(8,128)(2,1)} %collective-permute-done.7.got_ref, ...), custom_call_target="tpu_custom_call" | custom-call | tf_op jit(solution)/shard_map/pallas_call | solution.py:290
  84.4 0.0 collective-permute-done.8.refs_5_
  84.4 2.2 %shard_map.50 = f32[4,160,384]{2,1,0:T(8,128)S(1)} custom-call(bf16[2,8,8,1536]{3,2,1,0:T(8,128)(2,1)S(1)} %fusion.1.refs_0_, bf16[2,8,8,1536]{3,2,1,0:T(8,128)(2,1)S(1)} %collective-permute-done.4.refs_1_, bf16[2,16,8,1536]{3,2,1,0:T(8,128)(2,1)S(1)} %pad_maximum_fusion.refs_2_, bf16[2,16,8,1536]{3,2,1,0:T(8,128)(2,1)S(1)} %collective-permute-done.6.refs_3_, ...), custom_call_target="tpu_custom_call" | custom-call | tf_op jit(solution)/shard_map/pallas_call | solution.py:301
  86.6 0.0 collective-permute-done.13.refs_2_
  86.6 0.1 collective-permute-start.14
  86.8 1.8 %collective-permute-start.16 = (f32[160,384]{1,0:T(8,128)S(1)}, f32[160,384]{1,0:T(8,128)S(1)}, u32[]{:S(2)}, u32[]{:S(2)}) collective-permute-start(f32[160,384]{1,0:T(8,128)S(1)} %pad_maximum_fusion.6), channel_id=1, source_target_pairs={{0,192},{32,224},{64,0},{96,32},{128,64},{160,96},{192,128},{224,1... | collective-permute-start | bytes 737288 | tf_op jit(solution)/shard_map/ppermute | solution.py:202
  88.6 0.1 collective-permute-start.15
  88.7 3.5 %collective-permute-done.16 = f32[160,384]{1,0:T(8,128)S(1)} collective-permute-done((f32[160,384]{1,0:T(8,128)S(1)}, f32[160,384]{1,0:T(8,128)S(1)}, u32[]{:S(2)}, u32[]{:S(2)}) %collective-permute-start.16) | collective-permute-done | bytes 245792 | tf_op jit(solution)/shard_map/ppermute | solution.py:202
  92.2 2.7 %collective-permute-done.15 = f32[160,384]{1,0:T(8,128)S(1)} collective-permute-done((f32[160,384]{1,0:T(8,128)S(1)}, f32[160,384]{1,0:T(8,128)S(1)}, u32[]{:S(2)}, u32[]{:S(2)}) %collective-permute-start.15) | collective-permute-done | bytes 245792 | tf_op jit(solution)/shard_map/ppermute | solution.py:201
  94.9 3.3 %collective-permute-done.14.refs_3_ = bf16[2,8,8,1536]{3,2,1,0:T(8,128)(2,1)S(1)} collective-permute-done((bf16[2,8,8,1536]{3,2,1,0:T(8,128)(2,1)S(1)}, bf16[2,8,8,1536]{3,2,1,0:T(8,128)(2,1)S(1)}, u32[]{:S(2)}, u32[]{:S(2)}) %collective-permute-start.14) | collective-permute-done | bytes 393248 | tf_op jit(solution)/shard_map/ppermute | solution.py:271
  98.2 0.0 collective-permute-done.12.refs_1_
  98.2 1.4 %shard_map.51 = f32[4,96,384]{2,1,0:T(8,128)S(1)} custom-call(bf16[2,16,8,1536]{3,2,1,0:T(8,128)(2,1)S(1)} %collective-permute-done.11.refs_0_, bf16[2,16,8,1536]{3,2,1,0:T(8,128)(2,1)S(1)} %collective-permute-done.12.refs_1_, bf16[2,8,8,1536]{3,2,1,0:T(8,128)(2,1)S(1)} %collective-permute-done.13.refs_2_, ...), custom_call_target="tpu_custom_call" | custom-call | tf_op jit(solution)/shard_map/pallas_call | solution.py:301
  99.7 0.1 collective-permute-start.17
  99.8 2.7 %collective-permute-start.18 = (f32[176,384]{1,0:T(8,128)S(1)}, f32[176,384]{1,0:T(8,128)S(1)}, u32[]{:S(2)}, u32[]{:S(2)}) collective-permute-start(f32[176,384]{1,0:T(8,128)S(1)} %pad_maximum_fusion.4), channel_id=1, source_target_pairs={{0,192},{32,224},{64,0},{96,32},{128,64},{160,96},{192,128},{224,1... | collective-permute-start | bytes 811016 | tf_op jit(solution)/shard_map/ppermute | solution.py:317
  102.6 0.0 collective-permute-start.19
  102.6 4.3 %collective-permute-done.17 = f32[176,384]{1,0:T(8,128)S(1)} collective-permute-done((f32[176,384]{1,0:T(8,128)S(1)}, f32[176,384]{1,0:T(8,128)S(1)}, u32[]{:S(2)}, u32[]{:S(2)}) %collective-permute-start.17) | collective-permute-done | bytes 270368 | tf_op jit(solution)/shard_map/ppermute | solution.py:316
  106.9 0.9 collective-permute-done.18
  107.8 0.1 fusion.3
  107.8 3.8 %collective-permute-done.19 = f32[96,384]{1,0:T(8,128)S(1)} collective-permute-done((f32[96,384]{1,0:T(8,128)S(1)}, f32[96,384]{1,0:T(8,128)S(1)}, u32[]{:S(2)}, u32[]{:S(2)}) %collective-permute-start.19) | collective-permute-done | bytes 147488 | tf_op jit(solution)/shard_map/ppermute | solution.py:315
  111.7 1.6 %collective-permute-start.20 = (f32[256,384]{1,0:T(8,128)S(1)}, f32[256,384]{1,0:T(8,128)S(1)}, u32[]{:S(2)}, u32[]{:S(2)}) collective-permute-start(f32[256,384]{1,0:T(8,128)S(1)} %pad_maximum_fusion.2.mine_ref), channel_id=1, source_target_pairs={{0,32},{32,0},{64,96},{96,64},{128,160},{160,128},{192,224},{224,1... | collective-permute-start | bytes 1179656 | tf_op jit(solution)/shard_map/ppermute | solution.py:326
  113.3 1.3 %collective-permute-done.20.other_ref = f32[256,384]{1,0:T(8,128)S(1)} collective-permute-done((f32[256,384]{1,0:T(8,128)S(1)}, f32[256,384]{1,0:T(8,128)S(1)}, u32[]{:S(2)}, u32[]{:S(2)}) %collective-permute-start.20) | collective-permute-done | bytes 393248 | tf_op jit(solution)/shard_map/ppermute | solution.py:326
  114.7 0.8 shard_map.52
  (14 shorter events, 0.3 us)
Async XLA Ops:
  0.0 25.1 %collective-permute-start = (bf16[4608,384]{1,0:T(8,128)(2,1)}, bf16[4608,384]{1,0:T(8,128)(2,1)S(1)}, u32[]{:S(2)}, u32[]{:S(2)}) collective-permute-start(bf16[4608,384]{1,0:T(8,128)(2,1)} %bitcast.40), channel_id=1, source_target_pairs={{0,32},{32,0},{64,96},{96,64},{128,160},{160,128},{192,224},{224,1... | collective-permute-start | bytes 10616840 | tf_op jit(solution)/shard_map/ppermute | solution.py:228
  3.2 14.4 %all-to-all-start = ((bf16[8,8,4608]{2,1,0:T(8,128)(2,1)}), bf16[8,8,4608]{2,1,0:T(8,128)(2,1)}, u32[]{:S(2)}, u32[]{:S(2)}) async-start(bf16[8,8,4608]{2,1,0:T(8,128)(2,1)} %bitcast.43), calls=%async_computation | async-start | bytes 1179648 | tf_op jit(solution)/shard_map/all_to_all | solution.py:229
  19.5 0.7 copy-start.3
  20.2 15.7 %all-to-all-start.1 = ((bf16[16,8,1536]{2,1,0:T(8,128)(2,1)}), bf16[16,8,1536]{2,1,0:T(8,128)(2,1)}, u32[]{:S(2)}, u32[]{:S(2)}) async-start(bf16[16,8,1536]{2,1,0:T(8,128)(2,1)} %copy-done.3), calls=%async_computation.1 | async-start | bytes 786432 | tf_op jit(solution)/shard_map/all_to_all | solution.py:249
  25.1 2.0 %copy-start = (bf16[1,4608,384]{2,1,0:T(8,128)(2,1)S(1)}, bf16[1,4608,384]{2,1,0:T(8,128)(2,1)}, u32[]{:S(2)}) copy-start(bf16[1,4608,384]{2,1,0:T(8,128)(2,1)} %param.5) | copy-start | bytes 10616836
  28.6 1.4 %copy-start.2 = (bf16[3072,384]{1,0:T(8,128)(2,1)}, bf16[3072,384]{1,0:T(8,128)(2,1)S(1)}, u32[]{:S(2)}) copy-start(bf16[3072,384]{1,0:T(8,128)(2,1)S(1)} %shard_map.48) | copy-start | bytes 7077892
  35.9 31.7 %collective-permute-start.7 = (bf16[3072,384]{1,0:T(8,128)(2,1)}, bf16[3072,384]{1,0:T(8,128)(2,1)}, u32[]{:S(2)}, u32[]{:S(2)}) collective-permute-start(bf16[3072,384]{1,0:T(8,128)(2,1)} %copy-done.2), channel_id=1, source_target_pairs={{0,64},{32,224},{64,128},{96,32},{128,192},{160,96},{192,0},{224,1... | collective-permute-start | bytes 7077896 | tf_op jit(solution)/shard_map/ppermute | solution.py:262
  36.4 5.3 %collective-permute-start.1 = (bf16[16,8,1536]{2,1,0:T(8,128)(2,1)}, bf16[16,8,1536]{2,1,0:T(8,128)(2,1)}, u32[]{:S(2)}, u32[]{:S(2)}) collective-permute-start(bf16[16,8,1536]{2,1,0:T(8,128)(2,1)} %all-to-all-done.1), channel_id=1, source_target_pairs={{0,32},{32,0},{64,96},{96,64},{128,160},{160,128},{192,224},{224,1... | collective-permute-start | bytes 1179656 | tf_op jit(solution)/shard_map/ppermute | solution.py:273
  36.4 10.3 %collective-permute-start.2 = (bf16[16,8,1536]{2,1,0:T(8,128)(2,1)}, bf16[16,8,1536]{2,1,0:T(8,128)(2,1)}, u32[]{:S(2)}, u32[]{:S(2)}) collective-permute-start(bf16[16,8,1536]{2,1,0:T(8,128)(2,1)} %all-to-all-done.1), channel_id=1, source_target_pairs={{0,1},{1,2},{2,3},{3,4},{4,5},{5,6},{6,7},{7,0},{32,39},{33,32},{3... | collective-permute-start | bytes 1179656 | tf_op jit(solution)/shard_map/ppermute | solution.py:268
  41.6 9.2 %collective-permute-start.3 = (bf16[16,8,1536]{2,1,0:T(8,128)(2,1)}, bf16[16,8,1536]{2,1,0:T(8,128)(2,1)}, u32[]{:S(2)}, u32[]{:S(2)}) collective-permute-start(bf16[16,8,1536]{2,1,0:T(8,128)(2,1)} %collective-permute-done.1), channel_id=1, source_target_pairs={{0,1},{1,2},{2,3},{3,4},{4,5},{5,6},{6,7},{7,0},{32,39},{33,32},{3... | collective-permute-start | bytes 1179656 | tf_op jit(solution)/shard_map/ppermute | solution.py:268
  45.0 8.3 %collective-permute-start.4 = (bf16[2,8,8,1536]{3,2,1,0:T(8,128)(2,1)S(1)}, bf16[2,8,8,1536]{3,2,1,0:T(8,128)(2,1)S(1)}, u32[]{:S(2)}, u32[]{:S(2)}) collective-permute-start(bf16[2,8,8,1536]{3,2,1,0:T(8,128)(2,1)S(1)} %fusion.1.refs_0_), channel_id=1, source_target_pairs={{0,24},{8,0},{16,8},{24,16},{32,40},{40,48},{48,56},{56,32},{64,88... | collective-permute-start | bytes 1179656 | tf_op jit(solution)/shard_map/ppermute | solution.py:271
  52.1 30.0 %copy-start.1 = (bf16[1,4608,384]{2,1,0:T(8,128)(2,1)S(1)}, bf16[1,4608,384]{2,1,0:T(8,128)(2,1)}, u32[]{:S(2)}) copy-start(bf16[1,4608,384]{2,1,0:T(8,128)(2,1)} %param.5) | copy-start | bytes 10616836
  53.3 11.2 %collective-permute-start.5 = (bf16[2,16,8,1536]{3,2,1,0:T(8,128)(2,1)S(1)}, bf16[2,16,8,1536]{3,2,1,0:T(8,128)(2,1)S(1)}, u32[]{:S(2)}, u32[]{:S(2)}) collective-permute-start(bf16[2,16,8,1536]{3,2,1,0:T(8,128)(2,1)S(1)} %pad_maximum_fusion.refs_2_), channel_id=1, source_target_pairs={{0,1},{1,2},{2,3},{3,4},{4,5},{5,6},{6,7},{7,0},{32,39},{33,32},{3... | collective-permute-start | bytes 2359304 | tf_op jit(solution)/shard_map/ppermute | solution.py:268
  55.6 12.1 %collective-permute-start.6 = (bf16[2,16,8,1536]{3,2,1,0:T(8,128)(2,1)S(1)}, bf16[2,16,8,1536]{3,2,1,0:T(8,128)(2,1)S(1)}, u32[]{:S(2)}, u32[]{:S(2)}) collective-permute-start(bf16[2,16,8,1536]{3,2,1,0:T(8,128)(2,1)S(1)} %pad_maximum_fusion.refs_2_), channel_id=1, source_target_pairs={{0,24},{8,0},{16,8},{24,16},{32,40},{40,48},{48,56},{56,32},{64,88... | collective-permute-start | bytes 2359304 | tf_op jit(solution)/shard_map/ppermute | solution.py:271
  67.6 11.1 %collective-permute-start.11 = (bf16[2,16,8,1536]{3,2,1,0:T(8,128)(2,1)S(1)}, bf16[2,16,8,1536]{3,2,1,0:T(8,128)(2,1)S(1)}, u32[]{:S(2)}, u32[]{:S(2)}) collective-permute-start(bf16[2,16,8,1536]{3,2,1,0:T(8,128)(2,1)S(1)} %collective-permute-done.5.refs_4_), channel_id=1, source_target_pairs={{0,1},{1,2},{2,3},{3,4},{4,5},{5,6},{6,7},{7,0},{32,39},{33,32},{3... | collective-permute-start | bytes 2359304 | tf_op jit(solution)/shard_map/ppermute | solution.py:268
  71.3 10.7 %collective-permute-start.10 = (bf16[1536,384]{1,0:T(8,128)(2,1)S(1)}, bf16[1536,384]{1,0:T(8,128)(2,1)S(1)}, u32[]{:S(2)}, u32[]{:S(2)}) collective-permute-start(bf16[1536,384]{1,0:T(8,128)(2,1)S(1)} %get-tuple-element.35), channel_id=1, source_target_pairs={{0,32},{32,0},{64,96},{96,64},{128,160},{160,128},{192,224},{224,1... | collective-permute-start | bytes 3538952 | tf_op jit(solution)/shard_map/ppermute | solution.py:286
  71.4 10.6 %collective-permute-start.9 = (bf16[1536,384]{1,0:T(8,128)(2,1)S(1)}, bf16[1536,384]{1,0:T(8,128)(2,1)S(1)}, u32[]{:S(2)}, u32[]{:S(2)}) collective-permute-start(bf16[1536,384]{1,0:T(8,128)(2,1)S(1)} %get-tuple-element.36), channel_id=1, source_target_pairs={{0,32},{32,0},{64,96},{96,64},{128,160},{160,128},{192,224},{224,1... | collective-permute-start | bytes 3538952 | tf_op jit(solution)/shard_map/ppermute | solution.py:286
  71.9 12.4 %collective-permute-start.8 = (bf16[2,16,8,1536]{3,2,1,0:T(8,128)(2,1)S(1)}, bf16[2,16,8,1536]{3,2,1,0:T(8,128)(2,1)S(1)}, u32[]{:S(2)}, u32[]{:S(2)}) collective-permute-start(bf16[2,16,8,1536]{3,2,1,0:T(8,128)(2,1)S(1)} %collective-permute-done.5.refs_4_), channel_id=1, source_target_pairs={{0,24},{8,0},{16,8},{24,16},{32,40},{40,48},{48,56},{56,32},{64,88... | collective-permute-start | bytes 2359304 | tf_op jit(solution)/shard_map/ppermute | solution.py:271
  78.8 7.8 %collective-permute-start.13 = (bf16[2,8,8,1536]{3,2,1,0:T(8,128)(2,1)S(1)}, bf16[2,8,8,1536]{3,2,1,0:T(8,128)(2,1)S(1)}, u32[]{:S(2)}, u32[]{:S(2)}) collective-permute-start(bf16[2,8,8,1536]{3,2,1,0:T(8,128)(2,1)S(1)} %slice_select_fusion), channel_id=1, source_target_pairs={{0,1},{1,2},{2,3},{3,4},{4,5},{5,6},{6,7},{7,0},{32,39},{33,32},{3... | collective-permute-start | bytes 1179656 | tf_op jit(solution)/shard_map/ppermute | solution.py:268
  81.6 16.6 %collective-permute-start.12 = (bf16[2,16,8,1536]{3,2,1,0:T(8,128)(2,1)S(1)}, bf16[2,16,8,1536]{3,2,1,0:T(8,128)(2,1)S(1)}, u32[]{:S(2)}, u32[]{:S(2)}) collective-permute-start(bf16[2,16,8,1536]{3,2,1,0:T(8,128)(2,1)S(1)} %collective-permute-done.11.refs_0_), channel_id=1, source_target_pairs={{0,24},{8,0},{16,8},{24,16},{32,40},{40,48},{48,56},{56,32},{64,88... | collective-permute-start | bytes 2359304 | tf_op jit(solution)/shard_map/ppermute | solution.py:271
  86.6 11.6 %collective-permute-start.14 = (bf16[2,8,8,1536]{3,2,1,0:T(8,128)(2,1)S(1)}, bf16[2,8,8,1536]{3,2,1,0:T(8,128)(2,1)S(1)}, u32[]{:S(2)}, u32[]{:S(2)}) collective-permute-start(bf16[2,8,8,1536]{3,2,1,0:T(8,128)(2,1)S(1)} %collective-permute-done.13.refs_2_), channel_id=1, source_target_pairs={{0,24},{8,0},{16,8},{24,16},{32,40},{40,48},{48,56},{56,32},{64,88... | collective-permute-start | bytes 1179656 | tf_op jit(solution)/shard_map/ppermute | solution.py:271
  86.8 5.4 %collective-permute-start.16 = (f32[160,384]{1,0:T(8,128)S(1)}, f32[160,384]{1,0:T(8,128)S(1)}, u32[]{:S(2)}, u32[]{:S(2)}) collective-permute-start(f32[160,384]{1,0:T(8,128)S(1)} %pad_maximum_fusion.6), channel_id=1, source_target_pairs={{0,192},{32,224},{64,0},{96,32},{128,64},{160,96},{192,128},{224,1... | collective-permute-start | bytes 737288 | tf_op jit(solution)/shard_map/ppermute | solution.py:202
  88.6 6.3 %collective-permute-start.15 = (f32[160,384]{1,0:T(8,128)S(1)}, f32[160,384]{1,0:T(8,128)S(1)}, u32[]{:S(2)}, u32[]{:S(2)}) collective-permute-start(f32[160,384]{1,0:T(8,128)S(1)} %pad_maximum_fusion.5), channel_id=1, source_target_pairs={{0,64},{32,96},{64,128},{96,160},{128,192},{160,224},{192,0},{224,... | collective-permute-start | bytes 737288 | tf_op jit(solution)/shard_map/ppermute | solution.py:201
  99.7 7.2 %collective-permute-start.17 = (f32[176,384]{1,0:T(8,128)S(1)}, f32[176,384]{1,0:T(8,128)S(1)}, u32[]{:S(2)}, u32[]{:S(2)}) collective-permute-start(f32[176,384]{1,0:T(8,128)S(1)} %pad_maximum_fusion.3), channel_id=1, source_target_pairs={{0,64},{32,96},{64,128},{96,160},{128,192},{160,224},{192,0},{224,... | collective-permute-start | bytes 811016 | tf_op jit(solution)/shard_map/ppermute | solution.py:316
  99.8 8.0 %collective-permute-start.18 = (f32[176,384]{1,0:T(8,128)S(1)}, f32[176,384]{1,0:T(8,128)S(1)}, u32[]{:S(2)}, u32[]{:S(2)}) collective-permute-start(f32[176,384]{1,0:T(8,128)S(1)} %pad_maximum_fusion.4), channel_id=1, source_target_pairs={{0,192},{32,224},{64,0},{96,32},{128,64},{160,96},{192,128},{224,1... | collective-permute-start | bytes 811016 | tf_op jit(solution)/shard_map/ppermute | solution.py:317
  102.6 9.1 %collective-permute-start.19 = (f32[96,384]{1,0:T(8,128)S(1)}, f32[96,384]{1,0:T(8,128)S(1)}, u32[]{:S(2)}, u32[]{:S(2)}) collective-permute-start(f32[96,384]{1,0:T(8,128)S(1)} %get-tuple-element.44), channel_id=1, source_target_pairs={{0,128},{32,160},{64,192},{96,224},{128,0},{160,32},{192,64},{224,... | collective-permute-start | bytes 442376 | tf_op jit(solution)/shard_map/ppermute | solution.py:315
  111.7 2.9 %collective-permute-start.20 = (f32[256,384]{1,0:T(8,128)S(1)}, f32[256,384]{1,0:T(8,128)S(1)}, u32[]{:S(2)}, u32[]{:S(2)}) collective-permute-start(f32[256,384]{1,0:T(8,128)S(1)} %pad_maximum_fusion.2.mine_ref), channel_id=1, source_target_pairs={{0,32},{32,0},{64,96},{96,64},{128,160},{160,128},{192,224},{224,1... | collective-permute-start | bytes 1179656 | tf_op jit(solution)/shard_map/ppermute | solution.py:326

commit v11 on v10

--- a/solution.py
+++ b/solution.py
@@ -283,9 +283,9 @@
         if s == nz // 2 - 3:
             block, near, got = barrier((block, near, got))
         order += [near]
-    theirs = [lax.ppermute(part, "grp", swap) for part in jnp.split(got, 2)]
+    theirs = [lax.ppermute(got, "grp", swap)]
     end = z_step(half_of(block))
-    order += [block, y_step(block), end, y_step(end)]
+    order += [block, y_step(block)]
 
     held = pl.pallas_call(
         functools.partial(join_tiles, groups, share),
@@ -307,7 +307,9 @@
             compiler_params=limit,
         )(*parts, held)
 
-    early, late = sums(order[:6]), order[6:]
+    early = sums(order[:6])
+    end, early = barrier((end, early))
+    late = order[6:] + [end, y_step(end)]
     a, b = near_chips(early, up, down)
     *late, a, b = barrier((*late, a, b))
     late = sums(late)

time: 116 us -> 118 us (1.017)
  waiting for transfers between devices: 58.1 us -> 56 us
  local copies, waits for them, and re-layouts: 6.1 us -> 8.01 us
  starting transfers between devices: 35.5 us -> 37.3 us
    ppermute x1, waiting for transfers between devices: 4.32 us -> 9.25 us  [body(): lax.ppermute(jnp.concatenate([late[1], early[1, :h] + a[:h]]), 'grp', up)]
    ppermute x1, waiting for transfers between devices: 3.81 us -> 0.01 us  [body(): c = lax.ppermute(late[2], 'grp', opposite)]
    unnamed x8 -> x12, local copies, waits for them, and re-layouts: 4.15 us -> 7.93 us
    ppermute x5, starting transfers between devices: 14.3 us -> 17.1 us  [z_step(): return lax.ppermute(block, ('grp', 'col'), along)]
    ppermute x1, waiting for transfers between devices: 2.7 us -> 0.01 us  [near_chips(): a = lax.ppermute(jnp.concatenate([p[2, :h], p[1, h:]]), 'grp', up)]
    all_to_all x1, waiting for transfers between devices: 5.86 us -> 3.24 us  [body(): lax.all_to_all(packed, ('grp', 'row'), 0, 0, axis_index_groups=pairs, til...]
    ppermute x5, waiting for transfers between devices: 7.61 us -> 9.92 us  [y_step(): return lax.ppermute(block, ('grp', 'row'), beside)]
    ppermute x5, waiting for transfers between devices: 20.4 us -> 22.5 us  [z_step(): return lax.ppermute(block, ('grp', 'col'), along)]
  transfers between devices with their start and end apart: 23 -> 22, of which waited for: 15 -> 13; matrix products, arithmetic and copies ran while one was open for 5% -> 3% of each run, Pallas kernels for 9% -> 9%
where the time goes in v11:
time: 118 us
  waiting for transfers between devices  56 us (47%)
  starting transfers between devices  37.3 us (32%)
  Pallas kernels  12.9 us (11%)
  local copies, waits for them, and re-layouts  8.01 us (7%)
  other arithmetic  3.44 us (3%)
    ppermute x5, waiting for transfers between devices, z_step(): return lax.ppermute(block, ('grp', 'col'), along)  22.5 us
    ppermute x5, starting transfers between devices, z_step(): return lax.ppermute(block, ('grp', 'col'), along)  17.1 us
    ppermute x5, waiting for transfers between devices, y_step(): return lax.ppermute(block, ('grp', 'row'), beside)  9.92 us
    ppermute x1, waiting for transfers between devices, body(): lax.ppermute(jnp.concatenate([late[1], early[1, :h] + a[:h]]), 'grp', up)  9.25 us
    unnamed x12, local copies, waits for them, and re-layouts  7.93 us
    all_to_all x1, waiting for transfers between devices, body(): lax.all_to_all(amplitudes[0].reshape(groups, octet, cap), 'grp', 0, 0, ti...  7.59 us
    all_to_all x1, starting transfers between devices, body(): lax.all_to_all(packed, ('grp', 'row'), 0, 0, axis_index_groups=pairs, til...  4.83 us
    all_to_all x1, starting transfers between devices, body(): lax.all_to_all(amplitudes[0].reshape(groups, octet, cap), 'grp', 0, 0, ti...  4.15 us
  transfers between devices with their start and end apart: 22, of which 13 were waited for; matrix products, arithmetic and copies ran while one was open for 3% of the time, Pallas kernels for 9%

profile of v11, /device:TPU:1, one launch (start us, length us, event | category | flops | bytes accessed | tf_op | source)
XLA Modules:
  0.0 117.9 jit_solution(12903172705559191335)
XLA Ops:
  0.0 3.2 %collective-permute-start = (bf16[4608,384]{1,0:T(8,128)(2,1)}, bf16[4608,384]{1,0:T(8,128)(2,1)S(1)}, u32[]{:S(2)}, u32[]{:S(2)}) collective-permute-start(bf16[4608,384]{1,0:T(8,128)(2,1)} %bitcast.32), channel_id=1, source_target_pairs={{0,32},{32,0},{64,96},{96,64},{128,160},{160,128},{192,224},{224,1... | collective-permute-start | bytes 10616840 | tf_op jit(solution)/shard_map/ppermute | solution.py:228
  3.2 4.1 %all-to-all-start = ((bf16[8,8,4608]{2,1,0:T(8,128)(2,1)}), bf16[8,8,4608]{2,1,0:T(8,128)(2,1)}, u32[]{:S(2)}, u32[]{:S(2)}) async-start(bf16[8,8,4608]{2,1,0:T(8,128)(2,1)} %bitcast.35), calls=%async_computation | async-start | bytes 1179648 | tf_op jit(solution)/shard_map/all_to_all | solution.py:229
  7.4 0.7 pad_add_fusion.both_ref
  8.1 2.0 %shard_map.46.list_ref = s32[96]{0:T(128)S(1)} custom-call(s32[2,8]{1,0:T(2,128)S(1)} %pad_add_fusion.both_ref), custom_call_target="tpu_custom_call" | custom-call | tf_op jit(solution)/shard_map/pallas_call | solution.py:232
  10.0 7.6 %all-to-all-done.src_ref = bf16[8,8,4608]{2,1,0:T(8,128)(2,1)} async-done(((bf16[8,8,4608]{2,1,0:T(8,128)(2,1)}), bf16[8,8,4608]{2,1,0:T(8,128)(2,1)}, u32[]{:S(2)}, u32[]{:S(2)}) %all-to-all-start) | async-done | bytes 589856 | tf_op jit(solution)/shard_map/all_to_all | solution.py:229
  17.6 1.9 %shard_map.47 = bf16[16,8,1536]{2,1,0:T(8,128)(2,1)S(1)} custom-call(s32[96]{0:T(128)S(1)} %shard_map.46.list_ref, bf16[8,8,4608]{2,1,0:T(8,128)(2,1)} %all-to-all-done.src_ref), custom_call_target="tpu_custom_call" | custom-call | tf_op jit(solution)/shard_map/pallas_call | solution.py:241
  19.5 0.0 copy-start.5
  19.5 0.7 copy-done.5
  20.2 4.8 %all-to-all-start.1 = ((bf16[16,8,1536]{2,1,0:T(8,128)(2,1)}), bf16[16,8,1536]{2,1,0:T(8,128)(2,1)}, u32[]{:S(2)}, u32[]{:S(2)}) async-start(bf16[16,8,1536]{2,1,0:T(8,128)(2,1)} %copy-done.5), calls=%async_computation.1 | async-start | bytes 786432 | tf_op jit(solution)/shard_map/all_to_all | solution.py:249
  25.1 0.0 collective-permute-done.other_ref
  25.1 0.0 copy-start
  25.1 2.0 %copy-done = bf16[1,4608,384]{2,1,0:T(8,128)(2,1)S(1)} copy-done((bf16[1,4608,384]{2,1,0:T(8,128)(2,1)S(1)}, bf16[1,4608,384]{2,1,0:T(8,128)(2,1)}, u32[]{:S(2)}) %copy-start) | copy-done | bytes 3538968
  27.1 2.4 %shard_map.48 = bf16[3072,384]{1,0:T(8,128)(2,1)S(1)} custom-call(s32[2,8]{1,0:T(2,128)S(1)} %pad_add_fusion.both_ref, bf16[4608,384]{1,0:T(8,128)(2,1)S(1)} %bitcast.33, bf16[4608,384]{1,0:T(8,128)(2,1)S(1)} %collective-permute-done.other_ref), custom_call_target="tpu_custom_call" | custom-call | tf_op jit(solution)/shard_map/pallas_call | solution.py:253
  29.5 0.0 copy-start.2
  29.5 1.7 %copy-done.2 = bf16[4608,384]{1,0:T(8,128)(2,1)} copy-done((bf16[4608,384]{1,0:T(8,128)(2,1)}, bf16[4608,384]{1,0:T(8,128)(2,1)S(1)}, u32[]{:S(2)}) %copy-start.2) | copy-done | bytes 3538968
  31.2 1.4 %copy-done.4 = bf16[3072,384]{1,0:T(8,128)(2,1)} copy-done((bf16[3072,384]{1,0:T(8,128)(2,1)}, bf16[3072,384]{1,0:T(8,128)(2,1)S(1)}, u32[]{:S(2)}) %copy-start.4) | copy-done | bytes 2359320
  32.7 3.2 %all-to-all-done.1 = bf16[16,8,1536]{2,1,0:T(8,128)(2,1)} async-done(((bf16[16,8,1536]{2,1,0:T(8,128)(2,1)}), bf16[16,8,1536]{2,1,0:T(8,128)(2,1)}, u32[]{:S(2)}, u32[]{:S(2)}) %all-to-all-start.1) | async-done | bytes 393248 | tf_op jit(solution)/shard_map/all_to_all | solution.py:249
  35.9 0.4 collective-permute-start.7
  36.4 0.0 collective-permute-start.2
  36.4 5.3 %collective-permute-start.1 = (bf16[16,8,1536]{2,1,0:T(8,128)(2,1)}, bf16[16,8,1536]{2,1,0:T(8,128)(2,1)}, u32[]{:S(2)}, u32[]{:S(2)}) collective-permute-start(bf16[16,8,1536]{2,1,0:T(8,128)(2,1)} %all-to-all-done.1), channel_id=1, source_target_pairs={{0,1},{1,2},{2,3},{3,4},{4,5},{5,6},{6,7},{7,0},{32,39},{33,32},{3... | collective-permute-start | bytes 1179656 | tf_op jit(solution)/shard_map/ppermute | solution.py:268
  41.6 0.0 collective-permute-done.2
  41.6 2.1 %collective-permute-start.3 = (bf16[16,8,1536]{2,1,0:T(8,128)(2,1)}, bf16[16,8,1536]{2,1,0:T(8,128)(2,1)}, u32[]{:S(2)}, u32[]{:S(2)}) collective-permute-start(bf16[16,8,1536]{2,1,0:T(8,128)(2,1)} %collective-permute-done.2), channel_id=1, source_target_pairs={{0,1},{1,2},{2,3},{3,4},{4,5},{5,6},{6,7},{7,0},{32,39},{33,32},{3... | collective-permute-start | bytes 1179656 | tf_op jit(solution)/shard_map/ppermute | solution.py:268
  43.7 1.3 %fusion.1.refs_0_ = bf16[2,8,8,1536]{3,2,1,0:T(8,128)(2,1)S(1)} fusion(bf16[1,16,8,1536]{3,2,1,0:T(8,128)(2,1)} %bitcast.6, bf16[1,16,8,1536]{3,2,1,0:T(8,128)(2,1)} %bitcast.7, pred[]{:T(512)S(6)} %eq.4), kind=kLoop, calls=%fused_computation.4 | loop fusion | flops 589824 | bytes 1179649 | tf_op jit(solution)/shard_map/jit(_where)/select_n | solution.py:265
  45.0 0.5 collective-permute-start.4
  45.5 1.2 %collective-permute-done.1 = bf16[16,8,1536]{2,1,0:T(8,128)(2,1)} collective-permute-done((bf16[16,8,1536]{2,1,0:T(8,128)(2,1)}, bf16[16,8,1536]{2,1,0:T(8,128)(2,1)}, u32[]{:S(2)}, u32[]{:S(2)}) %collective-permute-start.1) | collective-permute-done | bytes 393248 | tf_op jit(solution)/shard_map/ppermute | solution.py:268
  46.7 4.2 %collective-permute-done.3 = bf16[16,8,1536]{2,1,0:T(8,128)(2,1)} collective-permute-done((bf16[16,8,1536]{2,1,0:T(8,128)(2,1)}, bf16[16,8,1536]{2,1,0:T(8,128)(2,1)}, u32[]{:S(2)}, u32[]{:S(2)}) %collective-permute-start.3) | collective-permute-done | bytes 393248 | tf_op jit(solution)/shard_map/ppermute | solution.py:268
  50.9 1.2 %pad_maximum_fusion.refs_2_ = bf16[2,16,8,1536]{3,2,1,0:T(8,128)(2,1)S(1)} fusion(bf16[1,16,8,1536]{3,2,1,0:T(8,128)(2,1)} %bitcast.5, bf16[1,16,8,1536]{3,2,1,0:T(8,128)(2,1)} %bitcast.4), kind=kLoop, calls=%fused_computation | loop fusion | flops 393216 | bytes 1572864 | tf_op jit(solution)/shard_map/stack | solution.py:276
  52.1 1.2 %collective-permute-done.4.refs_1_ = bf16[2,8,8,1536]{3,2,1,0:T(8,128)(2,1)S(1)} collective-permute-done((bf16[2,8,8,1536]{3,2,1,0:T(8,128)(2,1)S(1)}, bf16[2,8,8,1536]{3,2,1,0:T(8,128)(2,1)S(1)}, u32[]{:S(2)}, u32[]{:S(2)}) %collective-permute-start.4) | collective-permute-done | bytes 393248 | tf_op jit(solution)/shard_map/ppermute | solution.py:271
  53.3 2.3 %collective-permute-start.5 = (bf16[2,16,8,1536]{3,2,1,0:T(8,128)(2,1)S(1)}, bf16[2,16,8,1536]{3,2,1,0:T(8,128)(2,1)S(1)}, u32[]{:S(2)}, u32[]{:S(2)}) collective-permute-start(bf16[2,16,8,1536]{3,2,1,0:T(8,128)(2,1)S(1)} %pad_maximum_fusion.refs_2_), channel_id=1, source_target_pairs={{0,1},{1,2},{2,3},{3,4},{4,5},{5,6},{6,7},{7,0},{32,39},{33,32},{3... | collective-permute-start | bytes 2359304 | tf_op jit(solution)/shard_map/ppermute | solution.py:268
  55.6 0.4 collective-permute-start.6
  56.0 8.6 %collective-permute-done.5.refs_4_ = bf16[2,16,8,1536]{3,2,1,0:T(8,128)(2,1)S(1)} collective-permute-done((bf16[2,16,8,1536]{3,2,1,0:T(8,128)(2,1)S(1)}, bf16[2,16,8,1536]{3,2,1,0:T(8,128)(2,1)S(1)}, u32[]{:S(2)}, u32[]{:S(2)}) %collective-permute-start.5) | collective-permute-done | bytes 786464 | tf_op jit(solution)/shard_map/ppermute | solution.py:268
  64.6 3.1 %collective-permute-done.6.refs_3_ = bf16[2,16,8,1536]{3,2,1,0:T(8,128)(2,1)S(1)} collective-permute-done((bf16[2,16,8,1536]{3,2,1,0:T(8,128)(2,1)S(1)}, bf16[2,16,8,1536]{3,2,1,0:T(8,128)(2,1)S(1)}, u32[]{:S(2)}, u32[]{:S(2)}) %collective-permute-start.6) | collective-permute-done | bytes 786464 | tf_op jit(solution)/shard_map/ppermute | solution.py:271
  67.6 0.0 collective-permute-done.7.got_ref
  67.6 0.0 collective-permute-start.11
  67.6 4.3 %collective-permute-start.8 = (bf16[2,16,8,1536]{3,2,1,0:T(8,128)(2,1)S(1)}, bf16[2,16,8,1536]{3,2,1,0:T(8,128)(2,1)S(1)}, u32[]{:S(2)}, u32[]{:S(2)}) collective-permute-start(bf16[2,16,8,1536]{3,2,1,0:T(8,128)(2,1)S(1)} %collective-permute-done.5.refs_4_), channel_id=1, source_target_pairs={{0,1},{1,2},{2,3},{3,4},{4,5},{5,6},{6,7},{7,0},{32,39},{33,32},{3... | collective-permute-start | bytes 2359304 | tf_op jit(solution)/shard_map/ppermute | solution.py:268
  72.0 0.4 collective-permute-start.10
  72.4 8.5 %collective-permute-done.8.refs_0_ = bf16[2,16,8,1536]{3,2,1,0:T(8,128)(2,1)S(1)} collective-permute-done((bf16[2,16,8,1536]{3,2,1,0:T(8,128)(2,1)S(1)}, bf16[2,16,8,1536]{3,2,1,0:T(8,128)(2,1)S(1)}, u32[]{:S(2)}, u32[]{:S(2)}) %collective-permute-start.8) | collective-permute-done | bytes 786464 | tf_op jit(solution)/shard_map/ppermute | solution.py:268
  80.9 3.2 %collective-permute-start.9 = (bf16[2,8,8,1536]{3,2,1,0:T(8,128)(2,1)S(1)}, bf16[2,8,8,1536]{3,2,1,0:T(8,128)(2,1)S(1)}, u32[]{:S(2)}, u32[]{:S(2)}) collective-permute-start(bf16[2,8,8,1536]{3,2,1,0:T(8,128)(2,1)S(1)} %slice_select_fusion), channel_id=1, source_target_pairs={{0,1},{1,2},{2,3},{3,4},{4,5},{5,6},{6,7},{7,0},{32,39},{33,32},{3... | collective-permute-start | bytes 1179656 | tf_op jit(solution)/shard_map/ppermute | solution.py:268
  84.1 0.4 collective-permute-start.12
  84.5 0.0 collective-permute-done.11.refs_0_
  84.5 0.0 copy-done.1
  84.5 2.0 %copy-done.3 = bf16[4608,384]{1,0:T(8,128)(2,1)S(1)} copy-done((bf16[4608,384]{1,0:T(8,128)(2,1)S(1)}, bf16[4608,384]{1,0:T(8,128)(2,1)}, u32[]{:S(2)}) %copy-start.3) | copy-done | bytes 3538968
  86.5 2.3 %shard_map.49.refs_6_.refs_4_ = bf16[3072,384]{1,0:T(8,128)(2,1)S(1)} custom-call(s32[2,8]{1,0:T(2,128)S(1)} %pad_add_fusion.both_ref, bf16[4608,384]{1,0:T(8,128)(2,1)S(1)} %bitcast.34, bf16[4608,384]{1,0:T(8,128)(2,1)S(1)} %copy-done.3, bf16[3072,384]{1,0:T(8,128)(2,1)} %collective-permute-done.7.got_ref, bf16[3072,384]{1,0:T(8,128)(2,1)S(1)} %collective-permute-done.11.refs_0_), custom_call_target="tpu_custom_call" | custom-call | tf_op jit(solution)/shard_map/pallas_call | solution.py:290
  88.9 0.0 collective-permute-done.10.refs_5_
  88.9 2.2 %shard_map.50 = f32[4,160,384]{2,1,0:T(8,128)S(1)} custom-call(bf16[2,8,8,1536]{3,2,1,0:T(8,128)(2,1)S(1)} %fusion.1.refs_0_, bf16[2,8,8,1536]{3,2,1,0:T(8,128)(2,1)S(1)} %collective-permute-done.4.refs_1_, bf16[2,16,8,1536]{3,2,1,0:T(8,128)(2,1)S(1)} %pad_maximum_fusion.refs_2_, bf16[2,16,8,1536]{3,2,1,0:T(8,128)(2,1)S(1)} %collective-permute-done.6.refs_3_, ...), custom_call_target="tpu_custom_call" | custom-call | tf_op jit(solution)/shard_map/pallas_call | solution.py:301
  91.1 0.0 collective-permute-done.9.refs_2_
  91.1 0.1 collective-permute-start.13
  91.2 0.1 collective-permute-start.15
  91.4 1.5 %collective-permute-start.14 = (f32[160,384]{1,0:T(8,128)S(1)}, f32[160,384]{1,0:T(8,128)S(1)}, u32[]{:S(2)}, u32[]{:S(2)}) collective-permute-start(f32[160,384]{1,0:T(8,128)S(1)} %pad_maximum_fusion.5), channel_id=1, source_target_pairs={{0,64},{32,96},{64,128},{96,160},{128,192},{160,224},{192,0},{224,... | collective-permute-start | bytes 737288 | tf_op jit(solution)/shard_map/ppermute | solution.py:201
  92.9 3.3 %collective-permute-done.12.refs_1_ = bf16[2,16,8,1536]{3,2,1,0:T(8,128)(2,1)S(1)} collective-permute-done((bf16[2,16,8,1536]{3,2,1,0:T(8,128)(2,1)S(1)}, bf16[2,16,8,1536]{3,2,1,0:T(8,128)(2,1)S(1)}, u32[]{:S(2)}, u32[]{:S(2)}) %collective-permute-start.12) | collective-permute-done | bytes 786464 | tf_op jit(solution)/shard_map/ppermute | solution.py:271
  96.2 2.1 %collective-permute-done.15 = f32[160,384]{1,0:T(8,128)S(1)} collective-permute-done((f32[160,384]{1,0:T(8,128)S(1)}, f32[160,384]{1,0:T(8,128)S(1)}, u32[]{:S(2)}, u32[]{:S(2)}) %collective-permute-start.15) | collective-permute-done | bytes 245792 | tf_op jit(solution)/shard_map/ppermute | solution.py:202
  98.3 0.0 collective-permute-done.14
  98.3 2.3 %collective-permute-done.13.refs_3_ = bf16[2,8,8,1536]{3,2,1,0:T(8,128)(2,1)S(1)} collective-permute-done((bf16[2,8,8,1536]{3,2,1,0:T(8,128)(2,1)S(1)}, bf16[2,8,8,1536]{3,2,1,0:T(8,128)(2,1)S(1)}, u32[]{:S(2)}, u32[]{:S(2)}) %collective-permute-start.13) | collective-permute-done | bytes 393248 | tf_op jit(solution)/shard_map/ppermute | solution.py:271
  100.6 1.4 %shard_map.51 = f32[4,96,384]{2,1,0:T(8,128)S(1)} custom-call(bf16[2,16,8,1536]{3,2,1,0:T(8,128)(2,1)S(1)} %collective-permute-done.8.refs_0_, bf16[2,16,8,1536]{3,2,1,0:T(8,128)(2,1)S(1)} %collective-permute-done.12.refs_1_, bf16[2,8,8,1536]{3,2,1,0:T(8,128)(2,1)S(1)} %collective-permute-done.9.refs_2_, ...), custom_call_target="tpu_custom_call" | custom-call | tf_op jit(solution)/shard_map/pallas_call | solution.py:301
  102.1 0.1 collective-permute-start.16
  102.2 2.7 %collective-permute-start.17 = (f32[176,384]{1,0:T(8,128)S(1)}, f32[176,384]{1,0:T(8,128)S(1)}, u32[]{:S(2)}, u32[]{:S(2)}) collective-permute-start(f32[176,384]{1,0:T(8,128)S(1)} %pad_maximum_fusion.4), channel_id=1, source_target_pairs={{0,192},{32,224},{64,0},{96,32},{128,64},{160,96},{192,128},{224,1... | collective-permute-start | bytes 811016 | tf_op jit(solution)/shard_map/ppermute | solution.py:319
  105.0 0.0 collective-permute-start.18
  105.0 9.3 %collective-permute-done.16 = f32[176,384]{1,0:T(8,128)S(1)} collective-permute-done((f32[176,384]{1,0:T(8,128)S(1)}, f32[176,384]{1,0:T(8,128)S(1)}, u32[]{:S(2)}, u32[]{:S(2)}) %collective-permute-start.16) | collective-permute-done | bytes 270368 | tf_op jit(solution)/shard_map/ppermute | solution.py:318
  114.3 0.0 collective-permute-done.17
  114.3 0.1 fusion.2
  114.3 0.0 collective-permute-done.18
  114.4 1.3 %collective-permute-start.19 = (f32[256,384]{1,0:T(8,128)S(1)}, f32[256,384]{1,0:T(8,128)S(1)}, u32[]{:S(2)}, u32[]{:S(2)}) collective-permute-start(f32[256,384]{1,0:T(8,128)S(1)} %pad_maximum_fusion.2.mine_ref), channel_id=1, source_target_pairs={{0,32},{32,0},{64,96},{96,64},{128,160},{160,128},{192,224},{224,1... | collective-permute-start | bytes 1179656 | tf_op jit(solution)/shard_map/ppermute | solution.py:328
  115.7 1.3 %collective-permute-done.19.other_ref = f32[256,384]{1,0:T(8,128)S(1)} collective-permute-done((f32[256,384]{1,0:T(8,128)S(1)}, f32[256,384]{1,0:T(8,128)S(1)}, u32[]{:S(2)}, u32[]{:S(2)}) %collective-permute-start.19) | collective-permute-done | bytes 393248 | tf_op jit(solution)/shard_map/ppermute | solution.py:328
  117.1 0.8 shard_map.52
  (15 shorter events, 0.3 us)
Async XLA Ops:
  0.0 25.1 %collective-permute-start = (bf16[4608,384]{1,0:T(8,128)(2,1)}, bf16[4608,384]{1,0:T(8,128)(2,1)S(1)}, u32[]{:S(2)}, u32[]{:S(2)}) collective-permute-start(bf16[4608,384]{1,0:T(8,128)(2,1)} %bitcast.32), channel_id=1, source_target_pairs={{0,32},{32,0},{64,96},{96,64},{128,160},{160,128},{192,224},{224,1... | collective-permute-start | bytes 10616840 | tf_op jit(solution)/shard_map/ppermute | solution.py:228
  3.2 14.4 %all-to-all-start = ((bf16[8,8,4608]{2,1,0:T(8,128)(2,1)}), bf16[8,8,4608]{2,1,0:T(8,128)(2,1)}, u32[]{:S(2)}, u32[]{:S(2)}) async-start(bf16[8,8,4608]{2,1,0:T(8,128)(2,1)} %bitcast.35), calls=%async_computation | async-start | bytes 1179648 | tf_op jit(solution)/shard_map/all_to_all | solution.py:229
  19.5 0.7 copy-start.5
  20.2 15.7 %all-to-all-start.1 = ((bf16[16,8,1536]{2,1,0:T(8,128)(2,1)}), bf16[16,8,1536]{2,1,0:T(8,128)(2,1)}, u32[]{:S(2)}, u32[]{:S(2)}) async-start(bf16[16,8,1536]{2,1,0:T(8,128)(2,1)} %copy-done.5), calls=%async_computation.1 | async-start | bytes 786432 | tf_op jit(solution)/shard_map/all_to_all | solution.py:249
  25.1 2.0 %copy-start = (bf16[1,4608,384]{2,1,0:T(8,128)(2,1)S(1)}, bf16[1,4608,384]{2,1,0:T(8,128)(2,1)}, u32[]{:S(2)}) copy-start(bf16[1,4608,384]{2,1,0:T(8,128)(2,1)} %param.5) | copy-start | bytes 10616836
  29.5 1.7 %copy-start.2 = (bf16[4608,384]{1,0:T(8,128)(2,1)}, bf16[4608,384]{1,0:T(8,128)(2,1)S(1)}, u32[]{:S(2)}) copy-start(bf16[4608,384]{1,0:T(8,128)(2,1)S(1)} %collective-permute-done.other_ref) | copy-start | bytes 10616836
  31.2 1.4 %copy-start.4 = (bf16[3072,384]{1,0:T(8,128)(2,1)}, bf16[3072,384]{1,0:T(8,128)(2,1)S(1)}, u32[]{:S(2)}) copy-start(bf16[3072,384]{1,0:T(8,128)(2,1)S(1)} %shard_map.48) | copy-start | bytes 7077892
  32.7 51.9 %copy-start.1 = (bf16[1,4608,384]{2,1,0:T(8,128)(2,1)S(1)}, bf16[1,4608,384]{2,1,0:T(8,128)(2,1)}, u32[]{:S(2)}) copy-start(bf16[1,4608,384]{2,1,0:T(8,128)(2,1)} %param.5) | copy-start | bytes 10616836
  35.9 31.7 %collective-permute-start.7 = (bf16[3072,384]{1,0:T(8,128)(2,1)}, bf16[3072,384]{1,0:T(8,128)(2,1)}, u32[]{:S(2)}, u32[]{:S(2)}) collective-permute-start(bf16[3072,384]{1,0:T(8,128)(2,1)} %copy-done.4), channel_id=1, source_target_pairs={{0,64},{32,224},{64,128},{96,32},{128,192},{160,96},{192,0},{224,1... | collective-permute-start | bytes 7077896 | tf_op jit(solution)/shard_map/ppermute | solution.py:262
  36.4 5.3 %collective-permute-start.2 = (bf16[16,8,1536]{2,1,0:T(8,128)(2,1)}, bf16[16,8,1536]{2,1,0:T(8,128)(2,1)}, u32[]{:S(2)}, u32[]{:S(2)}) collective-permute-start(bf16[16,8,1536]{2,1,0:T(8,128)(2,1)} %all-to-all-done.1), channel_id=1, source_target_pairs={{0,32},{32,0},{64,96},{96,64},{128,160},{160,128},{192,224},{224,1... | collective-permute-start | bytes 1179656 | tf_op jit(solution)/shard_map/ppermute | solution.py:273
  36.4 10.3 %collective-permute-start.1 = (bf16[16,8,1536]{2,1,0:T(8,128)(2,1)}, bf16[16,8,1536]{2,1,0:T(8,128)(2,1)}, u32[]{:S(2)}, u32[]{:S(2)}) collective-permute-start(bf16[16,8,1536]{2,1,0:T(8,128)(2,1)} %all-to-all-done.1), channel_id=1, source_target_pairs={{0,1},{1,2},{2,3},{3,4},{4,5},{5,6},{6,7},{7,0},{32,39},{33,32},{3... | collective-permute-start | bytes 1179656 | tf_op jit(solution)/shard_map/ppermute | solution.py:268
  41.6 9.2 %collective-permute-start.3 = (bf16[16,8,1536]{2,1,0:T(8,128)(2,1)}, bf16[16,8,1536]{2,1,0:T(8,128)(2,1)}, u32[]{:S(2)}, u32[]{:S(2)}) collective-permute-start(bf16[16,8,1536]{2,1,0:T(8,128)(2,1)} %collective-permute-done.2), channel_id=1, source_target_pairs={{0,1},{1,2},{2,3},{3,4},{4,5},{5,6},{6,7},{7,0},{32,39},{33,32},{3... | collective-permute-start | bytes 1179656 | tf_op jit(solution)/shard_map/ppermute | solution.py:268
  45.0 8.3 %collective-permute-start.4 = (bf16[2,8,8,1536]{3,2,1,0:T(8,128)(2,1)S(1)}, bf16[2,8,8,1536]{3,2,1,0:T(8,128)(2,1)S(1)}, u32[]{:S(2)}, u32[]{:S(2)}) collective-permute-start(bf16[2,8,8,1536]{3,2,1,0:T(8,128)(2,1)S(1)} %fusion.1.refs_0_), channel_id=1, source_target_pairs={{0,24},{8,0},{16,8},{24,16},{32,40},{40,48},{48,56},{56,32},{64,88... | collective-permute-start | bytes 1179656 | tf_op jit(solution)/shard_map/ppermute | solution.py:271
  53.3 11.2 %collective-permute-start.5 = (bf16[2,16,8,1536]{3,2,1,0:T(8,128)(2,1)S(1)}, bf16[2,16,8,1536]{3,2,1,0:T(8,128)(2,1)S(1)}, u32[]{:S(2)}, u32[]{:S(2)}) collective-permute-start(bf16[2,16,8,1536]{3,2,1,0:T(8,128)(2,1)S(1)} %pad_maximum_fusion.refs_2_), channel_id=1, source_target_pairs={{0,1},{1,2},{2,3},{3,4},{4,5},{5,6},{6,7},{7,0},{32,39},{33,32},{3... | collective-permute-start | bytes 2359304 | tf_op jit(solution)/shard_map/ppermute | solution.py:268
  55.6 12.1 %collective-permute-start.6 = (bf16[2,16,8,1536]{3,2,1,0:T(8,128)(2,1)S(1)}, bf16[2,16,8,1536]{3,2,1,0:T(8,128)(2,1)S(1)}, u32[]{:S(2)}, u32[]{:S(2)}) collective-permute-start(bf16[2,16,8,1536]{3,2,1,0:T(8,128)(2,1)S(1)} %pad_maximum_fusion.refs_2_), channel_id=1, source_target_pairs={{0,24},{8,0},{16,8},{24,16},{32,40},{40,48},{48,56},{56,32},{64,88... | collective-permute-start | bytes 2359304 | tf_op jit(solution)/shard_map/ppermute | solution.py:271
  67.6 16.9 %collective-permute-start.11 = (bf16[3072,384]{1,0:T(8,128)(2,1)}, bf16[3072,384]{1,0:T(8,128)(2,1)S(1)}, u32[]{:S(2)}, u32[]{:S(2)}) collective-permute-start(bf16[3072,384]{1,0:T(8,128)(2,1)} %collective-permute-done.7.got_ref), channel_id=1, source_target_pairs={{0,32},{32,0},{64,96},{96,64},{128,160},{160,128},{192,224},{224,1... | collective-permute-start | bytes 7077896 | tf_op jit(solution)/shard_map/ppermute | solution.py:286
  67.6 13.3 %collective-permute-start.8 = (bf16[2,16,8,1536]{3,2,1,0:T(8,128)(2,1)S(1)}, bf16[2,16,8,1536]{3,2,1,0:T(8,128)(2,1)S(1)}, u32[]{:S(2)}, u32[]{:S(2)}) collective-permute-start(bf16[2,16,8,1536]{3,2,1,0:T(8,128)(2,1)S(1)} %collective-permute-done.5.refs_4_), channel_id=1, source_target_pairs={{0,1},{1,2},{2,3},{3,4},{4,5},{5,6},{6,7},{7,0},{32,39},{33,32},{3... | collective-permute-start | bytes 2359304 | tf_op jit(solution)/shard_map/ppermute | solution.py:268
  72.0 16.9 %collective-permute-start.10 = (bf16[2,16,8,1536]{3,2,1,0:T(8,128)(2,1)S(1)}, bf16[2,16,8,1536]{3,2,1,0:T(8,128)(2,1)S(1)}, u32[]{:S(2)}, u32[]{:S(2)}) collective-permute-start(bf16[2,16,8,1536]{3,2,1,0:T(8,128)(2,1)S(1)} %collective-permute-done.5.refs_4_), channel_id=1, source_target_pairs={{0,24},{8,0},{16,8},{24,16},{32,40},{40,48},{48,56},{56,32},{64,88... | collective-permute-start | bytes 2359304 | tf_op jit(solution)/shard_map/ppermute | solution.py:271
  80.9 10.1 %collective-permute-start.9 = (bf16[2,8,8,1536]{3,2,1,0:T(8,128)(2,1)S(1)}, bf16[2,8,8,1536]{3,2,1,0:T(8,128)(2,1)S(1)}, u32[]{:S(2)}, u32[]{:S(2)}) collective-permute-start(bf16[2,8,8,1536]{3,2,1,0:T(8,128)(2,1)S(1)} %slice_select_fusion), channel_id=1, source_target_pairs={{0,1},{1,2},{2,3},{3,4},{4,5},{5,6},{6,7},{7,0},{32,39},{33,32},{3... | collective-permute-start | bytes 1179656 | tf_op jit(solution)/shard_map/ppermute | solution.py:268
  84.1 12.1 %collective-permute-start.12 = (bf16[2,16,8,1536]{3,2,1,0:T(8,128)(2,1)S(1)}, bf16[2,16,8,1536]{3,2,1,0:T(8,128)(2,1)S(1)}, u32[]{:S(2)}, u32[]{:S(2)}) collective-permute-start(bf16[2,16,8,1536]{3,2,1,0:T(8,128)(2,1)S(1)} %collective-permute-done.8.refs_0_), channel_id=1, source_target_pairs={{0,24},{8,0},{16,8},{24,16},{32,40},{40,48},{48,56},{56,32},{64,88... | collective-permute-start | bytes 2359304 | tf_op jit(solution)/shard_map/ppermute | solution.py:271
  84.5 2.0 %copy-start.3 = (bf16[4608,384]{1,0:T(8,128)(2,1)S(1)}, bf16[4608,384]{1,0:T(8,128)(2,1)}, u32[]{:S(2)}) copy-start(bf16[4608,384]{1,0:T(8,128)(2,1)} %copy-done.2) | copy-start | bytes 10616836
  91.1 9.5 %collective-permute-start.13 = (bf16[2,8,8,1536]{3,2,1,0:T(8,128)(2,1)S(1)}, bf16[2,8,8,1536]{3,2,1,0:T(8,128)(2,1)S(1)}, u32[]{:S(2)}, u32[]{:S(2)}) collective-permute-start(bf16[2,8,8,1536]{3,2,1,0:T(8,128)(2,1)S(1)} %collective-permute-done.9.refs_2_), channel_id=1, source_target_pairs={{0,24},{8,0},{16,8},{24,16},{32,40},{40,48},{48,56},{56,32},{64,88... | collective-permute-start | bytes 1179656 | tf_op jit(solution)/shard_map/ppermute | solution.py:271
  91.2 7.1 %collective-permute-start.15 = (f32[160,384]{1,0:T(8,128)S(1)}, f32[160,384]{1,0:T(8,128)S(1)}, u32[]{:S(2)}, u32[]{:S(2)}) collective-permute-start(f32[160,384]{1,0:T(8,128)S(1)} %pad_maximum_fusion.6), channel_id=1, source_target_pairs={{0,192},{32,224},{64,0},{96,32},{128,64},{160,96},{192,128},{224,1... | collective-permute-start | bytes 737288 | tf_op jit(solution)/shard_map/ppermute | solution.py:202
  91.4 7.0 %collective-permute-start.14 = (f32[160,384]{1,0:T(8,128)S(1)}, f32[160,384]{1,0:T(8,128)S(1)}, u32[]{:S(2)}, u32[]{:S(2)}) collective-permute-start(f32[160,384]{1,0:T(8,128)S(1)} %pad_maximum_fusion.5), channel_id=1, source_target_pairs={{0,64},{32,96},{64,128},{96,160},{128,192},{160,224},{192,0},{224,... | collective-permute-start | bytes 737288 | tf_op jit(solution)/shard_map/ppermute | solution.py:201
  102.1 12.1 %collective-permute-start.16 = (f32[176,384]{1,0:T(8,128)S(1)}, f32[176,384]{1,0:T(8,128)S(1)}, u32[]{:S(2)}, u32[]{:S(2)}) collective-permute-start(f32[176,384]{1,0:T(8,128)S(1)} %pad_maximum_fusion.3), channel_id=1, source_target_pairs={{0,64},{32,96},{64,128},{96,160},{128,192},{160,224},{192,0},{224,... | collective-permute-start | bytes 811016 | tf_op jit(solution)/shard_map/ppermute | solution.py:318
  102.2 12.0 %collective-permute-start.17 = (f32[176,384]{1,0:T(8,128)S(1)}, f32[176,384]{1,0:T(8,128)S(1)}, u32[]{:S(2)}, u32[]{:S(2)}) collective-permute-start(f32[176,384]{1,0:T(8,128)S(1)} %pad_maximum_fusion.4), channel_id=1, source_target_pairs={{0,192},{32,224},{64,0},{96,32},{128,64},{160,96},{192,128},{224,1... | collective-permute-start | bytes 811016 | tf_op jit(solution)/shard_map/ppermute | solution.py:319
  105.0 9.4 %collective-permute-start.18 = (f32[96,384]{1,0:T(8,128)S(1)}, f32[96,384]{1,0:T(8,128)S(1)}, u32[]{:S(2)}, u32[]{:S(2)}) collective-permute-start(f32[96,384]{1,0:T(8,128)S(1)} %get-tuple-element.46), channel_id=1, source_target_pairs={{0,128},{32,160},{64,192},{96,224},{128,0},{160,32},{192,64},{224,... | collective-permute-start | bytes 442376 | tf_op jit(solution)/shard_map/ppermute | solution.py:317
  114.4 2.7 %collective-permute-start.19 = (f32[256,384]{1,0:T(8,128)S(1)}, f32[256,384]{1,0:T(8,128)S(1)}, u32[]{:S(2)}, u32[]{:S(2)}) collective-permute-start(f32[256,384]{1,0:T(8,128)S(1)} %pad_maximum_fusion.2.mine_ref), channel_id=1, source_target_pairs={{0,32},{32,0},{64,96},{96,64},{128,160},{160,128},{192,224},{224,1... | collective-permute-start | bytes 1179656 | tf_op jit(solution)/shard_map/ppermute | solution.py:328

commit v12 on v10

--- a/solution.py
+++ b/solution.py
@@ -202,6 +202,23 @@
     return a, lax.ppermute(jnp.concatenate([p[2, h:], p[3, :h]]), "grp", down)
 
 
+def nothing(*refs):
+    pass
+
+
+def collect(*arrays):
+    shapes = tuple(jax.ShapeDtypeStruct(array.shape, array.dtype) for array in arrays)
+    return pl.pallas_call(
+        nothing,
+        out_shape=shapes,
+        in_specs=[ANY] * len(arrays),
+        out_specs=(ANY,) * len(arrays),
+        input_output_aliases={i: i for i in range(len(arrays))},
+        cost_estimate=pl.CostEstimate(flops=3000000000, bytes_accessed=0, transcendentals=0),
+        compiler_params=pltpu.CompilerParams(vmem_limit_bytes=2**20),
+    )(*arrays)
+
+
 def body(amplitudes, integrals, block_tiles, assign):
     groups = assign.shape[0]
     _, rows, cap = amplitudes.shape
@@ -309,6 +326,7 @@
 
     early, late = sums(order[:6]), order[6:]
     a, b = near_chips(early, up, down)
+    a, b = collect(a, b)
     *late, a, b = barrier((*late, a, b))
     late = sums(late)
     h, n = early.shape[1] // 2, late.shape[1]

time: 116 us -> 116 us (level)
    ppermute x5, waiting for transfers between devices: 7.61 us -> 6.07 us  [y_step(): return lax.ppermute(block, ('grp', 'row'), beside)]
    ppermute x1, waiting for transfers between devices: 3.55 us -> 5.08 us  [near_chips(): return (a, lax.ppermute(jnp.concatenate([p[2, h:], p[3, :h]]), 'grp', down))]
  transfers between devices with their start and end apart: 23 -> 23, of which waited for: 15 -> 14; matrix products, arithmetic and copies ran while one was open for 5% -> 5% of each run, Pallas kernels for 9% -> 8%
where the time goes in v12:
time: 116 us; the launch traced here: 115 us
  waiting for transfers between devices  58.8 us (51%)
  starting transfers between devices  35.2 us (30%)
  Pallas kernels  11.4 us (10%)
  local copies, waits for them, and re-layouts  6.09 us (5%)
  other arithmetic  3.44 us (3%)
    ppermute x5, waiting for transfers between devices, z_step(): return lax.ppermute(block, ('grp', 'col'), along)  20.4 us
    ppermute x5, starting transfers between devices, z_step(): return lax.ppermute(block, ('grp', 'col'), along)  14.3 us
    all_to_all x1, waiting for transfers between devices, body(): lax.all_to_all(amplitudes[0].reshape(groups, octet, cap), 'grp', 0, 0, ti...  7.58 us
    all_to_all x1, waiting for transfers between devices, body(): lax.all_to_all(packed, ('grp', 'row'), 0, 0, axis_index_groups=pairs, til...  6.55 us
    ppermute x5, waiting for transfers between devices, y_step(): return lax.ppermute(block, ('grp', 'row'), beside)  6.07 us
    ppermute x1, waiting for transfers between devices, body(): lax.ppermute(jnp.concatenate([late[1], early[1, :h] + a[:h]]), 'grp', up)  5.18 us
    ppermute x1, waiting for transfers between devices, near_chips(): return (a, lax.ppermute(jnp.concatenate([p[2, h:], p[3, :h]]), 'grp', down))  5.08 us
    all_to_all x1, starting transfers between devices, body(): lax.all_to_all(packed, ('grp', 'row'), 0, 0, axis_index_groups=pairs, til...  4.83 us
  transfers between devices with their start and end apart: 23, of which 14 were waited for; matrix products, arithmetic and copies ran while one was open for 5% of the time, Pallas kernels for 8%

profile of v12, /device:TPU:1, one launch (start us, length us, event | category | flops | bytes accessed | tf_op | source)
XLA Modules:
  0.0 115.2 jit_solution(13597416001316431567)
XLA Ops:
  0.0 3.2 %collective-permute-start = (bf16[4608,384]{1,0:T(8,128)(2,1)}, bf16[4608,384]{1,0:T(8,128)(2,1)S(1)}, u32[]{:S(2)}, u32[]{:S(2)}) collective-permute-start(bf16[4608,384]{1,0:T(8,128)(2,1)} %bitcast.40), channel_id=1, source_target_pairs={{0,32},{32,0},{64,96},{96,64},{128,160},{160,128},{192,224},{224,1... | collective-permute-start | bytes 10616840 | tf_op jit(solution)/shard_map/ppermute | solution.py:245
  3.2 4.1 %all-to-all-start = ((bf16[8,8,4608]{2,1,0:T(8,128)(2,1)}), bf16[8,8,4608]{2,1,0:T(8,128)(2,1)}, u32[]{:S(2)}, u32[]{:S(2)}) async-start(bf16[8,8,4608]{2,1,0:T(8,128)(2,1)} %bitcast.43), calls=%async_computation | async-start | bytes 1179648 | tf_op jit(solution)/shard_map/all_to_all | solution.py:246
  7.4 0.7 pad_add_fusion.both_ref
  8.1 1.9 %shard_map.46.list_ref = s32[96]{0:T(128)S(1)} custom-call(s32[2,8]{1,0:T(2,128)S(1)} %pad_add_fusion.both_ref), custom_call_target="tpu_custom_call" | custom-call | tf_op jit(solution)/shard_map/pallas_call | solution.py:249
  10.0 7.6 %all-to-all-done.src_ref = bf16[8,8,4608]{2,1,0:T(8,128)(2,1)} async-done(((bf16[8,8,4608]{2,1,0:T(8,128)(2,1)}), bf16[8,8,4608]{2,1,0:T(8,128)(2,1)}, u32[]{:S(2)}, u32[]{:S(2)}) %all-to-all-start) | async-done | bytes 589856 | tf_op jit(solution)/shard_map/all_to_all | solution.py:246
  17.6 1.9 %shard_map.47 = bf16[16,8,1536]{2,1,0:T(8,128)(2,1)S(1)} custom-call(s32[96]{0:T(128)S(1)} %shard_map.46.list_ref, bf16[8,8,4608]{2,1,0:T(8,128)(2,1)} %all-to-all-done.src_ref), custom_call_target="tpu_custom_call" | custom-call | tf_op jit(solution)/shard_map/pallas_call | solution.py:258
  19.5 0.0 copy-start.3
  19.5 0.7 copy-done.3
  20.2 4.8 %all-to-all-start.1 = ((bf16[16,8,1536]{2,1,0:T(8,128)(2,1)}), bf16[16,8,1536]{2,1,0:T(8,128)(2,1)}, u32[]{:S(2)}, u32[]{:S(2)}) async-start(bf16[16,8,1536]{2,1,0:T(8,128)(2,1)} %copy-done.3), calls=%async_computation.1 | async-start | bytes 786432 | tf_op jit(solution)/shard_map/all_to_all | solution.py:266
  25.1 0.0 collective-permute-done.other_ref
  25.1 0.0 copy-start
  25.1 2.0 %copy-done = bf16[1,4608,384]{2,1,0:T(8,128)(2,1)S(1)} copy-done((bf16[1,4608,384]{2,1,0:T(8,128)(2,1)S(1)}, bf16[1,4608,384]{2,1,0:T(8,128)(2,1)}, u32[]{:S(2)}) %copy-start) | copy-done | bytes 3538968
  27.1 0.9 shard_map.48
  27.9 1.4 %copy-done.2 = bf16[3072,384]{1,0:T(8,128)(2,1)} copy-done((bf16[3072,384]{1,0:T(8,128)(2,1)}, bf16[3072,384]{1,0:T(8,128)(2,1)S(1)}, u32[]{:S(2)}) %copy-start.2) | copy-done | bytes 2359320
  29.3 6.6 %all-to-all-done.1 = bf16[16,8,1536]{2,1,0:T(8,128)(2,1)} async-done(((bf16[16,8,1536]{2,1,0:T(8,128)(2,1)}), bf16[16,8,1536]{2,1,0:T(8,128)(2,1)}, u32[]{:S(2)}, u32[]{:S(2)}) %all-to-all-start.1) | async-done | bytes 393248 | tf_op jit(solution)/shard_map/all_to_all | solution.py:266
  35.9 0.4 collective-permute-start.7
  36.3 0.0 collective-permute-start.1
  36.3 5.3 %collective-permute-start.2 = (bf16[16,8,1536]{2,1,0:T(8,128)(2,1)}, bf16[16,8,1536]{2,1,0:T(8,128)(2,1)}, u32[]{:S(2)}, u32[]{:S(2)}) collective-permute-start(bf16[16,8,1536]{2,1,0:T(8,128)(2,1)} %all-to-all-done.1), channel_id=1, source_target_pairs={{0,1},{1,2},{2,3},{3,4},{4,5},{5,6},{6,7},{7,0},{32,39},{33,32},{3... | collective-permute-start | bytes 1179656 | tf_op jit(solution)/shard_map/ppermute | solution.py:285
  41.6 0.0 collective-permute-done.1
  41.6 2.1 %collective-permute-start.3 = (bf16[16,8,1536]{2,1,0:T(8,128)(2,1)}, bf16[16,8,1536]{2,1,0:T(8,128)(2,1)}, u32[]{:S(2)}, u32[]{:S(2)}) collective-permute-start(bf16[16,8,1536]{2,1,0:T(8,128)(2,1)} %collective-permute-done.1), channel_id=1, source_target_pairs={{0,1},{1,2},{2,3},{3,4},{4,5},{5,6},{6,7},{7,0},{32,39},{33,32},{3... | collective-permute-start | bytes 1179656 | tf_op jit(solution)/shard_map/ppermute | solution.py:285
  43.7 1.3 %fusion.1.refs_0_ = bf16[2,8,8,1536]{3,2,1,0:T(8,128)(2,1)S(1)} fusion(bf16[1,16,8,1536]{3,2,1,0:T(8,128)(2,1)} %bitcast.4, bf16[1,16,8,1536]{3,2,1,0:T(8,128)(2,1)} %bitcast.5, pred[]{:T(512)S(6)} %eq.4), kind=kLoop, calls=%fused_computation.4 | loop fusion | flops 589824 | bytes 1179649 | tf_op jit(solution)/shard_map/jit(_where)/select_n | solution.py:282
  45.0 0.5 collective-permute-start.4
  45.5 1.2 %collective-permute-done.2 = bf16[16,8,1536]{2,1,0:T(8,128)(2,1)} collective-permute-done((bf16[16,8,1536]{2,1,0:T(8,128)(2,1)}, bf16[16,8,1536]{2,1,0:T(8,128)(2,1)}, u32[]{:S(2)}, u32[]{:S(2)}) %collective-permute-start.2) | collective-permute-done | bytes 393248 | tf_op jit(solution)/shard_map/ppermute | solution.py:285
  46.7 4.2 %collective-permute-done.3 = bf16[16,8,1536]{2,1,0:T(8,128)(2,1)} collective-permute-done((bf16[16,8,1536]{2,1,0:T(8,128)(2,1)}, bf16[16,8,1536]{2,1,0:T(8,128)(2,1)}, u32[]{:S(2)}, u32[]{:S(2)}) %collective-permute-start.3) | collective-permute-done | bytes 393248 | tf_op jit(solution)/shard_map/ppermute | solution.py:285
  50.9 1.2 %pad_maximum_fusion.refs_2_ = bf16[2,16,8,1536]{3,2,1,0:T(8,128)(2,1)S(1)} fusion(bf16[1,16,8,1536]{3,2,1,0:T(8,128)(2,1)} %bitcast.7, bf16[1,16,8,1536]{3,2,1,0:T(8,128)(2,1)} %bitcast.6), kind=kLoop, calls=%fused_computation.2 | loop fusion | flops 393216 | bytes 1572864 | tf_op jit(solution)/shard_map/stack | solution.py:293
  52.1 0.0 copy-start.1
  52.1 1.2 %collective-permute-done.4.refs_1_ = bf16[2,8,8,1536]{3,2,1,0:T(8,128)(2,1)S(1)} collective-permute-done((bf16[2,8,8,1536]{3,2,1,0:T(8,128)(2,1)S(1)}, bf16[2,8,8,1536]{3,2,1,0:T(8,128)(2,1)S(1)}, u32[]{:S(2)}, u32[]{:S(2)}) %collective-permute-start.4) | collective-permute-done | bytes 393248 | tf_op jit(solution)/shard_map/ppermute | solution.py:288
  53.3 2.3 %collective-permute-start.5 = (bf16[2,16,8,1536]{3,2,1,0:T(8,128)(2,1)S(1)}, bf16[2,16,8,1536]{3,2,1,0:T(8,128)(2,1)S(1)}, u32[]{:S(2)}, u32[]{:S(2)}) collective-permute-start(bf16[2,16,8,1536]{3,2,1,0:T(8,128)(2,1)S(1)} %pad_maximum_fusion.refs_2_), channel_id=1, source_target_pairs={{0,1},{1,2},{2,3},{3,4},{4,5},{5,6},{6,7},{7,0},{32,39},{33,32},{3... | collective-permute-start | bytes 2359304 | tf_op jit(solution)/shard_map/ppermute | solution.py:285
  55.6 0.4 collective-permute-start.6
  56.0 8.6 %collective-permute-done.5.refs_4_ = bf16[2,16,8,1536]{3,2,1,0:T(8,128)(2,1)S(1)} collective-permute-done((bf16[2,16,8,1536]{3,2,1,0:T(8,128)(2,1)S(1)}, bf16[2,16,8,1536]{3,2,1,0:T(8,128)(2,1)S(1)}, u32[]{:S(2)}, u32[]{:S(2)}) %collective-permute-start.5) | collective-permute-done | bytes 786464 | tf_op jit(solution)/shard_map/ppermute | solution.py:285
  64.6 3.1 %collective-permute-done.6.refs_3_ = bf16[2,16,8,1536]{3,2,1,0:T(8,128)(2,1)S(1)} collective-permute-done((bf16[2,16,8,1536]{3,2,1,0:T(8,128)(2,1)S(1)}, bf16[2,16,8,1536]{3,2,1,0:T(8,128)(2,1)S(1)}, u32[]{:S(2)}, u32[]{:S(2)}) %collective-permute-start.6) | collective-permute-done | bytes 786464 | tf_op jit(solution)/shard_map/ppermute | solution.py:288
  67.6 0.0 collective-permute-done.7.got_ref
  67.6 1.8 %collective-permute-start.11 = (bf16[2,16,8,1536]{3,2,1,0:T(8,128)(2,1)S(1)}, bf16[2,16,8,1536]{3,2,1,0:T(8,128)(2,1)S(1)}, u32[]{:S(2)}, u32[]{:S(2)}) collective-permute-start(bf16[2,16,8,1536]{3,2,1,0:T(8,128)(2,1)S(1)} %collective-permute-done.5.refs_4_), channel_id=1, source_target_pairs={{0,1},{1,2},{2,3},{3,4},{4,5},{5,6},{6,7},{7,0},{32,39},{33,32},{3... | collective-permute-start | bytes 2359304 | tf_op jit(solution)/shard_map/ppermute | solution.py:285
  69.5 1.9 %fusion.7 = (bf16[1536,384]{1,0:T(8,128)(2,1)S(1)}, bf16[1536,384]{1,0:T(8,128)(2,1)S(1)}) fusion(bf16[3072,384]{1,0:T(8,128)(2,1)} %collective-permute-done.7.got_ref), kind=kLoop, calls=%fused_computation.31 | loop fusion | bytes 4718592 | tf_op jit(solution)/shard_map/split | solution.py:303
  71.3 0.1 collective-permute-start.10
  71.4 0.5 collective-permute-start.9
  71.9 0.4 collective-permute-start.8
  72.3 6.5 %collective-permute-done.11.refs_0_ = bf16[2,16,8,1536]{3,2,1,0:T(8,128)(2,1)S(1)} collective-permute-done((bf16[2,16,8,1536]{3,2,1,0:T(8,128)(2,1)S(1)}, bf16[2,16,8,1536]{3,2,1,0:T(8,128)(2,1)S(1)}, u32[]{:S(2)}, u32[]{:S(2)}) %collective-permute-start.11) | collective-permute-done | bytes 786464 | tf_op jit(solution)/shard_map/ppermute | solution.py:285
  78.8 2.8 %collective-permute-start.13 = (bf16[2,8,8,1536]{3,2,1,0:T(8,128)(2,1)S(1)}, bf16[2,8,8,1536]{3,2,1,0:T(8,128)(2,1)S(1)}, u32[]{:S(2)}, u32[]{:S(2)}) collective-permute-start(bf16[2,8,8,1536]{3,2,1,0:T(8,128)(2,1)S(1)} %slice_select_fusion), channel_id=1, source_target_pairs={{0,1},{1,2},{2,3},{3,4},{4,5},{5,6},{6,7},{7,0},{32,39},{33,32},{3... | collective-permute-start | bytes 1179656 | tf_op jit(solution)/shard_map/ppermute | solution.py:285
  81.6 0.4 collective-permute-start.12
  82.0 0.0 collective-permute-done.10.refs_1_
  82.0 0.0 collective-permute-done.9.refs_0_
  82.1 2.3 %shard_map.49.refs_6_.refs_4_ = bf16[3072,384]{1,0:T(8,128)(2,1)S(1)} custom-call(s32[2,8]{1,0:T(2,128)S(1)} %pad_add_fusion.both_ref, bf16[4608,384]{1,0:T(8,128)(2,1)S(1)} %bitcast.42, bf16[4608,384]{1,0:T(8,128)(2,1)S(1)} %collective-permute-done.other_ref, bf16[3072,384]{1,0:T(8,128)(2,1)} %collective-permute-done.7.got_ref, ...), custom_call_target="tpu_custom_call" | custom-call | tf_op jit(solution)/shard_map/pallas_call | solution.py:307
  84.3 0.0 collective-permute-done.8.refs_5_
  84.4 2.2 %shard_map.50 = f32[4,160,384]{2,1,0:T(8,128)S(1)} custom-call(bf16[2,8,8,1536]{3,2,1,0:T(8,128)(2,1)S(1)} %fusion.1.refs_0_, bf16[2,8,8,1536]{3,2,1,0:T(8,128)(2,1)S(1)} %collective-permute-done.4.refs_1_, bf16[2,16,8,1536]{3,2,1,0:T(8,128)(2,1)S(1)} %pad_maximum_fusion.refs_2_, bf16[2,16,8,1536]{3,2,1,0:T(8,128)(2,1)S(1)} %collective-permute-done.6.refs_3_, ...), custom_call_target="tpu_custom_call" | custom-call | tf_op jit(solution)/shard_map/pallas_call | solution.py:318
  86.6 1.5 %collective-permute-start.16 = (f32[160,384]{1,0:T(8,128)S(1)}, f32[160,384]{1,0:T(8,128)S(1)}, u32[]{:S(2)}, u32[]{:S(2)}) collective-permute-start(f32[160,384]{1,0:T(8,128)S(1)} %pad_maximum_fusion.6), channel_id=1, source_target_pairs={{0,192},{32,224},{64,0},{96,32},{128,64},{160,96},{192,128},{224,1... | collective-permute-start | bytes 737288 | tf_op jit(solution)/shard_map/ppermute | solution.py:202
  88.1 0.1 collective-permute-start.15
  88.3 0.0 collective-permute-done.13.refs_2_
  88.3 0.1 collective-permute-start.14
  88.3 5.1 %collective-permute-done.16.refs_1_ = f32[160,384]{1,0:T(8,128)S(1)} collective-permute-done((f32[160,384]{1,0:T(8,128)S(1)}, f32[160,384]{1,0:T(8,128)S(1)}, u32[]{:S(2)}, u32[]{:S(2)}) %collective-permute-start.16) | collective-permute-done | bytes 245792 | tf_op jit(solution)/shard_map/ppermute | solution.py:202
  93.4 2.7 %collective-permute-done.15.refs_0_ = f32[160,384]{1,0:T(8,128)S(1)} collective-permute-done((f32[160,384]{1,0:T(8,128)S(1)}, f32[160,384]{1,0:T(8,128)S(1)}, u32[]{:S(2)}, u32[]{:S(2)}) %collective-permute-start.15) | collective-permute-done | bytes 245792 | tf_op jit(solution)/shard_map/ppermute | solution.py:201
  96.1 1.8 %collective-permute-done.14.refs_3_ = bf16[2,8,8,1536]{3,2,1,0:T(8,128)(2,1)S(1)} collective-permute-done((bf16[2,8,8,1536]{3,2,1,0:T(8,128)(2,1)S(1)}, bf16[2,8,8,1536]{3,2,1,0:T(8,128)(2,1)S(1)}, u32[]{:S(2)}, u32[]{:S(2)}) %collective-permute-start.14) | collective-permute-done | bytes 393248 | tf_op jit(solution)/shard_map/ppermute | solution.py:288
  97.9 0.0 collective-permute-done.12.refs_1_
  97.9 1.4 %shard_map.52 = f32[4,96,384]{2,1,0:T(8,128)S(1)} custom-call(bf16[2,16,8,1536]{3,2,1,0:T(8,128)(2,1)S(1)} %collective-permute-done.11.refs_0_, bf16[2,16,8,1536]{3,2,1,0:T(8,128)(2,1)S(1)} %collective-permute-done.12.refs_1_, bf16[2,8,8,1536]{3,2,1,0:T(8,128)(2,1)S(1)} %collective-permute-done.13.refs_2_, ...), custom_call_target="tpu_custom_call" | custom-call | tf_op jit(solution)/shard_map/pallas_call | solution.py:318
  99.4 0.1 collective-permute-start.17
  99.5 2.7 %collective-permute-start.18 = (f32[176,384]{1,0:T(8,128)S(1)}, f32[176,384]{1,0:T(8,128)S(1)}, u32[]{:S(2)}, u32[]{:S(2)}) collective-permute-start(f32[176,384]{1,0:T(8,128)S(1)} %pad_maximum_fusion.4), channel_id=1, source_target_pairs={{0,192},{32,224},{64,0},{96,32},{128,64},{160,96},{192,128},{224,1... | collective-permute-start | bytes 811016 | tf_op jit(solution)/shard_map/ppermute | solution.py:335
  102.3 0.0 collective-permute-start.19
  102.3 5.2 %collective-permute-done.17 = f32[176,384]{1,0:T(8,128)S(1)} collective-permute-done((f32[176,384]{1,0:T(8,128)S(1)}, f32[176,384]{1,0:T(8,128)S(1)}, u32[]{:S(2)}, u32[]{:S(2)}) %collective-permute-start.17) | collective-permute-done | bytes 270368 | tf_op jit(solution)/shard_map/ppermute | solution.py:334
  107.5 0.0 collective-permute-done.18
  107.5 0.1 fusion.3
  107.6 3.8 %collective-permute-done.19 = f32[96,384]{1,0:T(8,128)S(1)} collective-permute-done((f32[96,384]{1,0:T(8,128)S(1)}, f32[96,384]{1,0:T(8,128)S(1)}, u32[]{:S(2)}, u32[]{:S(2)}) %collective-permute-start.19) | collective-permute-done | bytes 147488 | tf_op jit(solution)/shard_map/ppermute | solution.py:333
  111.5 1.5 %collective-permute-start.20 = (f32[256,384]{1,0:T(8,128)S(1)}, f32[256,384]{1,0:T(8,128)S(1)}, u32[]{:S(2)}, u32[]{:S(2)}) collective-permute-start(f32[256,384]{1,0:T(8,128)S(1)} %pad_maximum_fusion.2.mine_ref), channel_id=1, source_target_pairs={{0,32},{32,0},{64,96},{96,64},{128,160},{160,128},{192,224},{224,1... | collective-permute-start | bytes 1179656 | tf_op jit(solution)/shard_map/ppermute | solution.py:344
  113.0 1.3 %collective-permute-done.20.other_ref = f32[256,384]{1,0:T(8,128)S(1)} collective-permute-done((f32[256,384]{1,0:T(8,128)S(1)}, f32[256,384]{1,0:T(8,128)S(1)}, u32[]{:S(2)}, u32[]{:S(2)}) %collective-permute-start.20) | collective-permute-done | bytes 393248 | tf_op jit(solution)/shard_map/ppermute | solution.py:344
  114.4 0.8 shard_map.53
  (15 shorter events, 0.3 us)
Async XLA Ops:
  0.0 25.1 %collective-permute-start = (bf16[4608,384]{1,0:T(8,128)(2,1)}, bf16[4608,384]{1,0:T(8,128)(2,1)S(1)}, u32[]{:S(2)}, u32[]{:S(2)}) collective-permute-start(bf16[4608,384]{1,0:T(8,128)(2,1)} %bitcast.40), channel_id=1, source_target_pairs={{0,32},{32,0},{64,96},{96,64},{128,160},{160,128},{192,224},{224,1... | collective-permute-start | bytes 10616840 | tf_op jit(solution)/shard_map/ppermute | solution.py:245
  3.2 14.4 %all-to-all-start = ((bf16[8,8,4608]{2,1,0:T(8,128)(2,1)}), bf16[8,8,4608]{2,1,0:T(8,128)(2,1)}, u32[]{:S(2)}, u32[]{:S(2)}) async-start(bf16[8,8,4608]{2,1,0:T(8,128)(2,1)} %bitcast.43), calls=%async_computation | async-start | bytes 1179648 | tf_op jit(solution)/shard_map/all_to_all | solution.py:246
  19.5 0.7 copy-start.3
  20.2 15.7 %all-to-all-start.1 = ((bf16[16,8,1536]{2,1,0:T(8,128)(2,1)}), bf16[16,8,1536]{2,1,0:T(8,128)(2,1)}, u32[]{:S(2)}, u32[]{:S(2)}) async-start(bf16[16,8,1536]{2,1,0:T(8,128)(2,1)} %copy-done.3), calls=%async_computation.1 | async-start | bytes 786432 | tf_op jit(solution)/shard_map/all_to_all | solution.py:266
  25.1 2.0 %copy-start = (bf16[1,4608,384]{2,1,0:T(8,128)(2,1)S(1)}, bf16[1,4608,384]{2,1,0:T(8,128)(2,1)}, u32[]{:S(2)}) copy-start(bf16[1,4608,384]{2,1,0:T(8,128)(2,1)} %param.5) | copy-start | bytes 10616836
  27.9 1.4 %copy-start.2 = (bf16[3072,384]{1,0:T(8,128)(2,1)}, bf16[3072,384]{1,0:T(8,128)(2,1)S(1)}, u32[]{:S(2)}) copy-start(bf16[3072,384]{1,0:T(8,128)(2,1)S(1)} %shard_map.48) | copy-start | bytes 7077892
  35.9 31.7 %collective-permute-start.7 = (bf16[3072,384]{1,0:T(8,128)(2,1)}, bf16[3072,384]{1,0:T(8,128)(2,1)}, u32[]{:S(2)}, u32[]{:S(2)}) collective-permute-start(bf16[3072,384]{1,0:T(8,128)(2,1)} %copy-done.2), channel_id=1, source_target_pairs={{0,64},{32,224},{64,128},{96,32},{128,192},{160,96},{192,0},{224,1... | collective-permute-start | bytes 7077896 | tf_op jit(solution)/shard_map/ppermute | solution.py:279
  36.3 5.3 %collective-permute-start.1 = (bf16[16,8,1536]{2,1,0:T(8,128)(2,1)}, bf16[16,8,1536]{2,1,0:T(8,128)(2,1)}, u32[]{:S(2)}, u32[]{:S(2)}) collective-permute-start(bf16[16,8,1536]{2,1,0:T(8,128)(2,1)} %all-to-all-done.1), channel_id=1, source_target_pairs={{0,32},{32,0},{64,96},{96,64},{128,160},{160,128},{192,224},{224,1... | collective-permute-start | bytes 1179656 | tf_op jit(solution)/shard_map/ppermute | solution.py:290
  36.3 10.3 %collective-permute-start.2 = (bf16[16,8,1536]{2,1,0:T(8,128)(2,1)}, bf16[16,8,1536]{2,1,0:T(8,128)(2,1)}, u32[]{:S(2)}, u32[]{:S(2)}) collective-permute-start(bf16[16,8,1536]{2,1,0:T(8,128)(2,1)} %all-to-all-done.1), channel_id=1, source_target_pairs={{0,1},{1,2},{2,3},{3,4},{4,5},{5,6},{6,7},{7,0},{32,39},{33,32},{3... | collective-permute-start | bytes 1179656 | tf_op jit(solution)/shard_map/ppermute | solution.py:285
  41.6 9.2 %collective-permute-start.3 = (bf16[16,8,1536]{2,1,0:T(8,128)(2,1)}, bf16[16,8,1536]{2,1,0:T(8,128)(2,1)}, u32[]{:S(2)}, u32[]{:S(2)}) collective-permute-start(bf16[16,8,1536]{2,1,0:T(8,128)(2,1)} %collective-permute-done.1), channel_id=1, source_target_pairs={{0,1},{1,2},{2,3},{3,4},{4,5},{5,6},{6,7},{7,0},{32,39},{33,32},{3... | collective-permute-start | bytes 1179656 | tf_op jit(solution)/shard_map/ppermute | solution.py:285
  45.0 8.3 %collective-permute-start.4 = (bf16[2,8,8,1536]{3,2,1,0:T(8,128)(2,1)S(1)}, bf16[2,8,8,1536]{3,2,1,0:T(8,128)(2,1)S(1)}, u32[]{:S(2)}, u32[]{:S(2)}) collective-permute-start(bf16[2,8,8,1536]{3,2,1,0:T(8,128)(2,1)S(1)} %fusion.1.refs_0_), channel_id=1, source_target_pairs={{0,24},{8,0},{16,8},{24,16},{32,40},{40,48},{48,56},{56,32},{64,88... | collective-permute-start | bytes 1179656 | tf_op jit(solution)/shard_map/ppermute | solution.py:288
  52.1 30.0 %copy-start.1 = (bf16[1,4608,384]{2,1,0:T(8,128)(2,1)S(1)}, bf16[1,4608,384]{2,1,0:T(8,128)(2,1)}, u32[]{:S(2)}) copy-start(bf16[1,4608,384]{2,1,0:T(8,128)(2,1)} %param.5) | copy-start | bytes 10616836
  53.3 11.2 %collective-permute-start.5 = (bf16[2,16,8,1536]{3,2,1,0:T(8,128)(2,1)S(1)}, bf16[2,16,8,1536]{3,2,1,0:T(8,128)(2,1)S(1)}, u32[]{:S(2)}, u32[]{:S(2)}) collective-permute-start(bf16[2,16,8,1536]{3,2,1,0:T(8,128)(2,1)S(1)} %pad_maximum_fusion.refs_2_), channel_id=1, source_target_pairs={{0,1},{1,2},{2,3},{3,4},{4,5},{5,6},{6,7},{7,0},{32,39},{33,32},{3... | collective-permute-start | bytes 2359304 | tf_op jit(solution)/shard_map/ppermute | solution.py:285
  55.6 12.1 %collective-permute-start.6 = (bf16[2,16,8,1536]{3,2,1,0:T(8,128)(2,1)S(1)}, bf16[2,16,8,1536]{3,2,1,0:T(8,128)(2,1)S(1)}, u32[]{:S(2)}, u32[]{:S(2)}) collective-permute-start(bf16[2,16,8,1536]{3,2,1,0:T(8,128)(2,1)S(1)} %pad_maximum_fusion.refs_2_), channel_id=1, source_target_pairs={{0,24},{8,0},{16,8},{24,16},{32,40},{40,48},{48,56},{56,32},{64,88... | collective-permute-start | bytes 2359304 | tf_op jit(solution)/shard_map/ppermute | solution.py:288
  67.6 11.1 %collective-permute-start.11 = (bf16[2,16,8,1536]{3,2,1,0:T(8,128)(2,1)S(1)}, bf16[2,16,8,1536]{3,2,1,0:T(8,128)(2,1)S(1)}, u32[]{:S(2)}, u32[]{:S(2)}) collective-permute-start(bf16[2,16,8,1536]{3,2,1,0:T(8,128)(2,1)S(1)} %collective-permute-done.5.refs_4_), channel_id=1, source_target_pairs={{0,1},{1,2},{2,3},{3,4},{4,5},{5,6},{6,7},{7,0},{32,39},{33,32},{3... | collective-permute-start | bytes 2359304 | tf_op jit(solution)/shard_map/ppermute | solution.py:285
  71.3 10.7 %collective-permute-start.10 = (bf16[1536,384]{1,0:T(8,128)(2,1)S(1)}, bf16[1536,384]{1,0:T(8,128)(2,1)S(1)}, u32[]{:S(2)}, u32[]{:S(2)}) collective-permute-start(bf16[1536,384]{1,0:T(8,128)(2,1)S(1)} %get-tuple-element.39), channel_id=1, source_target_pairs={{0,32},{32,0},{64,96},{96,64},{128,160},{160,128},{192,224},{224,1... | collective-permute-start | bytes 3538952 | tf_op jit(solution)/shard_map/ppermute | solution.py:303
  71.4 10.6 %collective-permute-start.9 = (bf16[1536,384]{1,0:T(8,128)(2,1)S(1)}, bf16[1536,384]{1,0:T(8,128)(2,1)S(1)}, u32[]{:S(2)}, u32[]{:S(2)}) collective-permute-start(bf16[1536,384]{1,0:T(8,128)(2,1)S(1)} %get-tuple-element.40), channel_id=1, source_target_pairs={{0,32},{32,0},{64,96},{96,64},{128,160},{160,128},{192,224},{224,1... | collective-permute-start | bytes 3538952 | tf_op jit(solution)/shard_map/ppermute | solution.py:303
  71.9 12.4 %collective-permute-start.8 = (bf16[2,16,8,1536]{3,2,1,0:T(8,128)(2,1)S(1)}, bf16[2,16,8,1536]{3,2,1,0:T(8,128)(2,1)S(1)}, u32[]{:S(2)}, u32[]{:S(2)}) collective-permute-start(bf16[2,16,8,1536]{3,2,1,0:T(8,128)(2,1)S(1)} %collective-permute-done.5.refs_4_), channel_id=1, source_target_pairs={{0,24},{8,0},{16,8},{24,16},{32,40},{40,48},{48,56},{56,32},{64,88... | collective-permute-start | bytes 2359304 | tf_op jit(solution)/shard_map/ppermute | solution.py:288
  78.8 9.5 %collective-permute-start.13 = (bf16[2,8,8,1536]{3,2,1,0:T(8,128)(2,1)S(1)}, bf16[2,8,8,1536]{3,2,1,0:T(8,128)(2,1)S(1)}, u32[]{:S(2)}, u32[]{:S(2)}) collective-permute-start(bf16[2,8,8,1536]{3,2,1,0:T(8,128)(2,1)S(1)} %slice_select_fusion), channel_id=1, source_target_pairs={{0,1},{1,2},{2,3},{3,4},{4,5},{5,6},{6,7},{7,0},{32,39},{33,32},{3... | collective-permute-start | bytes 1179656 | tf_op jit(solution)/shard_map/ppermute | solution.py:285
  81.6 16.3 %collective-permute-start.12 = (bf16[2,16,8,1536]{3,2,1,0:T(8,128)(2,1)S(1)}, bf16[2,16,8,1536]{3,2,1,0:T(8,128)(2,1)S(1)}, u32[]{:S(2)}, u32[]{:S(2)}) collective-permute-start(bf16[2,16,8,1536]{3,2,1,0:T(8,128)(2,1)S(1)} %collective-permute-done.11.refs_0_), channel_id=1, source_target_pairs={{0,24},{8,0},{16,8},{24,16},{32,40},{40,48},{48,56},{56,32},{64,88... | collective-permute-start | bytes 2359304 | tf_op jit(solution)/shard_map/ppermute | solution.py:288
  86.6 6.8 %collective-permute-start.16 = (f32[160,384]{1,0:T(8,128)S(1)}, f32[160,384]{1,0:T(8,128)S(1)}, u32[]{:S(2)}, u32[]{:S(2)}) collective-permute-start(f32[160,384]{1,0:T(8,128)S(1)} %pad_maximum_fusion.6), channel_id=1, source_target_pairs={{0,192},{32,224},{64,0},{96,32},{128,64},{160,96},{192,128},{224,1... | collective-permute-start | bytes 737288 | tf_op jit(solution)/shard_map/ppermute | solution.py:202
  88.1 8.0 %collective-permute-start.15 = (f32[160,384]{1,0:T(8,128)S(1)}, f32[160,384]{1,0:T(8,128)S(1)}, u32[]{:S(2)}, u32[]{:S(2)}) collective-permute-start(f32[160,384]{1,0:T(8,128)S(1)} %pad_maximum_fusion.5), channel_id=1, source_target_pairs={{0,64},{32,96},{64,128},{96,160},{128,192},{160,224},{192,0},{224,... | collective-permute-start | bytes 737288 | tf_op jit(solution)/shard_map/ppermute | solution.py:201
  88.3 9.6 %collective-permute-start.14 = (bf16[2,8,8,1536]{3,2,1,0:T(8,128)(2,1)S(1)}, bf16[2,8,8,1536]{3,2,1,0:T(8,128)(2,1)S(1)}, u32[]{:S(2)}, u32[]{:S(2)}) collective-permute-start(bf16[2,8,8,1536]{3,2,1,0:T(8,128)(2,1)S(1)} %collective-permute-done.13.refs_2_), channel_id=1, source_target_pairs={{0,24},{8,0},{16,8},{24,16},{32,40},{40,48},{48,56},{56,32},{64,88... | collective-permute-start | bytes 1179656 | tf_op jit(solution)/shard_map/ppermute | solution.py:288
  99.4 8.1 %collective-permute-start.17 = (f32[176,384]{1,0:T(8,128)S(1)}, f32[176,384]{1,0:T(8,128)S(1)}, u32[]{:S(2)}, u32[]{:S(2)}) collective-permute-start(f32[176,384]{1,0:T(8,128)S(1)} %pad_maximum_fusion.3), channel_id=1, source_target_pairs={{0,64},{32,96},{64,128},{96,160},{128,192},{160,224},{192,0},{224,... | collective-permute-start | bytes 811016 | tf_op jit(solution)/shard_map/ppermute | solution.py:334
  99.5 8.0 %collective-permute-start.18 = (f32[176,384]{1,0:T(8,128)S(1)}, f32[176,384]{1,0:T(8,128)S(1)}, u32[]{:S(2)}, u32[]{:S(2)}) collective-permute-start(f32[176,384]{1,0:T(8,128)S(1)} %pad_maximum_fusion.4), channel_id=1, source_target_pairs={{0,192},{32,224},{64,0},{96,32},{128,64},{160,96},{192,128},{224,1... | collective-permute-start | bytes 811016 | tf_op jit(solution)/shard_map/ppermute | solution.py:335
  102.3 9.2 %collective-permute-start.19 = (f32[96,384]{1,0:T(8,128)S(1)}, f32[96,384]{1,0:T(8,128)S(1)}, u32[]{:S(2)}, u32[]{:S(2)}) collective-permute-start(f32[96,384]{1,0:T(8,128)S(1)} %get-tuple-element.48), channel_id=1, source_target_pairs={{0,128},{32,160},{64,192},{96,224},{128,0},{160,32},{192,64},{224,... | collective-permute-start | bytes 442376 | tf_op jit(solution)/shard_map/ppermute | solution.py:333
  111.5 2.9 %collective-permute-start.20 = (f32[256,384]{1,0:T(8,128)S(1)}, f32[256,384]{1,0:T(8,128)S(1)}, u32[]{:S(2)}, u32[]{:S(2)}) collective-permute-start(f32[256,384]{1,0:T(8,128)S(1)} %pad_maximum_fusion.2.mine_ref), channel_id=1, source_target_pairs={{0,32},{32,0},{64,96},{96,64},{128,160},{160,128},{192,224},{224,1... | collective-permute-start | bytes 1179656 | tf_op jit(solution)/shard_map/ppermute | solution.py:344

commit v13 on v12

--- a/solution.py
+++ b/solution.py
@@ -330,7 +330,7 @@
     *late, a, b = barrier((*late, a, b))
     late = sums(late)
     h, n = early.shape[1] // 2, late.shape[1]
-    c = lax.ppermute(late[2], "grp", opposite)
+    (c,) = collect(lax.ppermute(late[2], "grp", opposite))
     a2 = lax.ppermute(jnp.concatenate([late[1], early[1, :h] + a[:h]]), "grp", up)
     b2 = lax.ppermute(jnp.concatenate([late[3], early[3, h:] + b[:h]]), "grp", down)
     early = early[0] + jnp.concatenate([a2[n:], a[h:]]) + jnp.concatenate([b[h:], b2[n:]])

time: 116 us -> 116 us (level)
    ppermute x1, waiting for transfers between devices: 3.84 us -> 1.38 us  [body(): c, = collect(lax.ppermute(late[2], 'grp', opposite))]
    ppermute x1, waiting for transfers between devices: 5.18 us -> 7.43 us  [body(): lax.ppermute(jnp.concatenate([late[1], early[1, :h] + a[:h]]), 'grp', up)]
    ppermute x1, starting transfers between devices: 0.03 us -> 1.33 us  [body(): c, = collect(lax.ppermute(late[2], 'grp', opposite))]
where the time goes in v13:
time: 116 us; the launch traced here: 115 us
  waiting for transfers between devices  58.6 us (51%)
  starting transfers between devices  35.7 us (31%)
  Pallas kernels  11.4 us (10%)
  local copies, waits for them, and re-layouts  6.09 us (5%)
  other arithmetic  3.45 us (3%)
    ppermute x5, waiting for transfers between devices, z_step(): return lax.ppermute(block, ('grp', 'col'), along)  20.4 us
    ppermute x5, starting transfers between devices, z_step(): return lax.ppermute(block, ('grp', 'col'), along)  14.3 us
    all_to_all x1, waiting for transfers between devices, body(): lax.all_to_all(amplitudes[0].reshape(groups, octet, cap), 'grp', 0, 0, ti...  7.57 us
    ppermute x1, waiting for transfers between devices, body(): lax.ppermute(jnp.concatenate([late[1], early[1, :h] + a[:h]]), 'grp', up)  7.43 us
    all_to_all x1, waiting for transfers between devices, body(): lax.all_to_all(packed, ('grp', 'row'), 0, 0, axis_index_groups=pairs, til...  6.55 us
    ppermute x5, waiting for transfers between devices, y_step(): return lax.ppermute(block, ('grp', 'row'), beside)  6.07 us
    ppermute x1, waiting for transfers between devices, near_chips(): return (a, lax.ppermute(jnp.concatenate([p[2, h:], p[3, :h]]), 'grp', down))  5.09 us
    all_to_all x1, starting transfers between devices, body(): lax.all_to_all(packed, ('grp', 'row'), 0, 0, axis_index_groups=pairs, til...  4.83 us
  transfers between devices with their start and end apart: 23, of which 14 were waited for; matrix products, arithmetic and copies ran while one was open for 5% of the time, Pallas kernels for 8%

profile of v13, /device:TPU:1, one launch (start us, length us, event | category | flops | bytes accessed | tf_op | source)
XLA Modules:
  0.0 115.4 jit_solution(6605908110561205240)
XLA Ops:
  0.0 3.2 %collective-permute-start = (bf16[4608,384]{1,0:T(8,128)(2,1)}, bf16[4608,384]{1,0:T(8,128)(2,1)S(1)}, u32[]{:S(2)}, u32[]{:S(2)}) collective-permute-start(bf16[4608,384]{1,0:T(8,128)(2,1)} %bitcast.40), channel_id=1, source_target_pairs={{0,32},{32,0},{64,96},{96,64},{128,160},{160,128},{192,224},{224,1... | collective-permute-start | bytes 10616840 | tf_op jit(solution)/shard_map/ppermute | solution.py:245
  3.2 4.1 %all-to-all-start = ((bf16[8,8,4608]{2,1,0:T(8,128)(2,1)}), bf16[8,8,4608]{2,1,0:T(8,128)(2,1)}, u32[]{:S(2)}, u32[]{:S(2)}) async-start(bf16[8,8,4608]{2,1,0:T(8,128)(2,1)} %bitcast.43), calls=%async_computation | async-start | bytes 1179648 | tf_op jit(solution)/shard_map/all_to_all | solution.py:246
  7.4 0.7 pad_add_fusion.both_ref
  8.1 2.0 %shard_map.46.list_ref = s32[96]{0:T(128)S(1)} custom-call(s32[2,8]{1,0:T(2,128)S(1)} %pad_add_fusion.both_ref), custom_call_target="tpu_custom_call" | custom-call | tf_op jit(solution)/shard_map/pallas_call | solution.py:249
  10.0 7.6 %all-to-all-done.src_ref = bf16[8,8,4608]{2,1,0:T(8,128)(2,1)} async-done(((bf16[8,8,4608]{2,1,0:T(8,128)(2,1)}), bf16[8,8,4608]{2,1,0:T(8,128)(2,1)}, u32[]{:S(2)}, u32[]{:S(2)}) %all-to-all-start) | async-done | bytes 589856 | tf_op jit(solution)/shard_map/all_to_all | solution.py:246
  17.6 1.9 %shard_map.47 = bf16[16,8,1536]{2,1,0:T(8,128)(2,1)S(1)} custom-call(s32[96]{0:T(128)S(1)} %shard_map.46.list_ref, bf16[8,8,4608]{2,1,0:T(8,128)(2,1)} %all-to-all-done.src_ref), custom_call_target="tpu_custom_call" | custom-call | tf_op jit(solution)/shard_map/pallas_call | solution.py:258
  19.5 0.0 copy-start.3
  19.5 0.7 copy-done.3
  20.2 4.8 %all-to-all-start.1 = ((bf16[16,8,1536]{2,1,0:T(8,128)(2,1)}), bf16[16,8,1536]{2,1,0:T(8,128)(2,1)}, u32[]{:S(2)}, u32[]{:S(2)}) async-start(bf16[16,8,1536]{2,1,0:T(8,128)(2,1)} %copy-done.3), calls=%async_computation.1 | async-start | bytes 786432 | tf_op jit(solution)/shard_map/all_to_all | solution.py:266
  25.1 0.0 collective-permute-done.other_ref
  25.1 0.0 copy-start
  25.1 2.0 %copy-done = bf16[1,4608,384]{2,1,0:T(8,128)(2,1)S(1)} copy-done((bf16[1,4608,384]{2,1,0:T(8,128)(2,1)S(1)}, bf16[1,4608,384]{2,1,0:T(8,128)(2,1)}, u32[]{:S(2)}) %copy-start) | copy-done | bytes 3538968
  27.1 0.9 shard_map.48
  27.9 1.4 %copy-done.2 = bf16[3072,384]{1,0:T(8,128)(2,1)} copy-done((bf16[3072,384]{1,0:T(8,128)(2,1)}, bf16[3072,384]{1,0:T(8,128)(2,1)S(1)}, u32[]{:S(2)}) %copy-start.2) | copy-done | bytes 2359320
  29.3 6.6 %all-to-all-done.1 = bf16[16,8,1536]{2,1,0:T(8,128)(2,1)} async-done(((bf16[16,8,1536]{2,1,0:T(8,128)(2,1)}), bf16[16,8,1536]{2,1,0:T(8,128)(2,1)}, u32[]{:S(2)}, u32[]{:S(2)}) %all-to-all-start.1) | async-done | bytes 393248 | tf_op jit(solution)/shard_map/all_to_all | solution.py:266
  35.9 0.4 collective-permute-start.7
  36.3 0.0 collective-permute-start.1
  36.3 5.3 %collective-permute-start.2 = (bf16[16,8,1536]{2,1,0:T(8,128)(2,1)}, bf16[16,8,1536]{2,1,0:T(8,128)(2,1)}, u32[]{:S(2)}, u32[]{:S(2)}) collective-permute-start(bf16[16,8,1536]{2,1,0:T(8,128)(2,1)} %all-to-all-done.1), channel_id=1, source_target_pairs={{0,1},{1,2},{2,3},{3,4},{4,5},{5,6},{6,7},{7,0},{32,39},{33,32},{3... | collective-permute-start | bytes 1179656 | tf_op jit(solution)/shard_map/ppermute | solution.py:285
  41.6 0.0 collective-permute-done.1
  41.6 2.1 %collective-permute-start.3 = (bf16[16,8,1536]{2,1,0:T(8,128)(2,1)}, bf16[16,8,1536]{2,1,0:T(8,128)(2,1)}, u32[]{:S(2)}, u32[]{:S(2)}) collective-permute-start(bf16[16,8,1536]{2,1,0:T(8,128)(2,1)} %collective-permute-done.1), channel_id=1, source_target_pairs={{0,1},{1,2},{2,3},{3,4},{4,5},{5,6},{6,7},{7,0},{32,39},{33,32},{3... | collective-permute-start | bytes 1179656 | tf_op jit(solution)/shard_map/ppermute | solution.py:285
  43.7 1.3 %fusion.1.refs_0_ = bf16[2,8,8,1536]{3,2,1,0:T(8,128)(2,1)S(1)} fusion(bf16[1,16,8,1536]{3,2,1,0:T(8,128)(2,1)} %bitcast.4, bf16[1,16,8,1536]{3,2,1,0:T(8,128)(2,1)} %bitcast.5, pred[]{:T(512)S(6)} %eq.4), kind=kLoop, calls=%fused_computation.4 | loop fusion | flops 589824 | bytes 1179649 | tf_op jit(solution)/shard_map/jit(_where)/select_n | solution.py:282
  45.0 0.5 collective-permute-start.4
  45.5 1.2 %collective-permute-done.2 = bf16[16,8,1536]{2,1,0:T(8,128)(2,1)} collective-permute-done((bf16[16,8,1536]{2,1,0:T(8,128)(2,1)}, bf16[16,8,1536]{2,1,0:T(8,128)(2,1)}, u32[]{:S(2)}, u32[]{:S(2)}) %collective-permute-start.2) | collective-permute-done | bytes 393248 | tf_op jit(solution)/shard_map/ppermute | solution.py:285
  46.7 4.2 %collective-permute-done.3 = bf16[16,8,1536]{2,1,0:T(8,128)(2,1)} collective-permute-done((bf16[16,8,1536]{2,1,0:T(8,128)(2,1)}, bf16[16,8,1536]{2,1,0:T(8,128)(2,1)}, u32[]{:S(2)}, u32[]{:S(2)}) %collective-permute-start.3) | collective-permute-done | bytes 393248 | tf_op jit(solution)/shard_map/ppermute | solution.py:285
  50.9 1.2 %pad_maximum_fusion.refs_2_ = bf16[2,16,8,1536]{3,2,1,0:T(8,128)(2,1)S(1)} fusion(bf16[1,16,8,1536]{3,2,1,0:T(8,128)(2,1)} %bitcast.7, bf16[1,16,8,1536]{3,2,1,0:T(8,128)(2,1)} %bitcast.6), kind=kLoop, calls=%fused_computation.2 | loop fusion | flops 393216 | bytes 1572864 | tf_op jit(solution)/shard_map/stack | solution.py:293
  52.1 0.0 copy-start.1
  52.1 1.2 %collective-permute-done.4.refs_1_ = bf16[2,8,8,1536]{3,2,1,0:T(8,128)(2,1)S(1)} collective-permute-done((bf16[2,8,8,1536]{3,2,1,0:T(8,128)(2,1)S(1)}, bf16[2,8,8,1536]{3,2,1,0:T(8,128)(2,1)S(1)}, u32[]{:S(2)}, u32[]{:S(2)}) %collective-permute-start.4) | collective-permute-done | bytes 393248 | tf_op jit(solution)/shard_map/ppermute | solution.py:288
  53.3 2.3 %collective-permute-start.5 = (bf16[2,16,8,1536]{3,2,1,0:T(8,128)(2,1)S(1)}, bf16[2,16,8,1536]{3,2,1,0:T(8,128)(2,1)S(1)}, u32[]{:S(2)}, u32[]{:S(2)}) collective-permute-start(bf16[2,16,8,1536]{3,2,1,0:T(8,128)(2,1)S(1)} %pad_maximum_fusion.refs_2_), channel_id=1, source_target_pairs={{0,1},{1,2},{2,3},{3,4},{4,5},{5,6},{6,7},{7,0},{32,39},{33,32},{3... | collective-permute-start | bytes 2359304 | tf_op jit(solution)/shard_map/ppermute | solution.py:285
  55.6 0.4 collective-permute-start.6
  56.0 8.6 %collective-permute-done.5.refs_4_ = bf16[2,16,8,1536]{3,2,1,0:T(8,128)(2,1)S(1)} collective-permute-done((bf16[2,16,8,1536]{3,2,1,0:T(8,128)(2,1)S(1)}, bf16[2,16,8,1536]{3,2,1,0:T(8,128)(2,1)S(1)}, u32[]{:S(2)}, u32[]{:S(2)}) %collective-permute-start.5) | collective-permute-done | bytes 786464 | tf_op jit(solution)/shard_map/ppermute | solution.py:285
  64.6 3.1 %collective-permute-done.6.refs_3_ = bf16[2,16,8,1536]{3,2,1,0:T(8,128)(2,1)S(1)} collective-permute-done((bf16[2,16,8,1536]{3,2,1,0:T(8,128)(2,1)S(1)}, bf16[2,16,8,1536]{3,2,1,0:T(8,128)(2,1)S(1)}, u32[]{:S(2)}, u32[]{:S(2)}) %collective-permute-start.6) | collective-permute-done | bytes 786464 | tf_op jit(solution)/shard_map/ppermute | solution.py:288
  67.6 0.0 collective-permute-done.7.got_ref
  67.6 1.8 %collective-permute-start.11 = (bf16[2,16,8,1536]{3,2,1,0:T(8,128)(2,1)S(1)}, bf16[2,16,8,1536]{3,2,1,0:T(8,128)(2,1)S(1)}, u32[]{:S(2)}, u32[]{:S(2)}) collective-permute-start(bf16[2,16,8,1536]{3,2,1,0:T(8,128)(2,1)S(1)} %collective-permute-done.5.refs_4_), channel_id=1, source_target_pairs={{0,1},{1,2},{2,3},{3,4},{4,5},{5,6},{6,7},{7,0},{32,39},{33,32},{3... | collective-permute-start | bytes 2359304 | tf_op jit(solution)/shard_map/ppermute | solution.py:285
  69.5 1.9 %fusion.7 = (bf16[1536,384]{1,0:T(8,128)(2,1)S(1)}, bf16[1536,384]{1,0:T(8,128)(2,1)S(1)}) fusion(bf16[3072,384]{1,0:T(8,128)(2,1)} %collective-permute-done.7.got_ref), kind=kLoop, calls=%fused_computation.31 | loop fusion | bytes 4718592 | tf_op jit(solution)/shard_map/split | solution.py:303
  71.3 0.1 collective-permute-start.10
  71.4 0.5 collective-permute-start.9
  71.9 0.4 collective-permute-start.8
  72.3 6.5 %collective-permute-done.11.refs_0_ = bf16[2,16,8,1536]{3,2,1,0:T(8,128)(2,1)S(1)} collective-permute-done((bf16[2,16,8,1536]{3,2,1,0:T(8,128)(2,1)S(1)}, bf16[2,16,8,1536]{3,2,1,0:T(8,128)(2,1)S(1)}, u32[]{:S(2)}, u32[]{:S(2)}) %collective-permute-start.11) | collective-permute-done | bytes 786464 | tf_op jit(solution)/shard_map/ppermute | solution.py:285
  78.8 2.8 %collective-permute-start.13 = (bf16[2,8,8,1536]{3,2,1,0:T(8,128)(2,1)S(1)}, bf16[2,8,8,1536]{3,2,1,0:T(8,128)(2,1)S(1)}, u32[]{:S(2)}, u32[]{:S(2)}) collective-permute-start(bf16[2,8,8,1536]{3,2,1,0:T(8,128)(2,1)S(1)} %slice_select_fusion), channel_id=1, source_target_pairs={{0,1},{1,2},{2,3},{3,4},{4,5},{5,6},{6,7},{7,0},{32,39},{33,32},{3... | collective-permute-start | bytes 1179656 | tf_op jit(solution)/shard_map/ppermute | solution.py:285
  81.6 0.4 collective-permute-start.12
  82.0 0.0 collective-permute-done.10.refs_1_
  82.0 0.0 collective-permute-done.9.refs_0_
  82.1 2.3 %shard_map.49.refs_6_.refs_4_ = bf16[3072,384]{1,0:T(8,128)(2,1)S(1)} custom-call(s32[2,8]{1,0:T(2,128)S(1)} %pad_add_fusion.both_ref, bf16[4608,384]{1,0:T(8,128)(2,1)S(1)} %bitcast.42, bf16[4608,384]{1,0:T(8,128)(2,1)S(1)} %collective-permute-done.other_ref, bf16[3072,384]{1,0:T(8,128)(2,1)} %collective-permute-done.7.got_ref, ...), custom_call_target="tpu_custom_call" | custom-call | tf_op jit(solution)/shard_map/pallas_call | solution.py:307
  84.4 0.0 collective-permute-done.8.refs_5_
  84.4 2.2 %shard_map.50 = f32[4,160,384]{2,1,0:T(8,128)S(1)} custom-call(bf16[2,8,8,1536]{3,2,1,0:T(8,128)(2,1)S(1)} %fusion.1.refs_0_, bf16[2,8,8,1536]{3,2,1,0:T(8,128)(2,1)S(1)} %collective-permute-done.4.refs_1_, bf16[2,16,8,1536]{3,2,1,0:T(8,128)(2,1)S(1)} %pad_maximum_fusion.refs_2_, bf16[2,16,8,1536]{3,2,1,0:T(8,128)(2,1)S(1)} %collective-permute-done.6.refs_3_, ...), custom_call_target="tpu_custom_call" | custom-call | tf_op jit(solution)/shard_map/pallas_call | solution.py:318
  86.6 1.5 %collective-permute-start.16 = (f32[160,384]{1,0:T(8,128)S(1)}, f32[160,384]{1,0:T(8,128)S(1)}, u32[]{:S(2)}, u32[]{:S(2)}) collective-permute-start(f32[160,384]{1,0:T(8,128)S(1)} %pad_maximum_fusion.6), channel_id=1, source_target_pairs={{0,192},{32,224},{64,0},{96,32},{128,64},{160,96},{192,128},{224,1... | collective-permute-start | bytes 737288 | tf_op jit(solution)/shard_map/ppermute | solution.py:202
  88.1 0.1 collective-permute-start.15
  88.3 0.0 collective-permute-done.13.refs_2_
  88.3 0.0 collective-permute-start.14
  88.3 5.1 %collective-permute-done.16.refs_1_ = f32[160,384]{1,0:T(8,128)S(1)} collective-permute-done((f32[160,384]{1,0:T(8,128)S(1)}, f32[160,384]{1,0:T(8,128)S(1)}, u32[]{:S(2)}, u32[]{:S(2)}) %collective-permute-start.16) | collective-permute-done | bytes 245792 | tf_op jit(solution)/shard_map/ppermute | solution.py:202
  93.4 2.7 %collective-permute-done.15.refs_0_ = f32[160,384]{1,0:T(8,128)S(1)} collective-permute-done((f32[160,384]{1,0:T(8,128)S(1)}, f32[160,384]{1,0:T(8,128)S(1)}, u32[]{:S(2)}, u32[]{:S(2)}) %collective-permute-start.15) | collective-permute-done | bytes 245792 | tf_op jit(solution)/shard_map/ppermute | solution.py:201
  96.2 1.8 %collective-permute-done.14.refs_3_ = bf16[2,8,8,1536]{3,2,1,0:T(8,128)(2,1)S(1)} collective-permute-done((bf16[2,8,8,1536]{3,2,1,0:T(8,128)(2,1)S(1)}, bf16[2,8,8,1536]{3,2,1,0:T(8,128)(2,1)S(1)}, u32[]{:S(2)}, u32[]{:S(2)}) %collective-permute-start.14) | collective-permute-done | bytes 393248 | tf_op jit(solution)/shard_map/ppermute | solution.py:288
  97.9 0.0 collective-permute-done.12.refs_1_
  97.9 1.4 %shard_map.52 = f32[4,96,384]{2,1,0:T(8,128)S(1)} custom-call(bf16[2,16,8,1536]{3,2,1,0:T(8,128)(2,1)S(1)} %collective-permute-done.11.refs_0_, bf16[2,16,8,1536]{3,2,1,0:T(8,128)(2,1)S(1)} %collective-permute-done.12.refs_1_, bf16[2,8,8,1536]{3,2,1,0:T(8,128)(2,1)S(1)} %collective-permute-done.13.refs_2_, ...), custom_call_target="tpu_custom_call" | custom-call | tf_op jit(solution)/shard_map/pallas_call | solution.py:318
  99.3 1.3 %collective-permute-start.19 = (f32[96,384]{1,0:T(8,128)S(1)}, f32[96,384]{1,0:T(8,128)S(1)}, u32[]{:S(2)}, u32[]{:S(2)}) collective-permute-start(f32[96,384]{1,0:T(8,128)S(1)} %get-tuple-element.48), channel_id=1, source_target_pairs={{0,128},{32,160},{64,192},{96,224},{128,0},{160,32},{192,64},{224,... | collective-permute-start | bytes 442376 | tf_op jit(solution)/shard_map/ppermute | solution.py:333
  100.7 0.8 collective-permute-start.17
  101.6 2.0 %collective-permute-start.18 = (f32[176,384]{1,0:T(8,128)S(1)}, f32[176,384]{1,0:T(8,128)S(1)}, u32[]{:S(2)}, u32[]{:S(2)}) collective-permute-start(f32[176,384]{1,0:T(8,128)S(1)} %pad_maximum_fusion.4), channel_id=1, source_target_pairs={{0,192},{32,224},{64,0},{96,32},{128,64},{160,96},{192,128},{224,1... | collective-permute-start | bytes 811016 | tf_op jit(solution)/shard_map/ppermute | solution.py:335
  103.6 1.4 %collective-permute-done.19.refs_0_ = f32[96,384]{1,0:T(8,128)S(1)} collective-permute-done((f32[96,384]{1,0:T(8,128)S(1)}, f32[96,384]{1,0:T(8,128)S(1)}, u32[]{:S(2)}, u32[]{:S(2)}) %collective-permute-start.19) | collective-permute-done | bytes 147488 | tf_op jit(solution)/shard_map/ppermute | solution.py:333
  105.0 7.4 %collective-permute-done.17 = f32[176,384]{1,0:T(8,128)S(1)} collective-permute-done((f32[176,384]{1,0:T(8,128)S(1)}, f32[176,384]{1,0:T(8,128)S(1)}, u32[]{:S(2)}, u32[]{:S(2)}) %collective-permute-start.17) | collective-permute-done | bytes 270368 | tf_op jit(solution)/shard_map/ppermute | solution.py:334
  112.4 0.0 collective-permute-done.18
  112.4 0.1 fusion.3
  112.6 0.7 collective-permute-start.20
  113.2 1.3 %collective-permute-done.20.other_ref = f32[256,384]{1,0:T(8,128)S(1)} collective-permute-done((f32[256,384]{1,0:T(8,128)S(1)}, f32[256,384]{1,0:T(8,128)S(1)}, u32[]{:S(2)}, u32[]{:S(2)}) %collective-permute-start.20) | collective-permute-done | bytes 393248 | tf_op jit(solution)/shard_map/ppermute | solution.py:344
  114.6 0.8 shard_map.54
  (16 shorter events, 0.3 us)
Async XLA Ops:
  0.0 25.1 %collective-permute-start = (bf16[4608,384]{1,0:T(8,128)(2,1)}, bf16[4608,384]{1,0:T(8,128)(2,1)S(1)}, u32[]{:S(2)}, u32[]{:S(2)}) collective-permute-start(bf16[4608,384]{1,0:T(8,128)(2,1)} %bitcast.40), channel_id=1, source_target_pairs={{0,32},{32,0},{64,96},{96,64},{128,160},{160,128},{192,224},{224,1... | collective-permute-start | bytes 10616840 | tf_op jit(solution)/shard_map/ppermute | solution.py:245
  3.2 14.4 %all-to-all-start = ((bf16[8,8,4608]{2,1,0:T(8,128)(2,1)}), bf16[8,8,4608]{2,1,0:T(8,128)(2,1)}, u32[]{:S(2)}, u32[]{:S(2)}) async-start(bf16[8,8,4608]{2,1,0:T(8,128)(2,1)} %bitcast.43), calls=%async_computation | async-start | bytes 1179648 | tf_op jit(solution)/shard_map/all_to_all | solution.py:246
  19.5 0.7 copy-start.3
  20.2 15.7 %all-to-all-start.1 = ((bf16[16,8,1536]{2,1,0:T(8,128)(2,1)}), bf16[16,8,1536]{2,1,0:T(8,128)(2,1)}, u32[]{:S(2)}, u32[]{:S(2)}) async-start(bf16[16,8,1536]{2,1,0:T(8,128)(2,1)} %copy-done.3), calls=%async_computation.1 | async-start | bytes 786432 | tf_op jit(solution)/shard_map/all_to_all | solution.py:266
  25.1 2.0 %copy-start = (bf16[1,4608,384]{2,1,0:T(8,128)(2,1)S(1)}, bf16[1,4608,384]{2,1,0:T(8,128)(2,1)}, u32[]{:S(2)}) copy-start(bf16[1,4608,384]{2,1,0:T(8,128)(2,1)} %param.5) | copy-start | bytes 10616836
  27.9 1.4 %copy-start.2 = (bf16[3072,384]{1,0:T(8,128)(2,1)}, bf16[3072,384]{1,0:T(8,128)(2,1)S(1)}, u32[]{:S(2)}) copy-start(bf16[3072,384]{1,0:T(8,128)(2,1)S(1)} %shard_map.48) | copy-start | bytes 7077892
  35.9 31.7 %collective-permute-start.7 = (bf16[3072,384]{1,0:T(8,128)(2,1)}, bf16[3072,384]{1,0:T(8,128)(2,1)}, u32[]{:S(2)}, u32[]{:S(2)}) collective-permute-start(bf16[3072,384]{1,0:T(8,128)(2,1)} %copy-done.2), channel_id=1, source_target_pairs={{0,64},{32,224},{64,128},{96,32},{128,192},{160,96},{192,0},{224,1... | collective-permute-start | bytes 7077896 | tf_op jit(solution)/shard_map/ppermute | solution.py:279
  36.3 5.3 %collective-permute-start.1 = (bf16[16,8,1536]{2,1,0:T(8,128)(2,1)}, bf16[16,8,1536]{2,1,0:T(8,128)(2,1)}, u32[]{:S(2)}, u32[]{:S(2)}) collective-permute-start(bf16[16,8,1536]{2,1,0:T(8,128)(2,1)} %all-to-all-done.1), channel_id=1, source_target_pairs={{0,32},{32,0},{64,96},{96,64},{128,160},{160,128},{192,224},{224,1... | collective-permute-start | bytes 1179656 | tf_op jit(solution)/shard_map/ppermute | solution.py:290
  36.3 10.3 %collective-permute-start.2 = (bf16[16,8,1536]{2,1,0:T(8,128)(2,1)}, bf16[16,8,1536]{2,1,0:T(8,128)(2,1)}, u32[]{:S(2)}, u32[]{:S(2)}) collective-permute-start(bf16[16,8,1536]{2,1,0:T(8,128)(2,1)} %all-to-all-done.1), channel_id=1, source_target_pairs={{0,1},{1,2},{2,3},{3,4},{4,5},{5,6},{6,7},{7,0},{32,39},{33,32},{3... | collective-permute-start | bytes 1179656 | tf_op jit(solution)/shard_map/ppermute | solution.py:285
  41.6 9.2 %collective-permute-start.3 = (bf16[16,8,1536]{2,1,0:T(8,128)(2,1)}, bf16[16,8,1536]{2,1,0:T(8,128)(2,1)}, u32[]{:S(2)}, u32[]{:S(2)}) collective-permute-start(bf16[16,8,1536]{2,1,0:T(8,128)(2,1)} %collective-permute-done.1), channel_id=1, source_target_pairs={{0,1},{1,2},{2,3},{3,4},{4,5},{5,6},{6,7},{7,0},{32,39},{33,32},{3... | collective-permute-start | bytes 1179656 | tf_op jit(solution)/shard_map/ppermute | solution.py:285
  45.0 8.3 %collective-permute-start.4 = (bf16[2,8,8,1536]{3,2,1,0:T(8,128)(2,1)S(1)}, bf16[2,8,8,1536]{3,2,1,0:T(8,128)(2,1)S(1)}, u32[]{:S(2)}, u32[]{:S(2)}) collective-permute-start(bf16[2,8,8,1536]{3,2,1,0:T(8,128)(2,1)S(1)} %fusion.1.refs_0_), channel_id=1, source_target_pairs={{0,24},{8,0},{16,8},{24,16},{32,40},{40,48},{48,56},{56,32},{64,88... | collective-permute-start | bytes 1179656 | tf_op jit(solution)/shard_map/ppermute | solution.py:288
  52.1 30.0 %copy-start.1 = (bf16[1,4608,384]{2,1,0:T(8,128)(2,1)S(1)}, bf16[1,4608,384]{2,1,0:T(8,128)(2,1)}, u32[]{:S(2)}) copy-start(bf16[1,4608,384]{2,1,0:T(8,128)(2,1)} %param.5) | copy-start | bytes 10616836
  53.3 11.2 %collective-permute-start.5 = (bf16[2,16,8,1536]{3,2,1,0:T(8,128)(2,1)S(1)}, bf16[2,16,8,1536]{3,2,1,0:T(8,128)(2,1)S(1)}, u32[]{:S(2)}, u32[]{:S(2)}) collective-permute-start(bf16[2,16,8,1536]{3,2,1,0:T(8,128)(2,1)S(1)} %pad_maximum_fusion.refs_2_), channel_id=1, source_target_pairs={{0,1},{1,2},{2,3},{3,4},{4,5},{5,6},{6,7},{7,0},{32,39},{33,32},{3... | collective-permute-start | bytes 2359304 | tf_op jit(solution)/shard_map/ppermute | solution.py:285
  55.6 12.1 %collective-permute-start.6 = (bf16[2,16,8,1536]{3,2,1,0:T(8,128)(2,1)S(1)}, bf16[2,16,8,1536]{3,2,1,0:T(8,128)(2,1)S(1)}, u32[]{:S(2)}, u32[]{:S(2)}) collective-permute-start(bf16[2,16,8,1536]{3,2,1,0:T(8,128)(2,1)S(1)} %pad_maximum_fusion.refs_2_), channel_id=1, source_target_pairs={{0,24},{8,0},{16,8},{24,16},{32,40},{40,48},{48,56},{56,32},{64,88... | collective-permute-start | bytes 2359304 | tf_op jit(solution)/shard_map/ppermute | solution.py:288
  67.6 11.1 %collective-permute-start.11 = (bf16[2,16,8,1536]{3,2,1,0:T(8,128)(2,1)S(1)}, bf16[2,16,8,1536]{3,2,1,0:T(8,128)(2,1)S(1)}, u32[]{:S(2)}, u32[]{:S(2)}) collective-permute-start(bf16[2,16,8,1536]{3,2,1,0:T(8,128)(2,1)S(1)} %collective-permute-done.5.refs_4_), channel_id=1, source_target_pairs={{0,1},{1,2},{2,3},{3,4},{4,5},{5,6},{6,7},{7,0},{32,39},{33,32},{3... | collective-permute-start | bytes 2359304 | tf_op jit(solution)/shard_map/ppermute | solution.py:285
  71.3 10.7 %collective-permute-start.10 = (bf16[1536,384]{1,0:T(8,128)(2,1)S(1)}, bf16[1536,384]{1,0:T(8,128)(2,1)S(1)}, u32[]{:S(2)}, u32[]{:S(2)}) collective-permute-start(bf16[1536,384]{1,0:T(8,128)(2,1)S(1)} %get-tuple-element.39), channel_id=1, source_target_pairs={{0,32},{32,0},{64,96},{96,64},{128,160},{160,128},{192,224},{224,1... | collective-permute-start | bytes 3538952 | tf_op jit(solution)/shard_map/ppermute | solution.py:303
  71.4 10.6 %collective-permute-start.9 = (bf16[1536,384]{1,0:T(8,128)(2,1)S(1)}, bf16[1536,384]{1,0:T(8,128)(2,1)S(1)}, u32[]{:S(2)}, u32[]{:S(2)}) collective-permute-start(bf16[1536,384]{1,0:T(8,128)(2,1)S(1)} %get-tuple-element.40), channel_id=1, source_target_pairs={{0,32},{32,0},{64,96},{96,64},{128,160},{160,128},{192,224},{224,1... | collective-permute-start | bytes 3538952 | tf_op jit(solution)/shard_map/ppermute | solution.py:303
  71.9 12.4 %collective-permute-start.8 = (bf16[2,16,8,1536]{3,2,1,0:T(8,128)(2,1)S(1)}, bf16[2,16,8,1536]{3,2,1,0:T(8,128)(2,1)S(1)}, u32[]{:S(2)}, u32[]{:S(2)}) collective-permute-start(bf16[2,16,8,1536]{3,2,1,0:T(8,128)(2,1)S(1)} %collective-permute-done.5.refs_4_), channel_id=1, source_target_pairs={{0,24},{8,0},{16,8},{24,16},{32,40},{40,48},{48,56},{56,32},{64,88... | collective-permute-start | bytes 2359304 | tf_op jit(solution)/shard_map/ppermute | solution.py:288
  78.8 9.5 %collective-permute-start.13 = (bf16[2,8,8,1536]{3,2,1,0:T(8,128)(2,1)S(1)}, bf16[2,8,8,1536]{3,2,1,0:T(8,128)(2,1)S(1)}, u32[]{:S(2)}, u32[]{:S(2)}) collective-permute-start(bf16[2,8,8,1536]{3,2,1,0:T(8,128)(2,1)S(1)} %slice_select_fusion), channel_id=1, source_target_pairs={{0,1},{1,2},{2,3},{3,4},{4,5},{5,6},{6,7},{7,0},{32,39},{33,32},{3... | collective-permute-start | bytes 1179656 | tf_op jit(solution)/shard_map/ppermute | solution.py:285
  81.6 16.3 %collective-permute-start.12 = (bf16[2,16,8,1536]{3,2,1,0:T(8,128)(2,1)S(1)}, bf16[2,16,8,1536]{3,2,1,0:T(8,128)(2,1)S(1)}, u32[]{:S(2)}, u32[]{:S(2)}) collective-permute-start(bf16[2,16,8,1536]{3,2,1,0:T(8,128)(2,1)S(1)} %collective-permute-done.11.refs_0_), channel_id=1, source_target_pairs={{0,24},{8,0},{16,8},{24,16},{32,40},{40,48},{48,56},{56,32},{64,88... | collective-permute-start | bytes 2359304 | tf_op jit(solution)/shard_map/ppermute | solution.py:288
  86.6 6.8 %collective-permute-start.16 = (f32[160,384]{1,0:T(8,128)S(1)}, f32[160,384]{1,0:T(8,128)S(1)}, u32[]{:S(2)}, u32[]{:S(2)}) collective-permute-start(f32[160,384]{1,0:T(8,128)S(1)} %pad_maximum_fusion.6), channel_id=1, source_target_pairs={{0,192},{32,224},{64,0},{96,32},{128,64},{160,96},{192,128},{224,1... | collective-permute-start | bytes 737288 | tf_op jit(solution)/shard_map/ppermute | solution.py:202
  88.1 8.0 %collective-permute-start.15 = (f32[160,384]{1,0:T(8,128)S(1)}, f32[160,384]{1,0:T(8,128)S(1)}, u32[]{:S(2)}, u32[]{:S(2)}) collective-permute-start(f32[160,384]{1,0:T(8,128)S(1)} %pad_maximum_fusion.5), channel_id=1, source_target_pairs={{0,64},{32,96},{64,128},{96,160},{128,192},{160,224},{192,0},{224,... | collective-permute-start | bytes 737288 | tf_op jit(solution)/shard_map/ppermute | solution.py:201
  88.3 9.6 %collective-permute-start.14 = (bf16[2,8,8,1536]{3,2,1,0:T(8,128)(2,1)S(1)}, bf16[2,8,8,1536]{3,2,1,0:T(8,128)(2,1)S(1)}, u32[]{:S(2)}, u32[]{:S(2)}) collective-permute-start(bf16[2,8,8,1536]{3,2,1,0:T(8,128)(2,1)S(1)} %collective-permute-done.13.refs_2_), channel_id=1, source_target_pairs={{0,24},{8,0},{16,8},{24,16},{32,40},{40,48},{48,56},{56,32},{64,88... | collective-permute-start | bytes 1179656 | tf_op jit(solution)/shard_map/ppermute | solution.py:288
  99.3 5.6 %collective-permute-start.19 = (f32[96,384]{1,0:T(8,128)S(1)}, f32[96,384]{1,0:T(8,128)S(1)}, u32[]{:S(2)}, u32[]{:S(2)}) collective-permute-start(f32[96,384]{1,0:T(8,128)S(1)} %get-tuple-element.48), channel_id=1, source_target_pairs={{0,128},{32,160},{64,192},{96,224},{128,0},{160,32},{192,64},{224,... | collective-permute-start | bytes 442376 | tf_op jit(solution)/shard_map/ppermute | solution.py:333
  100.7 11.7 %collective-permute-start.17 = (f32[176,384]{1,0:T(8,128)S(1)}, f32[176,384]{1,0:T(8,128)S(1)}, u32[]{:S(2)}, u32[]{:S(2)}) collective-permute-start(f32[176,384]{1,0:T(8,128)S(1)} %pad_maximum_fusion.3), channel_id=1, source_target_pairs={{0,64},{32,96},{64,128},{96,160},{128,192},{160,224},{192,0},{224,... | collective-permute-start | bytes 811016 | tf_op jit(solution)/shard_map/ppermute | solution.py:334
  101.6 10.9 %collective-permute-start.18 = (f32[176,384]{1,0:T(8,128)S(1)}, f32[176,384]{1,0:T(8,128)S(1)}, u32[]{:S(2)}, u32[]{:S(2)}) collective-permute-start(f32[176,384]{1,0:T(8,128)S(1)} %pad_maximum_fusion.4), channel_id=1, source_target_pairs={{0,192},{32,224},{64,0},{96,32},{128,64},{160,96},{192,128},{224,1... | collective-permute-start | bytes 811016 | tf_op jit(solution)/shard_map/ppermute | solution.py:335
  112.6 2.0 %collective-permute-start.20 = (f32[256,384]{1,0:T(8,128)S(1)}, f32[256,384]{1,0:T(8,128)S(1)}, u32[]{:S(2)}, u32[]{:S(2)}) collective-permute-start(f32[256,384]{1,0:T(8,128)S(1)} %pad_maximum_fusion.2.mine_ref), channel_id=1, source_target_pairs={{0,32},{32,0},{64,96},{96,64},{128,160},{160,128},{192,224},{224,1... | collective-permute-start | bytes 1179656 | tf_op jit(solution)/shard_map/ppermute | solution.py:344

commit v14 on v10

--- a/solution.py
+++ b/solution.py
@@ -244,7 +244,7 @@
         in_specs=[SMEM, VMEM],
         out_specs=pl.BlockSpec(memory_space=pltpu.HBM),
         scratch_shapes=[pltpu.VMEM(packed.shape, packed.dtype), pltpu.SemaphoreType.DMA((groups // 2,))],
-        compiler_params=little,
+        compiler_params=pltpu.CompilerParams(vmem_limit_bytes=60 * 2**20),
     )(listed, moved)
     pair = lax.all_to_all(packed, ("grp", "row"), 0, 0, axis_index_groups=pairs, tiled=True)
 

time: 116 us -> 115 us (level)
  transfers between devices with their start and end apart: 23 -> 23, of which waited for: 15 -> 15; matrix products, arithmetic and copies ran while one was open for 5% -> 5% of each run, Pallas kernels for 9% -> 8%
where the time goes in v14:
time: 115 us
  waiting for transfers between devices  58.2 us (51%)
  starting transfers between devices  35.6 us (31%)
  Pallas kernels  11.5 us (10%)
  local copies, waits for them, and re-layouts  5.93 us (5%)
  other arithmetic  3.44 us (3%)
    ppermute x5, waiting for transfers between devices, z_step(): return lax.ppermute(block, ('grp', 'col'), along)  20.4 us
    ppermute x5, starting transfers between devices, z_step(): return lax.ppermute(block, ('grp', 'col'), along)  14.3 us
    ppermute x5, waiting for transfers between devices, y_step(): return lax.ppermute(block, ('grp', 'row'), beside)  7.61 us
    all_to_all x1, waiting for transfers between devices, body(): lax.all_to_all(amplitudes[0].reshape(groups, octet, cap), 'grp', 0, 0, ti...  7.01 us
    all_to_all x1, waiting for transfers between devices, body(): lax.all_to_all(packed, ('grp', 'row'), 0, 0, axis_index_groups=pairs, til...  6.55 us
    all_to_all x1, starting transfers between devices, body(): lax.all_to_all(packed, ('grp', 'row'), 0, 0, axis_index_groups=pairs, til...  4.84 us
    ppermute x1, waiting for transfers between devices, body(): lax.ppermute(jnp.concatenate([late[1], early[1, :h] + a[:h]]), 'grp', up)  4.32 us
    all_to_all x1, starting transfers between devices, body(): lax.all_to_all(amplitudes[0].reshape(groups, octet, cap), 'grp', 0, 0, ti...  4.15 us
  transfers between devices with their start and end apart: 23, of which 15 were waited for; matrix products, arithmetic and copies ran while one was open for 5% of the time, Pallas kernels for 8%

profile of v14, /device:TPU:1, one launch (start us, length us, event | category | flops | bytes accessed | tf_op | source)
XLA Modules:
  0.0 114.9 jit_solution(8886812163784815020)
XLA Ops:
  0.0 3.2 %collective-permute-start = (bf16[4608,384]{1,0:T(8,128)(2,1)}, bf16[4608,384]{1,0:T(8,128)(2,1)S(1)}, u32[]{:S(2)}, u32[]{:S(2)}) collective-permute-start(bf16[4608,384]{1,0:T(8,128)(2,1)} %bitcast.40), channel_id=1, source_target_pairs={{0,32},{32,0},{64,96},{96,64},{128,160},{160,128},{192,224},{224,1... | collective-permute-start | bytes 10616840 | tf_op jit(solution)/shard_map/ppermute | solution.py:228
  3.2 4.1 %all-to-all-start = ((bf16[8,8,4608]{2,1,0:T(8,128)(2,1)}), bf16[8,8,4608]{2,1,0:T(8,128)(2,1)}, u32[]{:S(2)}, u32[]{:S(2)}) async-start(bf16[8,8,4608]{2,1,0:T(8,128)(2,1)} %bitcast.43), calls=%async_computation | async-start | bytes 1179648 | tf_op jit(solution)/shard_map/all_to_all | solution.py:229
  7.4 0.7 pad_add_fusion.both_ref
  8.1 2.0 %shard_map.46.list_ref = s32[96]{0:T(128)S(1)} custom-call(s32[2,8]{1,0:T(2,128)S(1)} %pad_add_fusion.both_ref), custom_call_target="tpu_custom_call" | custom-call | tf_op jit(solution)/shard_map/pallas_call | solution.py:232
  10.0 0.0 copy-start.3
  10.1 0.6 copy-done.3
  10.6 7.0 %all-to-all-done.src_ref = bf16[8,8,4608]{2,1,0:T(8,128)(2,1)} async-done(((bf16[8,8,4608]{2,1,0:T(8,128)(2,1)}), bf16[8,8,4608]{2,1,0:T(8,128)(2,1)}, u32[]{:S(2)}, u32[]{:S(2)}) %all-to-all-start) | async-done | bytes 589856 | tf_op jit(solution)/shard_map/all_to_all | solution.py:229
  17.6 2.0 %shard_map.47 = bf16[16,8,1536]{2,1,0:T(8,128)(2,1)} custom-call(s32[96]{0:T(128)} %copy-done.3, bf16[8,8,4608]{2,1,0:T(8,128)(2,1)} %all-to-all-done.src_ref), custom_call_target="tpu_custom_call" | custom-call | tf_op jit(solution)/shard_map/pallas_call | solution.py:241
  19.6 4.8 %all-to-all-start.1 = ((bf16[16,8,1536]{2,1,0:T(8,128)(2,1)}), bf16[16,8,1536]{2,1,0:T(8,128)(2,1)}, u32[]{:S(2)}, u32[]{:S(2)}) async-start(bf16[16,8,1536]{2,1,0:T(8,128)(2,1)} %shard_map.47), calls=%async_computation.1 | async-start | bytes 786432 | tf_op jit(solution)/shard_map/all_to_all | solution.py:249
  24.5 0.0 collective-permute-done.other_ref
  24.5 0.0 copy-start
  24.5 2.0 %copy-done = bf16[1,4608,384]{2,1,0:T(8,128)(2,1)S(1)} copy-done((bf16[1,4608,384]{2,1,0:T(8,128)(2,1)S(1)}, bf16[1,4608,384]{2,1,0:T(8,128)(2,1)}, u32[]{:S(2)}) %copy-start) | copy-done | bytes 3538968
  26.5 0.9 shard_map.48
  27.4 1.4 %copy-done.2 = bf16[3072,384]{1,0:T(8,128)(2,1)} copy-done((bf16[3072,384]{1,0:T(8,128)(2,1)}, bf16[3072,384]{1,0:T(8,128)(2,1)S(1)}, u32[]{:S(2)}) %copy-start.2) | copy-done | bytes 2359320
  28.8 6.5 %all-to-all-done.1 = bf16[16,8,1536]{2,1,0:T(8,128)(2,1)} async-done(((bf16[16,8,1536]{2,1,0:T(8,128)(2,1)}), bf16[16,8,1536]{2,1,0:T(8,128)(2,1)}, u32[]{:S(2)}, u32[]{:S(2)}) %all-to-all-start.1) | async-done | bytes 393248 | tf_op jit(solution)/shard_map/all_to_all | solution.py:249
  35.3 0.4 collective-permute-start.7
  35.7 0.0 collective-permute-start.1
  35.7 5.3 %collective-permute-start.2 = (bf16[16,8,1536]{2,1,0:T(8,128)(2,1)}, bf16[16,8,1536]{2,1,0:T(8,128)(2,1)}, u32[]{:S(2)}, u32[]{:S(2)}) collective-permute-start(bf16[16,8,1536]{2,1,0:T(8,128)(2,1)} %all-to-all-done.1), channel_id=1, source_target_pairs={{0,1},{1,2},{2,3},{3,4},{4,5},{5,6},{6,7},{7,0},{32,39},{33,32},{3... | collective-permute-start | bytes 1179656 | tf_op jit(solution)/shard_map/ppermute | solution.py:268
  41.0 0.0 collective-permute-done.1
  41.0 2.1 %collective-permute-start.3 = (bf16[16,8,1536]{2,1,0:T(8,128)(2,1)}, bf16[16,8,1536]{2,1,0:T(8,128)(2,1)}, u32[]{:S(2)}, u32[]{:S(2)}) collective-permute-start(bf16[16,8,1536]{2,1,0:T(8,128)(2,1)} %collective-permute-done.1), channel_id=1, source_target_pairs={{0,1},{1,2},{2,3},{3,4},{4,5},{5,6},{6,7},{7,0},{32,39},{33,32},{3... | collective-permute-start | bytes 1179656 | tf_op jit(solution)/shard_map/ppermute | solution.py:268
  43.1 1.3 %fusion.1.refs_0_ = bf16[2,8,8,1536]{3,2,1,0:T(8,128)(2,1)S(1)} fusion(bf16[1,16,8,1536]{3,2,1,0:T(8,128)(2,1)} %bitcast.4, bf16[1,16,8,1536]{3,2,1,0:T(8,128)(2,1)} %bitcast.5, pred[]{:T(512)S(6)} %eq.4), kind=kLoop, calls=%fused_computation.4 | loop fusion | flops 589824 | bytes 1179649 | tf_op jit(solution)/shard_map/jit(_where)/select_n | solution.py:265
  44.4 0.5 collective-permute-start.4
  44.9 1.2 %collective-permute-done.2 = bf16[16,8,1536]{2,1,0:T(8,128)(2,1)} collective-permute-done((bf16[16,8,1536]{2,1,0:T(8,128)(2,1)}, bf16[16,8,1536]{2,1,0:T(8,128)(2,1)}, u32[]{:S(2)}, u32[]{:S(2)}) %collective-permute-start.2) | collective-permute-done | bytes 393248 | tf_op jit(solution)/shard_map/ppermute | solution.py:268
  46.1 4.2 %collective-permute-done.3 = bf16[16,8,1536]{2,1,0:T(8,128)(2,1)} collective-permute-done((bf16[16,8,1536]{2,1,0:T(8,128)(2,1)}, bf16[16,8,1536]{2,1,0:T(8,128)(2,1)}, u32[]{:S(2)}, u32[]{:S(2)}) %collective-permute-start.3) | collective-permute-done | bytes 393248 | tf_op jit(solution)/shard_map/ppermute | solution.py:268
  50.3 1.2 %pad_maximum_fusion.refs_2_ = bf16[2,16,8,1536]{3,2,1,0:T(8,128)(2,1)S(1)} fusion(bf16[1,16,8,1536]{3,2,1,0:T(8,128)(2,1)} %bitcast.7, bf16[1,16,8,1536]{3,2,1,0:T(8,128)(2,1)} %bitcast.6), kind=kLoop, calls=%fused_computation.2 | loop fusion | flops 393216 | bytes 1572864 | tf_op jit(solution)/shard_map/stack | solution.py:276
  51.5 0.0 copy-start.1
  51.5 1.2 %collective-permute-done.4.refs_1_ = bf16[2,8,8,1536]{3,2,1,0:T(8,128)(2,1)S(1)} collective-permute-done((bf16[2,8,8,1536]{3,2,1,0:T(8,128)(2,1)S(1)}, bf16[2,8,8,1536]{3,2,1,0:T(8,128)(2,1)S(1)}, u32[]{:S(2)}, u32[]{:S(2)}) %collective-permute-start.4) | collective-permute-done | bytes 393248 | tf_op jit(solution)/shard_map/ppermute | solution.py:271
  52.7 2.3 %collective-permute-start.5 = (bf16[2,16,8,1536]{3,2,1,0:T(8,128)(2,1)S(1)}, bf16[2,16,8,1536]{3,2,1,0:T(8,128)(2,1)S(1)}, u32[]{:S(2)}, u32[]{:S(2)}) collective-permute-start(bf16[2,16,8,1536]{3,2,1,0:T(8,128)(2,1)S(1)} %pad_maximum_fusion.refs_2_), channel_id=1, source_target_pairs={{0,1},{1,2},{2,3},{3,4},{4,5},{5,6},{6,7},{7,0},{32,39},{33,32},{3... | collective-permute-start | bytes 2359304 | tf_op jit(solution)/shard_map/ppermute | solution.py:268
  55.0 0.4 collective-permute-start.6
  55.4 8.6 %collective-permute-done.5.refs_4_ = bf16[2,16,8,1536]{3,2,1,0:T(8,128)(2,1)S(1)} collective-permute-done((bf16[2,16,8,1536]{3,2,1,0:T(8,128)(2,1)S(1)}, bf16[2,16,8,1536]{3,2,1,0:T(8,128)(2,1)S(1)}, u32[]{:S(2)}, u32[]{:S(2)}) %collective-permute-start.5) | collective-permute-done | bytes 786464 | tf_op jit(solution)/shard_map/ppermute | solution.py:268
  63.9 3.1 %collective-permute-done.6.refs_3_ = bf16[2,16,8,1536]{3,2,1,0:T(8,128)(2,1)S(1)} collective-permute-done((bf16[2,16,8,1536]{3,2,1,0:T(8,128)(2,1)S(1)}, bf16[2,16,8,1536]{3,2,1,0:T(8,128)(2,1)S(1)}, u32[]{:S(2)}, u32[]{:S(2)}) %collective-permute-start.6) | collective-permute-done | bytes 786464 | tf_op jit(solution)/shard_map/ppermute | solution.py:271
  67.0 0.0 collective-permute-done.7.got_ref
  67.0 1.8 %collective-permute-start.11 = (bf16[2,16,8,1536]{3,2,1,0:T(8,128)(2,1)S(1)}, bf16[2,16,8,1536]{3,2,1,0:T(8,128)(2,1)S(1)}, u32[]{:S(2)}, u32[]{:S(2)}) collective-permute-start(bf16[2,16,8,1536]{3,2,1,0:T(8,128)(2,1)S(1)} %collective-permute-done.5.refs_4_), channel_id=1, source_target_pairs={{0,1},{1,2},{2,3},{3,4},{4,5},{5,6},{6,7},{7,0},{32,39},{33,32},{3... | collective-permute-start | bytes 2359304 | tf_op jit(solution)/shard_map/ppermute | solution.py:268
  68.9 1.9 %fusion.7 = (bf16[1536,384]{1,0:T(8,128)(2,1)S(1)}, bf16[1536,384]{1,0:T(8,128)(2,1)S(1)}) fusion(bf16[3072,384]{1,0:T(8,128)(2,1)} %collective-permute-done.7.got_ref), kind=kLoop, calls=%fused_computation.31 | loop fusion | bytes 4718592 | tf_op jit(solution)/shard_map/split | solution.py:286
  70.7 0.1 collective-permute-start.10
  70.8 0.5 collective-permute-start.9
  71.3 0.4 collective-permute-start.8
  71.7 6.5 %collective-permute-done.11.refs_0_ = bf16[2,16,8,1536]{3,2,1,0:T(8,128)(2,1)S(1)} collective-permute-done((bf16[2,16,8,1536]{3,2,1,0:T(8,128)(2,1)S(1)}, bf16[2,16,8,1536]{3,2,1,0:T(8,128)(2,1)S(1)}, u32[]{:S(2)}, u32[]{:S(2)}) %collective-permute-start.11) | collective-permute-done | bytes 786464 | tf_op jit(solution)/shard_map/ppermute | solution.py:268
  78.2 2.8 %collective-permute-start.13 = (bf16[2,8,8,1536]{3,2,1,0:T(8,128)(2,1)S(1)}, bf16[2,8,8,1536]{3,2,1,0:T(8,128)(2,1)S(1)}, u32[]{:S(2)}, u32[]{:S(2)}) collective-permute-start(bf16[2,8,8,1536]{3,2,1,0:T(8,128)(2,1)S(1)} %slice_select_fusion), channel_id=1, source_target_pairs={{0,1},{1,2},{2,3},{3,4},{4,5},{5,6},{6,7},{7,0},{32,39},{33,32},{3... | collective-permute-start | bytes 1179656 | tf_op jit(solution)/shard_map/ppermute | solution.py:268
  81.0 0.4 collective-permute-start.12
  81.4 0.0 collective-permute-done.10.refs_1_
  81.4 0.0 collective-permute-done.9.refs_0_
  81.4 2.3 %shard_map.49.refs_6_.refs_4_ = bf16[3072,384]{1,0:T(8,128)(2,1)S(1)} custom-call(s32[2,8]{1,0:T(2,128)S(1)} %pad_add_fusion.both_ref, bf16[4608,384]{1,0:T(8,128)(2,1)S(1)} %bitcast.42, bf16[4608,384]{1,0:T(8,128)(2,1)S(1)} %collective-permute-done.other_ref, bf16[3072,384]{1,0:T(8,128)(2,1)} %collective-permute-done.7.got_ref, ...), custom_call_target="tpu_custom_call" | custom-call | tf_op jit(solution)/shard_map/pallas_call | solution.py:290
  83.7 0.0 collective-permute-done.8.refs_5_
  83.8 2.2 %shard_map.50 = f32[4,160,384]{2,1,0:T(8,128)S(1)} custom-call(bf16[2,8,8,1536]{3,2,1,0:T(8,128)(2,1)S(1)} %fusion.1.refs_0_, bf16[2,8,8,1536]{3,2,1,0:T(8,128)(2,1)S(1)} %collective-permute-done.4.refs_1_, bf16[2,16,8,1536]{3,2,1,0:T(8,128)(2,1)S(1)} %pad_maximum_fusion.refs_2_, bf16[2,16,8,1536]{3,2,1,0:T(8,128)(2,1)S(1)} %collective-permute-done.6.refs_3_, ...), custom_call_target="tpu_custom_call" | custom-call | tf_op jit(solution)/shard_map/pallas_call | solution.py:301
  86.0 0.0 collective-permute-done.13.refs_2_
  86.0 0.1 collective-permute-start.14
  86.2 1.8 %collective-permute-start.16 = (f32[160,384]{1,0:T(8,128)S(1)}, f32[160,384]{1,0:T(8,128)S(1)}, u32[]{:S(2)}, u32[]{:S(2)}) collective-permute-start(f32[160,384]{1,0:T(8,128)S(1)} %pad_maximum_fusion.6), channel_id=1, source_target_pairs={{0,192},{32,224},{64,0},{96,32},{128,64},{160,96},{192,128},{224,1... | collective-permute-start | bytes 737288 | tf_op jit(solution)/shard_map/ppermute | solution.py:202
  88.0 0.1 collective-permute-start.15
  88.0 3.5 %collective-permute-done.16 = f32[160,384]{1,0:T(8,128)S(1)} collective-permute-done((f32[160,384]{1,0:T(8,128)S(1)}, f32[160,384]{1,0:T(8,128)S(1)}, u32[]{:S(2)}, u32[]{:S(2)}) %collective-permute-start.16) | collective-permute-done | bytes 245792 | tf_op jit(solution)/shard_map/ppermute | solution.py:202
  91.6 2.7 %collective-permute-done.15 = f32[160,384]{1,0:T(8,128)S(1)} collective-permute-done((f32[160,384]{1,0:T(8,128)S(1)}, f32[160,384]{1,0:T(8,128)S(1)}, u32[]{:S(2)}, u32[]{:S(2)}) %collective-permute-start.15) | collective-permute-done | bytes 245792 | tf_op jit(solution)/shard_map/ppermute | solution.py:201
  94.3 3.3 %collective-permute-done.14.refs_3_ = bf16[2,8,8,1536]{3,2,1,0:T(8,128)(2,1)S(1)} collective-permute-done((bf16[2,8,8,1536]{3,2,1,0:T(8,128)(2,1)S(1)}, bf16[2,8,8,1536]{3,2,1,0:T(8,128)(2,1)S(1)}, u32[]{:S(2)}, u32[]{:S(2)}) %collective-permute-start.14) | collective-permute-done | bytes 393248 | tf_op jit(solution)/shard_map/ppermute | solution.py:271
  97.6 0.0 collective-permute-done.12.refs_1_
  97.6 1.4 %shard_map.51 = f32[4,96,384]{2,1,0:T(8,128)S(1)} custom-call(bf16[2,16,8,1536]{3,2,1,0:T(8,128)(2,1)S(1)} %collective-permute-done.11.refs_0_, bf16[2,16,8,1536]{3,2,1,0:T(8,128)(2,1)S(1)} %collective-permute-done.12.refs_1_, bf16[2,8,8,1536]{3,2,1,0:T(8,128)(2,1)S(1)} %collective-permute-done.13.refs_2_, ...), custom_call_target="tpu_custom_call" | custom-call | tf_op jit(solution)/shard_map/pallas_call | solution.py:301
  99.1 0.1 collective-permute-start.17
  99.2 2.7 %collective-permute-start.18 = (f32[176,384]{1,0:T(8,128)S(1)}, f32[176,384]{1,0:T(8,128)S(1)}, u32[]{:S(2)}, u32[]{:S(2)}) collective-permute-start(f32[176,384]{1,0:T(8,128)S(1)} %pad_maximum_fusion.4), channel_id=1, source_target_pairs={{0,192},{32,224},{64,0},{96,32},{128,64},{160,96},{192,128},{224,1... | collective-permute-start | bytes 811016 | tf_op jit(solution)/shard_map/ppermute | solution.py:317
  101.9 0.0 collective-permute-start.19
  102.0 4.3 %collective-permute-done.17 = f32[176,384]{1,0:T(8,128)S(1)} collective-permute-done((f32[176,384]{1,0:T(8,128)S(1)}, f32[176,384]{1,0:T(8,128)S(1)}, u32[]{:S(2)}, u32[]{:S(2)}) %collective-permute-start.17) | collective-permute-done | bytes 270368 | tf_op jit(solution)/shard_map/ppermute | solution.py:316
  106.3 0.9 collective-permute-done.18
  107.2 0.1 fusion.3
  107.2 3.8 %collective-permute-done.19 = f32[96,384]{1,0:T(8,128)S(1)} collective-permute-done((f32[96,384]{1,0:T(8,128)S(1)}, f32[96,384]{1,0:T(8,128)S(1)}, u32[]{:S(2)}, u32[]{:S(2)}) %collective-permute-start.19) | collective-permute-done | bytes 147488 | tf_op jit(solution)/shard_map/ppermute | solution.py:315
  111.1 1.6 %collective-permute-start.20 = (f32[256,384]{1,0:T(8,128)S(1)}, f32[256,384]{1,0:T(8,128)S(1)}, u32[]{:S(2)}, u32[]{:S(2)}) collective-permute-start(f32[256,384]{1,0:T(8,128)S(1)} %pad_maximum_fusion.2.mine_ref), channel_id=1, source_target_pairs={{0,32},{32,0},{64,96},{96,64},{128,160},{160,128},{192,224},{224,1... | collective-permute-start | bytes 1179656 | tf_op jit(solution)/shard_map/ppermute | solution.py:326
  112.7 1.3 %collective-permute-done.20.other_ref = f32[256,384]{1,0:T(8,128)S(1)} collective-permute-done((f32[256,384]{1,0:T(8,128)S(1)}, f32[256,384]{1,0:T(8,128)S(1)}, u32[]{:S(2)}, u32[]{:S(2)}) %collective-permute-start.20) | collective-permute-done | bytes 393248 | tf_op jit(solution)/shard_map/ppermute | solution.py:326
  114.1 0.8 shard_map.52
  (14 shorter events, 0.3 us)
Async XLA Ops:
  0.0 24.5 %collective-permute-start = (bf16[4608,384]{1,0:T(8,128)(2,1)}, bf16[4608,384]{1,0:T(8,128)(2,1)S(1)}, u32[]{:S(2)}, u32[]{:S(2)}) collective-permute-start(bf16[4608,384]{1,0:T(8,128)(2,1)} %bitcast.40), channel_id=1, source_target_pairs={{0,32},{32,0},{64,96},{96,64},{128,160},{160,128},{192,224},{224,1... | collective-permute-start | bytes 10616840 | tf_op jit(solution)/shard_map/ppermute | solution.py:228
  3.2 14.4 %all-to-all-start = ((bf16[8,8,4608]{2,1,0:T(8,128)(2,1)}), bf16[8,8,4608]{2,1,0:T(8,128)(2,1)}, u32[]{:S(2)}, u32[]{:S(2)}) async-start(bf16[8,8,4608]{2,1,0:T(8,128)(2,1)} %bitcast.43), calls=%async_computation | async-start | bytes 1179648 | tf_op jit(solution)/shard_map/all_to_all | solution.py:229
  10.0 0.6 copy-start.3
  19.6 15.7 %all-to-all-start.1 = ((bf16[16,8,1536]{2,1,0:T(8,128)(2,1)}), bf16[16,8,1536]{2,1,0:T(8,128)(2,1)}, u32[]{:S(2)}, u32[]{:S(2)}) async-start(bf16[16,8,1536]{2,1,0:T(8,128)(2,1)} %shard_map.47), calls=%async_computation.1 | async-start | bytes 786432 | tf_op jit(solution)/shard_map/all_to_all | solution.py:249
  24.5 2.0 %copy-start = (bf16[1,4608,384]{2,1,0:T(8,128)(2,1)S(1)}, bf16[1,4608,384]{2,1,0:T(8,128)(2,1)}, u32[]{:S(2)}) copy-start(bf16[1,4608,384]{2,1,0:T(8,128)(2,1)} %param.5) | copy-start | bytes 10616836
  27.3 1.4 %copy-start.2 = (bf16[3072,384]{1,0:T(8,128)(2,1)}, bf16[3072,384]{1,0:T(8,128)(2,1)S(1)}, u32[]{:S(2)}) copy-start(bf16[3072,384]{1,0:T(8,128)(2,1)S(1)} %shard_map.48) | copy-start | bytes 7077892
  35.3 31.7 %collective-permute-start.7 = (bf16[3072,384]{1,0:T(8,128)(2,1)}, bf16[3072,384]{1,0:T(8,128)(2,1)}, u32[]{:S(2)}, u32[]{:S(2)}) collective-permute-start(bf16[3072,384]{1,0:T(8,128)(2,1)} %copy-done.2), channel_id=1, source_target_pairs={{0,64},{32,224},{64,128},{96,32},{128,192},{160,96},{192,0},{224,1... | collective-permute-start | bytes 7077896 | tf_op jit(solution)/shard_map/ppermute | solution.py:262
  35.7 5.3 %collective-permute-start.1 = (bf16[16,8,1536]{2,1,0:T(8,128)(2,1)}, bf16[16,8,1536]{2,1,0:T(8,128)(2,1)}, u32[]{:S(2)}, u32[]{:S(2)}) collective-permute-start(bf16[16,8,1536]{2,1,0:T(8,128)(2,1)} %all-to-all-done.1), channel_id=1, source_target_pairs={{0,32},{32,0},{64,96},{96,64},{128,160},{160,128},{192,224},{224,1... | collective-permute-start | bytes 1179656 | tf_op jit(solution)/shard_map/ppermute | solution.py:273
  35.7 10.3 %collective-permute-start.2 = (bf16[16,8,1536]{2,1,0:T(8,128)(2,1)}, bf16[16,8,1536]{2,1,0:T(8,128)(2,1)}, u32[]{:S(2)}, u32[]{:S(2)}) collective-permute-start(bf16[16,8,1536]{2,1,0:T(8,128)(2,1)} %all-to-all-done.1), channel_id=1, source_target_pairs={{0,1},{1,2},{2,3},{3,4},{4,5},{5,6},{6,7},{7,0},{32,39},{33,32},{3... | collective-permute-start | bytes 1179656 | tf_op jit(solution)/shard_map/ppermute | solution.py:268
  41.0 9.2 %collective-permute-start.3 = (bf16[16,8,1536]{2,1,0:T(8,128)(2,1)}, bf16[16,8,1536]{2,1,0:T(8,128)(2,1)}, u32[]{:S(2)}, u32[]{:S(2)}) collective-permute-start(bf16[16,8,1536]{2,1,0:T(8,128)(2,1)} %collective-permute-done.1), channel_id=1, source_target_pairs={{0,1},{1,2},{2,3},{3,4},{4,5},{5,6},{6,7},{7,0},{32,39},{33,32},{3... | collective-permute-start | bytes 1179656 | tf_op jit(solution)/shard_map/ppermute | solution.py:268
  44.4 8.3 %collective-permute-start.4 = (bf16[2,8,8,1536]{3,2,1,0:T(8,128)(2,1)S(1)}, bf16[2,8,8,1536]{3,2,1,0:T(8,128)(2,1)S(1)}, u32[]{:S(2)}, u32[]{:S(2)}) collective-permute-start(bf16[2,8,8,1536]{3,2,1,0:T(8,128)(2,1)S(1)} %fusion.1.refs_0_), channel_id=1, source_target_pairs={{0,24},{8,0},{16,8},{24,16},{32,40},{40,48},{48,56},{56,32},{64,88... | collective-permute-start | bytes 1179656 | tf_op jit(solution)/shard_map/ppermute | solution.py:271
  51.5 30.0 %copy-start.1 = (bf16[1,4608,384]{2,1,0:T(8,128)(2,1)S(1)}, bf16[1,4608,384]{2,1,0:T(8,128)(2,1)}, u32[]{:S(2)}) copy-start(bf16[1,4608,384]{2,1,0:T(8,128)(2,1)} %param.5) | copy-start | bytes 10616836
  52.7 11.2 %collective-permute-start.5 = (bf16[2,16,8,1536]{3,2,1,0:T(8,128)(2,1)S(1)}, bf16[2,16,8,1536]{3,2,1,0:T(8,128)(2,1)S(1)}, u32[]{:S(2)}, u32[]{:S(2)}) collective-permute-start(bf16[2,16,8,1536]{3,2,1,0:T(8,128)(2,1)S(1)} %pad_maximum_fusion.refs_2_), channel_id=1, source_target_pairs={{0,1},{1,2},{2,3},{3,4},{4,5},{5,6},{6,7},{7,0},{32,39},{33,32},{3... | collective-permute-start | bytes 2359304 | tf_op jit(solution)/shard_map/ppermute | solution.py:268
  55.0 12.1 %collective-permute-start.6 = (bf16[2,16,8,1536]{3,2,1,0:T(8,128)(2,1)S(1)}, bf16[2,16,8,1536]{3,2,1,0:T(8,128)(2,1)S(1)}, u32[]{:S(2)}, u32[]{:S(2)}) collective-permute-start(bf16[2,16,8,1536]{3,2,1,0:T(8,128)(2,1)S(1)} %pad_maximum_fusion.refs_2_), channel_id=1, source_target_pairs={{0,24},{8,0},{16,8},{24,16},{32,40},{40,48},{48,56},{56,32},{64,88... | collective-permute-start | bytes 2359304 | tf_op jit(solution)/shard_map/ppermute | solution.py:271
  67.0 11.1 %collective-permute-start.11 = (bf16[2,16,8,1536]{3,2,1,0:T(8,128)(2,1)S(1)}, bf16[2,16,8,1536]{3,2,1,0:T(8,128)(2,1)S(1)}, u32[]{:S(2)}, u32[]{:S(2)}) collective-permute-start(bf16[2,16,8,1536]{3,2,1,0:T(8,128)(2,1)S(1)} %collective-permute-done.5.refs_4_), channel_id=1, source_target_pairs={{0,1},{1,2},{2,3},{3,4},{4,5},{5,6},{6,7},{7,0},{32,39},{33,32},{3... | collective-permute-start | bytes 2359304 | tf_op jit(solution)/shard_map/ppermute | solution.py:268
  70.7 10.7 %collective-permute-start.10 = (bf16[1536,384]{1,0:T(8,128)(2,1)S(1)}, bf16[1536,384]{1,0:T(8,128)(2,1)S(1)}, u32[]{:S(2)}, u32[]{:S(2)}) collective-permute-start(bf16[1536,384]{1,0:T(8,128)(2,1)S(1)} %get-tuple-element.35), channel_id=1, source_target_pairs={{0,32},{32,0},{64,96},{96,64},{128,160},{160,128},{192,224},{224,1... | collective-permute-start | bytes 3538952 | tf_op jit(solution)/shard_map/ppermute | solution.py:286
  70.8 10.6 %collective-permute-start.9 = (bf16[1536,384]{1,0:T(8,128)(2,1)S(1)}, bf16[1536,384]{1,0:T(8,128)(2,1)S(1)}, u32[]{:S(2)}, u32[]{:S(2)}) collective-permute-start(bf16[1536,384]{1,0:T(8,128)(2,1)S(1)} %get-tuple-element.36), channel_id=1, source_target_pairs={{0,32},{32,0},{64,96},{96,64},{128,160},{160,128},{192,224},{224,1... | collective-permute-start | bytes 3538952 | tf_op jit(solution)/shard_map/ppermute | solution.py:286
  71.3 12.4 %collective-permute-start.8 = (bf16[2,16,8,1536]{3,2,1,0:T(8,128)(2,1)S(1)}, bf16[2,16,8,1536]{3,2,1,0:T(8,128)(2,1)S(1)}, u32[]{:S(2)}, u32[]{:S(2)}) collective-permute-start(bf16[2,16,8,1536]{3,2,1,0:T(8,128)(2,1)S(1)} %collective-permute-done.5.refs_4_), channel_id=1, source_target_pairs={{0,24},{8,0},{16,8},{24,16},{32,40},{40,48},{48,56},{56,32},{64,88... | collective-permute-start | bytes 2359304 | tf_op jit(solution)/shard_map/ppermute | solution.py:271
  78.2 7.8 %collective-permute-start.13 = (bf16[2,8,8,1536]{3,2,1,0:T(8,128)(2,1)S(1)}, bf16[2,8,8,1536]{3,2,1,0:T(8,128)(2,1)S(1)}, u32[]{:S(2)}, u32[]{:S(2)}) collective-permute-start(bf16[2,8,8,1536]{3,2,1,0:T(8,128)(2,1)S(1)} %slice_select_fusion), channel_id=1, source_target_pairs={{0,1},{1,2},{2,3},{3,4},{4,5},{5,6},{6,7},{7,0},{32,39},{33,32},{3... | collective-permute-start | bytes 1179656 | tf_op jit(solution)/shard_map/ppermute | solution.py:268
  81.0 16.6 %collective-permute-start.12 = (bf16[2,16,8,1536]{3,2,1,0:T(8,128)(2,1)S(1)}, bf16[2,16,8,1536]{3,2,1,0:T(8,128)(2,1)S(1)}, u32[]{:S(2)}, u32[]{:S(2)}) collective-permute-start(bf16[2,16,8,1536]{3,2,1,0:T(8,128)(2,1)S(1)} %collective-permute-done.11.refs_0_), channel_id=1, source_target_pairs={{0,24},{8,0},{16,8},{24,16},{32,40},{40,48},{48,56},{56,32},{64,88... | collective-permute-start | bytes 2359304 | tf_op jit(solution)/shard_map/ppermute | solution.py:271
  86.0 11.6 %collective-permute-start.14 = (bf16[2,8,8,1536]{3,2,1,0:T(8,128)(2,1)S(1)}, bf16[2,8,8,1536]{3,2,1,0:T(8,128)(2,1)S(1)}, u32[]{:S(2)}, u32[]{:S(2)}) collective-permute-start(bf16[2,8,8,1536]{3,2,1,0:T(8,128)(2,1)S(1)} %collective-permute-done.13.refs_2_), channel_id=1, source_target_pairs={{0,24},{8,0},{16,8},{24,16},{32,40},{40,48},{48,56},{56,32},{64,88... | collective-permute-start | bytes 1179656 | tf_op jit(solution)/shard_map/ppermute | solution.py:271
  86.2 5.4 %collective-permute-start.16 = (f32[160,384]{1,0:T(8,128)S(1)}, f32[160,384]{1,0:T(8,128)S(1)}, u32[]{:S(2)}, u32[]{:S(2)}) collective-permute-start(f32[160,384]{1,0:T(8,128)S(1)} %pad_maximum_fusion.6), channel_id=1, source_target_pairs={{0,192},{32,224},{64,0},{96,32},{128,64},{160,96},{192,128},{224,1... | collective-permute-start | bytes 737288 | tf_op jit(solution)/shard_map/ppermute | solution.py:202
  88.0 6.3 %collective-permute-start.15 = (f32[160,384]{1,0:T(8,128)S(1)}, f32[160,384]{1,0:T(8,128)S(1)}, u32[]{:S(2)}, u32[]{:S(2)}) collective-permute-start(f32[160,384]{1,0:T(8,128)S(1)} %pad_maximum_fusion.5), channel_id=1, source_target_pairs={{0,64},{32,96},{64,128},{96,160},{128,192},{160,224},{192,0},{224,... | collective-permute-start | bytes 737288 | tf_op jit(solution)/shard_map/ppermute | solution.py:201
  99.1 7.2 %collective-permute-start.17 = (f32[176,384]{1,0:T(8,128)S(1)}, f32[176,384]{1,0:T(8,128)S(1)}, u32[]{:S(2)}, u32[]{:S(2)}) collective-permute-start(f32[176,384]{1,0:T(8,128)S(1)} %pad_maximum_fusion.3), channel_id=1, source_target_pairs={{0,64},{32,96},{64,128},{96,160},{128,192},{160,224},{192,0},{224,... | collective-permute-start | bytes 811016 | tf_op jit(solution)/shard_map/ppermute | solution.py:316
  99.2 8.0 %collective-permute-start.18 = (f32[176,384]{1,0:T(8,128)S(1)}, f32[176,384]{1,0:T(8,128)S(1)}, u32[]{:S(2)}, u32[]{:S(2)}) collective-permute-start(f32[176,384]{1,0:T(8,128)S(1)} %pad_maximum_fusion.4), channel_id=1, source_target_pairs={{0,192},{32,224},{64,0},{96,32},{128,64},{160,96},{192,128},{224,1... | collective-permute-start | bytes 811016 | tf_op jit(solution)/shard_map/ppermute | solution.py:317
  101.9 9.1 %collective-permute-start.19 = (f32[96,384]{1,0:T(8,128)S(1)}, f32[96,384]{1,0:T(8,128)S(1)}, u32[]{:S(2)}, u32[]{:S(2)}) collective-permute-start(f32[96,384]{1,0:T(8,128)S(1)} %get-tuple-element.44), channel_id=1, source_target_pairs={{0,128},{32,160},{64,192},{96,224},{128,0},{160,32},{192,64},{224,... | collective-permute-start | bytes 442376 | tf_op jit(solution)/shard_map/ppermute | solution.py:315
  111.1 2.9 %collective-permute-start.20 = (f32[256,384]{1,0:T(8,128)S(1)}, f32[256,384]{1,0:T(8,128)S(1)}, u32[]{:S(2)}, u32[]{:S(2)}) collective-permute-start(f32[256,384]{1,0:T(8,128)S(1)} %pad_maximum_fusion.2.mine_ref), channel_id=1, source_target_pairs={{0,32},{32,0},{64,96},{96,64},{128,160},{160,128},{192,224},{224,1... | collective-permute-start | bytes 1179656 | tf_op jit(solution)/shard_map/ppermute | solution.py:326
